TPU v7x, 128 devices: a whole 4x4x4 slice. The times are simulated.
128 devices in a mesh: branch: 8 (over z, core), tensor: 16 (over x, y).
Axes of the slice: x: 4, y: 4, z: 4, core: 2. Of those that a mesh axis runs over, the one named last changes fastest.
Arguments:
- tokens: bfloat16 [4096, 8192], P('branch', 'tensor'), may hold values from -6 to 6
- gain: bfloat16 [8192], replicated, may hold values from 0.099609375 to 1.8984375
- w_query: bfloat16 [8192, 8192], P(None, 'tensor'), may hold values from -0.0625 to 0.0625
- w_keyvalue: bfloat16 [2, 8192, 1024], P(None, 'tensor'), may hold values from -0.0625 to 0.0625
- w_output: bfloat16 [8192, 8192], P('tensor'), may hold values from -0.0625 to 0.0625
- cache: bfloat16 [2, 128, 64, 1024], P(None, 'branch'), may hold values from -800 to 800
- parents: int32 [64, 4], replicated, may hold values from 0 to 127, as said below
- lengths: int32 [64], replicated, may hold values from 1 to 4
Outputs:
- attended: bfloat16 [4096, 8192], P('branch', 'tensor')
Inputs may be any that keep to these rules, and one draw needn't show every extreme that they name: `parents`: block p lies with owner p // 16. The entries of one branch's list lie with different owners; entries at or past the branch's length are unused but follow the same rules. The branches of one index of branch name at most 4 distinct blocks of any one owner, and exactly 4 of some owner.
All inputs are finite; a program needn't handle non-finite values.
Results may differ from a plain program's by a relative error of at most 0.025.
Values may be sent and summed in bfloat16 or wider, within the bound.
No kernel may reach another device: no remote copies, remote signals or barrier semaphores. Data moves between devices by JAX's collectives and lax.ppermute only.
A program may use at most 128 MiB of HBM per device.

v0:
```python
import math

import jax
import jax.numpy as jnp
from jax import lax
from jax.sharding import PartitionSpec as P

HEADS = 64
KVH = 8
HD = 128
PB = 64
PDEPTH = 4


def normalize(tokens, gain):
    values = tokens.astype(jnp.float32)
    meansq = jnp.mean(values * values, axis=-1, keepdims=True)
    return (values * lax.rsqrt(meansq + 1e-06) * gain.astype(jnp.float32)).astype(jnp.bfloat16)


def rotate(values, positions, heads):
    halfway = HD // 2
    frequency = jnp.exp(jnp.arange(halfway, dtype=jnp.float32) * (-2.0 * math.log(1000000.0) / HD))
    angles = positions.astype(jnp.float32)[:, None] * frequency[None, :]
    cos_part = jnp.cos(angles)[:, None, :]
    sin_part = jnp.sin(angles)[:, None, :]
    shaped = values.reshape(values.shape[0], heads, HD)
    leading = shaped[..., :halfway]
    trailing = shaped[..., halfway:]
    joined = jnp.concatenate(
        [leading * cos_part - trailing * sin_part, trailing * cos_part + leading * sin_part],
        axis=-1,
    )
    return joined.reshape(values.shape[0], heads * HD)


def visible(lengths):
    span = PDEPTH * PB + PB
    column = jnp.arange(span, dtype=jnp.int32)
    within = jnp.arange(PB, dtype=jnp.int32)
    prefix_ok = (column[None, None, :] < PDEPTH * PB) & (
        (column // PB)[None, None, :] < lengths[:, None, None]
    )
    own_ok = (column[None, None, :] >= PDEPTH * PB) & (
        (column - PDEPTH * PB)[None, None, :] <= within[None, :, None]
    )
    return prefix_ok | own_ok


def local(tokens, gain, w_query, w_keyvalue, w_output, cache, parents, lengths):
    own_group = lax.axis_index("branch")
    tensor_pos = lax.axis_index("tensor")
    row_count = tokens.shape[0]
    branch_count = row_count // PB
    full = lax.all_gather(tokens, "tensor", axis=1, tiled=True)
    normed = normalize(full, gain)
    my_lengths = lax.dynamic_slice_in_dim(lengths, own_group * branch_count, branch_count, 0)
    my_parents = lax.dynamic_slice_in_dim(parents, own_group * branch_count, branch_count, 0)
    positions = jnp.repeat(my_lengths, PB) * PB + jnp.tile(
        jnp.arange(PB, dtype=jnp.int32), branch_count
    )
    local_heads = w_query.shape[1] // HD
    kv_head = tensor_pos * local_heads // (HEADS // KVH)
    query = rotate(
        jnp.dot(normed, w_query, preferred_element_type=jnp.float32), positions, local_heads
    ).astype(jnp.bfloat16)
    feature_count = w_keyvalue.shape[1]
    own_features = lax.dynamic_slice_in_dim(normed, tensor_pos * feature_count, feature_count, 1)
    partial_kv = jnp.einsum(
        "rd,kdc->krc", own_features, w_keyvalue, preferred_element_type=jnp.float32
    )
    summed = lax.psum(partial_kv.astype(jnp.bfloat16), "tensor").astype(jnp.float32)
    head_kv = lax.dynamic_slice_in_dim(summed, kv_head * HD, HD, 2)
    new_keys = rotate(head_kv[0], positions, 1).astype(jnp.bfloat16)
    new_values = head_kv[1].astype(jnp.bfloat16)
    cache_head = lax.dynamic_slice_in_dim(cache, kv_head * HD, HD, 3)
    flat_ids = my_parents.reshape(-1)
    pool = lax.all_gather(cache_head, "branch", axis=1, tiled=True)
    pre_keys = pool[0, flat_ids]
    pre_values = pool[1, flat_ids]
    keys = jnp.concatenate(
        [pre_keys.reshape(branch_count, PDEPTH * PB, HD), new_keys.reshape(branch_count, PB, HD)],
        axis=1,
    )
    values = jnp.concatenate(
        [
            pre_values.reshape(branch_count, PDEPTH * PB, HD),
            new_values.reshape(branch_count, PB, HD),
        ],
        axis=1,
    )
    queries = query.reshape(branch_count, PB, local_heads, HD)
    scores = jnp.einsum("bihd,bjd->bhij", queries, keys, preferred_element_type=jnp.float32) * (
        1.0 / math.sqrt(HD)
    )
    scores = jnp.where(visible(my_lengths)[:, None], scores, -1e30)
    highest = jnp.max(scores, axis=-1, keepdims=True)
    expo = jnp.exp(scores - highest)
    probs = (expo / jnp.sum(expo, axis=-1, keepdims=True)).astype(jnp.bfloat16)
    mixed = jnp.einsum("bhij,bjd->bihd", probs, values, preferred_element_type=jnp.float32).astype(
        jnp.bfloat16
    )
    heads_out = mixed.reshape(row_count, local_heads * HD)
    partial_out = jnp.dot(heads_out, w_output, preferred_element_type=jnp.float32)
    total = lax.psum(partial_out.astype(jnp.bfloat16), "tensor").astype(jnp.float32)
    share = total.shape[1] // lax.axis_size("tensor")
    result = lax.dynamic_slice_in_dim(total, tensor_pos * share, share, 1)
    return result.astype(jnp.bfloat16)


def solution(mesh):
    return jax.shard_map(
        local,
        mesh=mesh,
        in_specs=(
            P("branch", "tensor"),
            P(),
            P(None, "tensor"),
            P(None, "tensor", None),
            P("tensor", None),
            P(None, "branch", None, None),
            P(),
            P(),
        ),
        out_specs=P("branch", "tensor"),
        check_vma=False,
    )
```

profile of v0, /device:TPU:6, one launch (start us, length us, event | category | flops | bytes accessed | tf_op | source)
XLA Modules:
  0.0 393.4 jit_solution(13069521971901430589)
XLA Ops:
  6.5 0.0 copy-start
  6.5 2.0 constant_dynamic-slice_fusion.1
  8.6 0.0 all-gather.3.cloned.1.call-update
  8.6 0.0 all-gather.5.cloned.1.call-start
  8.6 0.7 all-gather.5.cloned.1.call-update
  9.3 0.0 all-reduce.5.cloned.1.call-start
  9.4 0.7 convert_element_type.63
  10.1 0.7 broadcast_multiply_fusion
  10.8 0.1 add_convert_fusion.1
  10.9 0.1 convert_element_type.70
  11.0 0.8 constant_dynamic-slice_fusion
  11.7 0.1 copy.23
  11.8 0.1 reshape.294
  12.0 0.1 compare_and_fusion
  12.1 0.8 broadcast_or_fusion
  12.9 1.7 multiply_cosine_fusion
  14.6 29.1 %all-gather.3.cloned.1.call-done = bf16[2,128,64,128]{3,2,1,0:T(8,128)(2,1)} async-done(((bf16[2,16,64,128]{3,2,1,0:T(8,128)(2,1)}), bf16[2,128,64,128]{3,2,1,0:T(8,128)(2,1)}) %all-gather.3.cloned.1.call-update) | async-done | bytes 4194320 | tf_op jit(solution)/shard_map/all_gather | solution.py:78
  43.7 2.9 gather_fusion.1
  46.6 3.6 gather_fusion
  50.2 73.4 %all-gather.5.cloned.1.call-done = bf16[512,8192]{1,0:T(8,128)(2,1)} async-done(((bf16[512,512]{1,0:T(8,128)(2,1)}), bf16[512,8192]{1,0:T(8,128)(2,1)}) %all-gather.5.cloned.1.call-update) | async-done | bytes 8388624 | tf_op jit(solution)/shard_map/all_gather | solution.py:55
  123.6 5.1 %fusion.1 = f32[512]{0:T(512)S(1)} fusion(bf16[512,8192]{1,0:T(8,128)(2,1)} %all-gather.5.cloned.1.call-done), kind=kLoop, calls=%fused_computation.5 | loop fusion | flops 12582400 | bytes 8390656 | tf_op jit(solution)/shard_map/reduce_sum | solution.py:17
  128.7 9.9 %fusion.3 = bf16[512,8192]{1,0:T(8,128)(2,1)} fusion(bf16[512,8192]{1,0:T(8,128)(2,1)} %all-gather.5.cloned.1.call-done, f32[8192]{0:T(1024)S(1)} %convert_element_type.63, f32[512]{0:T(512)S(1)} %add_rsqrt_fusion), kind=kLoop, calls=%fused_computation.7 | loop fusion | flops 16777216 | bytes 16812032 | tf_op jit(solution)/shard_map/convert_element_type | solution.py:18
  138.6 3.7 convert_bitcast_fusion
  142.2 0.0 all-reduce.5.cloned.1.call-update
  142.3 0.2 all-reduce.7.cloned.1.call-start
  142.5 9.5 %fusion.43 = f32[512,512]{0,1:T(8,128)S(1)} fusion(bf16[512,8192]{1,0:T(8,128)(2,1)} %fusion.3, bf16[8192,512]{1,0:T(8,128)(2,1)} %param.10), kind=kOutput, calls=%fused_computation.84 | convolution fusion | flops 4294967296 | bytes 17825792 | tf_op jit(solution)/shard_map/dot_general | solution.py:65
  151.9 0.1 fusion.41
  152.0 0.3 copy.35
  152.4 0.3 copy.34
  152.7 1.2 subtract_convert_fusion
  154.0 0.3 pad_maximum_fusion
  154.3 77.6 %all-reduce.5.cloned.1.call-done = bf16[2,512,1024]{1,2,0:T(8,128)(2,1)} async-done(((bf16[2,512,1024]{1,2,0:T(8,128)(2,1)}), bf16[2,512,1024]{1,2,0:T(8,128)(2,1)}) %all-reduce.5.cloned.1.call-update) | async-done | bytes 2097168 | tf_op jit(solution)/shard_map/psum | solution.py:72
  231.9 1.0 dynamic-slice_convert_fusion
  232.9 0.6 fusion.26
  233.5 0.1 copy.26
  233.7 0.1 copy.25
  233.8 0.6 fusion.13
  234.4 0.0 copy-start.2
  234.4 0.0 slice-start
  234.4 1.8 fusion.42
  236.2 0.0 slice-start.1
  236.3 0.7 fusion.10
  236.9 0.4 copy.30
  237.3 1.2 slice-done.1
  238.6 6.7 %convolution_convert_fusion = bf16[512,8192]{1,0:T(8,128)(2,1)} fusion(bf16[512,8192]{1,0:T(8,128)(2,1)S(1)} %bitcast.57, bf16[64,8,4,128]{3,2,1,0:T(4,128)(2,1)S(1)} %bitcast.54), kind=kOutput, calls=%fused_computation.8 | convolution fusion | flops 4299161600 | bytes 17301504 | tf_op jit(solution)/shard_map/dot_general | solution.py:104
  245.3 0.0 all-reduce.7.cloned.1.call-update
  245.3 139.7 %all-reduce.7.cloned.1.call-done = bf16[512,8192]{1,0:T(8,128)(2,1)} async-done(((bf16[512,8192]{1,0:T(8,128)(2,1)}), bf16[512,8192]{1,0:T(8,128)(2,1)}) %all-reduce.7.cloned.1.call-update) | async-done | bytes 8388624 | tf_op jit(solution)/shard_map/psum | solution.py:105
  385.0 1.9 convert_convert_fusion
  (20 shorter events, 0.1 us)
Async XLA Ops:
  6.5 132.0 %copy-start = (bf16[2,512,1024]{2,1,0:T(8,128)(2,1)S(1)}, bf16[2,512,1024]{2,1,0:T(8,128)(2,1)}, u32[]{:S(2)}) copy-start(bf16[2,512,1024]{2,1,0:T(8,128)(2,1)} %param.11) | copy-start | bytes 6291460
  6.5 37.2 %all-gather.3.cloned.1.call-start = ((), (), s32[]{:S(2)}) async-start(), calls=%async_computation | async-start | bytes 4718592 | tf_op jit(solution)/shard_map/all_gather | solution.py:78
  8.6 115.0 %all-gather.5.cloned.1.call-start = ((), (), s32[]{:S(2)}) async-start(), calls=%async_computation.1 | async-start | bytes 8912896 | tf_op jit(solution)/shard_map/all_gather | solution.py:55
  9.3 222.5 %all-reduce.5.cloned.1.call-start = ((), (), s32[]{:S(2)}) async-start(), calls=%async_computation.2 | async-start | bytes 4194304 | tf_op jit(solution)/shard_map/psum | solution.py:72
  142.3 242.8 %all-reduce.7.cloned.1.call-start = ((), (), s32[]{:S(2)}) async-start(), calls=%async_computation.3 | async-start | bytes 16777216 | tf_op jit(solution)/shard_map/psum | solution.py:105
  232.9 1.5 copy-start.3
  234.4 1.9 copy-start.2
  234.4 3.0 slice-start
  236.2 2.3 slice-start.1
  245.3 141.6 %copy-start.1 = (bf16[2,512,1024]{2,1,0:T(8,128)(2,1)S(1)}, bf16[2,512,1024]{2,1,0:T(8,128)(2,1)}, u32[]{:S(2)}) copy-start(bf16[2,512,1024]{2,1,0:T(8,128)(2,1)} %param.11) | copy-start | bytes 6291460
Sparse Core Ops, SparseCore 0:
  9.1 34.6 all-gather.2
  45.8 77.7 all-gather.4
  142.4 89.4 all-reduce.4
  245.4 139.5 all-reduce.6
where the time goes:
time: 396 us; the launch traced here: 393 us
  waiting for transfers between devices  321 us (81%)
  other arithmetic  25.9 us (7%)
  matrix products  21.1 us (5%)
  between operations  13.4 us (3%)
  local copies, waits for them, and re-layouts  12.2 us (3%)
    psum x1, waiting for transfers between devices, local(): lax.psum(partial_out.astype(jnp.bfloat16), 'tensor').astype(jnp.float32)  140 us
    psum x1, waiting for transfers between devices, local(): lax.psum(partial_kv.astype(jnp.bfloat16), 'tensor').astype(jnp.float32)  77.6 us
    all_gather x1, waiting for transfers between devices, local(): full = lax.all_gather(tokens, 'tensor', axis=1, tiled=True)  73.4 us
    all_gather x1, waiting for transfers between devices, local(): pool = lax.all_gather(cache_head, 'branch', axis=1, tiled=True)  29.1 us
    convert_element_type x1, other arithmetic, normalize(): (values * lax.rsqrt(meansq + 1e-06) * gain.astype(jnp.float32)).astype(jn...  9.86 us
    dot_general x1, matrix products, local(): jnp.dot(normed, w_query, preferred_element_type=jnp.float32)  9.46 us
  transfers between devices with their start and end apart: 4, of which 4 were waited for; matrix products, arithmetic and copies ran while one was open for 6% of the time, Pallas kernels for 0%

commit v1 on v0

v1 whole, which is shorter than its diff:
```python
import math

import jax
import jax.numpy as jnp
from jax import lax
from jax.experimental import pallas as pl
from jax.experimental.pallas import tpu as pltpu
from jax.sharding import PartitionSpec as P

HEADS = 64
KVH = 8
HD = 128
PB = 64
PDEPTH = 4
HALF = 256
AXES = ("branch", "tensor")
F32 = jnp.float32
BF16 = jnp.bfloat16
MIB = 1024 * 1024


def pairs(move):
    table = []
    for z in range(4):
        for c in range(2):
            for x in range(4):
                for y in range(4):
                    z2, c2, x2, y2 = move(z, c, x, y)
                    target = ((z2 % 4) * 2 + c2 % 2) * 16 + (x2 % 4) * 4 + y2 % 4
                    table.append(((z * 2 + c) * 16 + x * 4 + y, target))
    return table


HOPS = {}
for step in (1, -1):
    HOPS["first", step] = pairs(
        lambda z, c, x, y, s=step: (z, c, x, y + s) if c == 0 else (z, c, x + s, y)
    )
    HOPS["second", step] = pairs(
        lambda z, c, x, y, s=step: (z, c, x + s, y) if c == 0 else (z, c, x, y + s)
    )
HOPS["twin", 1] = pairs(lambda z, c, x, y: (z, c, x, y ^ 1))


def hop(value, axis, step):
    return lax.ppermute(value, AXES, HOPS[axis, step])


def both(forward, backward, axis):
    return hop(forward, axis, 1), hop(backward, axis, -1)


def stack_rows(*parts):
    return jnp.concatenate(parts, axis=0)


def plus(base, *terms):
    total = base.astype(F32)
    for term in terms:
        total = total + term.astype(F32)
    return total.astype(BF16)


def pack(block):
    quarter = block.shape[0] // 4
    return jnp.concatenate([block[k * quarter : (k + 1) * quarter] for k in range(4)], axis=1)


def unpack(block):
    return jnp.concatenate([block[:, k * HD : (k + 1) * HD] for k in range(4)], axis=0)


def params(mebibytes):
    return pltpu.CompilerParams(vmem_limit_bytes=mebibytes * MIB)


def kv_partial(tokens, gain_own, w_keyvalue, ids):
    count = ids.shape[0]
    rows, features = tokens.shape

    def body(ids_ref, t_ref, g_ref, w_ref, o_ref):
        scaled = (t_ref[...].astype(F32) * g_ref[...]).astype(BF16)
        o_ref[...] = jnp.dot(scaled, w_ref[0], preferred_element_type=F32).astype(BF16)

    return pl.pallas_call(
        body,
        out_shape=jax.ShapeDtypeStruct((rows, count * HD), BF16),
        grid_spec=pltpu.PrefetchScalarGridSpec(
            num_scalar_prefetch=1,
            grid=(count,),
            in_specs=[
                pl.BlockSpec((rows, features), lambda n, ids: (0, 0)),
                pl.BlockSpec((1, features), lambda n, ids: (0, 0)),
                pl.BlockSpec(
                    (1, features, HD), lambda n, ids: (lax.rem(ids[n], 2), 0, lax.div(ids[n], 2))
                ),
            ],
            out_specs=pl.BlockSpec((rows, HD), lambda n, ids: (0, n)),
        ),
        compiler_params=params(8),
        name="kv_partial",
    )(ids, tokens, gain_own, w_keyvalue)


def query_part(pieces, arrays, ids, gain, w_query, carry):
    rows, columns = 512, w_query.shape[1]
    count = len(pieces)
    first = carry is None
    n_arrays = len(arrays)

    def body(ids_ref, *refs):
        a_refs = refs[:n_arrays]
        g_ref, w_ref = refs[n_arrays : n_arrays + 2]
        q_ref, s_ref = refs[-2:]
        step = pl.program_id(0)

        @pl.when(step == 0)
        def _():
            if first:
                q_ref[...] = jnp.zeros_like(q_ref)
                s_ref[...] = jnp.zeros_like(s_ref)
            else:
                q_ref[...] = refs[n_arrays + 2][...]
                s_ref[...] = refs[n_arrays + 3][...]

        for number, parts in enumerate(pieces):

            @pl.when(step == number)
            def _(parts=parts):
                for which, start, target, size in parts:
                    values = a_refs[which][start : start + size, :].astype(F32)
                    squares = values * values
                    lanes = squares[:, :HD]
                    for k in range(1, 4):
                        lanes = lanes + squares[:, k * HD : (k + 1) * HD]
                    s_ref[target : target + size, :] += lanes
                    scaled = (values * g_ref[0]).astype(BF16)
                    q_ref[target : target + size, :] += jnp.dot(
                        scaled, w_ref[...], preferred_element_type=F32
                    )

    whole = pl.BlockSpec(memory_space=pltpu.VMEM)
    carried = [] if first else list(carry)
    return pl.pallas_call(
        body,
        out_shape=(
            jax.ShapeDtypeStruct((rows, columns), F32),
            jax.ShapeDtypeStruct((rows, HD), F32),
        ),
        grid_spec=pltpu.PrefetchScalarGridSpec(
            num_scalar_prefetch=1,
            grid=(count,),
            in_specs=[whole] * n_arrays
            + [
                pl.BlockSpec((1, 1, 512), lambda n, ids: (ids[n], 0, 0)),
                pl.BlockSpec((512, columns), lambda n, ids: (ids[n], 0)),
            ]
            + [whole] * len(carried),
            out_specs=[
                pl.BlockSpec((rows, columns), lambda n, ids: (0, 0)),
                pl.BlockSpec((rows, HD), lambda n, ids: (0, 0)),
            ],
        ),
        compiler_params=params(20),
        name="query_part",
    )(ids, *arrays, gain, w_query, *carried)


def attention(query, squares, keyvalue, cosine, sine, pool, parents, lengths):
    rows, columns = query.shape
    branches = rows // PB
    heads = columns // HD
    span = PDEPTH * PB + PB
    features = 8192.0
    scale = 1.0 / math.sqrt(HD)

    def body(par_ref, len_ref, q_ref, s_ref, k_ref, v_ref, c_ref, n_ref, p_ref, o_ref, qb, kb, vb):
        branch = pl.program_id(0)
        meansq = jnp.sum(s_ref[...], axis=1, keepdims=True) * (1.0 / features)
        factor = lax.rsqrt(meansq + 1e-06)
        cos_part = c_ref[...] * factor
        sin_part = n_ref[...] * factor

        def rope(v):
            return (v * cos_part + pltpu.roll(v, HD // 2, 1) * sin_part).astype(BF16)

        for h in range(heads):
            qb[h * PB : (h + 1) * PB, :] = rope(q_ref[:, h * HD : (h + 1) * HD])
        for d in range(PDEPTH):
            block = par_ref[branch, d]
            kb[d * PB : (d + 1) * PB, :] = p_ref[0, block]
            vb[d * PB : (d + 1) * PB, :] = p_ref[1, block]
        kb[PDEPTH * PB :, :] = rope(k_ref[...].astype(F32))
        vb[PDEPTH * PB :, :] = (v_ref[...].astype(F32) * factor).astype(BF16)
        scores = lax.dot_general(
            qb[...], kb[...], (((1,), (1,)), ((), ())), preferred_element_type=F32
        )
        column = lax.broadcasted_iota(jnp.int32, (heads * PB, span), 1)
        within = lax.broadcasted_iota(jnp.int32, (heads * PB, span), 0) % PB
        limit = len_ref[branch] * PB
        seen = (column < limit) | (
            (column >= PDEPTH * PB) & (column - PDEPTH * PB <= within)
        )
        scores = jnp.where(seen, scores * scale, -1e30)
        highest = jnp.max(scores, axis=1, keepdims=True)
        expo = jnp.exp(scores - highest)
        total = jnp.sum(expo, axis=1, keepdims=True)
        probs = (expo / total).astype(BF16)
        mixed = jnp.dot(probs, vb[...], preferred_element_type=F32).astype(BF16)
        for h in range(heads):
            o_ref[:, h * HD : (h + 1) * HD] = mixed[h * PB : (h + 1) * PB]

    def rows_of(width):
        return pl.BlockSpec((PB, width), lambda n, *_: (n, 0))

    return pl.pallas_call(
        body,
        out_shape=jax.ShapeDtypeStruct((rows, columns), BF16),
        grid_spec=pltpu.PrefetchScalarGridSpec(
            num_scalar_prefetch=2,
            grid=(branches,),
            in_specs=[
                rows_of(columns),
                rows_of(HD),
                rows_of(HD),
                rows_of(HD),
                rows_of(HD),
                rows_of(HD),
                pl.BlockSpec(memory_space=pltpu.VMEM),
            ],
            out_specs=rows_of(columns),
            scratch_shapes=[
                pltpu.VMEM((heads * PB, HD), BF16),
                pltpu.VMEM((span, HD), BF16),
                pltpu.VMEM((span, HD), BF16),
            ],
        ),
        compiler_params=params(16),
        name="attention",
    )(parents, lengths, query, squares, *keyvalue, cosine, sine, pool)


def output_part(heads_out, w_output, ids):
    rows, depth = heads_out.shape
    count = ids.shape[0]

    def body(ids_ref, h_ref, w_ref, o_ref):
        o_ref[0] = jnp.dot(h_ref[...], w_ref[...], preferred_element_type=F32).astype(BF16)

    return pl.pallas_call(
        body,
        out_shape=jax.ShapeDtypeStruct((count, rows, 512), BF16),
        grid_spec=pltpu.PrefetchScalarGridSpec(
            num_scalar_prefetch=1,
            grid=(count,),
            in_specs=[
                pl.BlockSpec((rows, depth), lambda n, ids: (0, 0)),
                pl.BlockSpec((depth, 512), lambda n, ids: (0, ids[n])),
            ],
            out_specs=pl.BlockSpec((1, rows, 512), lambda n, ids: (n, 0, 0)),
        ),
        compiler_params=params(12),
        name="output_part",
    )(ids, heads_out, w_output)


def local(tokens, gain, w_query, w_keyvalue, w_output, cache, parents, lengths):
    bar = lax.optimization_barrier
    group = lax.axis_index("branch")
    place = lax.axis_index("tensor")
    x, y = place // 4, place % 4
    core = group % 2
    row_count = tokens.shape[0]
    branch_count = row_count // PB

    ahead = jnp.arange(4, dtype=jnp.int32)
    i_step, j_step = ahead[:, None], ahead[None, :]
    dx = jnp.where(core == 0, j_step, i_step)
    dy = jnp.where(core == 0, i_step, j_step)
    order = ((x + dx) % 4) * 4 + (y + dy) % 4

    my_lengths = lax.dynamic_slice_in_dim(lengths, group * branch_count, branch_count, 0)
    my_parents = lax.dynamic_slice_in_dim(parents, group * branch_count, branch_count, 0)
    local_heads = w_query.shape[1] // HD
    kv_head = place * local_heads // (HEADS // KVH)
    cache_head = lax.dynamic_slice_in_dim(cache, kv_head * HD, HD, 3)
    pool = lax.all_gather(cache_head, "branch", axis=1, tiled=True)

    positions = jnp.repeat(my_lengths, PB) * PB + jnp.tile(
        jnp.arange(PB, dtype=jnp.int32), branch_count
    )
    halfway = HD // 2
    frequency = jnp.exp(jnp.arange(halfway, dtype=F32) * (-2.0 * math.log(1000000.0) / HD))
    angles = positions.astype(F32)[:, None] * frequency[None, :]
    cosine, sine = jnp.cos(angles), jnp.sin(angles)
    cosine = jnp.concatenate([cosine, cosine], axis=1)
    sine = jnp.concatenate([-sine, sine], axis=1)

    gain_all = gain.astype(F32).reshape(16, 1, 512)
    gain_own = lax.dynamic_slice_in_dim(gain, place * 512, 512, 0).astype(F32)[None, :]

    kv_far = kv_partial(tokens, gain_own, w_keyvalue, order[2])
    s1 = both(stack_rows(tokens, kv_far[:HALF]), stack_rows(tokens, kv_far[HALF:]), "first")
    s2 = both(tokens, tokens, "second")
    kv_near = kv_partial(
        tokens, gain_own, w_keyvalue, jnp.concatenate([order[0], order[1], order[3]])
    )
    (b1m, b1p) = bar(s1)
    k1 = kv_near[:, 512:1024]
    k3 = kv_near[:, 1024:]
    k1 = stack_rows(plus(k1[:HALF], b1m[512:]), k1[HALF:])
    k3 = stack_rows(k3[:HALF], plus(k3[HALF:], b1p[512:]))
    s3 = both(stack_rows(b1m[:HALF], k1), stack_rows(b1p[HALF:512], k3), "first")
    near = stack_rows(b1p[:512], b1m[:512])
    s4 = both(near, near, "second")
    b2m, b2p, b3m, b3p = bar((*s2, *s3))
    part = query_part(
        [[(0, 0, 0, 512)], [(1, 0, 0, 512)], [(2, 0, 0, 512)], [(3, 0, 0, 512)], [(4, 0, 0, 512)]],
        [tokens, b1p, b1m, b2p, b2m],
        jnp.stack([order[0, 0], order[1, 0], order[3, 0], order[0, 1], order[0, 3]]),
        gain_all,
        w_query,
        None,
    )
    ksum = plus(kv_near[:, :512], b3m[HALF:], b3p[HALF:])
    kfar = ksum[:, 2 * HD : 3 * HD]
    opposite = stack_rows(b3m[:HALF], b3p[:HALF])
    s5 = both(
        stack_rows(opposite, b2m[:HALF], pack(kfar[:HALF])),
        stack_rows(opposite, b2p[HALF:], pack(kfar[HALF:])),
        "second",
    )
    b4m, b4p = bar(s4)
    part = query_part(
        [
            [(0, 0, 0, HALF), (1, 0, HALF, HALF)],
            [(2, 0, 0, 512)],
            [(2, 512, 0, 512)],
            [(3, 0, 0, 512)],
            [(3, 512, 0, 512)],
        ],
        [b3m, b3p, b4p, b4m],
        jnp.stack([order[2, 0], order[1, 1], order[3, 1], order[1, 3], order[3, 3]]),
        gain_all,
        w_query,
        part,
    )
    s6 = both(
        stack_rows(b4m[:HALF], b4m[512 : 512 + HALF]),
        stack_rows(b4p[HALF:512], b4p[512 + HALF :]),
        "second",
    )
    b5m, b5p = bar(s5)
    k1 = ksum[:, HD : 2 * HD]
    k3 = ksum[:, 3 * HD :]
    k1 = stack_rows(plus(k1[:HALF], unpack(b5m[768:])), k1[HALF:])
    k3 = stack_rows(k3[:HALF], plus(k3[HALF:], unpack(b5p[768:])))
    s7 = both(
        stack_rows(b5m[:HALF], pack(k1)), stack_rows(b5p[HALF:512], pack(k3)), "second"
    )
    part = query_part(
        [[(0, 0, 0, 512)], [(1, 0, 0, 512)], [(1, 512, 0, HALF), (0, 512, HALF, HALF)]],
        [b5p, b5m],
        jnp.stack([order[2, 1], order[2, 3], order[0, 2]]),
        gain_all,
        w_query,
        part,
    )
    b6m, b6p, b7m, b7p = bar((*s6, *s7))
    mine = plus(ksum[:, :HD], unpack(b7m[HALF:]), unpack(b7p[HALF:]))
    other = hop(mine, "twin", 1)
    even = place % 2 == 0
    new_key = jnp.where(even, mine, other)
    new_value = jnp.where(even, other, mine)
    query, squares = query_part(
        [
            [(0, 0, 0, HALF), (1, 0, HALF, HALF)],
            [(0, HALF, 0, HALF), (1, HALF, HALF, HALF)],
            [(2, 0, 0, HALF), (3, 0, HALF, HALF)],
        ],
        [b6m, b6p, b7m, b7p],
        jnp.stack([order[1, 2], order[3, 2], order[2, 2]]),
        gain_all,
        w_query,
        part,
    )
    heads_out = attention(
        query, squares, (new_key, new_value), cosine, sine, pool, my_parents, my_lengths
    )

    far = output_part(
        heads_out, w_output, jnp.stack([order[2, 2], order[1, 2], order[3, 2], order[0, 2]])
    )
    r1 = both(far[0, :HALF], far[0, HALF:], "second")
    r2 = both(
        stack_rows(far[1, :HALF], far[2, :HALF]),
        stack_rows(far[1, HALF:], far[2, HALF:]),
        "second",
    )
    rest = output_part(
        heads_out,
        w_output,
        jnp.concatenate(
            [
                jnp.stack([order[2, 1], order[2, 3], order[1, 1], order[3, 1], order[1, 3]]),
                jnp.stack([order[3, 3], order[2, 0], order[0, 1], order[0, 3], order[1, 0]]),
                jnp.stack([order[3, 0], order[0, 0]]),
            ]
        ),
    )
    q21, q23, q11, q31, q13, q33, q20, q01, q03, q10, q30, q00 = [rest[n] for n in range(12)]
    r1m, r1p = bar(r1)
    r3 = both(
        stack_rows(plus(q21[:HALF], r1m), q21[HALF:], far[3, :HALF]),
        stack_rows(q23[:HALF], plus(q23[HALF:], r1p), far[3, HALF:]),
        "second",
    )
    r2m, r2p = bar(r2)
    r4 = both(
        stack_rows(plus(q11[:HALF], r2m[:HALF]), q11[HALF:], plus(q31[:HALF], r2m[HALF:]), q31[HALF:]),
        stack_rows(q13[:HALF], plus(q13[HALF:], r2p[:HALF]), q33[:HALF], plus(q33[HALF:], r2p[HALF:])),
        "second",
    )
    r3m, r3p = bar(r3)
    sum2 = plus(q20, r3m[:512], r3p[:512])
    r5 = both(sum2[:HALF], sum2[HALF:], "first")
    r6 = both(
        stack_rows(plus(q01[:HALF], r3m[512:]), q01[HALF:]),
        stack_rows(q03[:HALF], plus(q03[HALF:], r3p[512:])),
        "second",
    )
    r4m, r4p, r5m, r5p = bar((*r4, *r5))
    sum1 = stack_rows(
        plus(q10[:HALF], r4m[:HALF], r4p[:HALF], r5m), plus(q10[HALF:], r4m[HALF:512], r4p[HALF:512])
    )
    sum3 = stack_rows(
        plus(q30[:HALF], r4m[512 : 512 + HALF], r4p[512 : 512 + HALF]),
        plus(q30[HALF:], r4m[512 + HALF :], r4p[512 + HALF :], r5p),
    )
    r7 = both(sum1, sum3, "first")
    return plus(q00, *r6, *r7)


def solution(mesh):
    return jax.shard_map(
        local,
        mesh=mesh,
        in_specs=(
            P("branch", "tensor"),
            P(),
            P(None, "tensor"),
            P(None, "tensor", None),
            P("tensor", None),
            P(None, "branch", None, None),
            P(),
            P(),
        ),
        out_specs=P("branch", "tensor"),
        check_vma=False,
    )
```

time: 396 us -> 220 us (0.56)
  waiting for transfers between devices: 321 us -> 57.4 us
  starting transfers between devices: 0.3 us -> 44.6 us
  Pallas kernels: 0 us -> 36.1 us
  local copies, waits for them, and re-layouts: 12.2 us -> 41.7 us
  matrix products: 21.1 us -> 0 us
    psum x2 -> x0, waiting for transfers between devices: 217 us -> none  [the longest x1 140 us: local(): lax.psum(partial_out.astype(jnp.bfloat16), 'tensor').astype(jnp.float32)]
    all_gather x1 -> x0, waiting for transfers between devices: 73.4 us -> none  [local(): full = lax.all_gather(tokens, 'tensor', axis=1, tiled=True)]
    ppermute x0 -> x29, waiting for transfers between devices: none -> 57.3 us  [hop(): return lax.ppermute(value, AXES, HOPS[axis, step])]
    ppermute x0 -> x29, starting transfers between devices: none -> 44.6 us  [hop(): return lax.ppermute(value, AXES, HOPS[axis, step])]
    pallas_call x0 -> x9, Pallas kernels: none -> 36.1 us  [the longest x4 14 us: query_part(): pl.pallas_call(body, out_shape=(jax.ShapeDtypeStruct((rows, columns), F32...]
    all_gather x1, waiting for transfers between devices: 29.1 us -> 0.02 us  [local(): pool = lax.all_gather(cache_head, 'branch', axis=1, tiled=True)]
    dot_general x5 -> x0, matrix products: 21.1 us -> none  [the longest x1 9.46 us: local(): jnp.dot(normed, w_query, preferred_element_type=jnp.float32)]
    unnamed x14 -> x47, local copies, waits for them, and re-layouts: 1.9 us -> 18.3 us
  transfers between devices with their start and end apart: 4 -> 30, of which waited for: 4 -> 16; matrix products, arithmetic and copies ran while one was open for 6% -> 20% of each run, Pallas kernels for 0% -> 13%
where the time goes in v1:
time: 220 us; the launch traced here: 217 us
  waiting for transfers between devices  57.4 us (26%)
  starting transfers between devices  44.6 us (20%)
  local copies, waits for them, and re-layouts  41.7 us (19%)
  Pallas kernels  36.1 us (16%)
  other arithmetic  23.6 us (11%)
  between operations  14 us (6%)
    ppermute x29, waiting for transfers between devices, hop(): return lax.ppermute(value, AXES, HOPS[axis, step])  57.3 us
    ppermute x29, starting transfers between devices, hop(): return lax.ppermute(value, AXES, HOPS[axis, step])  44.6 us
    unnamed x47, local copies, waits for them, and re-layouts  18.3 us
    pallas_call x4, Pallas kernels, query_part(): pl.pallas_call(body, out_shape=(jax.ShapeDtypeStruct((rows, columns), F32...  14 us
    pallas_call x2, Pallas kernels, output_part(): pl.pallas_call(body, out_shape=jax.ShapeDtypeStruct((count, rows, 512), B...  8.95 us
    concatenate x1, local copies, waits for them, and re-layouts, local(): jnp.concatenate([jnp.stack([order[2, 1], order[2, 3], order[1, 1], order[...  7.87 us
    pallas_call x2, Pallas kernels, kv_partial(): pl.pallas_call(body, out_shape=jax.ShapeDtypeStruct((rows, count * HD), B...  7.17 us
    concatenate x19, other arithmetic, stack_rows(): return jnp.concatenate(parts, axis=0)  6.04 us
  transfers between devices with their start and end apart: 30, of which 16 were waited for; matrix products, arithmetic and copies ran while one was open for 20% of the time, Pallas kernels for 13%

profile of v1, /device:TPU:6, one launch (start us, length us, event | category | flops | bytes accessed | tf_op | source)
XLA Modules:
  0.0 217.3 jit_solution(16515077264233082312)
XLA Ops:
  6.5 2.0 constant_dynamic-slice_fusion
  10.9 2.1 kv_partial.2
  13.2 1.6 collective-permute-start
  14.9 1.7 collective-permute-start.1
  16.6 5.1 %kv_partial.3 = bf16[512,1536]{1,0:T(8,128)(2,1)S(1)} custom-call(s32[12]{0:T(128)S(1)} %pad_add_fusion.1.ids_ref, bf16[512,512]{1,0:T(8,128)(2,1)S(1)} %copy-done.8, f32[1,512]{1,0:T(1,128)S(1)} %bitcast.133, bf16[2,512,1024]{2,1,0:T(8,128)(2,1)S(1)} %copy-done.7), custom_call_target="tpu_custom_call" | custom-call | tf_op jit(solution)/shard_map/kv_partial/pallas_call | solution.py:85
  21.7 4.8 %collective-permute-done.refs_2_ = bf16[768,512]{1,0:T(8,128)(2,1)S(1)} collective-permute-done((bf16[768,512]{1,0:T(8,128)(2,1)S(1)}, bf16[768,512]{1,0:T(8,128)(2,1)S(1)}, u32[]{:S(2)}, u32[]{:S(2)}) %collective-permute-start) | collective-permute-done | bytes 786464 | tf_op jit(solution)/shard_map/ppermute | solution.py:46
  28.9 2.9 %collective-permute-start.9 = (bf16[768,512]{1,0:T(8,128)(2,1)}, bf16[768,512]{1,0:T(8,128)(2,1)}, u32[]{:S(2)}, u32[]{:S(2)}) collective-permute-start(bf16[768,512]{1,0:T(8,128)(2,1)} %pad_maximum_fusion.7), channel_id=1, source_target_pairs={{0,3},{1,0},{2,1},{3,2},{4,7},{5,4},{6,5},{7,6},{8,11},{9,8},{10,9... | collective-permute-start | bytes 2359304 | tf_op jit(solution)/shard_map/ppermute | solution.py:46
  33.1 1.6 collective-permute-start.7
  35.7 1.7 collective-permute-start.2
  37.4 8.4 %collective-permute-done.6.refs_4_ = bf16[512,512]{1,0:T(8,128)(2,1)} collective-permute-done((bf16[512,512]{1,0:T(8,128)(2,1)S(1)}, bf16[512,512]{1,0:T(8,128)(2,1)}, u32[]{:S(2)}, u32[]{:S(2)}) %collective-permute-start.6) | collective-permute-done | bytes 524320 | tf_op jit(solution)/shard_map/ppermute | solution.py:46
  47.2 7.5 %collective-permute-done.8.refs_0_ = bf16[768,512]{1,0:T(8,128)(2,1)} collective-permute-done((bf16[768,512]{1,0:T(8,128)(2,1)}, bf16[768,512]{1,0:T(8,128)(2,1)}, u32[]{:S(2)}, u32[]{:S(2)}) %collective-permute-start.8) | collective-permute-done | bytes 786464 | tf_op jit(solution)/shard_map/ppermute | solution.py:46
  62.3 2.0 pad_add_fusion.ids_ref
  67.1 2.4 %collective-permute-start.4 = (bf16[512,512]{1,0:T(8,128)(2,1)}, bf16[512,512]{1,0:T(8,128)(2,1)}, u32[]{:S(2)}, u32[]{:S(2)}) collective-permute-start(bf16[512,512]{1,0:T(8,128)(2,1)} %pad_maximum_fusion.10), channel_id=1, source_target_pairs={{0,4},{1,5},{2,6},{3,7},{4,8},{5,9},{6,10},{7,11},{8,12},{9,13},{1... | collective-permute-start | bytes 1572872 | tf_op jit(solution)/shard_map/ppermute | solution.py:46
  69.5 3.5 %collective-permute-done.10.refs_1_ = bf16[832,512]{1,0:T(8,128)(2,1)S(1)} collective-permute-done((bf16[832,512]{1,0:T(8,128)(2,1)S(1)}, bf16[832,512]{1,0:T(8,128)(2,1)S(1)}, u32[]{:S(2)}, u32[]{:S(2)}) %collective-permute-start.10) | collective-permute-done | bytes 852000 | tf_op jit(solution)/shard_map/ppermute | solution.py:46
  76.8 2.8 %collective-permute-start.12 = (bf16[384,512]{1,0:T(8,128)(2,1)}, bf16[384,512]{1,0:T(8,128)(2,1)}, u32[]{:S(2)}, u32[]{:S(2)}) collective-permute-start(bf16[384,512]{1,0:T(8,128)(2,1)} %maximum_maximum_fusion.2), channel_id=1, source_target_pairs={{0,4},{1,5},{2,6},{3,7},{4,8},{5,9},{6,10},{7,11},{8,12},{9,13},{1... | collective-permute-start | bytes 1179656 | tf_op jit(solution)/shard_map/ppermute | solution.py:46
  79.6 2.6 %pad_add_fusion.3.ids_ref = s32[4]{0:T(128)S(1)} fusion(s32[1]{0:T(128)} %bitcast.21, s32[1]{0:T(128)} %bitcast.13, s32[1]{0:T(128)} %bitcast.12, s32[1]{0:T(128)} %bitcast.14), kind=kLoop, calls=%fused_computation.118 | loop fusion | flops 12 | bytes 32 | tf_op jit(solution)/shard_map/stack | solution.py:392
  82.3 1.9 fusion.24
  87.7 2.0 pad_add_fusion.2.ids_ref
  89.7 3.3 %stack.18.ids_ref = s32[5]{0:T(128)S(1)} concatenate(s32[1]{0:T(128)} %bitcast.11, s32[1]{0:T(128)} %bitcast.9, s32[1]{0:T(128)} %bitcast.10, s32[1]{0:T(128)} %bitcast.7, s32[1]{0:T(128)} %bitcast.8), dimensions={0} | concatenate | bytes 40 | tf_op jit(solution)/shard_map/stack | solution.py:320
  93.0 3.3 %stack.17.ids_ref = s32[5]{0:T(128)S(1)} concatenate(s32[1]{0:T(128)} %bitcast.6, s32[1]{0:T(128)} %bitcast.2, s32[1]{0:T(128)} %bitcast.3, s32[1]{0:T(128)} %bitcast.4, s32[1]{0:T(128)} %bitcast.5), dimensions={0} | concatenate | bytes 40 | tf_op jit(solution)/shard_map/stack | solution.py:343
  97.8 3.4 %copy-done.2 = bf16[8192,512]{1,0:T(8,128)(2,1)S(1)} copy-done((bf16[8192,512]{1,0:T(8,128)(2,1)S(1)}, bf16[8192,512]{1,0:T(8,128)(2,1)}, u32[]{:S(2)}) %copy-start.2) | copy-done | bytes 8388632
  101.1 4.3 %query_part.4 = (f32[512,512]{1,0:T(8,128)S(1)}, f32[512,128]{1,0:T(8,128)S(1)}) custom-call(s32[5]{0:T(128)S(1)} %stack.18.ids_ref, bf16[512,512]{1,0:T(8,128)(2,1)S(1)} %copy-done.8, bf16[768,512]{1,0:T(8,128)(2,1)S(1)} %copy-done.10, bf16[768,512]{1,0:T(8,128)(2,1)S(1)} %collective-permute-done.refs_2_, bf16[512,512]{1,0:T(8,128)(2,1)} %collective-permute-done.7.refs_3_, ...), custom_call_target="tpu_custom_call" | custom-call | tf_op jit(solution)/shard_map/query_part/pallas_call | solution.py:144
  105.5 3.4 %copy-done.3 = bf16[8192,512]{1,0:T(8,128)(2,1)S(1)} copy-done((bf16[8192,512]{1,0:T(8,128)(2,1)S(1)}, bf16[8192,512]{1,0:T(8,128)(2,1)}, u32[]{:S(2)}) %copy-start.3) | copy-done | bytes 8388632
  108.8 4.4 %query_part.5 = (f32[512,512]{1,0:T(8,128)S(1)}, f32[512,128]{1,0:T(8,128)S(1)}) custom-call(s32[5]{0:T(128)S(1)} %stack.17.ids_ref, bf16[768,512]{1,0:T(8,128)(2,1)} %collective-permute-done.8.refs_0_, bf16[768,512]{1,0:T(8,128)(2,1)} %collective-permute-done.9.refs_1_, bf16[1024,512]{1,0:T(8,128)(2,1)S(1)} %copy-done.15, bf16[1024,512]{1,0:T(8,128)(2,1)S(1)} %copy-done.13, ...), custom_call_target="tpu_custom_call" | custom-call | tf_op jit(solution)/shard_map/query_part/pallas_call | solution.py:144
  113.3 2.0 query_part.6
  115.3 3.3 %query_part.7 = (f32[512,512]{1,0:T(8,128)S(1)}, f32[512,128]{1,0:T(8,128)S(1)}) custom-call(s32[3]{0:T(128)S(1)} %pad_add_fusion.ids_ref, bf16[512,512]{1,0:T(8,128)(2,1)} %collective-permute-done.4.refs_0_, bf16[512,512]{1,0:T(8,128)(2,1)} %collective-permute-done.5.refs_1_, bf16[384,512]{1,0:T(8,128)(2,1)} %collective-permute-done.12.refs_2_, ...), custom_call_target="tpu_custom_call" | custom-call | tf_op jit(solution)/shard_map/query_part/pallas_call | solution.py:144
  119.7 2.2 %copy-done.11 = bf16[2,128,64,128]{3,2,1,0:T(8,128)(2,1)S(1)} copy-done((bf16[2,128,64,128]{3,2,1,0:T(8,128)(2,1)S(1)}, bf16[2,128,64,128]{3,2,1,0:T(8,128)(2,1)}, u32[]{:S(2)}) %copy-start.11) | copy-done | bytes 4194328
  121.9 5.9 %attention.1.h_ref = bf16[512,512]{1,0:T(8,128)(2,1)S(1)} custom-call(s32[8,4]{1,0:T(8,128)S(1)} %copy.10.par_ref, s32[8]{0:T(128)S(1)} %get-tuple-element.70.len_ref, f32[512,512]{1,0:T(8,128)S(1)} %get-tuple-element.57.q_ref, f32[512,128]{1,0:T(8,128)S(1)} %get-tuple-element.58.s_ref, bf16[512,128]{1,0:T(8,128)(2,1)S(1)} %get-tuple-element.146.k_ref, ...), custom_call_target="tpu_custom_call" | custom-call | tf_op jit(solution)/shard_map/attention/pallas_call | solution.py:216
  127.8 3.4 %copy-done.4 = bf16[512,8192]{1,0:T(8,128)(2,1)S(1)} copy-done((bf16[512,8192]{1,0:T(8,128)(2,1)S(1)}, bf16[512,8192]{1,0:T(8,128)(2,1)}, u32[]{:S(2)}) %copy-start.4) | copy-done | bytes 8388632
  131.2 2.5 %output_part.3 = bf16[4,512,512]{2,1,0:T(8,128)(2,1)S(1)} custom-call(s32[4]{0:T(128)S(1)} %pad_add_fusion.3.ids_ref, bf16[512,512]{1,0:T(8,128)(2,1)S(1)} %attention.1.h_ref, bf16[512,8192]{1,0:T(8,128)(2,1)S(1)} %copy-done.4), custom_call_target="tpu_custom_call" | custom-call | tf_op jit(solution)/shard_map/output_part/pallas_call | solution.py:250
  135.2 3.3 %collective-permute-start.21 = (bf16[512,512]{1,0:T(8,128)(2,1)S(1)}, bf16[512,512]{1,0:T(8,128)(2,1)S(1)}, u32[]{:S(2)}, u32[]{:S(2)}) collective-permute-start(bf16[512,512]{1,0:T(8,128)(2,1)S(1)} %pad_maximum_fusion.14), channel_id=1, source_target_pairs={{0,4},{1,5},{2,6},{3,7},{4,8},{5,9},{6,10},{7,11},{8,12},{9,13},{1... | collective-permute-start | bytes 1572872 | tf_op jit(solution)/shard_map/ppermute | solution.py:46
  138.5 7.9 %concatenate.102.ids_ref = s32[12]{0:T(128)S(1)} concatenate(s32[1]{0:T(128)} %bitcast, s32[1]{0:T(128)} %bitcast.1, s32[1]{0:T(128)} %bitcast.2, s32[1]{0:T(128)} %bitcast.3, s32[1]{0:T(128)} %bitcast.4, s32[1]{0:T(128)} %bitcast.5, s32[1]{0:T(128)} %bitcast.6, s32[1]{0:T(128)} %bitcast.7, s32[1]{0:T(128)} %bitcast.8, s32[1]{0:T(128)} %bitcast.9, s32[1]{0:T(128)} %bitcast.10, ...), dimensions={0} | concatenate | bytes 96 | tf_op jit(solution)/shard_map/concatenate | solution.py:403
  146.3 2.1 collective-permute-start.15
  148.4 3.4 %copy-done.5 = bf16[512,8192]{1,0:T(8,128)(2,1)S(1)} copy-done((bf16[512,8192]{1,0:T(8,128)(2,1)S(1)}, bf16[512,8192]{1,0:T(8,128)(2,1)}, u32[]{:S(2)}) %copy-start.5) | copy-done | bytes 8388632
  151.8 6.4 %output_part.2 = bf16[12,512,512]{2,1,0:T(8,128)(2,1)S(1)} custom-call(s32[12]{0:T(128)S(1)} %concatenate.102.ids_ref, bf16[512,512]{1,0:T(8,128)(2,1)S(1)} %attention.1.h_ref, bf16[512,8192]{1,0:T(8,128)(2,1)S(1)} %copy-done.5), custom_call_target="tpu_custom_call" | custom-call | tf_op jit(solution)/shard_map/output_part/pallas_call | solution.py:250
  159.0 3.3 %collective-permute-start.17 = (bf16[768,512]{1,0:T(8,128)(2,1)S(1)}, bf16[768,512]{1,0:T(8,128)(2,1)S(1)}, u32[]{:S(2)}, u32[]{:S(2)}) collective-permute-start(bf16[768,512]{1,0:T(8,128)(2,1)S(1)} %pad_maximum_fusion.8), channel_id=1, source_target_pairs={{0,4},{1,5},{2,6},{3,7},{4,8},{5,9},{6,10},{7,11},{8,12},{9,13},{1... | collective-permute-start | bytes 2359304 | tf_op jit(solution)/shard_map/ppermute | solution.py:46
  162.3 2.1 collective-permute-start.23
  164.4 7.7 %collective-permute-done.18 = bf16[768,512]{1,0:T(8,128)(2,1)S(1)} collective-permute-done((bf16[768,512]{1,0:T(8,128)(2,1)S(1)}, bf16[768,512]{1,0:T(8,128)(2,1)S(1)}, u32[]{:S(2)}, u32[]{:S(2)}) %collective-permute-start.18) | collective-permute-done | bytes 786464 | tf_op jit(solution)/shard_map/ppermute | solution.py:46
  172.1 2.5 %collective-permute-done.17 = bf16[768,512]{1,0:T(8,128)(2,1)S(1)} collective-permute-done((bf16[768,512]{1,0:T(8,128)(2,1)S(1)}, bf16[768,512]{1,0:T(8,128)(2,1)S(1)}, u32[]{:S(2)}, u32[]{:S(2)}) %collective-permute-start.17) | collective-permute-done | bytes 786464 | tf_op jit(solution)/shard_map/ppermute | solution.py:46
  175.0 2.2 collective-permute-start.24
  177.4 2.1 collective-permute-start.25
  180.7 1.9 collective-permute-start.19
  182.7 6.0 %collective-permute-done.23 = bf16[1024,512]{1,0:T(8,128)(2,1)S(1)} collective-permute-done((bf16[1024,512]{1,0:T(8,128)(2,1)S(1)}, bf16[1024,512]{1,0:T(8,128)(2,1)S(1)}, u32[]{:S(2)}, u32[]{:S(2)}) %collective-permute-start.23) | collective-permute-done | bytes 1048608 | tf_op jit(solution)/shard_map/ppermute | solution.py:46
  188.7 3.1 %collective-permute-start.20 = (bf16[512,512]{1,0:T(8,128)(2,1)S(1)}, bf16[512,512]{1,0:T(8,128)(2,1)S(1)}, u32[]{:S(2)}, u32[]{:S(2)}) collective-permute-start(bf16[512,512]{1,0:T(8,128)(2,1)S(1)} %pad_maximum_fusion.13), channel_id=1, source_target_pairs={{0,12},{1,13},{2,14},{3,15},{4,0},{5,1},{6,2},{7,3},{8,4},{9,5},{1... | collective-permute-start | bytes 1572872 | tf_op jit(solution)/shard_map/ppermute | solution.py:46
  191.9 5.2 %collective-permute-done.24 = bf16[1024,512]{1,0:T(8,128)(2,1)S(1)} collective-permute-done((bf16[1024,512]{1,0:T(8,128)(2,1)S(1)}, bf16[1024,512]{1,0:T(8,128)(2,1)S(1)}, u32[]{:S(2)}, u32[]{:S(2)}) %collective-permute-start.24) | collective-permute-done | bytes 1048608 | tf_op jit(solution)/shard_map/ppermute | solution.py:46
  197.6 2.4 %collective-permute-start.27 = (bf16[512,512]{1,0:T(8,128)(2,1)S(1)}, bf16[512,512]{1,0:T(8,128)(2,1)S(1)}, u32[]{:S(2)}, u32[]{:S(2)}) collective-permute-start(bf16[512,512]{1,0:T(8,128)(2,1)S(1)} %pad_maximum_fusion.16), channel_id=1, source_target_pairs={{0,1},{1,2},{2,3},{3,0},{4,5},{5,6},{6,7},{7,4},{8,9},{9,10},{10,1... | collective-permute-start | bytes 1572872 | tf_op jit(solution)/shard_map/ppermute | solution.py:46
  201.1 1.9 collective-permute-done.20
  203.0 5.1 %collective-permute-done.27 = bf16[512,512]{1,0:T(8,128)(2,1)S(1)} collective-permute-done((bf16[512,512]{1,0:T(8,128)(2,1)S(1)}, bf16[512,512]{1,0:T(8,128)(2,1)S(1)}, u32[]{:S(2)}, u32[]{:S(2)}) %collective-permute-start.27) | collective-permute-done | bytes 524320 | tf_op jit(solution)/shard_map/ppermute | solution.py:46
  (142 shorter events, 37.1 us)
Async XLA Ops:
  6.5 75.7 %copy-start = (s32[64,4]{0,1:T(4,128)S(1)}, s32[64,4]{0,1:T(4,128)}, u32[]{:S(2)}) copy-start(s32[64,4]{0,1:T(4,128)} %param.14) | copy-start | bytes 3076
  6.5 2.8 %copy-start.8 = (bf16[512,512]{1,0:T(8,128)(2,1)S(1)}, bf16[512,512]{1,0:T(8,128)(2,1)}, u32[]{:S(2)}) copy-start(bf16[512,512]{1,0:T(8,128)(2,1)} %refs_0_.1) | copy-start | bytes 1572868
  6.5 113.1 %all-gather.2.cloned.1.call-start = ((), (), s32[]{:S(2)}) async-start(), calls=%async_computation | async-start | bytes 4718592 | tf_op jit(solution)/shard_map/all_gather | solution.py:287
  13.0 3.6 %copy-start.7 = (bf16[2,512,1024]{2,1,0:T(8,128)(2,1)S(1)}, bf16[2,512,1024]{2,1,0:T(8,128)(2,1)}, u32[]{:S(2)}) copy-start(bf16[2,512,1024]{2,1,0:T(8,128)(2,1)} %w_ref.5) | copy-start | bytes 6291460
  13.2 13.3 %collective-permute-start = (bf16[768,512]{1,0:T(8,128)(2,1)S(1)}, bf16[768,512]{1,0:T(8,128)(2,1)S(1)}, u32[]{:S(2)}, u32[]{:S(2)}) collective-permute-start(bf16[768,512]{1,0:T(8,128)(2,1)S(1)} %get-tuple-element.134), channel_id=1, source_target_pairs={{0,1},{1,2},{2,3},{3,0},{4,5},{5,6},{6,7},{7,4},{8,9},{9,10},{10,1... | collective-permute-start | bytes 2359304 | tf_op jit(solution)/shard_map/ppermute | solution.py:46
  14.9 12.0 %collective-permute-start.1 = (bf16[768,512]{1,0:T(8,128)(2,1)S(1)}, bf16[768,512]{1,0:T(8,128)(2,1)S(1)}, u32[]{:S(2)}, u32[]{:S(2)}) collective-permute-start(bf16[768,512]{1,0:T(8,128)(2,1)S(1)} %get-tuple-element.133), channel_id=1, source_target_pairs={{0,3},{1,0},{2,1},{3,2},{4,7},{5,4},{6,5},{7,6},{8,11},{9,8},{10,9... | collective-permute-start | bytes 2359304 | tf_op jit(solution)/shard_map/ppermute | solution.py:46
  27.9 6.8 %copy-start.22 = (s32[64]{0:T(128)S(1)}, s32[64]{0:T(128)}, u32[]{:S(2)}) copy-start(s32[64]{0:T(128)} %param.15) | copy-start | bytes 772
  28.9 18.3 %collective-permute-start.9 = (bf16[768,512]{1,0:T(8,128)(2,1)}, bf16[768,512]{1,0:T(8,128)(2,1)}, u32[]{:S(2)}, u32[]{:S(2)}) collective-permute-start(bf16[768,512]{1,0:T(8,128)(2,1)} %pad_maximum_fusion.7), channel_id=1, source_target_pairs={{0,3},{1,0},{2,1},{3,2},{4,7},{5,4},{6,5},{7,6},{8,11},{9,8},{10,9... | collective-permute-start | bytes 2359304 | tf_op jit(solution)/shard_map/ppermute | solution.py:46
  31.7 3.9 %slice-start = ((bf16[768,512]{1,0:T(8,128)(2,1)}), bf16[512,512]{1,0:T(8,128)(2,1)S(1)}, s32[]{:S(2)}) async-start(bf16[768,512]{1,0:T(8,128)(2,1)} %copy-done.9), calls=%async_computation.1 | async-start | bytes 1048576 | tf_op jit(solution)/shard_map/slice | solution.py:314
  32.7 22.0 %collective-permute-start.8 = (bf16[768,512]{1,0:T(8,128)(2,1)}, bf16[768,512]{1,0:T(8,128)(2,1)}, u32[]{:S(2)}, u32[]{:S(2)}) collective-permute-start(bf16[768,512]{1,0:T(8,128)(2,1)} %pad_maximum_fusion.6), channel_id=1, source_target_pairs={{0,1},{1,2},{2,3},{3,0},{4,5},{5,6},{6,7},{7,4},{8,9},{9,10},{10,1... | collective-permute-start | bytes 2359304 | tf_op jit(solution)/shard_map/ppermute | solution.py:46
  32.7 13.1 %collective-permute-start.6 = (bf16[512,512]{1,0:T(8,128)(2,1)S(1)}, bf16[512,512]{1,0:T(8,128)(2,1)}, u32[]{:S(2)}, u32[]{:S(2)}) collective-permute-start(bf16[512,512]{1,0:T(8,128)(2,1)S(1)} %copy-done.8), channel_id=1, source_target_pairs={{0,4},{1,5},{2,6},{3,7},{4,8},{5,9},{6,10},{7,11},{8,12},{9,13},{1... | collective-permute-start | bytes 1572872 | tf_op jit(solution)/shard_map/ppermute | solution.py:46
  33.1 13.5 %collective-permute-start.7 = (bf16[512,512]{1,0:T(8,128)(2,1)S(1)}, bf16[512,512]{1,0:T(8,128)(2,1)}, u32[]{:S(2)}, u32[]{:S(2)}) collective-permute-start(bf16[512,512]{1,0:T(8,128)(2,1)S(1)} %copy-done.8), channel_id=1, source_target_pairs={{0,12},{1,13},{2,14},{3,15},{4,0},{5,1},{6,2},{7,3},{8,4},{9,5},{1... | collective-permute-start | bytes 1572872 | tf_op jit(solution)/shard_map/ppermute | solution.py:46
  35.7 28.6 %collective-permute-start.2 = (bf16[1024,512]{1,0:T(8,128)(2,1)S(1)}, bf16[1024,512]{1,0:T(8,128)(2,1)S(1)}, u32[]{:S(2)}, u32[]{:S(2)}) collective-permute-start(bf16[1024,512]{1,0:T(8,128)(2,1)S(1)} %pad_maximum_fusion), channel_id=1, source_target_pairs={{0,4},{1,5},{2,6},{3,7},{4,8},{5,9},{6,10},{7,11},{8,12},{9,13},{1... | collective-permute-start | bytes 3145736 | tf_op jit(solution)/shard_map/ppermute | solution.py:46
  45.7 18.6 %collective-permute-start.3 = (bf16[1024,512]{1,0:T(8,128)(2,1)S(1)}, bf16[1024,512]{1,0:T(8,128)(2,1)S(1)}, u32[]{:S(2)}, u32[]{:S(2)}) collective-permute-start(bf16[1024,512]{1,0:T(8,128)(2,1)S(1)} %pad_maximum_fusion), channel_id=1, source_target_pairs={{0,12},{1,13},{2,14},{3,15},{4,0},{5,1},{6,2},{7,3},{8,4},{9,5},{1... | collective-permute-start | bytes 3145736 | tf_op jit(solution)/shard_map/ppermute | solution.py:46
  60.0 14.6 %copy-start.20 = (bf16[512,512]{1,0:T(8,128)(2,1)}, bf16[512,512]{1,0:T(8,128)(2,1)S(1)}, u32[]{:S(2)}) copy-start(bf16[512,512]{1,0:T(8,128)(2,1)S(1)} %add_convert_fusion) | copy-start | bytes 1572868
  60.2 12.8 %collective-permute-start.10 = (bf16[832,512]{1,0:T(8,128)(2,1)S(1)}, bf16[832,512]{1,0:T(8,128)(2,1)S(1)}, u32[]{:S(2)}, u32[]{:S(2)}) collective-permute-start(bf16[832,512]{1,0:T(8,128)(2,1)S(1)} %get-tuple-element.124), channel_id=1, source_target_pairs={{0,4},{1,5},{2,6},{3,7},{4,8},{5,9},{6,10},{7,11},{8,12},{9,13},{1... | collective-permute-start | bytes 2555912 | tf_op jit(solution)/shard_map/ppermute | solution.py:46
  60.7 13.9 %collective-permute-start.11 = (bf16[832,512]{1,0:T(8,128)(2,1)S(1)}, bf16[832,512]{1,0:T(8,128)(2,1)S(1)}, u32[]{:S(2)}, u32[]{:S(2)}) collective-permute-start(bf16[832,512]{1,0:T(8,128)(2,1)S(1)} %get-tuple-element.123), channel_id=1, source_target_pairs={{0,12},{1,13},{2,14},{3,15},{4,0},{5,1},{6,2},{7,3},{8,4},{9,5},{1... | collective-permute-start | bytes 2555912 | tf_op jit(solution)/shard_map/ppermute | solution.py:46
  64.4 2.7 %copy-start.12 = (bf16[1024,512]{1,0:T(8,128)(2,1)}, bf16[1024,512]{1,0:T(8,128)(2,1)S(1)}, u32[]{:S(2)}) copy-start(bf16[1024,512]{1,0:T(8,128)(2,1)S(1)} %collective-permute-done.2.refs_3_) | copy-start | bytes 3145732
  65.4 18.7 %collective-permute-start.5 = (bf16[512,512]{1,0:T(8,128)(2,1)}, bf16[512,512]{1,0:T(8,128)(2,1)}, u32[]{:S(2)}, u32[]{:S(2)}) collective-permute-start(bf16[512,512]{1,0:T(8,128)(2,1)} %pad_maximum_fusion.11), channel_id=1, source_target_pairs={{0,12},{1,13},{2,14},{3,15},{4,0},{5,1},{6,2},{7,3},{8,4},{9,5},{1... | collective-permute-start | bytes 1572872 | tf_op jit(solution)/shard_map/ppermute | solution.py:46
  67.1 17.1 %collective-permute-start.4 = (bf16[512,512]{1,0:T(8,128)(2,1)}, bf16[512,512]{1,0:T(8,128)(2,1)}, u32[]{:S(2)}, u32[]{:S(2)}) collective-permute-start(bf16[512,512]{1,0:T(8,128)(2,1)} %pad_maximum_fusion.10), channel_id=1, source_target_pairs={{0,4},{1,5},{2,6},{3,7},{4,8},{5,9},{6,10},{7,11},{8,12},{9,13},{1... | collective-permute-start | bytes 1572872 | tf_op jit(solution)/shard_map/ppermute | solution.py:46
  74.7 14.9 %copy-start.21 = (bf16[8192]{0:T(1024)(128)(2,1)S(1)}, bf16[8192]{0:T(1024)(128)(2,1)}, u32[]{:S(2)}) copy-start(bf16[8192]{0:T(1024)(128)(2,1)} %param.9) | copy-start | bytes 49156
  75.5 9.2 %collective-permute-start.13 = (bf16[384,512]{1,0:T(8,128)(2,1)}, bf16[384,512]{1,0:T(8,128)(2,1)S(1)}, u32[]{:S(2)}, u32[]{:S(2)}) collective-permute-start(bf16[384,512]{1,0:T(8,128)(2,1)} %maximum_maximum_fusion.3), channel_id=1, source_target_pairs={{0,12},{1,13},{2,14},{3,15},{4,0},{5,1},{6,2},{7,3},{8,4},{9,5},{1... | collective-permute-start | bytes 1179656 | tf_op jit(solution)/shard_map/ppermute | solution.py:46
  76.8 21.0 %copy-start.10 = (bf16[768,512]{1,0:T(8,128)(2,1)S(1)}, bf16[768,512]{1,0:T(8,128)(2,1)}, u32[]{:S(2)}) copy-start(bf16[768,512]{1,0:T(8,128)(2,1)} %copy-done.9) | copy-start | bytes 2359300
  76.8 8.4 %collective-permute-start.12 = (bf16[384,512]{1,0:T(8,128)(2,1)}, bf16[384,512]{1,0:T(8,128)(2,1)}, u32[]{:S(2)}, u32[]{:S(2)}) collective-permute-start(bf16[384,512]{1,0:T(8,128)(2,1)} %maximum_maximum_fusion.2), channel_id=1, source_target_pairs={{0,4},{1,5},{2,6},{3,7},{4,8},{5,9},{6,10},{7,11},{8,12},{9,13},{1... | collective-permute-start | bytes 1179656 | tf_op jit(solution)/shard_map/ppermute | solution.py:46
  84.7 11.6 %copy-start.18 = (bf16[384,512]{1,0:T(8,128)(2,1)}, bf16[384,512]{1,0:T(8,128)(2,1)S(1)}, u32[]{:S(2)}) copy-start(bf16[384,512]{1,0:T(8,128)(2,1)S(1)} %collective-permute-done.13.refs_3_) | copy-start | bytes 1179652
  87.7 31.0 %collective-permute-start.14 = (bf16[512,128]{1,0:T(8,128)(2,1)}, bf16[512,128]{1,0:T(8,128)(2,1)}, u32[]{:S(2)}, u32[]{:S(2)}) collective-permute-start(bf16[512,128]{1,0:T(8,128)(2,1)} %add_convert_fusion.3), channel_id=1, source_target_pairs={{0,1},{1,0},{2,3},{3,2},{4,5},{5,4},{6,7},{7,6},{8,9},{9,8},{10,11... | collective-permute-start | bytes 393224 | tf_op jit(solution)/shard_map/ppermute | solution.py:46
  97.8 3.4 %copy-start.2 = (bf16[8192,512]{1,0:T(8,128)(2,1)S(1)}, bf16[8192,512]{1,0:T(8,128)(2,1)}, u32[]{:S(2)}) copy-start(bf16[8192,512]{1,0:T(8,128)(2,1)} %refs_5_.3) | copy-start | bytes 25165828
  101.1 4.3 %copy-start.13 = (bf16[1024,512]{1,0:T(8,128)(2,1)S(1)}, bf16[1024,512]{1,0:T(8,128)(2,1)}, u32[]{:S(2)}) copy-start(bf16[1024,512]{1,0:T(8,128)(2,1)} %copy-done.12) | copy-start | bytes 3145732
  101.1 4.3 %copy-start.15 = (bf16[1024,512]{1,0:T(8,128)(2,1)S(1)}, bf16[1024,512]{1,0:T(8,128)(2,1)}, u32[]{:S(2)}) copy-start(bf16[1024,512]{1,0:T(8,128)(2,1)} %copy-done.14) | copy-start | bytes 3145732
  105.5 3.4 %copy-start.3 = (bf16[8192,512]{1,0:T(8,128)(2,1)S(1)}, bf16[8192,512]{1,0:T(8,128)(2,1)}, u32[]{:S(2)}) copy-start(bf16[8192,512]{1,0:T(8,128)(2,1)} %refs_5_.3) | copy-start | bytes 25165828
  108.8 4.4 %copy-start.17 = (bf16[832,512]{1,0:T(8,128)(2,1)S(1)}, bf16[832,512]{1,0:T(8,128)(2,1)}, u32[]{:S(2)}) copy-start(bf16[832,512]{1,0:T(8,128)(2,1)} %copy-done.16) | copy-start | bytes 2555908
  127.8 3.4 %copy-start.4 = (bf16[512,8192]{1,0:T(8,128)(2,1)S(1)}, bf16[512,8192]{1,0:T(8,128)(2,1)}, u32[]{:S(2)}) copy-start(bf16[512,8192]{1,0:T(8,128)(2,1)} %w_ref.7) | copy-start | bytes 25165828
  134.6 23.9 %collective-permute-start.22 = (bf16[512,512]{1,0:T(8,128)(2,1)S(1)}, bf16[512,512]{1,0:T(8,128)(2,1)S(1)}, u32[]{:S(2)}, u32[]{:S(2)}) collective-permute-start(bf16[512,512]{1,0:T(8,128)(2,1)S(1)} %pad_maximum_fusion.15), channel_id=1, source_target_pairs={{0,12},{1,13},{2,14},{3,15},{4,0},{5,1},{6,2},{7,3},{8,4},{9,5},{1... | collective-permute-start | bytes 1572872 | tf_op jit(solution)/shard_map/ppermute | solution.py:46
  135.2 23.3 %collective-permute-start.21 = (bf16[512,512]{1,0:T(8,128)(2,1)S(1)}, bf16[512,512]{1,0:T(8,128)(2,1)S(1)}, u32[]{:S(2)}, u32[]{:S(2)}) collective-permute-start(bf16[512,512]{1,0:T(8,128)(2,1)S(1)} %pad_maximum_fusion.14), channel_id=1, source_target_pairs={{0,4},{1,5},{2,6},{3,7},{4,8},{5,9},{6,10},{7,11},{8,12},{9,13},{1... | collective-permute-start | bytes 1572872 | tf_op jit(solution)/shard_map/ppermute | solution.py:46
  146.3 12.1 %collective-permute-start.15 = (bf16[256,512]{1,0:T(8,128)(2,1)}, bf16[256,512]{1,0:T(8,128)(2,1)S(1)}, u32[]{:S(2)}, u32[]{:S(2)}) collective-permute-start(bf16[256,512]{1,0:T(8,128)(2,1)} %get-tuple-element.98), channel_id=1, source_target_pairs={{0,4},{1,5},{2,6},{3,7},{4,8},{5,9},{6,10},{7,11},{8,12},{9,13},{1... | collective-permute-start | bytes 786440 | tf_op jit(solution)/shard_map/ppermute | solution.py:46
  148.4 10.0 %collective-permute-start.16 = (bf16[256,512]{1,0:T(8,128)(2,1)S(1)}, bf16[256,512]{1,0:T(8,128)(2,1)S(1)}, u32[]{:S(2)}, u32[]{:S(2)}) collective-permute-start(bf16[256,512]{1,0:T(8,128)(2,1)S(1)} %get-tuple-element.97), channel_id=1, source_target_pairs={{0,12},{1,13},{2,14},{3,15},{4,0},{5,1},{6,2},{7,3},{8,4},{9,5},{1... | collective-permute-start | bytes 786440 | tf_op jit(solution)/shard_map/ppermute | solution.py:46
  148.4 3.4 %copy-start.5 = (bf16[512,8192]{1,0:T(8,128)(2,1)S(1)}, bf16[512,8192]{1,0:T(8,128)(2,1)}, u32[]{:S(2)}) copy-start(bf16[512,8192]{1,0:T(8,128)(2,1)} %w_ref.7) | copy-start | bytes 25165828
  158.8 13.3 %collective-permute-start.18 = (bf16[768,512]{1,0:T(8,128)(2,1)S(1)}, bf16[768,512]{1,0:T(8,128)(2,1)S(1)}, u32[]{:S(2)}, u32[]{:S(2)}) collective-permute-start(bf16[768,512]{1,0:T(8,128)(2,1)S(1)} %pad_maximum_fusion.9), channel_id=1, source_target_pairs={{0,12},{1,13},{2,14},{3,15},{4,0},{5,1},{6,2},{7,3},{8,4},{9,5},{1... | collective-permute-start | bytes 2359304 | tf_op jit(solution)/shard_map/ppermute | solution.py:46
  159.0 15.6 %collective-permute-start.17 = (bf16[768,512]{1,0:T(8,128)(2,1)S(1)}, bf16[768,512]{1,0:T(8,128)(2,1)S(1)}, u32[]{:S(2)}, u32[]{:S(2)}) collective-permute-start(bf16[768,512]{1,0:T(8,128)(2,1)S(1)} %pad_maximum_fusion.8), channel_id=1, source_target_pairs={{0,4},{1,5},{2,6},{3,7},{4,8},{5,9},{6,10},{7,11},{8,12},{9,13},{1... | collective-permute-start | bytes 2359304 | tf_op jit(solution)/shard_map/ppermute | solution.py:46
  162.3 26.4 %collective-permute-start.23 = (bf16[1024,512]{1,0:T(8,128)(2,1)S(1)}, bf16[1024,512]{1,0:T(8,128)(2,1)S(1)}, u32[]{:S(2)}, u32[]{:S(2)}) collective-permute-start(bf16[1024,512]{1,0:T(8,128)(2,1)S(1)} %pad_maximum_fusion.1), channel_id=1, source_target_pairs={{0,4},{1,5},{2,6},{3,7},{4,8},{5,9},{6,10},{7,11},{8,12},{9,13},{1... | collective-permute-start | bytes 3145736 | tf_op jit(solution)/shard_map/ppermute | solution.py:46
  175.0 22.1 %collective-permute-start.24 = (bf16[1024,512]{1,0:T(8,128)(2,1)S(1)}, bf16[1024,512]{1,0:T(8,128)(2,1)S(1)}, u32[]{:S(2)}, u32[]{:S(2)}) collective-permute-start(bf16[1024,512]{1,0:T(8,128)(2,1)S(1)} %pad_maximum_fusion.2), channel_id=1, source_target_pairs={{0,12},{1,13},{2,14},{3,15},{4,0},{5,1},{6,2},{7,3},{8,4},{9,5},{1... | collective-permute-start | bytes 3145736 | tf_op jit(solution)/shard_map/ppermute | solution.py:46
  177.4 14.5 %collective-permute-start.25 = (bf16[256,512]{1,0:T(8,128)(2,1)S(1)}, bf16[256,512]{1,0:T(8,128)(2,1)S(1)}, u32[]{:S(2)}, u32[]{:S(2)}) collective-permute-start(bf16[256,512]{1,0:T(8,128)(2,1)S(1)} %get-tuple-element.116), channel_id=1, source_target_pairs={{0,1},{1,2},{2,3},{3,0},{4,5},{5,6},{6,7},{7,4},{8,9},{9,10},{10,1... | collective-permute-start | bytes 786440 | tf_op jit(solution)/shard_map/ppermute | solution.py:46
  179.5 12.4 %collective-permute-start.26 = (bf16[256,512]{1,0:T(8,128)(2,1)S(1)}, bf16[256,512]{1,0:T(8,128)(2,1)S(1)}, u32[]{:S(2)}, u32[]{:S(2)}) collective-permute-start(bf16[256,512]{1,0:T(8,128)(2,1)S(1)} %get-tuple-element.115), channel_id=1, source_target_pairs={{0,3},{1,0},{2,1},{3,2},{4,7},{5,4},{6,5},{7,6},{8,11},{9,8},{10,9... | collective-permute-start | bytes 786440 | tf_op jit(solution)/shard_map/ppermute | solution.py:46
  180.7 20.3 %collective-permute-start.19 = (bf16[512,512]{1,0:T(8,128)(2,1)S(1)}, bf16[512,512]{1,0:T(8,128)(2,1)S(1)}, u32[]{:S(2)}, u32[]{:S(2)}) collective-permute-start(bf16[512,512]{1,0:T(8,128)(2,1)S(1)} %pad_maximum_fusion.12), channel_id=1, source_target_pairs={{0,4},{1,5},{2,6},{3,7},{4,8},{5,9},{6,10},{7,11},{8,12},{9,13},{1... | collective-permute-start | bytes 1572872 | tf_op jit(solution)/shard_map/ppermute | solution.py:46
  188.7 14.3 %collective-permute-start.20 = (bf16[512,512]{1,0:T(8,128)(2,1)S(1)}, bf16[512,512]{1,0:T(8,128)(2,1)S(1)}, u32[]{:S(2)}, u32[]{:S(2)}) collective-permute-start(bf16[512,512]{1,0:T(8,128)(2,1)S(1)} %pad_maximum_fusion.13), channel_id=1, source_target_pairs={{0,12},{1,13},{2,14},{3,15},{4,0},{5,1},{6,2},{7,3},{8,4},{9,5},{1... | collective-permute-start | bytes 1572872 | tf_op jit(solution)/shard_map/ppermute | solution.py:46
  197.6 10.5 %collective-permute-start.27 = (bf16[512,512]{1,0:T(8,128)(2,1)S(1)}, bf16[512,512]{1,0:T(8,128)(2,1)S(1)}, u32[]{:S(2)}, u32[]{:S(2)}) collective-permute-start(bf16[512,512]{1,0:T(8,128)(2,1)S(1)} %pad_maximum_fusion.16), channel_id=1, source_target_pairs={{0,1},{1,2},{2,3},{3,0},{4,5},{5,6},{6,7},{7,4},{8,9},{9,10},{10,1... | collective-permute-start | bytes 1572872 | tf_op jit(solution)/shard_map/ppermute | solution.py:46
  200.0 10.4 %copy-start.1 = (s32[64,4]{0,1:T(4,128)S(1)}, s32[64,4]{0,1:T(4,128)}, u32[]{:S(2)}) copy-start(s32[64,4]{0,1:T(4,128)} %param.14) | copy-start | bytes 3076
  200.1 9.2 %collective-permute-start.28 = (bf16[512,512]{1,0:T(8,128)(2,1)S(1)}, bf16[512,512]{1,0:T(8,128)(2,1)S(1)}, u32[]{:S(2)}, u32[]{:S(2)}) collective-permute-start(bf16[512,512]{1,0:T(8,128)(2,1)S(1)} %pad_maximum_fusion.17), channel_id=1, source_target_pairs={{0,3},{1,0},{2,1},{3,2},{4,7},{5,4},{6,5},{7,6},{8,11},{9,8},{10,9... | collective-permute-start | bytes 1572872 | tf_op jit(solution)/shard_map/ppermute | solution.py:46
  (6 other events, 11.6 us)
Sparse Core Ops, SparseCore 0:
  9.1 34.6 all-gather.1

commit v2 on v0

v2 whole, which is shorter than its diff:
```python
import math

import jax
import jax.numpy as jnp
from jax import lax
from jax.experimental import pallas as pl
from jax.experimental.pallas import tpu as pltpu
from jax.sharding import PartitionSpec as P

HEADS = 64
KVH = 8
HD = 128
PB = 64
PDEPTH = 4
HALF = 256
AXES = ("branch", "tensor")
F32 = jnp.float32
BF16 = jnp.bfloat16
MIB = 1024 * 1024


def pairs(move):
    table = []
    for z in range(4):
        for c in range(2):
            for x in range(4):
                for y in range(4):
                    z2, c2, x2, y2 = move(z, c, x, y)
                    target = ((z2 % 4) * 2 + c2 % 2) * 16 + (x2 % 4) * 4 + y2 % 4
                    table.append(((z * 2 + c) * 16 + x * 4 + y, target))
    return table


HOPS = {}
for step in (1, -1):
    HOPS["first", step] = pairs(
        lambda z, c, x, y, s=step: (z, c, x, y + s) if c == 0 else (z, c, x + s, y)
    )
    HOPS["second", step] = pairs(
        lambda z, c, x, y, s=step: (z, c, x + s, y) if c == 0 else (z, c, x, y + s)
    )
HOPS["twin", 1] = pairs(lambda z, c, x, y: (z, c, x, y ^ 1))
HOPS["z_one", 1] = pairs(lambda z, c, x, y: (z ^ 1 if c == 0 else 3 - z, c, x, y))
HOPS["z_two", 1] = pairs(lambda z, c, x, y: (3 - z if c == 0 else z ^ 1, c, x, y))
HOPS["core", 1] = pairs(lambda z, c, x, y: (z, c + 1, x, y))


def hop(value, axis, step):
    return lax.ppermute(value, AXES, HOPS[axis, step])


def both(forward, backward, axis):
    return hop(forward, axis, 1), hop(backward, axis, -1)


def stack_rows(*parts):
    return jnp.concatenate(parts, axis=0)


def plus(base, *terms):
    total = base.astype(F32)
    for term in terms:
        total = total + term.astype(F32)
    return total.astype(BF16)


def pack(block):
    quarter = block.shape[0] // 4
    return jnp.concatenate([block[k * quarter : (k + 1) * quarter] for k in range(4)], axis=1)


def unpack(block):
    return jnp.concatenate([block[:, k * HD : (k + 1) * HD] for k in range(4)], axis=0)


def params(mebibytes):
    return pltpu.CompilerParams(vmem_limit_bytes=mebibytes * MIB)


def estimate(flops, moved):
    return pl.CostEstimate(flops=flops, bytes_accessed=moved, transcendentals=0)


VMEM = pl.BlockSpec(memory_space=pltpu.VMEM)
SMEM = pl.BlockSpec(memory_space=pltpu.SMEM)
FIXED = pl.BlockSpec(memory_space=pltpu.HBM)
ANYWHERE = pl.BlockSpec(memory_space=pl.ANY)
GROUP = 2
CHUNK = 64
WIDE = 512


def in_vmem(arrays):
    return [pltpu.with_memory_space_constraint(a, pltpu.VMEM) for a in arrays]


def place_of(order_ref, i, j):
    return order_ref[i * 4 + j]


def assemble(arrays, outputs):
    n_arrays = len(arrays)

    def body(*refs):
        for o_ref, (_, pieces) in zip(refs[n_arrays:], outputs, strict=True):
            for row, column, rows, columns, terms in pieces:
                parts = [refs[a][r : r + rows, c : c + columns] for a, r, c in terms]
                if len(parts) > 1:
                    total = parts[0].astype(F32)
                    for part in parts[1:]:
                        total = total + part.astype(F32)
                    parts = [total.astype(BF16)]
                o_ref[row : row + rows, column : column + columns] = parts[0]

    return pl.pallas_call(
        body,
        out_shape=[pltpu.VMEM(shape, BF16) for shape, _ in outputs],
        in_specs=[VMEM] * n_arrays,
        out_specs=[VMEM] * len(outputs),
        compiler_params=params(8),
        cost_estimate=estimate(0, 0),
        name="assemble",
    )(*in_vmem(arrays))


def rows_piece(row, rows, *terms):
    return (row, 0, rows, WIDE, [(a, r, 0) for a, r in terms])


def packed(row, rows, *terms):
    quarter = rows // 4
    pieces = []
    for k in range(4):
        places = [(a, start + k * quarter, column) for a, start, column in terms]
        pieces.append((row, k * HD, quarter, HD, places))
    return pieces


def kv_partial(tokens, gain, w_keyvalue, order, steps):
    spots = [(i, j) for i in steps for j in range(4)]
    count = len(spots)

    def body(order_ref, t_ref, g_ref, w_ref, o_ref, weights, sems):
        copies = []
        for n, (i, j) in enumerate(spots):
            target = place_of(order_ref, i, j)
            column = pl.multiple_of(lax.div(target, 2) * HD, HD)
            copies.append(
                pltpu.make_async_copy(
                    w_ref.at[lax.rem(target, 2), :, pl.ds(column, HD)],
                    weights.at[:, pl.ds(n * HD, HD)],
                    sems.at[n],
                )
            )
        for copy in copies:
            copy.start()
        own = g_ref[pl.ds(place_of(order_ref, 0, 0), 1), :]
        scaled = (t_ref[...].astype(F32) * own).astype(BF16)
        for copy in copies:
            copy.wait()
        for n in range(0, count * HD, WIDE):
            o_ref[:, n : n + WIDE] = jnp.dot(
                scaled, weights[:, n : n + WIDE], preferred_element_type=F32
            ).astype(BF16)

    return pl.pallas_call(
        body,
        out_shape=jax.ShapeDtypeStruct((WIDE, count * HD), BF16),
        in_specs=[SMEM, VMEM, VMEM, FIXED],
        out_specs=VMEM,
        scratch_shapes=[
            pltpu.VMEM((WIDE, count * HD), BF16),
            pltpu.SemaphoreType.DMA((count,)),
        ],
        compiler_params=params(7),
        cost_estimate=estimate(0, 0),
        name="kv_partial",
    )(order, tokens, gain, w_keyvalue)


def query_part(blocks, arrays, order, gain, w_query, carry):
    count = len(blocks)
    n_arrays = len(arrays)
    first = carry is None

    def body(order_ref, *refs):
        a_refs = refs[:n_arrays]
        g_ref, w_ref = refs[n_arrays : n_arrays + 2]
        q_ref, s_ref, scaled, weights, sems = refs[-5:]
        places = [place_of(order_ref, *spot) for spot, _ in blocks]

        def fetch(n):
            return pltpu.make_async_copy(
                w_ref.at[pl.ds(pl.multiple_of(places[n] * WIDE, WIDE), WIDE), :],
                weights.at[n // GROUP % 2, pl.ds(n % GROUP * WIDE, WIDE), :],
                sems.at[n],
            )

        for n in range(min(count, 2 * GROUP)):
            fetch(n).start()
        s_ref[...] = jnp.zeros_like(s_ref) if first else refs[n_arrays + 3][...]
        for low in range(0, count, GROUP):
            members = range(low, min(low + GROUP, count))
            for n in members:
                own = g_ref[pl.ds(places[n], 1), :]
                lanes_at = pl.ds((n - low) * WIDE, WIDE)
                for which, start, target, size in blocks[n][1]:

                    @pl.loop(0, size // CHUNK)
                    def _(step, which=which, start=start, target=target, own=own, lanes_at=lanes_at):
                        row = pl.multiple_of(step * CHUNK, CHUNK)
                        values = a_refs[which][pl.ds(start + row, CHUNK), :].astype(F32)
                        squares = values * values
                        lanes = squares[:, :HD]
                        for k in range(1, WIDE // HD):
                            lanes = lanes + squares[:, k * HD : (k + 1) * HD]
                        s_ref[pl.ds(target + row, CHUNK), :] += lanes
                        scaled[pl.ds(target + row, CHUNK), lanes_at] = (values * own).astype(BF16)

            for n in members:
                fetch(n).wait()
            depth = len(members) * WIDE
            for half in range(2):
                rows = slice(half * HALF, (half + 1) * HALF)
                product = jnp.dot(
                    scaled[rows, :depth], weights[low // GROUP % 2, :depth, :], preferred_element_type=F32
                )
                if low:
                    q_ref[rows, :] += product
                else:
                    q_ref[rows, :] = product if first else refs[n_arrays + 2][rows, :] + product
            for n in range(low + 2 * GROUP, min(low + 3 * GROUP, count)):
                fetch(n).start()

    carried = [] if first else list(carry)
    return pl.pallas_call(
        body,
        out_shape=(
            jax.ShapeDtypeStruct((WIDE, WIDE), F32),
            jax.ShapeDtypeStruct((WIDE, HD), F32),
        ),
        in_specs=[SMEM] + [VMEM] * n_arrays + [VMEM, FIXED] + [VMEM] * len(carried),
        out_specs=(VMEM, VMEM),
        scratch_shapes=[
            pltpu.VMEM((WIDE, GROUP * WIDE), BF16),
            pltpu.VMEM((2, GROUP * WIDE, WIDE), BF16),
            pltpu.SemaphoreType.DMA((count,)),
        ],
        input_output_aliases={} if first else {n_arrays + 3: 0, n_arrays + 4: 1},
        compiler_params=params(14),
        cost_estimate=estimate(0, 0),
        name="query_part",
    )(order, *in_vmem(arrays), gain, w_query, *in_vmem(carried))


def gather_blocks(pools, codes):
    branches = codes.shape[0]
    span = PDEPTH * PB + PB

    def body(code_ref, *refs):
        pool_refs, (o_ref, sems) = refs[:4], refs[4:]
        for b in range(branches):
            for d in range(PDEPTH):
                code = code_ref[b, d]
                slot, block = lax.rem(lax.div(code, 16), 2), lax.rem(code, 16)
                for which, source in enumerate(pool_refs):

                    @pl.when(lax.div(code, 32) == which)
                    def _(source=source):
                        pltpu.make_async_copy(
                            source.at[slot, :, block], o_ref.at[b, :, pl.ds(d * PB, PB), :], sems.at[b, d]
                        ).start()

        for b in range(branches):
            for d in range(PDEPTH):
                pltpu.make_async_copy(
                    pool_refs[0].at[0, :, 0], o_ref.at[b, :, pl.ds(d * PB, PB), :], sems.at[b, d]
                ).wait()

    return pl.pallas_call(
        body,
        out_shape=jax.ShapeDtypeStruct((branches, 2, span, HD), BF16),
        in_specs=[SMEM] + [ANYWHERE] * 4,
        out_specs=VMEM,
        scratch_shapes=[pltpu.SemaphoreType.DMA((branches, PDEPTH))],
        compiler_params=params(8),
        cost_estimate=estimate(0, 0),
        name="gather_blocks",
    )(codes, *pools)


def middle(query, squares, order, keyvalue, tables, prefix, lengths, w_output):
    branches = WIDE // PB
    heads = WIDE // HD
    span = PDEPTH * PB + PB
    scale = 1.0 / math.sqrt(HD)
    spots = [(2, 2), (1, 2), (3, 2), (0, 2)]

    def body(
        order_ref, len_ref, q_ref, s_ref, mine_ref, other_ref, cos_ref, sin_ref, prefix_ref, wo_ref,
        heads_ref, far_ref, kv_ref,
        wo, qb, wsems,
    ):
        copies = []
        for n, (i, j) in enumerate(spots):
            column = pl.multiple_of(place_of(order_ref, i, j) * WIDE, WIDE)
            copies.append(
                pltpu.make_async_copy(wo_ref.at[:, pl.ds(column, WIDE)], wo.at[n], wsems.at[n])
            )
        for copy in copies:
            copy.start()
        total = jnp.sum(s_ref[...], axis=1, keepdims=True)
        factor = lax.rsqrt(total * (1.0 / 8192.0) + 1e-06)
        cos_part = cos_ref[...] * factor
        sin_part = sin_ref[...] * factor

        def rope(v, cos_part, sin_part):
            return (v * cos_part + pltpu.roll(v, HD // 2, 1) * sin_part).astype(BF16)

        even = lax.rem(place_of(order_ref, 0, 0), 2) == 0
        mine, other = mine_ref[...].astype(F32), other_ref[...].astype(F32)
        new_keys = rope(jnp.where(even, mine, other), cos_part, sin_part)
        new_values = (jnp.where(even, other, mine) * factor).astype(BF16)
        for b in range(branches):
            kv_ref[b, 0, PDEPTH * PB :, :] = new_keys[b * PB : (b + 1) * PB]
            kv_ref[b, 1, PDEPTH * PB :, :] = new_values[b * PB : (b + 1) * PB]
        cos_part, sin_part = cos_part * scale, sin_part * scale
        for h in range(heads):
            qb[h] = rope(q_ref[:, h * HD : (h + 1) * HD], cos_part, sin_part)
        column = lax.broadcasted_iota(jnp.int32, (heads * PB, span), 1)
        within = lax.rem(lax.broadcasted_iota(jnp.int32, (heads * PB, span), 0), PB)
        own_seen = (column >= PDEPTH * PB) & (column - PDEPTH * PB <= within)
        for b in range(branches):
            queries = qb[:, b * PB : (b + 1) * PB, :].reshape(heads * PB, HD)
            scores = lax.dot_general(
                queries, kv_ref[b, 0], (((1,), (1,)), ((), ())), preferred_element_type=F32
            )
            seen = (column < len_ref[b] * PB) | own_seen
            scores = jnp.where(seen, scores, -1e30)
            highest = jnp.max(scores, axis=1, keepdims=True)
            expo = jnp.exp(scores - highest)
            inverse = 1.0 / jnp.sum(expo, axis=1, keepdims=True)
            mixed = jnp.dot(expo.astype(BF16), kv_ref[b, 1], preferred_element_type=F32)
            mixed = (mixed * inverse).astype(BF16)
            for h in range(heads):
                heads_ref[b * PB : (b + 1) * PB, h * HD : (h + 1) * HD] = mixed[
                    h * PB : (h + 1) * PB
                ]
        for n, copy in enumerate(copies):
            copy.wait()
            far_ref[n] = jnp.dot(heads_ref[...], wo[n], preferred_element_type=F32).astype(BF16)

    return pl.pallas_call(
        body,
        out_shape=(
            jax.ShapeDtypeStruct((WIDE, WIDE), BF16),
            jax.ShapeDtypeStruct((len(spots), WIDE, WIDE), BF16),
            jax.ShapeDtypeStruct(prefix.shape, BF16),
        ),
        in_specs=[SMEM] * 2 + [VMEM] * 7 + [FIXED],
        out_specs=(VMEM, VMEM, VMEM),
        scratch_shapes=[
            pltpu.VMEM((len(spots), WIDE, WIDE), BF16),
            pltpu.VMEM((heads, WIDE, HD), BF16),
            pltpu.SemaphoreType.DMA((len(spots),)),
        ],
        input_output_aliases={8: 2},
        compiler_params=params(9),
        cost_estimate=estimate(0, 0),
        name="middle",
    )(
        order, lengths, *in_vmem([query, squares, *keyvalue, *tables, prefix]), w_output
    )[:2]


def output_part(heads_out, w_output, order, spots):
    count = len(spots)

    def body(order_ref, h_ref, w_ref, o_ref, weights, sems):
        copies = []
        for n, (i, j) in enumerate(spots):
            column = pl.multiple_of(place_of(order_ref, i, j) * WIDE, WIDE)
            copies.append(
                pltpu.make_async_copy(w_ref.at[:, pl.ds(column, WIDE)], weights.at[n], sems.at[n])
            )
        for copy in copies:
            copy.start()
        for n, copy in enumerate(copies):
            copy.wait()
            o_ref[n] = jnp.dot(h_ref[...], weights[n], preferred_element_type=F32).astype(BF16)

    return pl.pallas_call(
        body,
        out_shape=jax.ShapeDtypeStruct((count, WIDE, WIDE), BF16),
        in_specs=[SMEM, VMEM, FIXED],
        out_specs=VMEM,
        scratch_shapes=[
            pltpu.VMEM((count, WIDE, WIDE), BF16),
            pltpu.SemaphoreType.DMA((count,)),
        ],
        compiler_params=params(7),
        cost_estimate=estimate(0, 0),
        name="output_part",
    )(order, heads_out, w_output)


def local(tokens, gain, w_query, w_keyvalue, w_output, cache, parents, lengths):
    bar = lax.optimization_barrier
    group = lax.axis_index("branch")
    place = lax.axis_index("tensor")
    x, y = place // 4, place % 4
    z, core = group // 2, group % 2
    row_count = tokens.shape[0]
    branch_count = row_count // PB

    count = jnp.arange(16, dtype=jnp.int32)
    i_step, j_step = count // 4, count % 4
    dx = jnp.where(core == 0, j_step, i_step)
    dy = jnp.where(core == 0, i_step, j_step)
    order = ((x + dx) % 4) * 4 + (y + dy) % 4
    gains = gain.astype(F32).reshape(16, WIDE)
    w_query, w_keyvalue, w_output = [
        pltpu.with_memory_space_constraint(w, pltpu.HBM) for w in (w_query, w_keyvalue, w_output)
    ]

    s1 = both(tokens, tokens, "first")
    kv = kv_partial(tokens, gains, w_keyvalue, order, (0, 1, 3, 2))
    k_far = both(kv[:HALF, 3 * WIDE :], kv[HALF:, 3 * WIDE :], "first")
    b1m, b1p, k_m, k_p, kv_near, cache = bar((*s1, *k_far, kv, cache))
    (near,) = assemble(
        [tokens, b1p, b1m],
        [((3 * WIDE, WIDE), [rows_piece(n * WIDE, WIDE, (n, 0)) for n in range(3)])],
    )
    s2 = both(near, near, "second")
    s3 = both(
        *assemble(
            [b1m, b1p, kv_near, k_m, k_p],
            [
                (
                    (3 * HALF, WIDE),
                    [
                        rows_piece(0, HALF, (0, 0)),
                        (HALF, 0, HALF, WIDE, [(2, 0, WIDE), (3, 0, 0)]),
                        (2 * HALF, 0, HALF, WIDE, [(2, HALF, WIDE)]),
                    ],
                ),
                (
                    (3 * HALF, WIDE),
                    [
                        rows_piece(0, HALF, (1, HALF)),
                        (HALF, 0, HALF, WIDE, [(2, 0, 2 * WIDE)]),
                        (2 * HALF, 0, HALF, WIDE, [(2, HALF, 2 * WIDE), (4, 0, 0)]),
                    ],
                ),
            ],
        ),
        "first",
    )
    kv_head = place * (w_query.shape[1] // HD) // (HEADS // KVH)
    cache_head = lax.dynamic_slice_in_dim(cache, kv_head * HD, HD, 3)
    z_one = hop(cache_head, "z_one", 1)
    part = query_part(
        [((0, 0), [(0, 0, 0, WIDE)]), ((1, 0), [(1, 0, 0, WIDE)]), ((3, 0), [(2, 0, 0, WIDE)])],
        [tokens, b1p, b1m],
        order,
        gains,
        w_query,
        None,
    )
    b3m, b3p, b2m, b2p, z_one, *part = bar((*s3, *s2, z_one, *part))
    ksum, to_next, to_last = assemble(
        [b3m, b3p, kv_near, b2m, b2p],
        [
            ((WIDE, WIDE), [(0, 0, WIDE, WIDE, [(2, 0, 0), (0, HALF, 0), (1, HALF, 0)])]),
            (
                (5 * HALF + HALF // 4, WIDE),
                [rows_piece(0, HALF, (0, 0)), rows_piece(HALF, HALF, (1, 0))]
                + [rows_piece(WIDE + n * HALF, HALF, (3, n * WIDE)) for n in range(3)]
                + packed(5 * HALF, HALF, (2, 0, 2 * HD), (0, HALF, 2 * HD), (1, HALF, 2 * HD)),
            ),
            (
                (5 * HALF + HALF // 4, WIDE),
                [rows_piece(0, HALF, (0, 0)), rows_piece(HALF, HALF, (1, 0))]
                + [rows_piece(WIDE + n * HALF, HALF, (4, n * WIDE + HALF)) for n in range(3)]
                + packed(5 * HALF, HALF, (2, HALF, 2 * HD), (0, WIDE, 2 * HD), (1, WIDE, 2 * HD)),
            ),
        ],
    )
    s5 = both(to_next, to_last, "second")
    pool = jnp.stack([cache_head, z_one])
    z_two = hop(pool, "z_two", 1)
    near_twin = hop(pool, "core", 1)
    my_lengths = lax.dynamic_slice_in_dim(lengths, group * branch_count, branch_count, 0)
    my_parents = lax.dynamic_slice_in_dim(parents, group * branch_count, branch_count, 0)
    owner = my_parents // 16
    owner_z, owner_core = owner // 2, owner % 2
    across = z + 1 - 2 * (z % 2)
    partner = jnp.where(owner_core == 0, across, 3 - z)
    slot = jnp.where(
        owner_z == z, 0, jnp.where(owner_z == partner, 1, jnp.where(owner_z == (z + 2) % 4, 3, 2))
    )
    codes = jnp.where(owner_core == core, 0, 64) + slot * 16 + my_parents % 16

    positions = jnp.repeat(my_lengths, PB) * PB + jnp.tile(
        jnp.arange(PB, dtype=jnp.int32), branch_count
    )
    halfway = HD // 2
    frequency = jnp.exp(jnp.arange(halfway, dtype=F32) * (-2.0 * math.log(1000000.0) / HD))
    angles = positions.astype(F32)[:, None] * frequency[None, :]
    cosine, sine = jnp.cos(angles), jnp.sin(angles)
    cosine = jnp.concatenate([cosine, cosine], axis=1)
    sine = jnp.concatenate([-sine, sine], axis=1)

    part = query_part(
        [
            ((2, 0), [(0, 0, 0, HALF), (1, 0, HALF, HALF)]),
            ((0, 1), [(2, 0, 0, WIDE)]),
            ((1, 1), [(2, WIDE, 0, WIDE)]),
            ((3, 1), [(2, 2 * WIDE, 0, WIDE)]),
            ((0, 3), [(3, 0, 0, WIDE)]),
            ((1, 3), [(3, WIDE, 0, WIDE)]),
            ((3, 3), [(3, 2 * WIDE, 0, WIDE)]),
        ],
        [b3m, b3p, b2p, b2m],
        order,
        gains,
        w_query,
        part,
    )
    b5m, b5p, z_two, near_twin, cosine, sine, codes, *part = bar(
        (*s5, z_two, near_twin, cosine, sine, codes, *part)
    )
    quarter = HALF // 4
    s7 = both(
        *assemble(
            [b5m, b5p, ksum],
            [
                (
                    (HALF + WIDE // 4, WIDE),
                    [rows_piece(0, HALF, (0, 0))]
                    + [
                        piece
                        for k in range(4)
                        for piece in [
                            (
                                HALF,
                                k * HD,
                                2 * quarter,
                                HD,
                                [(2, k * 2 * quarter, HD)],
                            )
                        ]
                        if k >= 2
                    ]
                    + [
                        (
                            HALF + t * quarter,
                            k * HD,
                            quarter,
                            HD,
                            [(2, (2 * k + t) * quarter, HD), (0, 5 * HALF, (2 * k + t) * HD)],
                        )
                        for k in range(2)
                        for t in range(2)
                    ],
                ),
                (
                    (HALF + WIDE // 4, WIDE),
                    [rows_piece(0, HALF, (1, HALF))]
                    + [
                        (HALF, k * HD, 2 * quarter, HD, [(2, k * 2 * quarter, 3 * HD)])
                        for k in range(2)
                    ]
                    + [
                        (
                            HALF + t * quarter,
                            k * HD,
                            quarter,
                            HD,
                            [(2, (2 * k + t) * quarter, 3 * HD), (1, 5 * HALF, (2 * k + t - 4) * HD)],
                        )
                        for k in range(2, 4)
                        for t in range(2)
                    ],
                ),
            ],
        ),
        "second",
    )
    far_twin = hop(z_two, "core", 1)
    pools = [
        pltpu.with_memory_space_constraint(a, pltpu.HBM) for a in (pool, z_two, near_twin, far_twin)
    ]
    prefix = gather_blocks(pools, codes)
    part = query_part(
        [
            ((2, 1), [(0, 0, 0, WIDE)]),
            ((2, 3), [(1, 0, 0, WIDE)]),
            ((0, 2), [(1, WIDE, 0, HALF), (0, WIDE, HALF, HALF)]),
            ((1, 2), [(1, WIDE + HALF, 0, HALF), (0, WIDE + HALF, HALF, HALF)]),
            ((3, 2), [(1, 2 * WIDE, 0, HALF), (0, 2 * WIDE, HALF, HALF)]),
        ],
        [b5p, b5m],
        order,
        gains,
        w_query,
        part,
    )
    b7m, b7p, prefix, *part = bar((*s7, prefix, *part))
    (mine,) = assemble(
        [ksum, b7m, b7p],
        [
            (
                (WIDE, HD),
                [
                    (k * 128, 0, 128, HD, [(0, k * 128, 0), (1, HALF, k * HD), (2, HALF, k * HD)])
                    for k in range(4)
                ],
            )
        ],
    )
    other = hop(mine, "twin", 1)
    part = query_part(
        [
            ((2, 2), [(0, 0, 0, HALF), (1, 0, HALF, HALF)]),
        ],
        [b7m, b7p],
        order,
        gains,
        w_query,
        part,
    )
    heads_out, far = middle(
        *part, order, (mine, other), (cosine, sine), prefix, my_lengths, w_output
    )

    ra = both(far[0, :HALF], far[0, HALF:], "second")
    rb = both(
        stack_rows(far[1, :HALF], far[2, :HALF], far[3, :HALF]),
        stack_rows(far[1, HALF:], far[2, HALF:], far[3, HALF:]),
        "second",
    )
    spots = [(2, 1), (2, 3), (1, 1), (3, 1), (1, 3), (3, 3)]
    rest = output_part(heads_out, w_output, order, spots)
    ra_m, ra_p, rest = bar((*ra, rest))
    q21, q23, q11, q31, q13, q33 = [rest[n] for n in range(6)]
    rc = both(
        stack_rows(plus(q21[:HALF], ra_m), q21[HALF:]),
        stack_rows(q23[:HALF], plus(q23[HALF:], ra_p)),
        "second",
    )
    rb_m, rb_p = bar(rb)
    rd = both(
        stack_rows(
            plus(q11[:HALF], rb_m[:HALF]), q11[HALF:], plus(q31[:HALF], rb_m[HALF:WIDE]), q31[HALF:]
        ),
        stack_rows(
            q13[:HALF], plus(q13[HALF:], rb_p[:HALF]), q33[:HALF], plus(q33[HALF:], rb_p[HALF:WIDE])
        ),
        "second",
    )
    spots = [(2, 0), (0, 1), (0, 3), (1, 0), (3, 0), (0, 0)]
    heads_late, rb_m = bar((heads_out, rb_m))
    rest = output_part(heads_late, w_output, order, spots)
    rc_m, rc_p, rest = bar((*rc, rest))
    q20, q01, q03, q10, q30, q00 = [rest[n] for n in range(6)]
    sum2 = plus(q20, rc_m, rc_p)
    re = both(sum2[:HALF], sum2[HALF:], "first")
    rf = both(
        stack_rows(plus(q01[:HALF], rb_m[WIDE:]), q01[HALF:]),
        stack_rows(q03[:HALF], plus(q03[HALF:], rb_p[WIDE:])),
        "second",
    )
    rd_m, rd_p, re_m, re_p = bar((*rd, *re))
    sum1 = stack_rows(
        plus(q10[:HALF], rd_m[:HALF], rd_p[:HALF], re_m), plus(q10[HALF:], rd_m[HALF:WIDE], rd_p[HALF:WIDE])
    )
    sum3 = stack_rows(
        plus(q30[:HALF], rd_m[WIDE : WIDE + HALF], rd_p[WIDE : WIDE + HALF]),
        plus(q30[HALF:], rd_m[WIDE + HALF :], rd_p[WIDE + HALF :], re_p),
    )
    rg = both(sum1, sum3, "first")
    return plus(q00, *rf, *rg)


def solution(mesh):
    return jax.shard_map(
        local,
        mesh=mesh,
        in_specs=(
            P("branch", "tensor"),
            P(),
            P(None, "tensor"),
            P(None, "tensor", None),
            P("tensor", None),
            P(None, "branch", None, None),
            P(),
            P(),
        ),
        out_specs=P("branch", "tensor"),
        check_vma=False,
    )
```

time: 396 us -> 163 us (0.41)
  waiting for transfers between devices: 321 us -> 58.2 us
  Pallas kernels: 0 us -> 45.6 us
  starting transfers between devices: 0.3 us -> 41.6 us
  matrix products: 21.1 us -> 0 us
  other arithmetic: 25.9 us -> 6.61 us
  between operations: 13.4 us -> 0.36 us
    psum x2 -> x0, waiting for transfers between devices: 217 us -> none  [the longest x1 140 us: local(): lax.psum(partial_out.astype(jnp.bfloat16), 'tensor').astype(jnp.float32)]
    all_gather x2 -> x0, waiting for transfers between devices: 103 us -> none  [the longest x1 73.4 us: local(): full = lax.all_gather(tokens, 'tensor', axis=1, tiled=True)]
    ppermute x0 -> x31, waiting for transfers between devices: none -> 58.2 us  [hop(): return lax.ppermute(value, AXES, HOPS[axis, step])]
    pallas_call x0 -> x14, Pallas kernels: none -> 45.6 us  [the longest x4 16.9 us: query_part(): pl.pallas_call(body, out_shape=(jax.ShapeDtypeStruct((WIDE, WIDE), F32),...]
    ppermute x0 -> x31, starting transfers between devices: none -> 41.6 us  [hop(): return lax.ppermute(value, AXES, HOPS[axis, step])]
    dot_general x5 -> x0, matrix products: 21.1 us -> none  [the longest x1 9.46 us: local(): jnp.dot(normed, w_query, preferred_element_type=jnp.float32)]
    convert_element_type x5, other arithmetic: 13.5 us -> 2.64 us  [the longest x4 2.56 us: plus(): return total.astype(BF16)]
    gather x2 -> x0, local copies, waits for them, and re-layouts: 6.49 us -> none  [the longest x1 3.63 us: local(): pre_values = pool[1, flat_ids]]
  transfers between devices with their start and end apart: 4 -> 31, of which waited for: 4 -> 17; matrix products, arithmetic and copies ran while one was open for 6% -> 5% of each run, Pallas kernels for 0% -> 21%
where the time goes in v2:
time: 163 us
  waiting for transfers between devices  58.2 us (36%)
  Pallas kernels  45.6 us (28%)
  starting transfers between devices  41.6 us (26%)
  local copies, waits for them, and re-layouts  10.3 us (6%)
  other arithmetic  6.61 us (4%)
    ppermute x31, waiting for transfers between devices, hop(): return lax.ppermute(value, AXES, HOPS[axis, step])  58.2 us
    ppermute x31, starting transfers between devices, hop(): return lax.ppermute(value, AXES, HOPS[axis, step])  41.6 us
    pallas_call x4, Pallas kernels, query_part(): pl.pallas_call(body, out_shape=(jax.ShapeDtypeStruct((WIDE, WIDE), F32),...  16.9 us
    pallas_call x2, Pallas kernels, output_part(): pl.pallas_call(body, out_shape=jax.ShapeDtypeStruct((count, WIDE, WIDE),...  8.55 us
    pallas_call x5, Pallas kernels, assemble(): pl.pallas_call(body, out_shape=[pltpu.VMEM(shape, BF16) for shape, _ in o...  8.24 us
    unnamed x27, local copies, waits for them, and re-layouts  6.09 us
    pallas_call x1, Pallas kernels, middle(): pl.pallas_call(body, out_shape=(jax.ShapeDtypeStruct((WIDE, WIDE), BF16),...  6.05 us
    pallas_call x1, Pallas kernels, kv_partial(): pl.pallas_call(body, out_shape=jax.ShapeDtypeStruct((WIDE, count * HD), B...  3.62 us
  transfers between devices with their start and end apart: 31, of which 17 were waited for; matrix products, arithmetic and copies ran while one was open for 5% of the time, Pallas kernels for 21%

profile of v2, /device:TPU:6, one launch (start us, length us, event | category | flops | bytes accessed | tf_op | source)
XLA Modules:
  0.0 162.6 jit_solution(10812235403346930669)
XLA Ops:
  0.0 1.6 collective-permute-start
  1.6 1.7 %collective-permute-start.1 = (bf16[512,512]{1,0:T(8,128)(2,1)}, bf16[512,512]{1,0:T(8,128)(2,1)S(1)}, u32[]{:S(2)}, u32[]{:S(2)}) collective-permute-start(bf16[512,512]{1,0:T(8,128)(2,1)} %refs_0_.3), channel_id=1, source_target_pairs={{0,3},{1,0},{2,1},{3,2},{4,7},{5,4},{6,5},{7,6},{8,11},{9,8},{10,9... | collective-permute-start | bytes 1572872 | tf_op jit(solution)/shard_map/ppermute | solution.py:49
  5.0 3.6 %kv_partial.1.refs_2_ = bf16[512,2048]{1,0:T(8,128)(2,1)S(1)} custom-call(s32[16]{0:T(128)S(1)} %fusion.29.order_ref, bf16[512,512]{1,0:T(8,128)(2,1)S(1)} %copy-done.2, f32[16,512]{1,0:T(8,128)S(1)} %reshape.77.g_ref.refs_3_.refs_4_.refs_2_, bf16[2,512,1024]{2,1,0:T(8,128)(2,1)} %w_ref.3), custom_call_target="tpu_custom_call" | custom-call | tf_op jit(solution)/shard_map/kv_partial/pallas_call | solution.py:166
  9.1 2.9 %collective-permute-start.3 = (bf16[256,512]{1,0:T(8,128)(2,1)S(1)}, bf16[256,512]{1,0:T(8,128)(2,1)S(1)}, u32[]{:S(2)}, u32[]{:S(2)}) collective-permute-start(bf16[256,512]{1,0:T(8,128)(2,1)S(1)} %get-tuple-element.153), channel_id=1, source_target_pairs={{0,3},{1,0},{2,1},{3,2},{4,7},{5,4},{6,5},{7,6},{8,11},{9,8},{10,9... | collective-permute-start | bytes 786440 | tf_op jit(solution)/shard_map/ppermute | solution.py:49
  12.0 4.3 %collective-permute-done.2.refs_3_ = bf16[256,512]{1,0:T(8,128)(2,1)S(1)} collective-permute-done((bf16[256,512]{1,0:T(8,128)(2,1)S(1)}, bf16[256,512]{1,0:T(8,128)(2,1)S(1)}, u32[]{:S(2)}, u32[]{:S(2)}) %collective-permute-start.2) | collective-permute-done | bytes 262176 | tf_op jit(solution)/shard_map/ppermute | solution.py:49
  16.4 1.4 assemble.6
  18.2 1.6 %collective-permute-start.7 = (bf16[1536,512]{1,0:T(8,128)(2,1)}, bf16[1536,512]{1,0:T(8,128)(2,1)}, u32[]{:S(2)}, u32[]{:S(2)}) collective-permute-start(bf16[1536,512]{1,0:T(8,128)(2,1)} %assemble.6), channel_id=1, source_target_pairs={{0,12},{1,13},{2,14},{3,15},{4,0},{5,1},{6,2},{7,3},{8,4},{9,5},{1... | collective-permute-start | bytes 4718600 | tf_op jit(solution)/shard_map/ppermute | solution.py:49
  19.8 1.3 assemble.5
  21.8 2.6 %collective-permute-start.5 = (bf16[768,512]{1,0:T(8,128)(2,1)}, bf16[768,512]{1,0:T(8,128)(2,1)}, u32[]{:S(2)}, u32[]{:S(2)}) collective-permute-start(bf16[768,512]{1,0:T(8,128)(2,1)} %get-tuple-element.69), channel_id=1, source_target_pairs={{0,3},{1,0},{2,1},{3,2},{4,7},{5,4},{6,5},{7,6},{8,11},{9,8},{10,9... | collective-permute-start | bytes 2359304 | tf_op jit(solution)/shard_map/ppermute | solution.py:49
  24.4 1.9 %constant_dynamic-slice_fusion.1 = bf16[2,16,64,128]{3,2,1,0:T(8,128)(2,1)} fusion(bf16[2,16,64,1024]{3,2,1,0:T(8,128)(2,1)} %param.13, s32[]{:T(128)S(6)} %select_n.119), kind=kLoop, calls=%fused_computation.108 | loop fusion | bytes 1048580 | tf_op jit(solution)/shard_map/dynamic_slice | solution.py:460
  26.3 1.9 %collective-permute-start.8 = (bf16[2,16,64,128]{3,2,1,0:T(8,128)(2,1)}, bf16[2,16,64,128]{3,2,1,0:T(8,128)(2,1)}, u32[]{:S(2)}, u32[]{:S(2)}) collective-permute-start(bf16[2,16,64,128]{3,2,1,0:T(8,128)(2,1)} %constant_dynamic-slice_fusion.1), channel_id=1, source_target_pairs={{0,32},{1,33},{2,34},{3,35},{4,36},{5,37},{6,38},{7,39},{8,40},{9,... | collective-permute-start | bytes 1572872 | tf_op jit(solution)/shard_map/ppermute | solution.py:49
  31.3 3.0 %query_part.4 = (f32[512,512]{1,0:T(8,128)S(1)}, f32[512,128]{1,0:T(8,128)S(1)}) custom-call(s32[16]{0:T(128)S(1)} %fusion.29.order_ref, bf16[512,512]{1,0:T(8,128)(2,1)S(1)} %copy-done.4, bf16[512,512]{1,0:T(8,128)(2,1)S(1)} %copy-done.8, bf16[512,512]{1,0:T(8,128)(2,1)S(1)} %copy-done.6, f32[16,512]{1,0:T(8,128)S(1)} %reshape.77.g_ref.refs_3_.refs_4_.refs_2_, ...), custom_call_target="tpu_custom_call" | custom-call | tf_op jit(solution)/shard_map/query_part/pallas_call | solution.py:236
  34.3 1.5 collective-permute-done.8
  35.8 7.3 %collective-permute-done.4.refs_0_ = bf16[768,512]{1,0:T(8,128)(2,1)} collective-permute-done((bf16[768,512]{1,0:T(8,128)(2,1)}, bf16[768,512]{1,0:T(8,128)(2,1)}, u32[]{:S(2)}, u32[]{:S(2)}) %collective-permute-start.4) | collective-permute-done | bytes 786464 | tf_op jit(solution)/shard_map/ppermute | solution.py:49
  43.1 3.8 %collective-permute-done.6.refs_3_ = bf16[1536,512]{1,0:T(8,128)(2,1)} collective-permute-done((bf16[1536,512]{1,0:T(8,128)(2,1)}, bf16[1536,512]{1,0:T(8,128)(2,1)}, u32[]{:S(2)}, u32[]{:S(2)}) %collective-permute-start.6) | collective-permute-done | bytes 1572896 | tf_op jit(solution)/shard_map/ppermute | solution.py:49
  46.9 1.6 collective-permute-done.7.refs_4_.refs_2_
  48.5 4.1 %assemble.7 = (bf16[512,512]{1,0:T(8,128)(2,1)S(1)}, bf16[1344,512]{1,0:T(8,128)(2,1)}, bf16[1344,512]{1,0:T(8,128)(2,1)}) custom-call(bf16[768,512]{1,0:T(8,128)(2,1)} %collective-permute-done.4.refs_0_, bf16[768,512]{1,0:T(8,128)(2,1)} %collective-permute-done.5.refs_1_, bf16[512,2048]{1,0:T(8,128)(2,1)S(1)} %kv_partial.1.refs_2_, ...), custom_call_target="tpu_custom_call" | custom-call | tf_op jit(solution)/shard_map/assemble/pallas_call | solution.py:115
  53.8 1.7 %collective-permute-start.10 = (bf16[1344,512]{1,0:T(8,128)(2,1)}, bf16[1344,512]{1,0:T(8,128)(2,1)}, u32[]{:S(2)}, u32[]{:S(2)}) collective-permute-start(bf16[1344,512]{1,0:T(8,128)(2,1)} %get-tuple-element.78), channel_id=1, source_target_pairs={{0,12},{1,13},{2,14},{3,15},{4,0},{5,1},{6,2},{7,3},{8,4},{9,5},{1... | collective-permute-start | bytes 4128776 | tf_op jit(solution)/shard_map/ppermute | solution.py:49
  56.5 2.2 %pad_maximum_fusion.refs_0_ = bf16[2,2,16,64,128]{4,3,2,1,0:T(8,128)(2,1)} fusion(bf16[1,2,16,64,128]{4,3,2,1,0:T(8,128)(2,1)} %bitcast.1, bf16[1,2,16,64,128]{4,3,2,1,0:T(8,128)(2,1)S(1)} %fusion.37), kind=kLoop, calls=%fused_computation | loop fusion | flops 524288 | bytes 2097152 | tf_op jit(solution)/shard_map/stack | solution.py:490
  58.7 4.1 %collective-permute-start.11 = (bf16[2,2,16,64,128]{4,3,2,1,0:T(8,128)(2,1)}, bf16[2,2,16,64,128]{4,3,2,1,0:T(8,128)(2,1)}, u32[]{:S(2)}, u32[]{:S(2)}) collective-permute-start(bf16[2,2,16,64,128]{4,3,2,1,0:T(8,128)(2,1)} %pad_maximum_fusion.refs_0_), channel_id=1, source_target_pairs={{0,96},{1,97},{2,98},{3,99},{4,100},{5,101},{6,102},{7,103},{8,104... | collective-permute-start | bytes 3145736 | tf_op jit(solution)/shard_map/ppermute | solution.py:49
  64.5 7.0 %query_part.5 = (f32[512,512]{1,0:T(8,128)S(1)}, f32[512,128]{1,0:T(8,128)S(1)}) custom-call(s32[16]{0:T(128)S(1)} %fusion.29.order_ref, bf16[768,512]{1,0:T(8,128)(2,1)} %collective-permute-done.4.refs_0_, bf16[768,512]{1,0:T(8,128)(2,1)} %collective-permute-done.5.refs_1_, ...), custom_call_target="tpu_custom_call", output_to_operand_aliasing={{0}: (7, {}), {1}: (8, {})} | custom-call | tf_op jit(solution)/shard_map/query_part/pallas_call | solution.py:236
  71.5 4.4 %collective-permute-done.11.refs_1_ = bf16[2,2,16,64,128]{4,3,2,1,0:T(8,128)(2,1)} collective-permute-done((bf16[2,2,16,64,128]{4,3,2,1,0:T(8,128)(2,1)}, bf16[2,2,16,64,128]{4,3,2,1,0:T(8,128)(2,1)}, u32[]{:S(2)}, u32[]{:S(2)}) %collective-permute-start.11) | collective-permute-done | bytes 1048608 | tf_op jit(solution)/shard_map/ppermute | solution.py:49
  76.0 1.4 assemble.8
  77.5 1.6 collective-permute-start.13
  79.6 4.9 %query_part.6 = (f32[512,512]{1,0:T(8,128)S(1)}, f32[512,128]{1,0:T(8,128)S(1)}) custom-call(s32[16]{0:T(128)S(1)} %fusion.29.order_ref, bf16[1344,512]{1,0:T(8,128)(2,1)} %collective-permute-done.10.refs_1_.refs_0_, bf16[1344,512]{1,0:T(8,128)(2,1)S(1)} %collective-permute-done.9.refs_0_.refs_1_, ...), custom_call_target="tpu_custom_call", output_to_operand_aliasing={{0}: (5, {}), {1}: (6, {})} | custom-call | tf_op jit(solution)/shard_map/query_part/pallas_call | solution.py:236
  85.5 2.2 %gather_blocks.1.prefix_ref = bf16[8,2,320,128]{3,2,1,0:T(8,128)(2,1)S(1)} custom-call(s32[8,4]{1,0:T(8,128)S(1)} %fusion.25.code_ref, bf16[2,2,16,64,128]{4,3,2,1,0:T(8,128)(2,1)} %pad_maximum_fusion.refs_0_, bf16[2,2,16,64,128]{4,3,2,1,0:T(8,128)(2,1)} %collective-permute-done.11.refs_1_, bf16[2,2,16,64,128]{4,3,2,1,0:T(8,128)(2,1)} %collective-permute-done.12.refs_2_, ...), custom_call_target="tpu_custom_call" | custom-call | tf_op jit(solution)/shard_map/gather_blocks/pallas_call | solution.py:280
  88.6 2.0 %query_part.7 = (f32[512,512]{1,0:T(8,128)S(1)}, f32[512,128]{1,0:T(8,128)S(1)}) custom-call(s32[16]{0:T(128)S(1)} %fusion.29.order_ref, bf16[384,512]{1,0:T(8,128)(2,1)S(1)} %collective-permute-done.13.refs_0_.refs_1_, bf16[384,512]{1,0:T(8,128)(2,1)S(1)} %collective-permute-done.14.refs_1_.refs_2_, ...), custom_call_target="tpu_custom_call", output_to_operand_aliasing={{0}: (5, {}), {1}: (6, {})} | custom-call | tf_op jit(solution)/shard_map/query_part/pallas_call | solution.py:236
  90.6 3.6 %collective-permute-done.16.other_ref = bf16[512,128]{1,0:T(8,128)(2,1)S(1)} collective-permute-done((bf16[512,128]{1,0:T(8,128)(2,1)S(1)}, bf16[512,128]{1,0:T(8,128)(2,1)S(1)}, u32[]{:S(2)}, u32[]{:S(2)}) %collective-permute-start.16) | collective-permute-done | bytes 131104 | tf_op jit(solution)/shard_map/ppermute | solution.py:49
  94.3 6.1 %middle.1 = (bf16[512,512]{1,0:T(8,128)(2,1)S(1)}, bf16[4,512,512]{2,1,0:T(8,128)(2,1)S(1)}, bf16[8,2,320,128]{3,2,1,0:T(8,128)(2,1)S(1)}) custom-call(s32[16]{0:T(128)S(1)} %fusion.29.order_ref, s32[8]{0:T(128)S(1)} %get-tuple-element.122.len_ref, f32[512,512]{1,0:T(8,128)S(1)} %get-tuple-element.100.q_ref, ...), custom_call_target="tpu_custom_call", output_to_operand_aliasing={{2}: (8, {})} | custom-call | tf_op jit(solution)/shard_map/middle/pallas_call | solution.py:353
  100.6 2.0 %collective-permute-start.21 = (bf16[768,512]{1,0:T(8,128)(2,1)S(1)}, bf16[768,512]{1,0:T(8,128)(2,1)S(1)}, u32[]{:S(2)}, u32[]{:S(2)}) collective-permute-start(bf16[768,512]{1,0:T(8,128)(2,1)S(1)} %pad_maximum_fusion.3), channel_id=1, source_target_pairs={{0,4},{1,5},{2,6},{3,7},{4,8},{5,9},{6,10},{7,11},{8,12},{9,13},{1... | collective-permute-start | bytes 2359304 | tf_op jit(solution)/shard_map/ppermute | solution.py:49
  102.8 3.1 %collective-permute-start.17 = (bf16[256,512]{1,0:T(8,128)(2,1)S(1)}, bf16[256,512]{1,0:T(8,128)(2,1)S(1)}, u32[]{:S(2)}, u32[]{:S(2)}) collective-permute-start(bf16[256,512]{1,0:T(8,128)(2,1)S(1)} %get-tuple-element.152), channel_id=1, source_target_pairs={{0,4},{1,5},{2,6},{3,7},{4,8},{5,9},{6,10},{7,11},{8,12},{9,13},{1... | collective-permute-start | bytes 786440 | tf_op jit(solution)/shard_map/ppermute | solution.py:49
  105.9 4.3 %output_part.2 = bf16[6,512,512]{2,1,0:T(8,128)(2,1)S(1)} custom-call(s32[16]{0:T(128)S(1)} %fusion.29.order_ref, bf16[512,512]{1,0:T(8,128)(2,1)S(1)} %get-tuple-element.111.h_ref, bf16[512,8192]{1,0:T(8,128)(2,1)} %w_ref.5), custom_call_target="tpu_custom_call" | custom-call | tf_op jit(solution)/shard_map/output_part/pallas_call | solution.py:392
  110.2 5.3 %collective-permute-done.17 = bf16[256,512]{1,0:T(8,128)(2,1)S(1)} collective-permute-done((bf16[256,512]{1,0:T(8,128)(2,1)S(1)}, bf16[256,512]{1,0:T(8,128)(2,1)S(1)}, u32[]{:S(2)}, u32[]{:S(2)}) %collective-permute-start.17) | collective-permute-done | bytes 262176 | tf_op jit(solution)/shard_map/ppermute | solution.py:49
  115.4 3.2 %collective-permute-done.18 = bf16[256,512]{1,0:T(8,128)(2,1)S(1)} collective-permute-done((bf16[256,512]{1,0:T(8,128)(2,1)S(1)}, bf16[256,512]{1,0:T(8,128)(2,1)S(1)}, u32[]{:S(2)}, u32[]{:S(2)}) %collective-permute-start.18) | collective-permute-done | bytes 262176 | tf_op jit(solution)/shard_map/ppermute | solution.py:49
  119.4 2.1 %collective-permute-start.20 = (bf16[512,512]{1,0:T(8,128)(2,1)S(1)}, bf16[512,512]{1,0:T(8,128)(2,1)S(1)}, u32[]{:S(2)}, u32[]{:S(2)}) collective-permute-start(bf16[512,512]{1,0:T(8,128)(2,1)S(1)} %pad_maximum_fusion.6), channel_id=1, source_target_pairs={{0,12},{1,13},{2,14},{3,15},{4,0},{5,1},{6,2},{7,3},{8,4},{9,5},{1... | collective-permute-start | bytes 1572872 | tf_op jit(solution)/shard_map/ppermute | solution.py:49
  121.6 1.3 collective-permute-start.25
  124.1 4.3 %output_part.3 = bf16[6,512,512]{2,1,0:T(8,128)(2,1)S(1)} custom-call(s32[16]{0:T(128)S(1)} %fusion.29.order_ref, bf16[512,512]{1,0:T(8,128)(2,1)S(1)} %get-tuple-element.111.h_ref, bf16[512,8192]{1,0:T(8,128)(2,1)} %w_ref.5), custom_call_target="tpu_custom_call" | custom-call | tf_op jit(solution)/shard_map/output_part/pallas_call | solution.py:392
  128.6 1.3 collective-permute-done.20
  130.5 2.9 %collective-permute-start.28 = (bf16[256,512]{1,0:T(8,128)(2,1)S(1)}, bf16[256,512]{1,0:T(8,128)(2,1)S(1)}, u32[]{:S(2)}, u32[]{:S(2)}) collective-permute-start(bf16[256,512]{1,0:T(8,128)(2,1)S(1)} %get-tuple-element.155), channel_id=1, source_target_pairs={{0,3},{1,0},{2,1},{3,2},{4,7},{5,4},{6,5},{7,6},{8,11},{9,8},{10,9... | collective-permute-start | bytes 786440 | tf_op jit(solution)/shard_map/ppermute | solution.py:49
  133.5 6.7 %collective-permute-done.27 = bf16[256,512]{1,0:T(8,128)(2,1)S(1)} collective-permute-done((bf16[256,512]{1,0:T(8,128)(2,1)S(1)}, bf16[256,512]{1,0:T(8,128)(2,1)S(1)}, u32[]{:S(2)}, u32[]{:S(2)}) %collective-permute-start.27) | collective-permute-done | bytes 262176 | tf_op jit(solution)/shard_map/ppermute | solution.py:49
  140.2 2.4 %collective-permute-done.25 = bf16[1024,512]{1,0:T(8,128)(2,1)S(1)} collective-permute-done((bf16[1024,512]{1,0:T(8,128)(2,1)S(1)}, bf16[1024,512]{1,0:T(8,128)(2,1)S(1)}, u32[]{:S(2)}, u32[]{:S(2)}) %collective-permute-start.25) | collective-permute-done | bytes 1048608 | tf_op jit(solution)/shard_map/ppermute | solution.py:49
  142.6 1.3 collective-permute-done.26
  144.7 2.4 %collective-permute-start.30 = (bf16[512,512]{1,0:T(8,128)(2,1)S(1)}, bf16[512,512]{1,0:T(8,128)(2,1)S(1)}, u32[]{:S(2)}, u32[]{:S(2)}) collective-permute-start(bf16[512,512]{1,0:T(8,128)(2,1)S(1)} %pad_maximum_fusion.10), channel_id=1, source_target_pairs={{0,3},{1,0},{2,1},{3,2},{4,7},{5,4},{6,5},{7,6},{8,11},{9,8},{10,9... | collective-permute-start | bytes 1572872 | tf_op jit(solution)/shard_map/ppermute | solution.py:49
  147.3 1.6 %collective-permute-start.24 = (bf16[512,512]{1,0:T(8,128)(2,1)S(1)}, bf16[512,512]{1,0:T(8,128)(2,1)S(1)}, u32[]{:S(2)}, u32[]{:S(2)}) collective-permute-start(bf16[512,512]{1,0:T(8,128)(2,1)S(1)} %pad_maximum_fusion.8), channel_id=1, source_target_pairs={{0,12},{1,13},{2,14},{3,15},{4,0},{5,1},{6,2},{7,3},{8,4},{9,5},{1... | collective-permute-start | bytes 1572872 | tf_op jit(solution)/shard_map/ppermute | solution.py:49
  148.9 1.7 %collective-permute-start.23 = (bf16[512,512]{1,0:T(8,128)(2,1)S(1)}, bf16[512,512]{1,0:T(8,128)(2,1)S(1)}, u32[]{:S(2)}, u32[]{:S(2)}) collective-permute-start(bf16[512,512]{1,0:T(8,128)(2,1)S(1)} %pad_maximum_fusion.7), channel_id=1, source_target_pairs={{0,4},{1,5},{2,6},{3,7},{4,8},{5,9},{6,10},{7,11},{8,12},{9,13},{1... | collective-permute-start | bytes 1572872 | tf_op jit(solution)/shard_map/ppermute | solution.py:49
  150.7 7.2 %collective-permute-done.30 = bf16[512,512]{1,0:T(8,128)(2,1)S(1)} collective-permute-done((bf16[512,512]{1,0:T(8,128)(2,1)S(1)}, bf16[512,512]{1,0:T(8,128)(2,1)S(1)}, u32[]{:S(2)}, u32[]{:S(2)}) %collective-permute-start.30) | collective-permute-done | bytes 524320 | tf_op jit(solution)/shard_map/ppermute | solution.py:49
  157.9 3.5 %collective-permute-done.29 = bf16[512,512]{1,0:T(8,128)(2,1)S(1)} collective-permute-done((bf16[512,512]{1,0:T(8,128)(2,1)S(1)}, bf16[512,512]{1,0:T(8,128)(2,1)S(1)}, u32[]{:S(2)}, u32[]{:S(2)}) %collective-permute-start.29) | collective-permute-done | bytes 524320 | tf_op jit(solution)/shard_map/ppermute | solution.py:49
  161.4 1.1 fusion.5
  (87 shorter events, 17.2 us)
Async XLA Ops:
  0.0 63.1 %copy-start = (s32[64,4]{0,1:T(4,128)S(1)}, s32[64,4]{0,1:T(4,128)}, u32[]{:S(2)}) copy-start(s32[64,4]{0,1:T(4,128)} %param.14) | copy-start | bytes 3076
  0.0 16.4 %collective-permute-start = (bf16[512,512]{1,0:T(8,128)(2,1)}, bf16[512,512]{1,0:T(8,128)(2,1)S(1)}, u32[]{:S(2)}, u32[]{:S(2)}) collective-permute-start(bf16[512,512]{1,0:T(8,128)(2,1)} %refs_0_.3), channel_id=1, source_target_pairs={{0,1},{1,2},{2,3},{3,0},{4,5},{5,6},{6,7},{7,4},{8,9},{9,10},{10,1... | collective-permute-start | bytes 1572872 | tf_op jit(solution)/shard_map/ppermute | solution.py:49
  1.6 14.8 %collective-permute-start.1 = (bf16[512,512]{1,0:T(8,128)(2,1)}, bf16[512,512]{1,0:T(8,128)(2,1)S(1)}, u32[]{:S(2)}, u32[]{:S(2)}) collective-permute-start(bf16[512,512]{1,0:T(8,128)(2,1)} %refs_0_.3), channel_id=1, source_target_pairs={{0,3},{1,0},{2,1},{3,2},{4,7},{5,4},{6,5},{7,6},{8,11},{9,8},{10,9... | collective-permute-start | bytes 1572872 | tf_op jit(solution)/shard_map/ppermute | solution.py:49
  4.0 1.0 copy-start.2
  5.0 11.3 %copy-start.3 = (bf16[512,512]{1,0:T(8,128)(2,1)S(1)}, bf16[512,512]{1,0:T(8,128)(2,1)}, u32[]{:S(2)}) copy-start(bf16[512,512]{1,0:T(8,128)(2,1)} %refs_0_.3) | copy-start | bytes 1572868
  8.7 7.7 %collective-permute-start.2 = (bf16[256,512]{1,0:T(8,128)(2,1)S(1)}, bf16[256,512]{1,0:T(8,128)(2,1)S(1)}, u32[]{:S(2)}, u32[]{:S(2)}) collective-permute-start(bf16[256,512]{1,0:T(8,128)(2,1)S(1)} %get-tuple-element.154), channel_id=1, source_target_pairs={{0,1},{1,2},{2,3},{3,0},{4,5},{5,6},{6,7},{7,4},{8,9},{9,10},{10,1... | collective-permute-start | bytes 786440 | tf_op jit(solution)/shard_map/ppermute | solution.py:49
  9.1 7.2 %collective-permute-start.3 = (bf16[256,512]{1,0:T(8,128)(2,1)S(1)}, bf16[256,512]{1,0:T(8,128)(2,1)S(1)}, u32[]{:S(2)}, u32[]{:S(2)}) collective-permute-start(bf16[256,512]{1,0:T(8,128)(2,1)S(1)} %get-tuple-element.153), channel_id=1, source_target_pairs={{0,3},{1,0},{2,1},{3,2},{4,7},{5,4},{6,5},{7,6},{8,11},{9,8},{10,9... | collective-permute-start | bytes 786440 | tf_op jit(solution)/shard_map/ppermute | solution.py:49
  16.4 4.7 %copy-start.5 = (bf16[512,512]{1,0:T(8,128)(2,1)}, bf16[512,512]{1,0:T(8,128)(2,1)S(1)}, u32[]{:S(2)}) copy-start(bf16[512,512]{1,0:T(8,128)(2,1)S(1)} %collective-permute-done.refs_0_.refs_2_) | copy-start | bytes 1572868
  16.4 4.7 %copy-start.7 = (bf16[512,512]{1,0:T(8,128)(2,1)}, bf16[512,512]{1,0:T(8,128)(2,1)S(1)}, u32[]{:S(2)}) copy-start(bf16[512,512]{1,0:T(8,128)(2,1)S(1)} %collective-permute-done.1.refs_1_) | copy-start | bytes 1572868
  17.8 29.2 %collective-permute-start.6 = (bf16[1536,512]{1,0:T(8,128)(2,1)}, bf16[1536,512]{1,0:T(8,128)(2,1)}, u32[]{:S(2)}, u32[]{:S(2)}) collective-permute-start(bf16[1536,512]{1,0:T(8,128)(2,1)} %assemble.6), channel_id=1, source_target_pairs={{0,4},{1,5},{2,6},{3,7},{4,8},{5,9},{6,10},{7,11},{8,12},{9,13},{1... | collective-permute-start | bytes 4718600 | tf_op jit(solution)/shard_map/ppermute | solution.py:49
  18.2 30.4 %collective-permute-start.7 = (bf16[1536,512]{1,0:T(8,128)(2,1)}, bf16[1536,512]{1,0:T(8,128)(2,1)}, u32[]{:S(2)}, u32[]{:S(2)}) collective-permute-start(bf16[1536,512]{1,0:T(8,128)(2,1)} %assemble.6), channel_id=1, source_target_pairs={{0,12},{1,13},{2,14},{3,15},{4,0},{5,1},{6,2},{7,3},{8,4},{9,5},{1... | collective-permute-start | bytes 4718600 | tf_op jit(solution)/shard_map/ppermute | solution.py:49
  21.1 22.0 %collective-permute-start.4 = (bf16[768,512]{1,0:T(8,128)(2,1)}, bf16[768,512]{1,0:T(8,128)(2,1)}, u32[]{:S(2)}, u32[]{:S(2)}) collective-permute-start(bf16[768,512]{1,0:T(8,128)(2,1)} %get-tuple-element.68), channel_id=1, source_target_pairs={{0,1},{1,2},{2,3},{3,0},{4,5},{5,6},{6,7},{7,4},{8,9},{9,10},{10,1... | collective-permute-start | bytes 2359304 | tf_op jit(solution)/shard_map/ppermute | solution.py:49
  21.8 21.3 %collective-permute-start.5 = (bf16[768,512]{1,0:T(8,128)(2,1)}, bf16[768,512]{1,0:T(8,128)(2,1)}, u32[]{:S(2)}, u32[]{:S(2)}) collective-permute-start(bf16[768,512]{1,0:T(8,128)(2,1)} %get-tuple-element.69), channel_id=1, source_target_pairs={{0,3},{1,0},{2,1},{3,2},{4,7},{5,4},{6,5},{7,6},{8,11},{9,8},{10,9... | collective-permute-start | bytes 2359304 | tf_op jit(solution)/shard_map/ppermute | solution.py:49
  26.3 9.5 %collective-permute-start.8 = (bf16[2,16,64,128]{3,2,1,0:T(8,128)(2,1)}, bf16[2,16,64,128]{3,2,1,0:T(8,128)(2,1)}, u32[]{:S(2)}, u32[]{:S(2)}) collective-permute-start(bf16[2,16,64,128]{3,2,1,0:T(8,128)(2,1)} %constant_dynamic-slice_fusion.1), channel_id=1, source_target_pairs={{0,32},{1,33},{2,34},{3,35},{4,36},{5,37},{6,38},{7,39},{8,40},{9,... | collective-permute-start | bytes 1572872 | tf_op jit(solution)/shard_map/ppermute | solution.py:49
  28.2 1.0 copy-start.4
  29.3 1.0 copy-start.6
  30.3 1.0 copy-start.8
  52.6 0.8 copy-start.9
  53.4 9.4 %copy-start.12 = (s32[64]{0:T(128)S(1)}, s32[64]{0:T(128)}, u32[]{:S(2)}) copy-start(s32[64]{0:T(128)} %param.15) | copy-start | bytes 772
  53.4 22.5 %collective-permute-start.9 = (bf16[1344,512]{1,0:T(8,128)(2,1)}, bf16[1344,512]{1,0:T(8,128)(2,1)S(1)}, u32[]{:S(2)}, u32[]{:S(2)}) collective-permute-start(bf16[1344,512]{1,0:T(8,128)(2,1)} %get-tuple-element.77), channel_id=1, source_target_pairs={{0,4},{1,5},{2,6},{3,7},{4,8},{5,9},{6,10},{7,11},{8,12},{9,13},{1... | collective-permute-start | bytes 4128776 | tf_op jit(solution)/shard_map/ppermute | solution.py:49
  53.8 22.2 %collective-permute-start.10 = (bf16[1344,512]{1,0:T(8,128)(2,1)}, bf16[1344,512]{1,0:T(8,128)(2,1)}, u32[]{:S(2)}, u32[]{:S(2)}) collective-permute-start(bf16[1344,512]{1,0:T(8,128)(2,1)} %get-tuple-element.78), channel_id=1, source_target_pairs={{0,12},{1,13},{2,14},{3,15},{4,0},{5,1},{6,2},{7,3},{8,4},{9,5},{1... | collective-permute-start | bytes 4128776 | tf_op jit(solution)/shard_map/ppermute | solution.py:49
  58.7 17.2 %collective-permute-start.11 = (bf16[2,2,16,64,128]{4,3,2,1,0:T(8,128)(2,1)}, bf16[2,2,16,64,128]{4,3,2,1,0:T(8,128)(2,1)}, u32[]{:S(2)}, u32[]{:S(2)}) collective-permute-start(bf16[2,2,16,64,128]{4,3,2,1,0:T(8,128)(2,1)} %pad_maximum_fusion.refs_0_), channel_id=1, source_target_pairs={{0,96},{1,97},{2,98},{3,99},{4,100},{5,101},{6,102},{7,103},{8,104... | collective-permute-start | bytes 3145736 | tf_op jit(solution)/shard_map/ppermute | solution.py:49
  62.8 13.1 %collective-permute-start.12 = (bf16[2,2,16,64,128]{4,3,2,1,0:T(8,128)(2,1)}, bf16[2,2,16,64,128]{4,3,2,1,0:T(8,128)(2,1)}, u32[]{:S(2)}, u32[]{:S(2)}) collective-permute-start(bf16[2,2,16,64,128]{4,3,2,1,0:T(8,128)(2,1)} %pad_maximum_fusion.refs_0_), channel_id=1, source_target_pairs={{0,16},{1,17},{2,18},{3,19},{4,20},{5,21},{6,22},{7,23},{8,24},{9,... | collective-permute-start | bytes 3145736 | tf_op jit(solution)/shard_map/ppermute | solution.py:49
  64.5 11.5 %copy-start.10 = (bf16[512,512]{1,0:T(8,128)(2,1)S(1)}, bf16[512,512]{1,0:T(8,128)(2,1)}, u32[]{:S(2)}) copy-start(bf16[512,512]{1,0:T(8,128)(2,1)} %copy-done.9) | copy-start | bytes 1572868
  75.9 8.6 %collective-permute-start.15 = (bf16[2,2,16,64,128]{4,3,2,1,0:T(8,128)(2,1)}, bf16[2,2,16,64,128]{4,3,2,1,0:T(8,128)(2,1)S(1)}, u32[]{:S(2)}, u32[]{:S(2)}) collective-permute-start(bf16[2,2,16,64,128]{4,3,2,1,0:T(8,128)(2,1)} %collective-permute-done.11.refs_1_), channel_id=1, source_target_pairs={{0,16},{1,17},{2,18},{3,19},{4,20},{5,21},{6,22},{7,23},{8,24},{9,... | collective-permute-start | bytes 3145736 | tf_op jit(solution)/shard_map/ppermute | solution.py:49
  77.5 10.2 %collective-permute-start.13 = (bf16[384,512]{1,0:T(8,128)(2,1)S(1)}, bf16[384,512]{1,0:T(8,128)(2,1)S(1)}, u32[]{:S(2)}, u32[]{:S(2)}) collective-permute-start(bf16[384,512]{1,0:T(8,128)(2,1)S(1)} %get-tuple-element.87), channel_id=1, source_target_pairs={{0,4},{1,5},{2,6},{3,7},{4,8},{5,9},{6,10},{7,11},{8,12},{9,13},{1... | collective-permute-start | bytes 1179656 | tf_op jit(solution)/shard_map/ppermute | solution.py:49
  79.0 9.0 %collective-permute-start.14 = (bf16[384,512]{1,0:T(8,128)(2,1)S(1)}, bf16[384,512]{1,0:T(8,128)(2,1)S(1)}, u32[]{:S(2)}, u32[]{:S(2)}) collective-permute-start(bf16[384,512]{1,0:T(8,128)(2,1)S(1)} %get-tuple-element.88), channel_id=1, source_target_pairs={{0,12},{1,13},{2,14},{3,15},{4,0},{5,1},{6,2},{7,3},{8,4},{9,5},{1... | collective-permute-start | bytes 1179656 | tf_op jit(solution)/shard_map/ppermute | solution.py:49
  84.5 1.0 copy-start.11
  88.1 6.2 %collective-permute-start.16 = (bf16[512,128]{1,0:T(8,128)(2,1)S(1)}, bf16[512,128]{1,0:T(8,128)(2,1)S(1)}, u32[]{:S(2)}, u32[]{:S(2)}) collective-permute-start(bf16[512,128]{1,0:T(8,128)(2,1)S(1)} %assemble.9.mine_ref), channel_id=1, source_target_pairs={{0,1},{1,0},{2,3},{3,2},{4,5},{5,4},{6,7},{7,6},{8,9},{9,8},{10,11... | collective-permute-start | bytes 393224 | tf_op jit(solution)/shard_map/ppermute | solution.py:49
  100.6 18.2 %collective-permute-start.21 = (bf16[768,512]{1,0:T(8,128)(2,1)S(1)}, bf16[768,512]{1,0:T(8,128)(2,1)S(1)}, u32[]{:S(2)}, u32[]{:S(2)}) collective-permute-start(bf16[768,512]{1,0:T(8,128)(2,1)S(1)} %pad_maximum_fusion.3), channel_id=1, source_target_pairs={{0,4},{1,5},{2,6},{3,7},{4,8},{5,9},{6,10},{7,11},{8,12},{9,13},{1... | collective-permute-start | bytes 2359304 | tf_op jit(solution)/shard_map/ppermute | solution.py:49
  102.6 16.2 %collective-permute-start.22 = (bf16[768,512]{1,0:T(8,128)(2,1)S(1)}, bf16[768,512]{1,0:T(8,128)(2,1)S(1)}, u32[]{:S(2)}, u32[]{:S(2)}) collective-permute-start(bf16[768,512]{1,0:T(8,128)(2,1)S(1)} %pad_maximum_fusion.4), channel_id=1, source_target_pairs={{0,12},{1,13},{2,14},{3,15},{4,0},{5,1},{6,2},{7,3},{8,4},{9,5},{1... | collective-permute-start | bytes 2359304 | tf_op jit(solution)/shard_map/ppermute | solution.py:49
  102.8 12.6 %collective-permute-start.17 = (bf16[256,512]{1,0:T(8,128)(2,1)S(1)}, bf16[256,512]{1,0:T(8,128)(2,1)S(1)}, u32[]{:S(2)}, u32[]{:S(2)}) collective-permute-start(bf16[256,512]{1,0:T(8,128)(2,1)S(1)} %get-tuple-element.152), channel_id=1, source_target_pairs={{0,4},{1,5},{2,6},{3,7},{4,8},{5,9},{6,10},{7,11},{8,12},{9,13},{1... | collective-permute-start | bytes 786440 | tf_op jit(solution)/shard_map/ppermute | solution.py:49
  105.9 12.8 %collective-permute-start.18 = (bf16[256,512]{1,0:T(8,128)(2,1)S(1)}, bf16[256,512]{1,0:T(8,128)(2,1)S(1)}, u32[]{:S(2)}, u32[]{:S(2)}) collective-permute-start(bf16[256,512]{1,0:T(8,128)(2,1)S(1)} %get-tuple-element.151), channel_id=1, source_target_pairs={{0,12},{1,13},{2,14},{3,15},{4,0},{5,1},{6,2},{7,3},{8,4},{9,5},{1... | collective-permute-start | bytes 786440 | tf_op jit(solution)/shard_map/ppermute | solution.py:49
  119.3 9.2 %collective-permute-start.19 = (bf16[512,512]{1,0:T(8,128)(2,1)S(1)}, bf16[512,512]{1,0:T(8,128)(2,1)S(1)}, u32[]{:S(2)}, u32[]{:S(2)}) collective-permute-start(bf16[512,512]{1,0:T(8,128)(2,1)S(1)} %pad_maximum_fusion.5), channel_id=1, source_target_pairs={{0,4},{1,5},{2,6},{3,7},{4,8},{5,9},{6,10},{7,11},{8,12},{9,13},{1... | collective-permute-start | bytes 1572872 | tf_op jit(solution)/shard_map/ppermute | solution.py:49
  119.4 10.5 %collective-permute-start.20 = (bf16[512,512]{1,0:T(8,128)(2,1)S(1)}, bf16[512,512]{1,0:T(8,128)(2,1)S(1)}, u32[]{:S(2)}, u32[]{:S(2)}) collective-permute-start(bf16[512,512]{1,0:T(8,128)(2,1)S(1)} %pad_maximum_fusion.6), channel_id=1, source_target_pairs={{0,12},{1,13},{2,14},{3,15},{4,0},{5,1},{6,2},{7,3},{8,4},{9,5},{1... | collective-permute-start | bytes 1572872 | tf_op jit(solution)/shard_map/ppermute | solution.py:49
  121.6 21.0 %collective-permute-start.25 = (bf16[1024,512]{1,0:T(8,128)(2,1)S(1)}, bf16[1024,512]{1,0:T(8,128)(2,1)S(1)}, u32[]{:S(2)}, u32[]{:S(2)}) collective-permute-start(bf16[1024,512]{1,0:T(8,128)(2,1)S(1)} %pad_maximum_fusion.1), channel_id=1, source_target_pairs={{0,4},{1,5},{2,6},{3,7},{4,8},{5,9},{6,10},{7,11},{8,12},{9,13},{1... | collective-permute-start | bytes 3145736 | tf_op jit(solution)/shard_map/ppermute | solution.py:49
  123.0 21.0 %collective-permute-start.26 = (bf16[1024,512]{1,0:T(8,128)(2,1)S(1)}, bf16[1024,512]{1,0:T(8,128)(2,1)S(1)}, u32[]{:S(2)}, u32[]{:S(2)}) collective-permute-start(bf16[1024,512]{1,0:T(8,128)(2,1)S(1)} %pad_maximum_fusion.2), channel_id=1, source_target_pairs={{0,12},{1,13},{2,14},{3,15},{4,0},{5,1},{6,2},{7,3},{8,4},{9,5},{1... | collective-permute-start | bytes 3145736 | tf_op jit(solution)/shard_map/ppermute | solution.py:49
  130.2 10.1 %collective-permute-start.27 = (bf16[256,512]{1,0:T(8,128)(2,1)S(1)}, bf16[256,512]{1,0:T(8,128)(2,1)S(1)}, u32[]{:S(2)}, u32[]{:S(2)}) collective-permute-start(bf16[256,512]{1,0:T(8,128)(2,1)S(1)} %get-tuple-element.156), channel_id=1, source_target_pairs={{0,1},{1,2},{2,3},{3,0},{4,5},{5,6},{6,7},{7,4},{8,9},{9,10},{10,1... | collective-permute-start | bytes 786440 | tf_op jit(solution)/shard_map/ppermute | solution.py:49
  130.5 9.7 %collective-permute-start.28 = (bf16[256,512]{1,0:T(8,128)(2,1)S(1)}, bf16[256,512]{1,0:T(8,128)(2,1)S(1)}, u32[]{:S(2)}, u32[]{:S(2)}) collective-permute-start(bf16[256,512]{1,0:T(8,128)(2,1)S(1)} %get-tuple-element.155), channel_id=1, source_target_pairs={{0,3},{1,0},{2,1},{3,2},{4,7},{5,4},{6,5},{7,6},{8,11},{9,8},{10,9... | collective-permute-start | bytes 786440 | tf_op jit(solution)/shard_map/ppermute | solution.py:49
  144.7 13.2 %collective-permute-start.30 = (bf16[512,512]{1,0:T(8,128)(2,1)S(1)}, bf16[512,512]{1,0:T(8,128)(2,1)S(1)}, u32[]{:S(2)}, u32[]{:S(2)}) collective-permute-start(bf16[512,512]{1,0:T(8,128)(2,1)S(1)} %pad_maximum_fusion.10), channel_id=1, source_target_pairs={{0,3},{1,0},{2,1},{3,2},{4,7},{5,4},{6,5},{7,6},{8,11},{9,8},{10,9... | collective-permute-start | bytes 1572872 | tf_op jit(solution)/shard_map/ppermute | solution.py:49
  147.1 14.3 %collective-permute-start.29 = (bf16[512,512]{1,0:T(8,128)(2,1)S(1)}, bf16[512,512]{1,0:T(8,128)(2,1)S(1)}, u32[]{:S(2)}, u32[]{:S(2)}) collective-permute-start(bf16[512,512]{1,0:T(8,128)(2,1)S(1)} %pad_maximum_fusion.9), channel_id=1, source_target_pairs={{0,1},{1,2},{2,3},{3,0},{4,5},{5,6},{6,7},{7,4},{8,9},{9,10},{10,1... | collective-permute-start | bytes 1572872 | tf_op jit(solution)/shard_map/ppermute | solution.py:49
  147.3 14.1 %collective-permute-start.24 = (bf16[512,512]{1,0:T(8,128)(2,1)S(1)}, bf16[512,512]{1,0:T(8,128)(2,1)S(1)}, u32[]{:S(2)}, u32[]{:S(2)}) collective-permute-start(bf16[512,512]{1,0:T(8,128)(2,1)S(1)} %pad_maximum_fusion.8), channel_id=1, source_target_pairs={{0,12},{1,13},{2,14},{3,15},{4,0},{5,1},{6,2},{7,3},{8,4},{9,5},{1... | collective-permute-start | bytes 1572872 | tf_op jit(solution)/shard_map/ppermute | solution.py:49
  148.9 13.7 %copy-start.1 = (s32[64,4]{0,1:T(4,128)S(1)}, s32[64,4]{0,1:T(4,128)}, u32[]{:S(2)}) copy-start(s32[64,4]{0,1:T(4,128)} %param.14) | copy-start | bytes 3076
  148.9 12.5 %collective-permute-start.23 = (bf16[512,512]{1,0:T(8,128)(2,1)S(1)}, bf16[512,512]{1,0:T(8,128)(2,1)S(1)}, u32[]{:S(2)}, u32[]{:S(2)}) collective-permute-start(bf16[512,512]{1,0:T(8,128)(2,1)S(1)} %pad_maximum_fusion.7), channel_id=1, source_target_pairs={{0,4},{1,5},{2,6},{3,7},{4,8},{5,9},{6,10},{7,11},{8,12},{9,13},{1... | collective-permute-start | bytes 1572872 | tf_op jit(solution)/shard_map/ppermute | solution.py:49

commit v3 on v2

--- a/solution.py
+++ b/solution.py
@@ -117,7 +117,7 @@
         out_shape=[pltpu.VMEM(shape, BF16) for shape, _ in outputs],
         in_specs=[VMEM] * n_arrays,
         out_specs=[VMEM] * len(outputs),
-        compiler_params=params(8),
+        compiler_params=params(6),
         cost_estimate=estimate(0, 0),
         name="assemble",
     )(*in_vmem(arrays))
@@ -172,7 +172,7 @@
             pltpu.VMEM((WIDE, count * HD), BF16),
             pltpu.SemaphoreType.DMA((count,)),
         ],
-        compiler_params=params(7),
+        compiler_params=params(6),
         cost_estimate=estimate(0, 0),
         name="kv_partial",
     )(order, tokens, gain, w_keyvalue)
@@ -247,7 +247,7 @@
             pltpu.SemaphoreType.DMA((count,)),
         ],
         input_output_aliases={} if first else {n_arrays + 3: 0, n_arrays + 4: 1},
-        compiler_params=params(14),
+        compiler_params=params(8),
         cost_estimate=estimate(0, 0),
         name="query_part",
     )(order, *in_vmem(arrays), gain, w_query, *in_vmem(carried))
@@ -283,7 +283,7 @@
         in_specs=[SMEM] + [ANYWHERE] * 4,
         out_specs=VMEM,
         scratch_shapes=[pltpu.SemaphoreType.DMA((branches, PDEPTH))],
-        compiler_params=params(8),
+        compiler_params=params(6),
         cost_estimate=estimate(0, 0),
         name="gather_blocks",
     )(codes, *pools)
@@ -365,7 +365,7 @@
             pltpu.SemaphoreType.DMA((len(spots),)),
         ],
         input_output_aliases={8: 2},
-        compiler_params=params(9),
+        compiler_params=params(8),
         cost_estimate=estimate(0, 0),
         name="middle",
     )(
@@ -398,7 +398,7 @@
             pltpu.VMEM((count, WIDE, WIDE), BF16),
             pltpu.SemaphoreType.DMA((count,)),
         ],
-        compiler_params=params(7),
+        compiler_params=params(6),
         cost_estimate=estimate(0, 0),
         name="output_part",
     )(order, heads_out, w_output)
@@ -426,7 +426,10 @@
     s1 = both(tokens, tokens, "first")
     kv = kv_partial(tokens, gains, w_keyvalue, order, (0, 1, 3, 2))
     k_far = both(kv[:HALF, 3 * WIDE :], kv[HALF:, 3 * WIDE :], "first")
-    b1m, b1p, k_m, k_p, kv_near, cache = bar((*s1, *k_far, kv, cache))
+    kv_head = place * (w_query.shape[1] // HD) // (HEADS // KVH)
+    cache_head = lax.dynamic_slice_in_dim(cache, kv_head * HD, HD, 3)
+    z_one = hop(cache_head, "z_one", 1)
+    b1m, b1p, k_m, k_p, kv_near, z_one = bar((*s1, *k_far, kv, z_one))
     (near,) = assemble(
         [tokens, b1p, b1m],
         [((3 * WIDE, WIDE), [rows_piece(n * WIDE, WIDE, (n, 0)) for n in range(3)])],
@@ -456,9 +459,6 @@
         ),
         "first",
     )
-    kv_head = place * (w_query.shape[1] // HD) // (HEADS // KVH)
-    cache_head = lax.dynamic_slice_in_dim(cache, kv_head * HD, HD, 3)
-    z_one = hop(cache_head, "z_one", 1)
     part = query_part(
         [((0, 0), [(0, 0, 0, WIDE)]), ((1, 0), [(1, 0, 0, WIDE)]), ((3, 0), [(2, 0, 0, WIDE)])],
         [tokens, b1p, b1m],
@@ -467,29 +467,37 @@
         w_query,
         None,
     )
-    b3m, b3p, b2m, b2p, z_one, *part = bar((*s3, *s2, z_one, *part))
-    ksum, to_next, to_last = assemble(
-        [b3m, b3p, kv_near, b2m, b2p],
+    pool = jnp.stack([cache_head, z_one])
+    z_two = hop(pool, "z_two", 1)
+    b3m, b3p, b2m, b2p, pool, z_two, *part = bar((*s3, *s2, pool, z_two, *part))
+    (to_next,) = assemble(
+        [b3m, b3p, kv_near, b2m],
         [
-            ((WIDE, WIDE), [(0, 0, WIDE, WIDE, [(2, 0, 0), (0, HALF, 0), (1, HALF, 0)])]),
             (
                 (5 * HALF + HALF // 4, WIDE),
                 [rows_piece(0, HALF, (0, 0)), rows_piece(HALF, HALF, (1, 0))]
                 + [rows_piece(WIDE + n * HALF, HALF, (3, n * WIDE)) for n in range(3)]
                 + packed(5 * HALF, HALF, (2, 0, 2 * HD), (0, HALF, 2 * HD), (1, HALF, 2 * HD)),
-            ),
+            )
+        ],
+    )
+    (to_last,) = assemble(
+        [b3m, b3p, kv_near, b2p],
+        [
             (
                 (5 * HALF + HALF // 4, WIDE),
                 [rows_piece(0, HALF, (0, 0)), rows_piece(HALF, HALF, (1, 0))]
-                + [rows_piece(WIDE + n * HALF, HALF, (4, n * WIDE + HALF)) for n in range(3)]
+                + [rows_piece(WIDE + n * HALF, HALF, (3, n * WIDE + HALF)) for n in range(3)]
                 + packed(5 * HALF, HALF, (2, HALF, 2 * HD), (0, WIDE, 2 * HD), (1, WIDE, 2 * HD)),
-            ),
+            )
         ],
     )
     s5 = both(to_next, to_last, "second")
-    pool = jnp.stack([cache_head, z_one])
-    z_two = hop(pool, "z_two", 1)
-    near_twin = hop(pool, "core", 1)
+    (ksum,) = assemble(
+        [kv_near, b3m, b3p],
+        [((WIDE, WIDE), [(0, 0, WIDE, WIDE, [(0, 0, 0), (1, HALF, 0), (2, HALF, 0)])])],
+    )
+    near_twin, far_twin = hop(pool, "core", 1), hop(z_two, "core", 1)
     my_lengths = lax.dynamic_slice_in_dim(lengths, group * branch_count, branch_count, 0)
     my_parents = lax.dynamic_slice_in_dim(parents, group * branch_count, branch_count, 0)
     owner = my_parents // 16
@@ -527,9 +535,11 @@
         w_query,
         part,
     )
-    b5m, b5p, z_two, near_twin, cosine, sine, codes, *part = bar(
-        (*s5, z_two, near_twin, cosine, sine, codes, *part)
-    )
+    pools = [
+        pltpu.with_memory_space_constraint(a, pltpu.HBM) for a in (pool, z_two, near_twin, far_twin)
+    ]
+    prefix = gather_blocks(pools, codes)
+    b5m, b5p, prefix, cosine, sine, ksum, *part = bar((*s5, prefix, cosine, sine, ksum, *part))
     quarter = HALF // 4
     s7 = both(
         *assemble(
@@ -587,11 +597,6 @@
         ),
         "second",
     )
-    far_twin = hop(z_two, "core", 1)
-    pools = [
-        pltpu.with_memory_space_constraint(a, pltpu.HBM) for a in (pool, z_two, near_twin, far_twin)
-    ]
-    prefix = gather_blocks(pools, codes)
     part = query_part(
         [
             ((2, 1), [(0, 0, 0, WIDE)]),
@@ -606,7 +611,7 @@
         w_query,
         part,
     )
-    b7m, b7p, prefix, *part = bar((*s7, prefix, *part))
+    b7m, b7p, *part = bar((*s7, *part))
     (mine,) = assemble(
         [ksum, b7m, b7p],
         [
@@ -666,12 +671,13 @@
     q20, q01, q03, q10, q30, q00 = [rest[n] for n in range(6)]
     sum2 = plus(q20, rc_m, rc_p)
     re = both(sum2[:HALF], sum2[HALF:], "first")
+    re_m, re_p, rb_m, rb_p = bar((*re, rb_m, rb_p))
     rf = both(
         stack_rows(plus(q01[:HALF], rb_m[WIDE:]), q01[HALF:]),
         stack_rows(q03[:HALF], plus(q03[HALF:], rb_p[WIDE:])),
         "second",
     )
-    rd_m, rd_p, re_m, re_p = bar((*rd, *re))
+    rd_m, rd_p = bar(rd)
     sum1 = stack_rows(
         plus(q10[:HALF], rd_m[:HALF], rd_p[:HALF], re_m), plus(q10[HALF:], rd_m[HALF:WIDE], rd_p[HALF:WIDE])
     )

time: 163 us -> 166 us (1.018)
  waiting for transfers between devices: 58.2 us -> 67.9 us
  Pallas kernels: 45.6 us -> 40.9 us
    ppermute x31, waiting for transfers between devices: 58.2 us -> 67.9 us  [hop(): return lax.ppermute(value, AXES, HOPS[axis, step])]
    pallas_call x5 -> x7, Pallas kernels: 8.24 us -> 4.99 us  [assemble(): pl.pallas_call(body, out_shape=[pltpu.VMEM(shape, BF16) for shape, _ in o...]
    unnamed x27 -> x39, local copies, waits for them, and re-layouts: 6.09 us -> 5.76 us
  transfers between devices with their start and end apart: 31 -> 31, of which waited for: 17 -> 18; matrix products, arithmetic and copies ran while one was open for 5% -> 4% of each run, Pallas kernels for 21% -> 18%
where the time goes in v3:
time: 166 us; the launch traced here: 165 us
  waiting for transfers between devices  67.9 us (41%)
  Pallas kernels  40.9 us (25%)
  starting transfers between devices  40.6 us (24%)
  local copies, waits for them, and re-layouts  9.94 us (6%)
  other arithmetic  5.56 us (3%)
    ppermute x31, waiting for transfers between devices, hop(): return lax.ppermute(value, AXES, HOPS[axis, step])  67.9 us
    ppermute x31, starting transfers between devices, hop(): return lax.ppermute(value, AXES, HOPS[axis, step])  40.6 us
    pallas_call x4, Pallas kernels, query_part(): pl.pallas_call(body, out_shape=(jax.ShapeDtypeStruct((WIDE, WIDE), F32),...  15.5 us
    pallas_call x2, Pallas kernels, output_part(): pl.pallas_call(body, out_shape=jax.ShapeDtypeStruct((count, WIDE, WIDE),...  8.55 us
    pallas_call x1, Pallas kernels, middle(): pl.pallas_call(body, out_shape=(jax.ShapeDtypeStruct((WIDE, WIDE), BF16),...  6.05 us
    unnamed x39, local copies, waits for them, and re-layouts  5.76 us
    pallas_call x7, Pallas kernels, assemble(): pl.pallas_call(body, out_shape=[pltpu.VMEM(shape, BF16) for shape, _ in o...  4.99 us
    pallas_call x1, Pallas kernels, kv_partial(): pl.pallas_call(body, out_shape=jax.ShapeDtypeStruct((WIDE, count * HD), B...  3.62 us
  transfers between devices with their start and end apart: 31, of which 18 were waited for; matrix products, arithmetic and copies ran while one was open for 4% of the time, Pallas kernels for 18%

profile of v3, /device:TPU:6, one launch (start us, length us, event | category | flops | bytes accessed | tf_op | source)
XLA Modules:
  0.0 165.4 jit_solution(9475551385271988191)
XLA Ops:
  0.0 3.0 %collective-permute-start.1 = (bf16[512,512]{1,0:T(8,128)(2,1)}, bf16[512,512]{1,0:T(8,128)(2,1)S(1)}, u32[]{:S(2)}, u32[]{:S(2)}) collective-permute-start(bf16[512,512]{1,0:T(8,128)(2,1)} %refs_0_.3), channel_id=1, source_target_pairs={{0,3},{1,0},{2,1},{3,2},{4,7},{5,4},{6,5},{7,6},{8,11},{9,8},{10,9... | collective-permute-start | bytes 1572872 | tf_op jit(solution)/shard_map/ppermute | solution.py:49
  3.0 1.9 %constant_dynamic-slice_fusion.1 = bf16[2,16,64,128]{3,2,1,0:T(8,128)(2,1)} fusion(bf16[2,16,64,1024]{3,2,1,0:T(8,128)(2,1)} %param.13, s32[]{:T(128)S(6)} %select_n.119), kind=kLoop, calls=%fused_computation.108 | loop fusion | bytes 1048580 | tf_op jit(solution)/shard_map/dynamic_slice | solution.py:430
  4.9 1.9 %collective-permute-start.4 = (bf16[2,16,64,128]{3,2,1,0:T(8,128)(2,1)}, bf16[2,16,64,128]{3,2,1,0:T(8,128)(2,1)}, u32[]{:S(2)}, u32[]{:S(2)}) collective-permute-start(bf16[2,16,64,128]{3,2,1,0:T(8,128)(2,1)} %constant_dynamic-slice_fusion.1), channel_id=1, source_target_pairs={{0,32},{1,33},{2,34},{3,35},{4,36},{5,37},{6,38},{7,39},{8,40},{9,... | collective-permute-start | bytes 1572872 | tf_op jit(solution)/shard_map/ppermute | solution.py:49
  8.6 3.6 %kv_partial.1.refs_2_.refs_0_ = bf16[512,2048]{1,0:T(8,128)(2,1)S(1)} custom-call(s32[16]{0:T(128)S(1)} %fusion.29.order_ref, bf16[512,512]{1,0:T(8,128)(2,1)S(1)} %copy-done.10, f32[16,512]{1,0:T(8,128)S(1)} %reshape.77.g_ref.refs_3_.refs_4_.refs_2_, bf16[2,512,1024]{2,1,0:T(8,128)(2,1)} %w_ref.3), custom_call_target="tpu_custom_call" | custom-call | tf_op jit(solution)/shard_map/kv_partial/pallas_call | solution.py:166
  12.3 3.3 %collective-permute-start.3 = (bf16[256,512]{1,0:T(8,128)(2,1)S(1)}, bf16[256,512]{1,0:T(8,128)(2,1)S(1)}, u32[]{:S(2)}, u32[]{:S(2)}) collective-permute-start(bf16[256,512]{1,0:T(8,128)(2,1)S(1)} %get-tuple-element.149), channel_id=1, source_target_pairs={{0,3},{1,0},{2,1},{3,2},{4,7},{5,4},{6,5},{7,6},{8,11},{9,8},{10,9... | collective-permute-start | bytes 786440 | tf_op jit(solution)/shard_map/ppermute | solution.py:49
  15.6 3.9 %collective-permute-done.3.refs_4_ = bf16[256,512]{1,0:T(8,128)(2,1)S(1)} collective-permute-done((bf16[256,512]{1,0:T(8,128)(2,1)S(1)}, bf16[256,512]{1,0:T(8,128)(2,1)S(1)}, u32[]{:S(2)}, u32[]{:S(2)}) %collective-permute-start.3) | collective-permute-done | bytes 262176 | tf_op jit(solution)/shard_map/ppermute | solution.py:49
  19.5 3.7 %collective-permute-done.2.refs_3_ = bf16[256,512]{1,0:T(8,128)(2,1)S(1)} collective-permute-done((bf16[256,512]{1,0:T(8,128)(2,1)S(1)}, bf16[256,512]{1,0:T(8,128)(2,1)S(1)}, u32[]{:S(2)}, u32[]{:S(2)}) %collective-permute-start.2) | collective-permute-done | bytes 262176 | tf_op jit(solution)/shard_map/ppermute | solution.py:49
  24.2 2.4 %collective-permute-start.7 = (bf16[1536,512]{1,0:T(8,128)(2,1)S(1)}, bf16[1536,512]{1,0:T(8,128)(2,1)S(1)}, u32[]{:S(2)}, u32[]{:S(2)}) collective-permute-start(bf16[1536,512]{1,0:T(8,128)(2,1)S(1)} %assemble.8), channel_id=1, source_target_pairs={{0,4},{1,5},{2,6},{3,7},{4,8},{5,9},{6,10},{7,11},{8,12},{9,13},{1... | collective-permute-start | bytes 4718600 | tf_op jit(solution)/shard_map/ppermute | solution.py:49
  27.7 1.1 pad_maximum_fusion.refs_0_
  28.9 2.6 %collective-permute-start.9 = (bf16[2,2,16,64,128]{4,3,2,1,0:T(8,128)(2,1)S(1)}, bf16[2,2,16,64,128]{4,3,2,1,0:T(8,128)(2,1)S(1)}, u32[]{:S(2)}, u32[]{:S(2)}) collective-permute-start(bf16[2,2,16,64,128]{4,3,2,1,0:T(8,128)(2,1)S(1)} %pad_maximum_fusion.refs_0_), channel_id=1, source_target_pairs={{0,96},{1,97},{2,98},{3,99},{4,100},{5,101},{6,102},{7,103},{8,104... | collective-permute-start | bytes 3145736 | tf_op jit(solution)/shard_map/ppermute | solution.py:49
  31.7 3.2 %collective-permute-start.6 = (bf16[768,512]{1,0:T(8,128)(2,1)S(1)}, bf16[768,512]{1,0:T(8,128)(2,1)S(1)}, u32[]{:S(2)}, u32[]{:S(2)}) collective-permute-start(bf16[768,512]{1,0:T(8,128)(2,1)S(1)} %get-tuple-element.67), channel_id=1, source_target_pairs={{0,3},{1,0},{2,1},{3,2},{4,7},{5,4},{6,5},{7,6},{8,11},{9,8},{10,9... | collective-permute-start | bytes 2359304 | tf_op jit(solution)/shard_map/ppermute | solution.py:49
  37.0 3.0 %query_part.4 = (f32[512,512]{1,0:T(8,128)S(1)}, f32[512,128]{1,0:T(8,128)S(1)}) custom-call(s32[16]{0:T(128)S(1)} %fusion.29.order_ref, bf16[512,512]{1,0:T(8,128)(2,1)S(1)} %copy-done.11, bf16[512,512]{1,0:T(8,128)(2,1)S(1)} %copy-done.13, bf16[512,512]{1,0:T(8,128)(2,1)S(1)} %copy-done.15, f32[16,512]{1,0:T(8,128)S(1)} %reshape.77.g_ref.refs_3_.refs_4_.refs_2_, ...), custom_call_target="tpu_custom_call" | custom-call | tf_op jit(solution)/shard_map/query_part/pallas_call | solution.py:236
  40.0 12.3 %collective-permute-done.5.refs_0_.refs_1_ = bf16[768,512]{1,0:T(8,128)(2,1)S(1)} collective-permute-done((bf16[768,512]{1,0:T(8,128)(2,1)S(1)}, bf16[768,512]{1,0:T(8,128)(2,1)S(1)}, u32[]{:S(2)}, u32[]{:S(2)}) %collective-permute-start.5) | collective-permute-done | bytes 786464 | tf_op jit(solution)/shard_map/ppermute | solution.py:49
  52.3 1.1 collective-permute-done.8.refs_3_.refs_2_
  53.5 1.4 assemble.10
  55.5 1.3 assemble.9
  56.8 2.8 %collective-permute-start.10 = (bf16[1344,512]{1,0:T(8,128)(2,1)}, bf16[1344,512]{1,0:T(8,128)(2,1)}, u32[]{:S(2)}, u32[]{:S(2)}) collective-permute-start(bf16[1344,512]{1,0:T(8,128)(2,1)} %assemble.9), channel_id=1, source_target_pairs={{0,4},{1,5},{2,6},{3,7},{4,8},{5,9},{6,10},{7,11},{8,12},{9,13},{1... | collective-permute-start | bytes 4128776 | tf_op jit(solution)/shard_map/ppermute | solution.py:49
  62.1 1.2 copy-done.7
  63.8 5.1 %query_part.5 = (f32[512,512]{1,0:T(8,128)S(1)}, f32[512,128]{1,0:T(8,128)S(1)}) custom-call(s32[16]{0:T(128)S(1)} %fusion.29.order_ref, bf16[768,512]{1,0:T(8,128)(2,1)S(1)} %copy-done.3, bf16[768,512]{1,0:T(8,128)(2,1)S(1)} %copy-done.5, bf16[1536,512]{1,0:T(8,128)(2,1)S(1)} %copy-done.7, ...), custom_call_target="tpu_custom_call", output_to_operand_aliasing={{0}: (7, {}), {1}: (8, {})} | custom-call | tf_op jit(solution)/shard_map/query_part/pallas_call | solution.py:236
  68.9 2.2 %gather_blocks.1.prefix_ref = bf16[8,2,320,128]{3,2,1,0:T(8,128)(2,1)S(1)} custom-call(s32[8,4]{1,0:T(8,128)S(1)} %fusion.25.code_ref, bf16[2,2,16,64,128]{4,3,2,1,0:T(8,128)(2,1)} %copy-done.16, bf16[2,2,16,64,128]{4,3,2,1,0:T(8,128)(2,1)} %copy-done.17, bf16[2,2,16,64,128]{4,3,2,1,0:T(8,128)(2,1)} %collective-permute-done.12.refs_2_, ...), custom_call_target="tpu_custom_call" | custom-call | tf_op jit(solution)/shard_map/gather_blocks/pallas_call | solution.py:280
  71.1 4.6 %collective-permute-done.10.refs_0_.refs_1_ = bf16[1344,512]{1,0:T(8,128)(2,1)} collective-permute-done((bf16[1344,512]{1,0:T(8,128)(2,1)}, bf16[1344,512]{1,0:T(8,128)(2,1)}, u32[]{:S(2)}, u32[]{:S(2)}) %collective-permute-start.10) | collective-permute-done | bytes 1376288 | tf_op jit(solution)/shard_map/ppermute | solution.py:49
  75.8 3.7 %collective-permute-done.11.refs_1_.refs_0_ = bf16[1344,512]{1,0:T(8,128)(2,1)} collective-permute-done((bf16[1344,512]{1,0:T(8,128)(2,1)}, bf16[1344,512]{1,0:T(8,128)(2,1)}, u32[]{:S(2)}, u32[]{:S(2)}) %collective-permute-start.11) | collective-permute-done | bytes 1376288 | tf_op jit(solution)/shard_map/ppermute | solution.py:49
  79.5 1.8 %assemble.12 = (bf16[384,512]{1,0:T(8,128)(2,1)S(1)}, bf16[384,512]{1,0:T(8,128)(2,1)S(1)}) custom-call(bf16[1344,512]{1,0:T(8,128)(2,1)} %collective-permute-done.10.refs_0_.refs_1_, bf16[1344,512]{1,0:T(8,128)(2,1)} %collective-permute-done.11.refs_1_.refs_0_, bf16[512,512]{1,0:T(8,128)(2,1)S(1)} %assemble.11.refs_2_.refs_0_), custom_call_target="tpu_custom_call" | custom-call | tf_op jit(solution)/shard_map/assemble/pallas_call | solution.py:115
  81.6 2.0 %collective-permute-start.15 = (bf16[384,512]{1,0:T(8,128)(2,1)S(1)}, bf16[384,512]{1,0:T(8,128)(2,1)S(1)}, u32[]{:S(2)}, u32[]{:S(2)}) collective-permute-start(bf16[384,512]{1,0:T(8,128)(2,1)S(1)} %get-tuple-element.85), channel_id=1, source_target_pairs={{0,12},{1,13},{2,14},{3,15},{4,0},{5,1},{6,2},{7,3},{8,4},{9,5},{1... | collective-permute-start | bytes 1179656 | tf_op jit(solution)/shard_map/ppermute | solution.py:49
  83.6 5.3 %query_part.6 = (f32[512,512]{1,0:T(8,128)S(1)}, f32[512,128]{1,0:T(8,128)S(1)}) custom-call(s32[16]{0:T(128)S(1)} %fusion.29.order_ref, bf16[1344,512]{1,0:T(8,128)(2,1)} %collective-permute-done.11.refs_1_.refs_0_, bf16[1344,512]{1,0:T(8,128)(2,1)} %collective-permute-done.10.refs_0_.refs_1_, ...), custom_call_target="tpu_custom_call", output_to_operand_aliasing={{0}: (5, {}), {1}: (6, {})} | custom-call | tf_op jit(solution)/shard_map/query_part/pallas_call | solution.py:236
  89.3 1.3 collective-permute-done.15.refs_1_.refs_2_
  90.8 2.0 %query_part.7 = (f32[512,512]{1,0:T(8,128)S(1)}, f32[512,128]{1,0:T(8,128)S(1)}) custom-call(s32[16]{0:T(128)S(1)} %fusion.29.order_ref, bf16[384,512]{1,0:T(8,128)(2,1)S(1)} %collective-permute-done.14.refs_0_.refs_1_, bf16[384,512]{1,0:T(8,128)(2,1)S(1)} %collective-permute-done.15.refs_1_.refs_2_, ...), custom_call_target="tpu_custom_call", output_to_operand_aliasing={{0}: (5, {}), {1}: (6, {})} | custom-call | tf_op jit(solution)/shard_map/query_part/pallas_call | solution.py:236
  92.8 2.9 %collective-permute-done.16.other_ref = bf16[512,128]{1,0:T(8,128)(2,1)S(1)} collective-permute-done((bf16[512,128]{1,0:T(8,128)(2,1)S(1)}, bf16[512,128]{1,0:T(8,128)(2,1)S(1)}, u32[]{:S(2)}, u32[]{:S(2)}) %collective-permute-start.16) | collective-permute-done | bytes 131104 | tf_op jit(solution)/shard_map/ppermute | solution.py:49
  95.7 6.1 %middle.1 = (bf16[512,512]{1,0:T(8,128)(2,1)S(1)}, bf16[4,512,512]{2,1,0:T(8,128)(2,1)S(1)}, bf16[8,2,320,128]{3,2,1,0:T(8,128)(2,1)S(1)}) custom-call(s32[16]{0:T(128)S(1)} %fusion.29.order_ref, s32[8]{0:T(128)S(1)} %get-tuple-element.118.len_ref, f32[512,512]{1,0:T(8,128)S(1)} %get-tuple-element.94.q_ref, ...), custom_call_target="tpu_custom_call", output_to_operand_aliasing={{2}: (8, {})} | custom-call | tf_op jit(solution)/shard_map/middle/pallas_call | solution.py:353
  102.1 2.1 %collective-permute-start.22 = (bf16[768,512]{1,0:T(8,128)(2,1)S(1)}, bf16[768,512]{1,0:T(8,128)(2,1)S(1)}, u32[]{:S(2)}, u32[]{:S(2)}) collective-permute-start(bf16[768,512]{1,0:T(8,128)(2,1)S(1)} %pad_maximum_fusion.4), channel_id=1, source_target_pairs={{0,12},{1,13},{2,14},{3,15},{4,0},{5,1},{6,2},{7,3},{8,4},{9,5},{1... | collective-permute-start | bytes 2359304 | tf_op jit(solution)/shard_map/ppermute | solution.py:49
  105.2 2.3 %collective-permute-start.17 = (bf16[256,512]{1,0:T(8,128)(2,1)S(1)}, bf16[256,512]{1,0:T(8,128)(2,1)S(1)}, u32[]{:S(2)}, u32[]{:S(2)}) collective-permute-start(bf16[256,512]{1,0:T(8,128)(2,1)S(1)} %get-tuple-element.148), channel_id=1, source_target_pairs={{0,4},{1,5},{2,6},{3,7},{4,8},{5,9},{6,10},{7,11},{8,12},{9,13},{1... | collective-permute-start | bytes 786440 | tf_op jit(solution)/shard_map/ppermute | solution.py:49
  107.4 4.3 %output_part.2 = bf16[6,512,512]{2,1,0:T(8,128)(2,1)S(1)} custom-call(s32[16]{0:T(128)S(1)} %fusion.29.order_ref, bf16[512,512]{1,0:T(8,128)(2,1)S(1)} %get-tuple-element.105.h_ref, bf16[512,8192]{1,0:T(8,128)(2,1)} %w_ref.5), custom_call_target="tpu_custom_call" | custom-call | tf_op jit(solution)/shard_map/output_part/pallas_call | solution.py:392
  111.7 6.5 %collective-permute-done.18 = bf16[256,512]{1,0:T(8,128)(2,1)S(1)} collective-permute-done((bf16[256,512]{1,0:T(8,128)(2,1)S(1)}, bf16[256,512]{1,0:T(8,128)(2,1)S(1)}, u32[]{:S(2)}, u32[]{:S(2)}) %collective-permute-start.18) | collective-permute-done | bytes 262176 | tf_op jit(solution)/shard_map/ppermute | solution.py:49
  119.3 1.8 %collective-permute-start.20 = (bf16[512,512]{1,0:T(8,128)(2,1)S(1)}, bf16[512,512]{1,0:T(8,128)(2,1)S(1)}, u32[]{:S(2)}, u32[]{:S(2)}) collective-permute-start(bf16[512,512]{1,0:T(8,128)(2,1)S(1)} %pad_maximum_fusion.6), channel_id=1, source_target_pairs={{0,12},{1,13},{2,14},{3,15},{4,0},{5,1},{6,2},{7,3},{8,4},{9,5},{1... | collective-permute-start | bytes 1572872 | tf_op jit(solution)/shard_map/ppermute | solution.py:49
  121.2 1.6 collective-permute-start.27
  123.6 4.3 %output_part.3 = bf16[6,512,512]{2,1,0:T(8,128)(2,1)S(1)} custom-call(s32[16]{0:T(128)S(1)} %fusion.29.order_ref, bf16[512,512]{1,0:T(8,128)(2,1)S(1)} %get-tuple-element.105.h_ref, bf16[512,8192]{1,0:T(8,128)(2,1)} %w_ref.5), custom_call_target="tpu_custom_call" | custom-call | tf_op jit(solution)/shard_map/output_part/pallas_call | solution.py:392
  127.9 3.0 %collective-permute-done.19 = bf16[512,512]{1,0:T(8,128)(2,1)S(1)} collective-permute-done((bf16[512,512]{1,0:T(8,128)(2,1)S(1)}, bf16[512,512]{1,0:T(8,128)(2,1)S(1)}, u32[]{:S(2)}, u32[]{:S(2)}) %collective-permute-start.19) | collective-permute-done | bytes 524320 | tf_op jit(solution)/shard_map/ppermute | solution.py:49
  130.9 1.7 %collective-permute-done.20 = bf16[512,512]{1,0:T(8,128)(2,1)S(1)} collective-permute-done((bf16[512,512]{1,0:T(8,128)(2,1)S(1)}, bf16[512,512]{1,0:T(8,128)(2,1)S(1)}, u32[]{:S(2)}, u32[]{:S(2)}) %collective-permute-start.20) | collective-permute-done | bytes 524320 | tf_op jit(solution)/shard_map/ppermute | solution.py:49
  132.9 2.0 %collective-permute-start.23 = (bf16[256,512]{1,0:T(8,128)(2,1)S(1)}, bf16[256,512]{1,0:T(8,128)(2,1)S(1)}, u32[]{:S(2)}, u32[]{:S(2)}) collective-permute-start(bf16[256,512]{1,0:T(8,128)(2,1)S(1)} %get-tuple-element.152), channel_id=1, source_target_pairs={{0,1},{1,2},{2,3},{3,0},{4,5},{5,6},{6,7},{7,4},{8,9},{9,10},{10,1... | collective-permute-start | bytes 786440 | tf_op jit(solution)/shard_map/ppermute | solution.py:49
  135.0 7.1 %collective-permute-done.24 = bf16[256,512]{1,0:T(8,128)(2,1)S(1)} collective-permute-done((bf16[256,512]{1,0:T(8,128)(2,1)S(1)}, bf16[256,512]{1,0:T(8,128)(2,1)S(1)}, u32[]{:S(2)}, u32[]{:S(2)}) %collective-permute-start.24) | collective-permute-done | bytes 262176 | tf_op jit(solution)/shard_map/ppermute | solution.py:49
  142.0 4.1 %collective-permute-done.27 = bf16[1024,512]{1,0:T(8,128)(2,1)S(1)} collective-permute-done((bf16[1024,512]{1,0:T(8,128)(2,1)S(1)}, bf16[1024,512]{1,0:T(8,128)(2,1)S(1)}, u32[]{:S(2)}, u32[]{:S(2)}) %collective-permute-start.27) | collective-permute-done | bytes 1048608 | tf_op jit(solution)/shard_map/ppermute | solution.py:49
  146.1 3.3 %collective-permute-done.28 = bf16[1024,512]{1,0:T(8,128)(2,1)S(1)} collective-permute-done((bf16[1024,512]{1,0:T(8,128)(2,1)S(1)}, bf16[1024,512]{1,0:T(8,128)(2,1)S(1)}, u32[]{:S(2)}, u32[]{:S(2)}) %collective-permute-start.28) | collective-permute-done | bytes 1048608 | tf_op jit(solution)/shard_map/ppermute | solution.py:49
  151.0 2.7 %collective-permute-start.25 = (bf16[512,512]{1,0:T(8,128)(2,1)S(1)}, bf16[512,512]{1,0:T(8,128)(2,1)S(1)}, u32[]{:S(2)}, u32[]{:S(2)}) collective-permute-start(bf16[512,512]{1,0:T(8,128)(2,1)S(1)} %pad_maximum_fusion.7), channel_id=1, source_target_pairs={{0,4},{1,5},{2,6},{3,7},{4,8},{5,9},{6,10},{7,11},{8,12},{9,13},{1... | collective-permute-start | bytes 1572872 | tf_op jit(solution)/shard_map/ppermute | solution.py:49
  153.8 2.1 %collective-permute-start.29 = (bf16[512,512]{1,0:T(8,128)(2,1)S(1)}, bf16[512,512]{1,0:T(8,128)(2,1)S(1)}, u32[]{:S(2)}, u32[]{:S(2)}) collective-permute-start(bf16[512,512]{1,0:T(8,128)(2,1)S(1)} %pad_maximum_fusion.9), channel_id=1, source_target_pairs={{0,1},{1,2},{2,3},{3,0},{4,5},{5,6},{6,7},{7,4},{8,9},{9,10},{10,1... | collective-permute-start | bytes 1572872 | tf_op jit(solution)/shard_map/ppermute | solution.py:49
  155.9 3.6 %collective-permute-done.30 = bf16[512,512]{1,0:T(8,128)(2,1)S(1)} collective-permute-done((bf16[512,512]{1,0:T(8,128)(2,1)S(1)}, bf16[512,512]{1,0:T(8,128)(2,1)S(1)}, u32[]{:S(2)}, u32[]{:S(2)}) %collective-permute-start.30) | collective-permute-done | bytes 524320 | tf_op jit(solution)/shard_map/ppermute | solution.py:49
  159.5 1.3 collective-permute-done.26
  160.8 3.4 %collective-permute-done.29 = bf16[512,512]{1,0:T(8,128)(2,1)S(1)} collective-permute-done((bf16[512,512]{1,0:T(8,128)(2,1)S(1)}, bf16[512,512]{1,0:T(8,128)(2,1)S(1)}, u32[]{:S(2)}, u32[]{:S(2)}) %collective-permute-start.29) | collective-permute-done | bytes 524320 | tf_op jit(solution)/shard_map/ppermute | solution.py:49
  164.3 1.1 fusion.5
  (101 shorter events, 15.9 us)
Async XLA Ops:
  0.0 60.1 %copy-start = (s32[64,4]{0,1:T(4,128)S(1)}, s32[64,4]{0,1:T(4,128)}, u32[]{:S(2)}) copy-start(s32[64,4]{0,1:T(4,128)} %param.14) | copy-start | bytes 3076
  0.0 23.2 %collective-permute-start.1 = (bf16[512,512]{1,0:T(8,128)(2,1)}, bf16[512,512]{1,0:T(8,128)(2,1)S(1)}, u32[]{:S(2)}, u32[]{:S(2)}) collective-permute-start(bf16[512,512]{1,0:T(8,128)(2,1)} %refs_0_.3), channel_id=1, source_target_pairs={{0,3},{1,0},{2,1},{3,2},{4,7},{5,4},{6,5},{7,6},{8,11},{9,8},{10,9... | collective-permute-start | bytes 1572872 | tf_op jit(solution)/shard_map/ppermute | solution.py:49
  3.0 20.2 %collective-permute-start = (bf16[512,512]{1,0:T(8,128)(2,1)}, bf16[512,512]{1,0:T(8,128)(2,1)S(1)}, u32[]{:S(2)}, u32[]{:S(2)}) collective-permute-start(bf16[512,512]{1,0:T(8,128)(2,1)} %refs_0_.3), channel_id=1, source_target_pairs={{0,1},{1,2},{2,3},{3,0},{4,5},{5,6},{6,7},{7,4},{8,9},{9,10},{10,1... | collective-permute-start | bytes 1572872 | tf_op jit(solution)/shard_map/ppermute | solution.py:49
  4.9 18.3 %collective-permute-start.4 = (bf16[2,16,64,128]{3,2,1,0:T(8,128)(2,1)}, bf16[2,16,64,128]{3,2,1,0:T(8,128)(2,1)}, u32[]{:S(2)}, u32[]{:S(2)}) collective-permute-start(bf16[2,16,64,128]{3,2,1,0:T(8,128)(2,1)} %constant_dynamic-slice_fusion.1), channel_id=1, source_target_pairs={{0,32},{1,33},{2,34},{3,35},{4,36},{5,37},{6,38},{7,39},{8,40},{9,... | collective-permute-start | bytes 1572872 | tf_op jit(solution)/shard_map/ppermute | solution.py:49
  7.6 1.0 copy-start.10
  8.6 14.6 %copy-start.11 = (bf16[512,512]{1,0:T(8,128)(2,1)S(1)}, bf16[512,512]{1,0:T(8,128)(2,1)}, u32[]{:S(2)}) copy-start(bf16[512,512]{1,0:T(8,128)(2,1)} %refs_0_.3) | copy-start | bytes 1572868
  12.3 7.2 %collective-permute-start.3 = (bf16[256,512]{1,0:T(8,128)(2,1)S(1)}, bf16[256,512]{1,0:T(8,128)(2,1)S(1)}, u32[]{:S(2)}, u32[]{:S(2)}) collective-permute-start(bf16[256,512]{1,0:T(8,128)(2,1)S(1)} %get-tuple-element.149), channel_id=1, source_target_pairs={{0,3},{1,0},{2,1},{3,2},{4,7},{5,4},{6,5},{7,6},{8,11},{9,8},{10,9... | collective-permute-start | bytes 786440 | tf_op jit(solution)/shard_map/ppermute | solution.py:49
  15.6 7.6 %collective-permute-start.2 = (bf16[256,512]{1,0:T(8,128)(2,1)S(1)}, bf16[256,512]{1,0:T(8,128)(2,1)S(1)}, u32[]{:S(2)}, u32[]{:S(2)}) collective-permute-start(bf16[256,512]{1,0:T(8,128)(2,1)S(1)} %get-tuple-element.150), channel_id=1, source_target_pairs={{0,1},{1,2},{2,3},{3,0},{4,5},{5,6},{6,7},{7,4},{8,9},{9,10},{10,1... | collective-permute-start | bytes 786440 | tf_op jit(solution)/shard_map/ppermute | solution.py:49
  23.2 8.3 %copy-start.12 = (bf16[512,512]{1,0:T(8,128)(2,1)}, bf16[512,512]{1,0:T(8,128)(2,1)S(1)}, u32[]{:S(2)}) copy-start(bf16[512,512]{1,0:T(8,128)(2,1)S(1)} %collective-permute-done.1.refs_1_) | copy-start | bytes 1572868
  23.2 8.3 %copy-start.14 = (bf16[512,512]{1,0:T(8,128)(2,1)}, bf16[512,512]{1,0:T(8,128)(2,1)S(1)}, u32[]{:S(2)}) copy-start(bf16[512,512]{1,0:T(8,128)(2,1)S(1)} %collective-permute-done.refs_0_.refs_2_) | copy-start | bytes 1572868
  23.3 30.1 %collective-permute-start.8 = (bf16[1536,512]{1,0:T(8,128)(2,1)S(1)}, bf16[1536,512]{1,0:T(8,128)(2,1)S(1)}, u32[]{:S(2)}, u32[]{:S(2)}) collective-permute-start(bf16[1536,512]{1,0:T(8,128)(2,1)S(1)} %assemble.8), channel_id=1, source_target_pairs={{0,12},{1,13},{2,14},{3,15},{4,0},{5,1},{6,2},{7,3},{8,4},{9,5},{1... | collective-permute-start | bytes 4718600 | tf_op jit(solution)/shard_map/ppermute | solution.py:49
  24.2 29.2 %collective-permute-start.7 = (bf16[1536,512]{1,0:T(8,128)(2,1)S(1)}, bf16[1536,512]{1,0:T(8,128)(2,1)S(1)}, u32[]{:S(2)}, u32[]{:S(2)}) collective-permute-start(bf16[1536,512]{1,0:T(8,128)(2,1)S(1)} %assemble.8), channel_id=1, source_target_pairs={{0,4},{1,5},{2,6},{3,7},{4,8},{5,9},{6,10},{7,11},{8,12},{9,13},{1... | collective-permute-start | bytes 4718600 | tf_op jit(solution)/shard_map/ppermute | solution.py:49
  28.8 11.2 %copy-start.16 = (bf16[2,2,16,64,128]{4,3,2,1,0:T(8,128)(2,1)}, bf16[2,2,16,64,128]{4,3,2,1,0:T(8,128)(2,1)S(1)}, u32[]{:S(2)}) copy-start(bf16[2,2,16,64,128]{4,3,2,1,0:T(8,128)(2,1)S(1)} %pad_maximum_fusion.refs_0_) | copy-start | bytes 3145732
  28.9 23.5 %collective-permute-start.9 = (bf16[2,2,16,64,128]{4,3,2,1,0:T(8,128)(2,1)S(1)}, bf16[2,2,16,64,128]{4,3,2,1,0:T(8,128)(2,1)S(1)}, u32[]{:S(2)}, u32[]{:S(2)}) collective-permute-start(bf16[2,2,16,64,128]{4,3,2,1,0:T(8,128)(2,1)S(1)} %pad_maximum_fusion.refs_0_), channel_id=1, source_target_pairs={{0,96},{1,97},{2,98},{3,99},{4,100},{5,101},{6,102},{7,103},{8,104... | collective-permute-start | bytes 3145736 | tf_op jit(solution)/shard_map/ppermute | solution.py:49
  31.6 20.7 %collective-permute-start.5 = (bf16[768,512]{1,0:T(8,128)(2,1)S(1)}, bf16[768,512]{1,0:T(8,128)(2,1)S(1)}, u32[]{:S(2)}, u32[]{:S(2)}) collective-permute-start(bf16[768,512]{1,0:T(8,128)(2,1)S(1)} %get-tuple-element.66), channel_id=1, source_target_pairs={{0,1},{1,2},{2,3},{3,0},{4,5},{5,6},{6,7},{7,4},{8,9},{9,10},{10,1... | collective-permute-start | bytes 2359304 | tf_op jit(solution)/shard_map/ppermute | solution.py:49
  31.7 20.6 %collective-permute-start.6 = (bf16[768,512]{1,0:T(8,128)(2,1)S(1)}, bf16[768,512]{1,0:T(8,128)(2,1)S(1)}, u32[]{:S(2)}, u32[]{:S(2)}) collective-permute-start(bf16[768,512]{1,0:T(8,128)(2,1)S(1)} %get-tuple-element.67), channel_id=1, source_target_pairs={{0,3},{1,0},{2,1},{3,2},{4,7},{5,4},{6,5},{7,6},{8,11},{9,8},{10,9... | collective-permute-start | bytes 2359304 | tf_op jit(solution)/shard_map/ppermute | solution.py:49
  52.3 2.5 %copy-start.2 = (bf16[768,512]{1,0:T(8,128)(2,1)}, bf16[768,512]{1,0:T(8,128)(2,1)S(1)}, u32[]{:S(2)}) copy-start(bf16[768,512]{1,0:T(8,128)(2,1)S(1)} %collective-permute-done.5.refs_0_.refs_1_) | copy-start | bytes 2359300
  52.3 2.5 %copy-start.4 = (bf16[768,512]{1,0:T(8,128)(2,1)}, bf16[768,512]{1,0:T(8,128)(2,1)S(1)}, u32[]{:S(2)}) copy-start(bf16[768,512]{1,0:T(8,128)(2,1)S(1)} %collective-permute-done.6.refs_1_.refs_2_) | copy-start | bytes 2359300
  52.3 2.5 %copy-start.17 = (bf16[2,2,16,64,128]{4,3,2,1,0:T(8,128)(2,1)}, bf16[2,2,16,64,128]{4,3,2,1,0:T(8,128)(2,1)S(1)}, u32[]{:S(2)}) copy-start(bf16[2,2,16,64,128]{4,3,2,1,0:T(8,128)(2,1)S(1)} %collective-permute-done.9.refs_1_) | copy-start | bytes 3145732
  53.4 1.6 copy-start.6
  53.4 2.1 %copy-start.8 = (bf16[1536,512]{1,0:T(8,128)(2,1)}, bf16[1536,512]{1,0:T(8,128)(2,1)S(1)}, u32[]{:S(2)}) copy-start(bf16[1536,512]{1,0:T(8,128)(2,1)S(1)} %collective-permute-done.7.refs_3_) | copy-start | bytes 4718596
  55.5 4.8 %copy-start.18 = (s32[64]{0:T(128)S(1)}, s32[64]{0:T(128)}, u32[]{:S(2)}) copy-start(s32[64]{0:T(128)} %param.15) | copy-start | bytes 772
  56.8 18.9 %collective-permute-start.10 = (bf16[1344,512]{1,0:T(8,128)(2,1)}, bf16[1344,512]{1,0:T(8,128)(2,1)}, u32[]{:S(2)}, u32[]{:S(2)}) collective-permute-start(bf16[1344,512]{1,0:T(8,128)(2,1)} %assemble.9), channel_id=1, source_target_pairs={{0,4},{1,5},{2,6},{3,7},{4,8},{5,9},{6,10},{7,11},{8,12},{9,13},{1... | collective-permute-start | bytes 4128776 | tf_op jit(solution)/shard_map/ppermute | solution.py:49
  59.6 19.8 %collective-permute-start.11 = (bf16[1344,512]{1,0:T(8,128)(2,1)}, bf16[1344,512]{1,0:T(8,128)(2,1)}, u32[]{:S(2)}, u32[]{:S(2)}) collective-permute-start(bf16[1344,512]{1,0:T(8,128)(2,1)} %assemble.10), channel_id=1, source_target_pairs={{0,12},{1,13},{2,14},{3,15},{4,0},{5,1},{6,2},{7,3},{8,4},{9,5},{1... | collective-permute-start | bytes 4128776 | tf_op jit(solution)/shard_map/ppermute | solution.py:49
  59.6 9.3 %collective-permute-start.12 = (bf16[2,2,16,64,128]{4,3,2,1,0:T(8,128)(2,1)}, bf16[2,2,16,64,128]{4,3,2,1,0:T(8,128)(2,1)}, u32[]{:S(2)}, u32[]{:S(2)}) collective-permute-start(bf16[2,2,16,64,128]{4,3,2,1,0:T(8,128)(2,1)} %copy-done.16), channel_id=1, source_target_pairs={{0,16},{1,17},{2,18},{3,19},{4,20},{5,21},{6,22},{7,23},{8,24},{9,... | collective-permute-start | bytes 3145736 | tf_op jit(solution)/shard_map/ppermute | solution.py:49
  59.6 9.3 %collective-permute-start.13 = (bf16[2,2,16,64,128]{4,3,2,1,0:T(8,128)(2,1)}, bf16[2,2,16,64,128]{4,3,2,1,0:T(8,128)(2,1)}, u32[]{:S(2)}, u32[]{:S(2)}) collective-permute-start(bf16[2,2,16,64,128]{4,3,2,1,0:T(8,128)(2,1)} %copy-done.17), channel_id=1, source_target_pairs={{0,16},{1,17},{2,18},{3,19},{4,20},{5,21},{6,22},{7,23},{8,24},{9,... | collective-permute-start | bytes 3145736 | tf_op jit(solution)/shard_map/ppermute | solution.py:49
  60.5 1.3 copy-start.3
  60.5 1.4 copy-start.5
  61.9 1.4 copy-start.7
  61.9 1.9 %copy-start.9 = (bf16[1536,512]{1,0:T(8,128)(2,1)S(1)}, bf16[1536,512]{1,0:T(8,128)(2,1)}, u32[]{:S(2)}) copy-start(bf16[1536,512]{1,0:T(8,128)(2,1)} %copy-done.8) | copy-start | bytes 4718596
  81.3 8.0 %collective-permute-start.14 = (bf16[384,512]{1,0:T(8,128)(2,1)S(1)}, bf16[384,512]{1,0:T(8,128)(2,1)S(1)}, u32[]{:S(2)}, u32[]{:S(2)}) collective-permute-start(bf16[384,512]{1,0:T(8,128)(2,1)S(1)} %get-tuple-element.84), channel_id=1, source_target_pairs={{0,4},{1,5},{2,6},{3,7},{4,8},{5,9},{6,10},{7,11},{8,12},{9,13},{1... | collective-permute-start | bytes 1179656 | tf_op jit(solution)/shard_map/ppermute | solution.py:49
  81.6 9.1 %collective-permute-start.15 = (bf16[384,512]{1,0:T(8,128)(2,1)S(1)}, bf16[384,512]{1,0:T(8,128)(2,1)S(1)}, u32[]{:S(2)}, u32[]{:S(2)}) collective-permute-start(bf16[384,512]{1,0:T(8,128)(2,1)S(1)} %get-tuple-element.85), channel_id=1, source_target_pairs={{0,12},{1,13},{2,14},{3,15},{4,0},{5,1},{6,2},{7,3},{8,4},{9,5},{1... | collective-permute-start | bytes 1179656 | tf_op jit(solution)/shard_map/ppermute | solution.py:49
  90.7 5.0 %collective-permute-start.16 = (bf16[512,128]{1,0:T(8,128)(2,1)S(1)}, bf16[512,128]{1,0:T(8,128)(2,1)S(1)}, u32[]{:S(2)}, u32[]{:S(2)}) collective-permute-start(bf16[512,128]{1,0:T(8,128)(2,1)S(1)} %assemble.13.mine_ref), channel_id=1, source_target_pairs={{0,1},{1,0},{2,3},{3,2},{4,5},{5,4},{6,7},{7,6},{8,9},{9,8},{10,11... | collective-permute-start | bytes 393224 | tf_op jit(solution)/shard_map/ppermute | solution.py:49
  102.0 16.3 %collective-permute-start.21 = (bf16[768,512]{1,0:T(8,128)(2,1)S(1)}, bf16[768,512]{1,0:T(8,128)(2,1)S(1)}, u32[]{:S(2)}, u32[]{:S(2)}) collective-permute-start(bf16[768,512]{1,0:T(8,128)(2,1)S(1)} %pad_maximum_fusion.3), channel_id=1, source_target_pairs={{0,4},{1,5},{2,6},{3,7},{4,8},{5,9},{6,10},{7,11},{8,12},{9,13},{1... | collective-permute-start | bytes 2359304 | tf_op jit(solution)/shard_map/ppermute | solution.py:49
  102.1 16.2 %collective-permute-start.22 = (bf16[768,512]{1,0:T(8,128)(2,1)S(1)}, bf16[768,512]{1,0:T(8,128)(2,1)S(1)}, u32[]{:S(2)}, u32[]{:S(2)}) collective-permute-start(bf16[768,512]{1,0:T(8,128)(2,1)S(1)} %pad_maximum_fusion.4), channel_id=1, source_target_pairs={{0,12},{1,13},{2,14},{3,15},{4,0},{5,1},{6,2},{7,3},{8,4},{9,5},{1... | collective-permute-start | bytes 2359304 | tf_op jit(solution)/shard_map/ppermute | solution.py:49
  104.2 14.0 %collective-permute-start.18 = (bf16[256,512]{1,0:T(8,128)(2,1)S(1)}, bf16[256,512]{1,0:T(8,128)(2,1)S(1)}, u32[]{:S(2)}, u32[]{:S(2)}) collective-permute-start(bf16[256,512]{1,0:T(8,128)(2,1)S(1)} %get-tuple-element.147), channel_id=1, source_target_pairs={{0,12},{1,13},{2,14},{3,15},{4,0},{5,1},{6,2},{7,3},{8,4},{9,5},{1... | collective-permute-start | bytes 786440 | tf_op jit(solution)/shard_map/ppermute | solution.py:49
  105.2 13.0 %collective-permute-start.17 = (bf16[256,512]{1,0:T(8,128)(2,1)S(1)}, bf16[256,512]{1,0:T(8,128)(2,1)S(1)}, u32[]{:S(2)}, u32[]{:S(2)}) collective-permute-start(bf16[256,512]{1,0:T(8,128)(2,1)S(1)} %get-tuple-element.148), channel_id=1, source_target_pairs={{0,4},{1,5},{2,6},{3,7},{4,8},{5,9},{6,10},{7,11},{8,12},{9,13},{1... | collective-permute-start | bytes 786440 | tf_op jit(solution)/shard_map/ppermute | solution.py:49
  118.9 12.1 %collective-permute-start.19 = (bf16[512,512]{1,0:T(8,128)(2,1)S(1)}, bf16[512,512]{1,0:T(8,128)(2,1)S(1)}, u32[]{:S(2)}, u32[]{:S(2)}) collective-permute-start(bf16[512,512]{1,0:T(8,128)(2,1)S(1)} %pad_maximum_fusion.5), channel_id=1, source_target_pairs={{0,4},{1,5},{2,6},{3,7},{4,8},{5,9},{6,10},{7,11},{8,12},{9,13},{1... | collective-permute-start | bytes 1572872 | tf_op jit(solution)/shard_map/ppermute | solution.py:49
  119.3 13.3 %collective-permute-start.20 = (bf16[512,512]{1,0:T(8,128)(2,1)S(1)}, bf16[512,512]{1,0:T(8,128)(2,1)S(1)}, u32[]{:S(2)}, u32[]{:S(2)}) collective-permute-start(bf16[512,512]{1,0:T(8,128)(2,1)S(1)} %pad_maximum_fusion.6), channel_id=1, source_target_pairs={{0,12},{1,13},{2,14},{3,15},{4,0},{5,1},{6,2},{7,3},{8,4},{9,5},{1... | collective-permute-start | bytes 1572872 | tf_op jit(solution)/shard_map/ppermute | solution.py:49
  121.2 25.0 %collective-permute-start.27 = (bf16[1024,512]{1,0:T(8,128)(2,1)S(1)}, bf16[1024,512]{1,0:T(8,128)(2,1)S(1)}, u32[]{:S(2)}, u32[]{:S(2)}) collective-permute-start(bf16[1024,512]{1,0:T(8,128)(2,1)S(1)} %pad_maximum_fusion.1), channel_id=1, source_target_pairs={{0,4},{1,5},{2,6},{3,7},{4,8},{5,9},{6,10},{7,11},{8,12},{9,13},{1... | collective-permute-start | bytes 3145736 | tf_op jit(solution)/shard_map/ppermute | solution.py:49
  122.8 26.6 %collective-permute-start.28 = (bf16[1024,512]{1,0:T(8,128)(2,1)S(1)}, bf16[1024,512]{1,0:T(8,128)(2,1)S(1)}, u32[]{:S(2)}, u32[]{:S(2)}) collective-permute-start(bf16[1024,512]{1,0:T(8,128)(2,1)S(1)} %pad_maximum_fusion.2), channel_id=1, source_target_pairs={{0,12},{1,13},{2,14},{3,15},{4,0},{5,1},{6,2},{7,3},{8,4},{9,5},{1... | collective-permute-start | bytes 3145736 | tf_op jit(solution)/shard_map/ppermute | solution.py:49
  132.8 9.2 %collective-permute-start.24 = (bf16[256,512]{1,0:T(8,128)(2,1)S(1)}, bf16[256,512]{1,0:T(8,128)(2,1)S(1)}, u32[]{:S(2)}, u32[]{:S(2)}) collective-permute-start(bf16[256,512]{1,0:T(8,128)(2,1)S(1)} %get-tuple-element.151), channel_id=1, source_target_pairs={{0,3},{1,0},{2,1},{3,2},{4,7},{5,4},{6,5},{7,6},{8,11},{9,8},{10,9... | collective-permute-start | bytes 786440 | tf_op jit(solution)/shard_map/ppermute | solution.py:49
  132.9 9.1 %collective-permute-start.23 = (bf16[256,512]{1,0:T(8,128)(2,1)S(1)}, bf16[256,512]{1,0:T(8,128)(2,1)S(1)}, u32[]{:S(2)}, u32[]{:S(2)}) collective-permute-start(bf16[256,512]{1,0:T(8,128)(2,1)S(1)} %get-tuple-element.152), channel_id=1, source_target_pairs={{0,1},{1,2},{2,3},{3,0},{4,5},{5,6},{6,7},{7,4},{8,9},{9,10},{10,1... | collective-permute-start | bytes 786440 | tf_op jit(solution)/shard_map/ppermute | solution.py:49
  150.2 9.2 %collective-permute-start.30 = (bf16[512,512]{1,0:T(8,128)(2,1)S(1)}, bf16[512,512]{1,0:T(8,128)(2,1)S(1)}, u32[]{:S(2)}, u32[]{:S(2)}) collective-permute-start(bf16[512,512]{1,0:T(8,128)(2,1)S(1)} %pad_maximum_fusion.10), channel_id=1, source_target_pairs={{0,3},{1,0},{2,1},{3,2},{4,7},{5,4},{6,5},{7,6},{8,11},{9,8},{10,9... | collective-permute-start | bytes 1572872 | tf_op jit(solution)/shard_map/ppermute | solution.py:49
  150.3 10.5 %collective-permute-start.26 = (bf16[512,512]{1,0:T(8,128)(2,1)S(1)}, bf16[512,512]{1,0:T(8,128)(2,1)S(1)}, u32[]{:S(2)}, u32[]{:S(2)}) collective-permute-start(bf16[512,512]{1,0:T(8,128)(2,1)S(1)} %pad_maximum_fusion.8), channel_id=1, source_target_pairs={{0,12},{1,13},{2,14},{3,15},{4,0},{5,1},{6,2},{7,3},{8,4},{9,5},{1... | collective-permute-start | bytes 1572872 | tf_op jit(solution)/shard_map/ppermute | solution.py:49
  151.0 9.8 %collective-permute-start.25 = (bf16[512,512]{1,0:T(8,128)(2,1)S(1)}, bf16[512,512]{1,0:T(8,128)(2,1)S(1)}, u32[]{:S(2)}, u32[]{:S(2)}) collective-permute-start(bf16[512,512]{1,0:T(8,128)(2,1)S(1)} %pad_maximum_fusion.7), channel_id=1, source_target_pairs={{0,4},{1,5},{2,6},{3,7},{4,8},{5,9},{6,10},{7,11},{8,12},{9,13},{1... | collective-permute-start | bytes 1572872 | tf_op jit(solution)/shard_map/ppermute | solution.py:49
  153.8 11.6 %copy-start.1 = (s32[64,4]{0,1:T(4,128)S(1)}, s32[64,4]{0,1:T(4,128)}, u32[]{:S(2)}) copy-start(s32[64,4]{0,1:T(4,128)} %param.14) | copy-start | bytes 3076
  153.8 10.5 %collective-permute-start.29 = (bf16[512,512]{1,0:T(8,128)(2,1)S(1)}, bf16[512,512]{1,0:T(8,128)(2,1)S(1)}, u32[]{:S(2)}, u32[]{:S(2)}) collective-permute-start(bf16[512,512]{1,0:T(8,128)(2,1)S(1)} %pad_maximum_fusion.9), channel_id=1, source_target_pairs={{0,1},{1,2},{2,3},{3,0},{4,5},{5,6},{6,7},{7,4},{8,9},{9,10},{10,1... | collective-permute-start | bytes 1572872 | tf_op jit(solution)/shard_map/ppermute | solution.py:49
  (2 other events, 2.1 us)

commit v4 on v3

--- a/solution.py
+++ b/solution.py
@@ -426,10 +426,7 @@
     s1 = both(tokens, tokens, "first")
     kv = kv_partial(tokens, gains, w_keyvalue, order, (0, 1, 3, 2))
     k_far = both(kv[:HALF, 3 * WIDE :], kv[HALF:, 3 * WIDE :], "first")
-    kv_head = place * (w_query.shape[1] // HD) // (HEADS // KVH)
-    cache_head = lax.dynamic_slice_in_dim(cache, kv_head * HD, HD, 3)
-    z_one = hop(cache_head, "z_one", 1)
-    b1m, b1p, k_m, k_p, kv_near, z_one = bar((*s1, *k_far, kv, z_one))
+    b1m, b1p, k_m, k_p, kv_near, cache = bar((*s1, *k_far, kv, cache))
     (near,) = assemble(
         [tokens, b1p, b1m],
         [((3 * WIDE, WIDE), [rows_piece(n * WIDE, WIDE, (n, 0)) for n in range(3)])],
@@ -459,6 +456,9 @@
         ),
         "first",
     )
+    kv_head = place * (w_query.shape[1] // HD) // (HEADS // KVH)
+    cache_head = lax.dynamic_slice_in_dim(cache, kv_head * HD, HD, 3)
+    z_one = hop(cache_head, "z_one", 1)
     part = query_part(
         [((0, 0), [(0, 0, 0, WIDE)]), ((1, 0), [(1, 0, 0, WIDE)]), ((3, 0), [(2, 0, 0, WIDE)])],
         [tokens, b1p, b1m],
@@ -468,8 +468,7 @@
         None,
     )
     pool = jnp.stack([cache_head, z_one])
-    z_two = hop(pool, "z_two", 1)
-    b3m, b3p, b2m, b2p, pool, z_two, *part = bar((*s3, *s2, pool, z_two, *part))
+    b3m, b3p, b2m, b2p, pool, *part = bar((*s3, *s2, pool, *part))
     (to_next,) = assemble(
         [b3m, b3p, kv_near, b2m],
         [
@@ -497,7 +496,7 @@
         [kv_near, b3m, b3p],
         [((WIDE, WIDE), [(0, 0, WIDE, WIDE, [(0, 0, 0), (1, HALF, 0), (2, HALF, 0)])])],
     )
-    near_twin, far_twin = hop(pool, "core", 1), hop(z_two, "core", 1)
+    z_two, near_twin = hop(pool, "z_two", 1), hop(pool, "core", 1)
     my_lengths = lax.dynamic_slice_in_dim(lengths, group * branch_count, branch_count, 0)
     my_parents = lax.dynamic_slice_in_dim(parents, group * branch_count, branch_count, 0)
     owner = my_parents // 16
@@ -535,11 +534,9 @@
         w_query,
         part,
     )
-    pools = [
-        pltpu.with_memory_space_constraint(a, pltpu.HBM) for a in (pool, z_two, near_twin, far_twin)
-    ]
-    prefix = gather_blocks(pools, codes)
-    b5m, b5p, prefix, cosine, sine, ksum, *part = bar((*s5, prefix, cosine, sine, ksum, *part))
+    b5m, b5p, z_two, near_twin, cosine, sine, ksum, codes, *part = bar(
+        (*s5, z_two, near_twin, cosine, sine, ksum, codes, *part)
+    )
     quarter = HALF // 4
     s7 = both(
         *assemble(
@@ -597,6 +594,11 @@
         ),
         "second",
     )
+    far_twin = hop(z_two, "core", 1)
+    pools = [
+        pltpu.with_memory_space_constraint(a, pltpu.HBM) for a in (pool, z_two, near_twin, far_twin)
+    ]
+    prefix = gather_blocks(pools, codes)
     part = query_part(
         [
             ((2, 1), [(0, 0, 0, WIDE)]),
@@ -611,7 +613,7 @@
         w_query,
         part,
     )
-    b7m, b7p, *part = bar((*s7, *part))
+    b7m, b7p, prefix, *part = bar((*s7, prefix, *part))
     (mine,) = assemble(
         [ksum, b7m, b7p],
         [

time: 166 us -> 163 us (0.982)
  waiting for transfers between devices: 67.9 us -> 53.4 us
  starting transfers between devices: 40.6 us -> 47.5 us
  Pallas kernels: 40.9 us -> 46.2 us
    ppermute x31, waiting for transfers between devices: 67.9 us -> 53.4 us  [hop(): return lax.ppermute(value, AXES, HOPS[axis, step])]
    ppermute x31, starting transfers between devices: 40.6 us -> 47.5 us  [hop(): return lax.ppermute(value, AXES, HOPS[axis, step])]
    pallas_call x7, Pallas kernels: 4.99 us -> 8.98 us  [assemble(): pl.pallas_call(body, out_shape=[pltpu.VMEM(shape, BF16) for shape, _ in o...]
    unnamed x39 -> x35, local copies, waits for them, and re-layouts: 5.76 us -> 6.04 us
  transfers between devices with their start and end apart: 31 -> 31, of which waited for: 18 -> 14; matrix products, arithmetic and copies ran while one was open for 4% -> 4% of each run, Pallas kernels for 18% -> 22%
where the time goes in v4:
time: 163 us
  waiting for transfers between devices  53.4 us (33%)
  starting transfers between devices  47.5 us (29%)
  Pallas kernels  46.2 us (28%)
  local copies, waits for them, and re-layouts  9.51 us (6%)
  other arithmetic  5.46 us (3%)
    ppermute x31, waiting for transfers between devices, hop(): return lax.ppermute(value, AXES, HOPS[axis, step])  53.4 us
    ppermute x31, starting transfers between devices, hop(): return lax.ppermute(value, AXES, HOPS[axis, step])  47.5 us
    pallas_call x4, Pallas kernels, query_part(): pl.pallas_call(body, out_shape=(jax.ShapeDtypeStruct((WIDE, WIDE), F32),...  16.8 us
    pallas_call x7, Pallas kernels, assemble(): pl.pallas_call(body, out_shape=[pltpu.VMEM(shape, BF16) for shape, _ in o...  8.98 us
    pallas_call x2, Pallas kernels, output_part(): pl.pallas_call(body, out_shape=jax.ShapeDtypeStruct((count, WIDE, WIDE),...  8.55 us
    pallas_call x1, Pallas kernels, middle(): pl.pallas_call(body, out_shape=(jax.ShapeDtypeStruct((WIDE, WIDE), BF16),...  6.06 us
    unnamed x35, local copies, waits for them, and re-layouts  6.04 us
    pallas_call x1, Pallas kernels, kv_partial(): pl.pallas_call(body, out_shape=jax.ShapeDtypeStruct((WIDE, count * HD), B...  3.62 us
  transfers between devices with their start and end apart: 31, of which 14 were waited for; matrix products, arithmetic and copies ran while one was open for 4% of the time, Pallas kernels for 22%

profile of v4, /device:TPU:6, one launch (start us, length us, event | category | flops | bytes accessed | tf_op | source)
XLA Modules:
  0.0 162.5 jit_solution(11264702267916508538)
XLA Ops:
  0.0 1.6 collective-permute-start
  1.6 1.7 %collective-permute-start.1 = (bf16[512,512]{1,0:T(8,128)(2,1)}, bf16[512,512]{1,0:T(8,128)(2,1)S(1)}, u32[]{:S(2)}, u32[]{:S(2)}) collective-permute-start(bf16[512,512]{1,0:T(8,128)(2,1)} %refs_0_.3), channel_id=1, source_target_pairs={{0,3},{1,0},{2,1},{3,2},{4,7},{5,4},{6,5},{7,6},{8,11},{9,8},{10,9... | collective-permute-start | bytes 1572872 | tf_op jit(solution)/shard_map/ppermute | solution.py:49
  4.0 1.0 copy-done.6
  5.0 3.6 %kv_partial.1.refs_2_.refs_0_ = bf16[512,2048]{1,0:T(8,128)(2,1)S(1)} custom-call(s32[16]{0:T(128)S(1)} %fusion.29.order_ref, bf16[512,512]{1,0:T(8,128)(2,1)S(1)} %copy-done.6, f32[16,512]{1,0:T(8,128)S(1)} %reshape.77.g_ref.refs_3_.refs_4_.refs_2_, bf16[2,512,1024]{2,1,0:T(8,128)(2,1)} %w_ref.3), custom_call_target="tpu_custom_call" | custom-call | tf_op jit(solution)/shard_map/kv_partial/pallas_call | solution.py:166
  9.1 2.9 %collective-permute-start.3 = (bf16[256,512]{1,0:T(8,128)(2,1)S(1)}, bf16[256,512]{1,0:T(8,128)(2,1)S(1)}, u32[]{:S(2)}, u32[]{:S(2)}) collective-permute-start(bf16[256,512]{1,0:T(8,128)(2,1)S(1)} %get-tuple-element.153), channel_id=1, source_target_pairs={{0,3},{1,0},{2,1},{3,2},{4,7},{5,4},{6,5},{7,6},{8,11},{9,8},{10,9... | collective-permute-start | bytes 786440 | tf_op jit(solution)/shard_map/ppermute | solution.py:49
  12.0 4.3 %collective-permute-done.2.refs_3_ = bf16[256,512]{1,0:T(8,128)(2,1)S(1)} collective-permute-done((bf16[256,512]{1,0:T(8,128)(2,1)S(1)}, bf16[256,512]{1,0:T(8,128)(2,1)S(1)}, u32[]{:S(2)}, u32[]{:S(2)}) %collective-permute-start.2) | collective-permute-done | bytes 262176 | tf_op jit(solution)/shard_map/ppermute | solution.py:49
  17.1 1.4 assemble.8
  18.9 1.6 %collective-permute-start.7 = (bf16[1536,512]{1,0:T(8,128)(2,1)}, bf16[1536,512]{1,0:T(8,128)(2,1)}, u32[]{:S(2)}, u32[]{:S(2)}) collective-permute-start(bf16[1536,512]{1,0:T(8,128)(2,1)} %assemble.8), channel_id=1, source_target_pairs={{0,12},{1,13},{2,14},{3,15},{4,0},{5,1},{6,2},{7,3},{8,4},{9,5},{1... | collective-permute-start | bytes 4718600 | tf_op jit(solution)/shard_map/ppermute | solution.py:49
  22.5 2.6 %collective-permute-start.5 = (bf16[768,512]{1,0:T(8,128)(2,1)S(1)}, bf16[768,512]{1,0:T(8,128)(2,1)S(1)}, u32[]{:S(2)}, u32[]{:S(2)}) collective-permute-start(bf16[768,512]{1,0:T(8,128)(2,1)S(1)} %get-tuple-element.69), channel_id=1, source_target_pairs={{0,3},{1,0},{2,1},{3,2},{4,7},{5,4},{6,5},{7,6},{8,11},{9,8},{10,9... | collective-permute-start | bytes 2359304 | tf_op jit(solution)/shard_map/ppermute | solution.py:49
  25.1 1.1 constant_dynamic-slice_fusion.1
  26.1 2.0 %collective-permute-start.8 = (bf16[2,16,64,128]{3,2,1,0:T(8,128)(2,1)S(1)}, bf16[2,16,64,128]{3,2,1,0:T(8,128)(2,1)S(1)}, u32[]{:S(2)}, u32[]{:S(2)}) collective-permute-start(bf16[2,16,64,128]{3,2,1,0:T(8,128)(2,1)S(1)} %constant_dynamic-slice_fusion.1), channel_id=1, source_target_pairs={{0,32},{1,33},{2,34},{3,35},{4,36},{5,37},{6,38},{7,39},{8,40},{9,... | collective-permute-start | bytes 1572872 | tf_op jit(solution)/shard_map/ppermute | solution.py:49
  28.1 1.0 copy-done.10
  29.2 1.0 copy-done.12
  30.2 3.0 %query_part.4 = (f32[512,512]{1,0:T(8,128)S(1)}, f32[512,128]{1,0:T(8,128)S(1)}) custom-call(s32[16]{0:T(128)S(1)} %fusion.29.order_ref, bf16[512,512]{1,0:T(8,128)(2,1)S(1)} %copy-done.8, bf16[512,512]{1,0:T(8,128)(2,1)S(1)} %copy-done.12, bf16[512,512]{1,0:T(8,128)(2,1)S(1)} %copy-done.10, f32[16,512]{1,0:T(8,128)S(1)} %reshape.77.g_ref.refs_3_.refs_4_.refs_2_, ...), custom_call_target="tpu_custom_call" | custom-call | tf_op jit(solution)/shard_map/query_part/pallas_call | solution.py:236
  33.2 1.1 fusion.37
  34.3 1.1 collective-permute-done.8
  35.4 1.1 pad_maximum_fusion.refs_0_
  36.5 7.0 %collective-permute-done.4.refs_0_.refs_1_ = bf16[768,512]{1,0:T(8,128)(2,1)S(1)} collective-permute-done((bf16[768,512]{1,0:T(8,128)(2,1)S(1)}, bf16[768,512]{1,0:T(8,128)(2,1)S(1)}, u32[]{:S(2)}, u32[]{:S(2)}) %collective-permute-start.4) | collective-permute-done | bytes 786464 | tf_op jit(solution)/shard_map/ppermute | solution.py:49
  43.5 4.2 %collective-permute-done.6.refs_3_ = bf16[1536,512]{1,0:T(8,128)(2,1)} collective-permute-done((bf16[1536,512]{1,0:T(8,128)(2,1)}, bf16[1536,512]{1,0:T(8,128)(2,1)}, u32[]{:S(2)}, u32[]{:S(2)}) %collective-permute-start.6) | collective-permute-done | bytes 1572896 | tf_op jit(solution)/shard_map/ppermute | solution.py:49
  47.7 1.6 collective-permute-done.7.refs_3_.refs_2_
  49.3 2.6 %assemble.10 = bf16[1344,512]{1,0:T(8,128)(2,1)} custom-call(bf16[768,512]{1,0:T(8,128)(2,1)S(1)} %collective-permute-done.4.refs_0_.refs_1_, bf16[768,512]{1,0:T(8,128)(2,1)S(1)} %collective-permute-done.5.refs_1_.refs_2_, bf16[512,2048]{1,0:T(8,128)(2,1)S(1)} %kv_partial.1.refs_2_.refs_0_, bf16[1536,512]{1,0:T(8,128)(2,1)} %collective-permute-done.7.refs_3_.refs_2_), custom_call_target="tpu_custom_call" | custom-call | tf_op jit(solution)/shard_map/assemble/pallas_call | solution.py:115
  52.3 2.7 %assemble.9 = bf16[1344,512]{1,0:T(8,128)(2,1)} custom-call(bf16[768,512]{1,0:T(8,128)(2,1)S(1)} %collective-permute-done.4.refs_0_.refs_1_, bf16[768,512]{1,0:T(8,128)(2,1)S(1)} %collective-permute-done.5.refs_1_.refs_2_, bf16[512,2048]{1,0:T(8,128)(2,1)S(1)} %kv_partial.1.refs_2_.refs_0_, bf16[1536,512]{1,0:T(8,128)(2,1)} %collective-permute-done.6.refs_3_), custom_call_target="tpu_custom_call" | custom-call | tf_op jit(solution)/shard_map/assemble/pallas_call | solution.py:115
  55.0 2.8 %collective-permute-start.9 = (bf16[1344,512]{1,0:T(8,128)(2,1)}, bf16[1344,512]{1,0:T(8,128)(2,1)}, u32[]{:S(2)}, u32[]{:S(2)}) collective-permute-start(bf16[1344,512]{1,0:T(8,128)(2,1)} %assemble.9), channel_id=1, source_target_pairs={{0,4},{1,5},{2,6},{3,7},{4,8},{5,9},{6,10},{7,11},{8,12},{9,13},{1... | collective-permute-start | bytes 4128776 | tf_op jit(solution)/shard_map/ppermute | solution.py:49
  57.9 4.1 %collective-permute-start.11 = (bf16[2,2,16,64,128]{4,3,2,1,0:T(8,128)(2,1)}, bf16[2,2,16,64,128]{4,3,2,1,0:T(8,128)(2,1)}, u32[]{:S(2)}, u32[]{:S(2)}) collective-permute-start(bf16[2,2,16,64,128]{4,3,2,1,0:T(8,128)(2,1)} %pad_maximum_fusion.refs_0_), channel_id=1, source_target_pairs={{0,96},{1,97},{2,98},{3,99},{4,100},{5,101},{6,102},{7,103},{8,104... | collective-permute-start | bytes 3145736 | tf_op jit(solution)/shard_map/ppermute | solution.py:49
  63.9 6.5 %query_part.5 = (f32[512,512]{1,0:T(8,128)S(1)}, f32[512,128]{1,0:T(8,128)S(1)}) custom-call(s32[16]{0:T(128)S(1)} %fusion.29.order_ref, bf16[768,512]{1,0:T(8,128)(2,1)S(1)} %copy-done.3, bf16[768,512]{1,0:T(8,128)(2,1)S(1)} %copy-done.5, bf16[1536,512]{1,0:T(8,128)(2,1)} %collective-permute-done.7.refs_3_.refs_2_, ...), custom_call_target="tpu_custom_call", output_to_operand_aliasing={{0}: (7, {}), {1}: (8, {})} | custom-call | tf_op jit(solution)/shard_map/query_part/pallas_call | solution.py:236
  70.4 4.7 %collective-permute-done.11.refs_1_ = bf16[2,2,16,64,128]{4,3,2,1,0:T(8,128)(2,1)} collective-permute-done((bf16[2,2,16,64,128]{4,3,2,1,0:T(8,128)(2,1)}, bf16[2,2,16,64,128]{4,3,2,1,0:T(8,128)(2,1)}, u32[]{:S(2)}, u32[]{:S(2)}) %collective-permute-start.11) | collective-permute-done | bytes 1048608 | tf_op jit(solution)/shard_map/ppermute | solution.py:49
  75.2 1.8 %assemble.12 = (bf16[384,512]{1,0:T(8,128)(2,1)S(1)}, bf16[384,512]{1,0:T(8,128)(2,1)S(1)}) custom-call(bf16[1344,512]{1,0:T(8,128)(2,1)} %collective-permute-done.9.refs_0_.refs_1_, bf16[1344,512]{1,0:T(8,128)(2,1)} %collective-permute-done.10.refs_1_.refs_0_, bf16[512,512]{1,0:T(8,128)(2,1)S(1)} %assemble.11.refs_2_.refs_0_), custom_call_target="tpu_custom_call" | custom-call | tf_op jit(solution)/shard_map/assemble/pallas_call | solution.py:115
  77.0 2.6 %collective-permute-start.13 = (bf16[384,512]{1,0:T(8,128)(2,1)S(1)}, bf16[384,512]{1,0:T(8,128)(2,1)S(1)}, u32[]{:S(2)}, u32[]{:S(2)}) collective-permute-start(bf16[384,512]{1,0:T(8,128)(2,1)S(1)} %get-tuple-element.85), channel_id=1, source_target_pairs={{0,4},{1,5},{2,6},{3,7},{4,8},{5,9},{6,10},{7,11},{8,12},{9,13},{1... | collective-permute-start | bytes 1179656 | tf_op jit(solution)/shard_map/ppermute | solution.py:49
  79.6 5.3 %query_part.6 = (f32[512,512]{1,0:T(8,128)S(1)}, f32[512,128]{1,0:T(8,128)S(1)}) custom-call(s32[16]{0:T(128)S(1)} %fusion.29.order_ref, bf16[1344,512]{1,0:T(8,128)(2,1)} %collective-permute-done.10.refs_1_.refs_0_, bf16[1344,512]{1,0:T(8,128)(2,1)} %collective-permute-done.9.refs_0_.refs_1_, ...), custom_call_target="tpu_custom_call", output_to_operand_aliasing={{0}: (5, {}), {1}: (6, {})} | custom-call | tf_op jit(solution)/shard_map/query_part/pallas_call | solution.py:236
  86.0 2.2 %gather_blocks.1.prefix_ref = bf16[8,2,320,128]{3,2,1,0:T(8,128)(2,1)S(1)} custom-call(s32[8,4]{1,0:T(8,128)S(1)} %fusion.25.code_ref, bf16[2,2,16,64,128]{4,3,2,1,0:T(8,128)(2,1)} %pad_maximum_fusion.refs_0_, bf16[2,2,16,64,128]{4,3,2,1,0:T(8,128)(2,1)} %collective-permute-done.11.refs_1_, bf16[2,2,16,64,128]{4,3,2,1,0:T(8,128)(2,1)} %collective-permute-done.12.refs_2_, ...), custom_call_target="tpu_custom_call" | custom-call | tf_op jit(solution)/shard_map/gather_blocks/pallas_call | solution.py:280
  89.5 2.0 %query_part.7 = (f32[512,512]{1,0:T(8,128)S(1)}, f32[512,128]{1,0:T(8,128)S(1)}) custom-call(s32[16]{0:T(128)S(1)} %fusion.29.order_ref, bf16[384,512]{1,0:T(8,128)(2,1)S(1)} %collective-permute-done.13.refs_0_.refs_1_, bf16[384,512]{1,0:T(8,128)(2,1)S(1)} %collective-permute-done.14.refs_1_.refs_2_, ...), custom_call_target="tpu_custom_call", output_to_operand_aliasing={{0}: (5, {}), {1}: (6, {})} | custom-call | tf_op jit(solution)/shard_map/query_part/pallas_call | solution.py:236
  91.6 2.8 %collective-permute-done.16.other_ref = bf16[512,128]{1,0:T(8,128)(2,1)S(1)} collective-permute-done((bf16[512,128]{1,0:T(8,128)(2,1)S(1)}, bf16[512,128]{1,0:T(8,128)(2,1)S(1)}, u32[]{:S(2)}, u32[]{:S(2)}) %collective-permute-start.16) | collective-permute-done | bytes 131104 | tf_op jit(solution)/shard_map/ppermute | solution.py:49
  94.4 6.1 %middle.1 = (bf16[512,512]{1,0:T(8,128)(2,1)S(1)}, bf16[4,512,512]{2,1,0:T(8,128)(2,1)S(1)}, bf16[8,2,320,128]{3,2,1,0:T(8,128)(2,1)S(1)}) custom-call(s32[16]{0:T(128)S(1)} %fusion.29.order_ref, s32[8]{0:T(128)S(1)} %get-tuple-element.122.len_ref, f32[512,512]{1,0:T(8,128)S(1)} %get-tuple-element.98.q_ref, ...), custom_call_target="tpu_custom_call", output_to_operand_aliasing={{2}: (8, {})} | custom-call | tf_op jit(solution)/shard_map/middle/pallas_call | solution.py:353
  100.8 3.3 %collective-permute-start.21 = (bf16[768,512]{1,0:T(8,128)(2,1)S(1)}, bf16[768,512]{1,0:T(8,128)(2,1)S(1)}, u32[]{:S(2)}, u32[]{:S(2)}) collective-permute-start(bf16[768,512]{1,0:T(8,128)(2,1)S(1)} %pad_maximum_fusion.3), channel_id=1, source_target_pairs={{0,4},{1,5},{2,6},{3,7},{4,8},{5,9},{6,10},{7,11},{8,12},{9,13},{1... | collective-permute-start | bytes 2359304 | tf_op jit(solution)/shard_map/ppermute | solution.py:49
  104.1 1.4 collective-permute-start.17
  106.2 4.3 %output_part.2 = bf16[6,512,512]{2,1,0:T(8,128)(2,1)S(1)} custom-call(s32[16]{0:T(128)S(1)} %fusion.29.order_ref, bf16[512,512]{1,0:T(8,128)(2,1)S(1)} %get-tuple-element.109.h_ref, bf16[512,8192]{1,0:T(8,128)(2,1)} %w_ref.5), custom_call_target="tpu_custom_call" | custom-call | tf_op jit(solution)/shard_map/output_part/pallas_call | solution.py:392
  110.4 6.0 %collective-permute-done.17 = bf16[256,512]{1,0:T(8,128)(2,1)S(1)} collective-permute-done((bf16[256,512]{1,0:T(8,128)(2,1)S(1)}, bf16[256,512]{1,0:T(8,128)(2,1)S(1)}, u32[]{:S(2)}, u32[]{:S(2)}) %collective-permute-start.17) | collective-permute-done | bytes 262176 | tf_op jit(solution)/shard_map/ppermute | solution.py:49
  118.5 2.5 %collective-permute-start.19 = (bf16[512,512]{1,0:T(8,128)(2,1)S(1)}, bf16[512,512]{1,0:T(8,128)(2,1)S(1)}, u32[]{:S(2)}, u32[]{:S(2)}) collective-permute-start(bf16[512,512]{1,0:T(8,128)(2,1)S(1)} %pad_maximum_fusion.5), channel_id=1, source_target_pairs={{0,4},{1,5},{2,6},{3,7},{4,8},{5,9},{6,10},{7,11},{8,12},{9,13},{1... | collective-permute-start | bytes 1572872 | tf_op jit(solution)/shard_map/ppermute | solution.py:49
  121.3 3.5 %collective-permute-start.27 = (bf16[1024,512]{1,0:T(8,128)(2,1)S(1)}, bf16[1024,512]{1,0:T(8,128)(2,1)S(1)}, u32[]{:S(2)}, u32[]{:S(2)}) collective-permute-start(bf16[1024,512]{1,0:T(8,128)(2,1)S(1)} %pad_maximum_fusion.1), channel_id=1, source_target_pairs={{0,4},{1,5},{2,6},{3,7},{4,8},{5,9},{6,10},{7,11},{8,12},{9,13},{1... | collective-permute-start | bytes 3145736 | tf_op jit(solution)/shard_map/ppermute | solution.py:49
  124.8 4.3 %output_part.3 = bf16[6,512,512]{2,1,0:T(8,128)(2,1)S(1)} custom-call(s32[16]{0:T(128)S(1)} %fusion.29.order_ref, bf16[512,512]{1,0:T(8,128)(2,1)S(1)} %get-tuple-element.109.h_ref, bf16[512,8192]{1,0:T(8,128)(2,1)} %w_ref.5), custom_call_target="tpu_custom_call" | custom-call | tf_op jit(solution)/shard_map/output_part/pallas_call | solution.py:392
  129.7 3.0 %collective-permute-start.24 = (bf16[256,512]{1,0:T(8,128)(2,1)S(1)}, bf16[256,512]{1,0:T(8,128)(2,1)S(1)}, u32[]{:S(2)}, u32[]{:S(2)}) collective-permute-start(bf16[256,512]{1,0:T(8,128)(2,1)S(1)} %get-tuple-element.155), channel_id=1, source_target_pairs={{0,3},{1,0},{2,1},{3,2},{4,7},{5,4},{6,5},{7,6},{8,11},{9,8},{10,9... | collective-permute-start | bytes 786440 | tf_op jit(solution)/shard_map/ppermute | solution.py:49
  132.7 7.2 %collective-permute-done.23 = bf16[256,512]{1,0:T(8,128)(2,1)S(1)} collective-permute-done((bf16[256,512]{1,0:T(8,128)(2,1)S(1)}, bf16[256,512]{1,0:T(8,128)(2,1)S(1)}, u32[]{:S(2)}, u32[]{:S(2)}) %collective-permute-start.23) | collective-permute-done | bytes 262176 | tf_op jit(solution)/shard_map/ppermute | solution.py:49
  139.9 2.3 %collective-permute-done.28 = bf16[1024,512]{1,0:T(8,128)(2,1)S(1)} collective-permute-done((bf16[1024,512]{1,0:T(8,128)(2,1)S(1)}, bf16[1024,512]{1,0:T(8,128)(2,1)S(1)}, u32[]{:S(2)}, u32[]{:S(2)}) %collective-permute-start.28) | collective-permute-done | bytes 1048608 | tf_op jit(solution)/shard_map/ppermute | solution.py:49
  142.9 3.4 %collective-permute-start.25 = (bf16[512,512]{1,0:T(8,128)(2,1)S(1)}, bf16[512,512]{1,0:T(8,128)(2,1)S(1)}, u32[]{:S(2)}, u32[]{:S(2)}) collective-permute-start(bf16[512,512]{1,0:T(8,128)(2,1)S(1)} %pad_maximum_fusion.7), channel_id=1, source_target_pairs={{0,4},{1,5},{2,6},{3,7},{4,8},{5,9},{6,10},{7,11},{8,12},{9,13},{1... | collective-permute-start | bytes 1572872 | tf_op jit(solution)/shard_map/ppermute | solution.py:49
  146.9 3.0 %collective-permute-start.30 = (bf16[512,512]{1,0:T(8,128)(2,1)S(1)}, bf16[512,512]{1,0:T(8,128)(2,1)S(1)}, u32[]{:S(2)}, u32[]{:S(2)}) collective-permute-start(bf16[512,512]{1,0:T(8,128)(2,1)S(1)} %pad_maximum_fusion.10), channel_id=1, source_target_pairs={{0,3},{1,0},{2,1},{3,2},{4,7},{5,4},{6,5},{7,6},{8,11},{9,8},{10,9... | collective-permute-start | bytes 1572872 | tf_op jit(solution)/shard_map/ppermute | solution.py:49
  149.9 7.9 %collective-permute-done.25 = bf16[512,512]{1,0:T(8,128)(2,1)S(1)} collective-permute-done((bf16[512,512]{1,0:T(8,128)(2,1)S(1)}, bf16[512,512]{1,0:T(8,128)(2,1)S(1)}, u32[]{:S(2)}, u32[]{:S(2)}) %collective-permute-start.25) | collective-permute-done | bytes 524320 | tf_op jit(solution)/shard_map/ppermute | solution.py:49
  157.9 3.5 %collective-permute-done.26 = bf16[512,512]{1,0:T(8,128)(2,1)S(1)} collective-permute-done((bf16[512,512]{1,0:T(8,128)(2,1)S(1)}, bf16[512,512]{1,0:T(8,128)(2,1)S(1)}, u32[]{:S(2)}, u32[]{:S(2)}) %collective-permute-start.26) | collective-permute-done | bytes 524320 | tf_op jit(solution)/shard_map/ppermute | solution.py:49
  161.4 1.1 fusion.5
  (97 shorter events, 14.2 us)
Async XLA Ops:
  0.0 62.0 %copy-start = (s32[64,4]{0,1:T(4,128)S(1)}, s32[64,4]{0,1:T(4,128)}, u32[]{:S(2)}) copy-start(s32[64,4]{0,1:T(4,128)} %param.14) | copy-start | bytes 3076
  0.0 17.1 %collective-permute-start = (bf16[512,512]{1,0:T(8,128)(2,1)}, bf16[512,512]{1,0:T(8,128)(2,1)S(1)}, u32[]{:S(2)}, u32[]{:S(2)}) collective-permute-start(bf16[512,512]{1,0:T(8,128)(2,1)} %refs_0_.3), channel_id=1, source_target_pairs={{0,1},{1,2},{2,3},{3,0},{4,5},{5,6},{6,7},{7,4},{8,9},{9,10},{10,1... | collective-permute-start | bytes 1572872 | tf_op jit(solution)/shard_map/ppermute | solution.py:49
  1.6 15.5 %collective-permute-start.1 = (bf16[512,512]{1,0:T(8,128)(2,1)}, bf16[512,512]{1,0:T(8,128)(2,1)S(1)}, u32[]{:S(2)}, u32[]{:S(2)}) collective-permute-start(bf16[512,512]{1,0:T(8,128)(2,1)} %refs_0_.3), channel_id=1, source_target_pairs={{0,3},{1,0},{2,1},{3,2},{4,7},{5,4},{6,5},{7,6},{8,11},{9,8},{10,9... | collective-permute-start | bytes 1572872 | tf_op jit(solution)/shard_map/ppermute | solution.py:49
  4.0 1.0 copy-start.6
  5.0 12.1 %copy-start.7 = (bf16[512,512]{1,0:T(8,128)(2,1)S(1)}, bf16[512,512]{1,0:T(8,128)(2,1)}, u32[]{:S(2)}) copy-start(bf16[512,512]{1,0:T(8,128)(2,1)} %refs_0_.3) | copy-start | bytes 1572868
  8.7 7.7 %collective-permute-start.2 = (bf16[256,512]{1,0:T(8,128)(2,1)S(1)}, bf16[256,512]{1,0:T(8,128)(2,1)S(1)}, u32[]{:S(2)}, u32[]{:S(2)}) collective-permute-start(bf16[256,512]{1,0:T(8,128)(2,1)S(1)} %get-tuple-element.154), channel_id=1, source_target_pairs={{0,1},{1,2},{2,3},{3,0},{4,5},{5,6},{6,7},{7,4},{8,9},{9,10},{10,1... | collective-permute-start | bytes 786440 | tf_op jit(solution)/shard_map/ppermute | solution.py:49
  9.1 7.2 %collective-permute-start.3 = (bf16[256,512]{1,0:T(8,128)(2,1)S(1)}, bf16[256,512]{1,0:T(8,128)(2,1)S(1)}, u32[]{:S(2)}, u32[]{:S(2)}) collective-permute-start(bf16[256,512]{1,0:T(8,128)(2,1)S(1)} %get-tuple-element.153), channel_id=1, source_target_pairs={{0,3},{1,0},{2,1},{3,2},{4,7},{5,4},{6,5},{7,6},{8,11},{9,8},{10,9... | collective-permute-start | bytes 786440 | tf_op jit(solution)/shard_map/ppermute | solution.py:49
  16.4 0.7 copy-start.13
  17.1 4.6 %copy-start.9 = (bf16[512,512]{1,0:T(8,128)(2,1)}, bf16[512,512]{1,0:T(8,128)(2,1)S(1)}, u32[]{:S(2)}) copy-start(bf16[512,512]{1,0:T(8,128)(2,1)S(1)} %collective-permute-done.refs_0_.refs_2_) | copy-start | bytes 1572868
  17.1 4.6 %copy-start.11 = (bf16[512,512]{1,0:T(8,128)(2,1)}, bf16[512,512]{1,0:T(8,128)(2,1)S(1)}, u32[]{:S(2)}) copy-start(bf16[512,512]{1,0:T(8,128)(2,1)S(1)} %collective-permute-done.1.refs_1_) | copy-start | bytes 1572868
  18.5 29.2 %collective-permute-start.6 = (bf16[1536,512]{1,0:T(8,128)(2,1)}, bf16[1536,512]{1,0:T(8,128)(2,1)}, u32[]{:S(2)}, u32[]{:S(2)}) collective-permute-start(bf16[1536,512]{1,0:T(8,128)(2,1)} %assemble.8), channel_id=1, source_target_pairs={{0,4},{1,5},{2,6},{3,7},{4,8},{5,9},{6,10},{7,11},{8,12},{9,13},{1... | collective-permute-start | bytes 4718600 | tf_op jit(solution)/shard_map/ppermute | solution.py:49
  18.9 30.4 %collective-permute-start.7 = (bf16[1536,512]{1,0:T(8,128)(2,1)}, bf16[1536,512]{1,0:T(8,128)(2,1)}, u32[]{:S(2)}, u32[]{:S(2)}) collective-permute-start(bf16[1536,512]{1,0:T(8,128)(2,1)} %assemble.8), channel_id=1, source_target_pairs={{0,12},{1,13},{2,14},{3,15},{4,0},{5,1},{6,2},{7,3},{8,4},{9,5},{1... | collective-permute-start | bytes 4718600 | tf_op jit(solution)/shard_map/ppermute | solution.py:49
  20.5 0.9 copy-start.14
  21.5 6.7 %copy-start.8 = (bf16[512,512]{1,0:T(8,128)(2,1)S(1)}, bf16[512,512]{1,0:T(8,128)(2,1)}, u32[]{:S(2)}) copy-start(bf16[512,512]{1,0:T(8,128)(2,1)} %refs_0_.3) | copy-start | bytes 1572868
  21.7 21.8 %collective-permute-start.4 = (bf16[768,512]{1,0:T(8,128)(2,1)S(1)}, bf16[768,512]{1,0:T(8,128)(2,1)S(1)}, u32[]{:S(2)}, u32[]{:S(2)}) collective-permute-start(bf16[768,512]{1,0:T(8,128)(2,1)S(1)} %get-tuple-element.68), channel_id=1, source_target_pairs={{0,1},{1,2},{2,3},{3,0},{4,5},{5,6},{6,7},{7,4},{8,9},{9,10},{10,1... | collective-permute-start | bytes 2359304 | tf_op jit(solution)/shard_map/ppermute | solution.py:49
  22.5 21.0 %collective-permute-start.5 = (bf16[768,512]{1,0:T(8,128)(2,1)S(1)}, bf16[768,512]{1,0:T(8,128)(2,1)S(1)}, u32[]{:S(2)}, u32[]{:S(2)}) collective-permute-start(bf16[768,512]{1,0:T(8,128)(2,1)S(1)} %get-tuple-element.69), channel_id=1, source_target_pairs={{0,3},{1,0},{2,1},{3,2},{4,7},{5,4},{6,5},{7,6},{8,11},{9,8},{10,9... | collective-permute-start | bytes 2359304 | tf_op jit(solution)/shard_map/ppermute | solution.py:49
  26.1 9.3 %collective-permute-start.8 = (bf16[2,16,64,128]{3,2,1,0:T(8,128)(2,1)S(1)}, bf16[2,16,64,128]{3,2,1,0:T(8,128)(2,1)S(1)}, u32[]{:S(2)}, u32[]{:S(2)}) collective-permute-start(bf16[2,16,64,128]{3,2,1,0:T(8,128)(2,1)S(1)} %constant_dynamic-slice_fusion.1), channel_id=1, source_target_pairs={{0,32},{1,33},{2,34},{3,35},{4,36},{5,37},{6,38},{7,39},{8,40},{9,... | collective-permute-start | bytes 1572872 | tf_op jit(solution)/shard_map/ppermute | solution.py:49
  28.1 1.0 copy-start.10
  29.2 1.0 copy-start.12
  43.4 8.9 %copy-start.2 = (bf16[768,512]{1,0:T(8,128)(2,1)}, bf16[768,512]{1,0:T(8,128)(2,1)S(1)}, u32[]{:S(2)}) copy-start(bf16[768,512]{1,0:T(8,128)(2,1)S(1)} %collective-permute-done.4.refs_0_.refs_1_) | copy-start | bytes 2359300
  43.5 8.9 %copy-start.4 = (bf16[768,512]{1,0:T(8,128)(2,1)}, bf16[768,512]{1,0:T(8,128)(2,1)S(1)}, u32[]{:S(2)}) copy-start(bf16[768,512]{1,0:T(8,128)(2,1)S(1)} %collective-permute-done.5.refs_1_.refs_2_) | copy-start | bytes 2359300
  51.9 10.2 %copy-start.16 = (s32[64]{0:T(128)S(1)}, s32[64]{0:T(128)}, u32[]{:S(2)}) copy-start(s32[64]{0:T(128)} %param.15) | copy-start | bytes 772
  51.9 23.2 %collective-permute-start.10 = (bf16[1344,512]{1,0:T(8,128)(2,1)}, bf16[1344,512]{1,0:T(8,128)(2,1)}, u32[]{:S(2)}, u32[]{:S(2)}) collective-permute-start(bf16[1344,512]{1,0:T(8,128)(2,1)} %assemble.10), channel_id=1, source_target_pairs={{0,12},{1,13},{2,14},{3,15},{4,0},{5,1},{6,2},{7,3},{8,4},{9,5},{1... | collective-permute-start | bytes 4128776 | tf_op jit(solution)/shard_map/ppermute | solution.py:49
  55.0 20.0 %collective-permute-start.9 = (bf16[1344,512]{1,0:T(8,128)(2,1)}, bf16[1344,512]{1,0:T(8,128)(2,1)}, u32[]{:S(2)}, u32[]{:S(2)}) collective-permute-start(bf16[1344,512]{1,0:T(8,128)(2,1)} %assemble.9), channel_id=1, source_target_pairs={{0,4},{1,5},{2,6},{3,7},{4,8},{5,9},{6,10},{7,11},{8,12},{9,13},{1... | collective-permute-start | bytes 4128776 | tf_op jit(solution)/shard_map/ppermute | solution.py:49
  57.9 17.2 %collective-permute-start.11 = (bf16[2,2,16,64,128]{4,3,2,1,0:T(8,128)(2,1)}, bf16[2,2,16,64,128]{4,3,2,1,0:T(8,128)(2,1)}, u32[]{:S(2)}, u32[]{:S(2)}) collective-permute-start(bf16[2,2,16,64,128]{4,3,2,1,0:T(8,128)(2,1)} %pad_maximum_fusion.refs_0_), channel_id=1, source_target_pairs={{0,96},{1,97},{2,98},{3,99},{4,100},{5,101},{6,102},{7,103},{8,104... | collective-permute-start | bytes 3145736 | tf_op jit(solution)/shard_map/ppermute | solution.py:49
  62.0 13.1 %collective-permute-start.12 = (bf16[2,2,16,64,128]{4,3,2,1,0:T(8,128)(2,1)}, bf16[2,2,16,64,128]{4,3,2,1,0:T(8,128)(2,1)}, u32[]{:S(2)}, u32[]{:S(2)}) collective-permute-start(bf16[2,2,16,64,128]{4,3,2,1,0:T(8,128)(2,1)} %pad_maximum_fusion.refs_0_), channel_id=1, source_target_pairs={{0,16},{1,17},{2,18},{3,19},{4,20},{5,21},{6,22},{7,23},{8,24},{9,... | collective-permute-start | bytes 3145736 | tf_op jit(solution)/shard_map/ppermute | solution.py:49
  62.4 1.3 copy-start.3
  62.4 1.4 copy-start.5
  75.1 9.9 %collective-permute-start.15 = (bf16[2,2,16,64,128]{4,3,2,1,0:T(8,128)(2,1)}, bf16[2,2,16,64,128]{4,3,2,1,0:T(8,128)(2,1)S(1)}, u32[]{:S(2)}, u32[]{:S(2)}) collective-permute-start(bf16[2,2,16,64,128]{4,3,2,1,0:T(8,128)(2,1)} %collective-permute-done.11.refs_1_), channel_id=1, source_target_pairs={{0,16},{1,17},{2,18},{3,19},{4,20},{5,21},{6,22},{7,23},{8,24},{9,... | collective-permute-start | bytes 3145736 | tf_op jit(solution)/shard_map/ppermute | solution.py:49
  77.0 11.2 %collective-permute-start.13 = (bf16[384,512]{1,0:T(8,128)(2,1)S(1)}, bf16[384,512]{1,0:T(8,128)(2,1)S(1)}, u32[]{:S(2)}, u32[]{:S(2)}) collective-permute-start(bf16[384,512]{1,0:T(8,128)(2,1)S(1)} %get-tuple-element.85), channel_id=1, source_target_pairs={{0,4},{1,5},{2,6},{3,7},{4,8},{5,9},{6,10},{7,11},{8,12},{9,13},{1... | collective-permute-start | bytes 1179656 | tf_op jit(solution)/shard_map/ppermute | solution.py:49
  79.6 9.0 %collective-permute-start.14 = (bf16[384,512]{1,0:T(8,128)(2,1)S(1)}, bf16[384,512]{1,0:T(8,128)(2,1)S(1)}, u32[]{:S(2)}, u32[]{:S(2)}) collective-permute-start(bf16[384,512]{1,0:T(8,128)(2,1)S(1)} %get-tuple-element.86), channel_id=1, source_target_pairs={{0,12},{1,13},{2,14},{3,15},{4,0},{5,1},{6,2},{7,3},{8,4},{9,5},{1... | collective-permute-start | bytes 1179656 | tf_op jit(solution)/shard_map/ppermute | solution.py:49
  85.0 1.0 copy-start.15
  88.6 5.8 %collective-permute-start.16 = (bf16[512,128]{1,0:T(8,128)(2,1)S(1)}, bf16[512,128]{1,0:T(8,128)(2,1)S(1)}, u32[]{:S(2)}, u32[]{:S(2)}) collective-permute-start(bf16[512,128]{1,0:T(8,128)(2,1)S(1)} %assemble.13.mine_ref), channel_id=1, source_target_pairs={{0,1},{1,0},{2,3},{3,2},{4,5},{5,4},{6,7},{7,6},{8,9},{9,8},{10,11... | collective-permute-start | bytes 393224 | tf_op jit(solution)/shard_map/ppermute | solution.py:49
  100.7 16.3 %collective-permute-start.22 = (bf16[768,512]{1,0:T(8,128)(2,1)S(1)}, bf16[768,512]{1,0:T(8,128)(2,1)S(1)}, u32[]{:S(2)}, u32[]{:S(2)}) collective-permute-start(bf16[768,512]{1,0:T(8,128)(2,1)S(1)} %pad_maximum_fusion.4), channel_id=1, source_target_pairs={{0,12},{1,13},{2,14},{3,15},{4,0},{5,1},{6,2},{7,3},{8,4},{9,5},{1... | collective-permute-start | bytes 2359304 | tf_op jit(solution)/shard_map/ppermute | solution.py:49
  100.8 16.1 %collective-permute-start.21 = (bf16[768,512]{1,0:T(8,128)(2,1)S(1)}, bf16[768,512]{1,0:T(8,128)(2,1)S(1)}, u32[]{:S(2)}, u32[]{:S(2)}) collective-permute-start(bf16[768,512]{1,0:T(8,128)(2,1)S(1)} %pad_maximum_fusion.3), channel_id=1, source_target_pairs={{0,4},{1,5},{2,6},{3,7},{4,8},{5,9},{6,10},{7,11},{8,12},{9,13},{1... | collective-permute-start | bytes 2359304 | tf_op jit(solution)/shard_map/ppermute | solution.py:49
  104.1 12.3 %collective-permute-start.17 = (bf16[256,512]{1,0:T(8,128)(2,1)S(1)}, bf16[256,512]{1,0:T(8,128)(2,1)S(1)}, u32[]{:S(2)}, u32[]{:S(2)}) collective-permute-start(bf16[256,512]{1,0:T(8,128)(2,1)S(1)} %get-tuple-element.152), channel_id=1, source_target_pairs={{0,4},{1,5},{2,6},{3,7},{4,8},{5,9},{6,10},{7,11},{8,12},{9,13},{1... | collective-permute-start | bytes 786440 | tf_op jit(solution)/shard_map/ppermute | solution.py:49
  105.5 11.3 %collective-permute-start.18 = (bf16[256,512]{1,0:T(8,128)(2,1)S(1)}, bf16[256,512]{1,0:T(8,128)(2,1)S(1)}, u32[]{:S(2)}, u32[]{:S(2)}) collective-permute-start(bf16[256,512]{1,0:T(8,128)(2,1)S(1)} %get-tuple-element.151), channel_id=1, source_target_pairs={{0,12},{1,13},{2,14},{3,15},{4,0},{5,1},{6,2},{7,3},{8,4},{9,5},{1... | collective-permute-start | bytes 786440 | tf_op jit(solution)/shard_map/ppermute | solution.py:49
  117.5 11.6 %collective-permute-start.20 = (bf16[512,512]{1,0:T(8,128)(2,1)S(1)}, bf16[512,512]{1,0:T(8,128)(2,1)S(1)}, u32[]{:S(2)}, u32[]{:S(2)}) collective-permute-start(bf16[512,512]{1,0:T(8,128)(2,1)S(1)} %pad_maximum_fusion.6), channel_id=1, source_target_pairs={{0,12},{1,13},{2,14},{3,15},{4,0},{5,1},{6,2},{7,3},{8,4},{9,5},{1... | collective-permute-start | bytes 1572872 | tf_op jit(solution)/shard_map/ppermute | solution.py:49
  118.5 10.6 %collective-permute-start.19 = (bf16[512,512]{1,0:T(8,128)(2,1)S(1)}, bf16[512,512]{1,0:T(8,128)(2,1)S(1)}, u32[]{:S(2)}, u32[]{:S(2)}) collective-permute-start(bf16[512,512]{1,0:T(8,128)(2,1)S(1)} %pad_maximum_fusion.5), channel_id=1, source_target_pairs={{0,4},{1,5},{2,6},{3,7},{4,8},{5,9},{6,10},{7,11},{8,12},{9,13},{1... | collective-permute-start | bytes 1572872 | tf_op jit(solution)/shard_map/ppermute | solution.py:49
  121.1 21.0 %collective-permute-start.28 = (bf16[1024,512]{1,0:T(8,128)(2,1)S(1)}, bf16[1024,512]{1,0:T(8,128)(2,1)S(1)}, u32[]{:S(2)}, u32[]{:S(2)}) collective-permute-start(bf16[1024,512]{1,0:T(8,128)(2,1)S(1)} %pad_maximum_fusion.2), channel_id=1, source_target_pairs={{0,12},{1,13},{2,14},{3,15},{4,0},{5,1},{6,2},{7,3},{8,4},{9,5},{1... | collective-permute-start | bytes 3145736 | tf_op jit(solution)/shard_map/ppermute | solution.py:49
  121.3 20.8 %collective-permute-start.27 = (bf16[1024,512]{1,0:T(8,128)(2,1)S(1)}, bf16[1024,512]{1,0:T(8,128)(2,1)S(1)}, u32[]{:S(2)}, u32[]{:S(2)}) collective-permute-start(bf16[1024,512]{1,0:T(8,128)(2,1)S(1)} %pad_maximum_fusion.1), channel_id=1, source_target_pairs={{0,4},{1,5},{2,6},{3,7},{4,8},{5,9},{6,10},{7,11},{8,12},{9,13},{1... | collective-permute-start | bytes 3145736 | tf_op jit(solution)/shard_map/ppermute | solution.py:49
  129.4 10.5 %collective-permute-start.23 = (bf16[256,512]{1,0:T(8,128)(2,1)S(1)}, bf16[256,512]{1,0:T(8,128)(2,1)S(1)}, u32[]{:S(2)}, u32[]{:S(2)}) collective-permute-start(bf16[256,512]{1,0:T(8,128)(2,1)S(1)} %get-tuple-element.156), channel_id=1, source_target_pairs={{0,1},{1,2},{2,3},{3,0},{4,5},{5,6},{6,7},{7,4},{8,9},{9,10},{10,1... | collective-permute-start | bytes 786440 | tf_op jit(solution)/shard_map/ppermute | solution.py:49
  129.7 10.2 %collective-permute-start.24 = (bf16[256,512]{1,0:T(8,128)(2,1)S(1)}, bf16[256,512]{1,0:T(8,128)(2,1)S(1)}, u32[]{:S(2)}, u32[]{:S(2)}) collective-permute-start(bf16[256,512]{1,0:T(8,128)(2,1)S(1)} %get-tuple-element.155), channel_id=1, source_target_pairs={{0,3},{1,0},{2,1},{3,2},{4,7},{5,4},{6,5},{7,6},{8,11},{9,8},{10,9... | collective-permute-start | bytes 786440 | tf_op jit(solution)/shard_map/ppermute | solution.py:49
  142.9 14.9 %collective-permute-start.25 = (bf16[512,512]{1,0:T(8,128)(2,1)S(1)}, bf16[512,512]{1,0:T(8,128)(2,1)S(1)}, u32[]{:S(2)}, u32[]{:S(2)}) collective-permute-start(bf16[512,512]{1,0:T(8,128)(2,1)S(1)} %pad_maximum_fusion.7), channel_id=1, source_target_pairs={{0,4},{1,5},{2,6},{3,7},{4,8},{5,9},{6,10},{7,11},{8,12},{9,13},{1... | collective-permute-start | bytes 1572872 | tf_op jit(solution)/shard_map/ppermute | solution.py:49
  146.4 15.0 %collective-permute-start.26 = (bf16[512,512]{1,0:T(8,128)(2,1)S(1)}, bf16[512,512]{1,0:T(8,128)(2,1)S(1)}, u32[]{:S(2)}, u32[]{:S(2)}) collective-permute-start(bf16[512,512]{1,0:T(8,128)(2,1)S(1)} %pad_maximum_fusion.8), channel_id=1, source_target_pairs={{0,12},{1,13},{2,14},{3,15},{4,0},{5,1},{6,2},{7,3},{8,4},{9,5},{1... | collective-permute-start | bytes 1572872 | tf_op jit(solution)/shard_map/ppermute | solution.py:49
  146.5 14.9 %collective-permute-start.29 = (bf16[512,512]{1,0:T(8,128)(2,1)S(1)}, bf16[512,512]{1,0:T(8,128)(2,1)S(1)}, u32[]{:S(2)}, u32[]{:S(2)}) collective-permute-start(bf16[512,512]{1,0:T(8,128)(2,1)S(1)} %pad_maximum_fusion.9), channel_id=1, source_target_pairs={{0,1},{1,2},{2,3},{3,0},{4,5},{5,6},{6,7},{7,4},{8,9},{9,10},{10,1... | collective-permute-start | bytes 1572872 | tf_op jit(solution)/shard_map/ppermute | solution.py:49
  146.8 15.7 %copy-start.1 = (s32[64,4]{0,1:T(4,128)S(1)}, s32[64,4]{0,1:T(4,128)}, u32[]{:S(2)}) copy-start(s32[64,4]{0,1:T(4,128)} %param.14) | copy-start | bytes 3076
  146.9 14.5 %collective-permute-start.30 = (bf16[512,512]{1,0:T(8,128)(2,1)S(1)}, bf16[512,512]{1,0:T(8,128)(2,1)S(1)}, u32[]{:S(2)}, u32[]{:S(2)}) collective-permute-start(bf16[512,512]{1,0:T(8,128)(2,1)S(1)} %pad_maximum_fusion.10), channel_id=1, source_target_pairs={{0,3},{1,0},{2,1},{3,2},{4,7},{5,4},{6,5},{7,6},{8,11},{9,8},{10,9... | collective-permute-start | bytes 1572872 | tf_op jit(solution)/shard_map/ppermute | solution.py:49

commit v5 on v4

--- a/solution.py
+++ b/solution.py
@@ -99,28 +99,82 @@
 
 
 def assemble(arrays, outputs):
-    n_arrays = len(arrays)
+    n_arrays, n_outputs = len(arrays), len(outputs)
+    needed, plans = {}, []
+    for shape, pieces in outputs:
+        direct, summed = [], []
+        for piece in pieces:
+            _, _, rows, columns, terms = piece
+            whole = columns == shape[1] == arrays[terms[0][0]].shape[1]
+            if len(terms) == 1 and whole:
+                direct.append(piece)
+                continue
+            summed.append(piece)
+            for a, r, _ in terms:
+                low, high = needed.get(a, (r, r + rows))
+                needed[a] = (min(low, r), max(high, r + rows))
+        low = min([p[0] for p in summed], default=0)
+        high = max([p[0] + p[2] for p in summed], default=0)
+        plans.append((direct, summed, low, high))
+    staged = sorted(needed)
+    built = [n for n, plan in enumerate(plans) if plan[1]]
+    n_copies = len(staged) + len(built) + sum(len(plan[0]) for plan in plans)
 
     def body(*refs):
-        for o_ref, (_, pieces) in zip(refs[n_arrays:], outputs, strict=True):
-            for row, column, rows, columns, terms in pieces:
-                parts = [refs[a][r : r + rows, c : c + columns] for a, r, c in terms]
-                if len(parts) > 1:
-                    total = parts[0].astype(F32)
-                    for part in parts[1:]:
-                        total = total + part.astype(F32)
-                    parts = [total.astype(BF16)]
-                o_ref[row : row + rows, column : column + columns] = parts[0]
-
+        a_refs, o_refs = refs[:n_arrays], refs[n_arrays : n_arrays + n_outputs]
+        stage = dict(zip(staged, refs[n_arrays + n_outputs :]))
+        build = dict(zip(built, refs[n_arrays + n_outputs + len(staged) :]))
+        sems = refs[-1]
+        inward, outward = [], []
+        for n, a in enumerate(staged):
+            low, high = needed[a]
+            inward.append(
+                pltpu.make_async_copy(a_refs[a].at[pl.ds(low, high - low), :], stage[a], sems.at[n])
+            )
+        count = len(staged)
+        for o_ref, (direct, _, _, _) in zip(o_refs, plans):
+            for row, _, rows, _, terms in direct:
+                source, start, _ = terms[0]
+                outward.append(
+                    pltpu.make_async_copy(
+                        a_refs[source].at[pl.ds(start, rows), :], o_ref.at[pl.ds(row, rows), :], sems.at[count]
+                    )
+                )
+                count += 1
+        for copy in inward + outward:
+            copy.start()
+        for copy in inward:
+            copy.wait()
+        for n in built:
+            _, summed, first, last = plans[n]
+            for row, column, rows, columns, terms in summed:
+                total = None
+                for a, r, c in terms:
+                    r -= needed[a][0]
+                    part = stage[a][r : r + rows, c : c + columns]
+                    if len(terms) > 1:
+                        part = part.astype(F32)
+                    total = part if total is None else total + part
+                build[n][row - first : row - first + rows, column : column + columns] = total.astype(BF16)
+            copy = pltpu.make_async_copy(build[n], o_refs[n].at[pl.ds(first, last - first), :], sems.at[count])
+            copy.start()
+            outward.append(copy)
+            count += 1
+        for copy in outward:
+            copy.wait()
+
+    scratch = [pltpu.VMEM((needed[a][1] - needed[a][0], arrays[a].shape[1]), BF16) for a in staged]
+    scratch += [pltpu.VMEM((plans[n][3] - plans[n][2], outputs[n][0][1]), BF16) for n in built]
     return pl.pallas_call(
         body,
-        out_shape=[pltpu.VMEM(shape, BF16) for shape, _ in outputs],
-        in_specs=[VMEM] * n_arrays,
-        out_specs=[VMEM] * len(outputs),
+        out_shape=[jax.ShapeDtypeStruct(shape, BF16) for shape, _ in outputs],
+        in_specs=[ANYWHERE] * n_arrays,
+        out_specs=[ANYWHERE] * n_outputs,
+        scratch_shapes=[*scratch, pltpu.SemaphoreType.DMA((n_copies,))],
         compiler_params=params(6),
         cost_estimate=estimate(0, 0),
         name="assemble",
-    )(*in_vmem(arrays))
+    )(*arrays)
 
 
 def rows_piece(row, rows, *terms):
@@ -140,7 +194,8 @@
     spots = [(i, j) for i in steps for j in range(4)]
     count = len(spots)
 
-    def body(order_ref, t_ref, g_ref, w_ref, o_ref, weights, sems):
+    def body(order_ref, t_ref, g_ref, w_ref, *refs):
+        o_refs, (weights, sems) = refs[:-2], refs[-2:]
         copies = []
         for n, (i, j) in enumerate(spots):
             target = place_of(order_ref, i, j)
@@ -158,16 +213,16 @@
         scaled = (t_ref[...].astype(F32) * own).astype(BF16)
         for copy in copies:
             copy.wait()
-        for n in range(0, count * HD, WIDE):
-            o_ref[:, n : n + WIDE] = jnp.dot(
-                scaled, weights[:, n : n + WIDE], preferred_element_type=F32
+        for n, o_ref in enumerate(o_refs):
+            o_ref[...] = jnp.dot(
+                scaled, weights[:, n * WIDE : (n + 1) * WIDE], preferred_element_type=F32
             ).astype(BF16)
 
     return pl.pallas_call(
         body,
-        out_shape=jax.ShapeDtypeStruct((WIDE, count * HD), BF16),
+        out_shape=[jax.ShapeDtypeStruct((WIDE, WIDE), BF16)] * len(steps),
         in_specs=[SMEM, VMEM, VMEM, FIXED],
-        out_specs=VMEM,
+        out_specs=[VMEM] * len(steps),
         scratch_shapes=[
             pltpu.VMEM((WIDE, count * HD), BF16),
             pltpu.SemaphoreType.DMA((count,)),
@@ -251,6 +306,54 @@
         cost_estimate=estimate(0, 0),
         name="query_part",
     )(order, *in_vmem(arrays), gain, w_query, *in_vmem(carried))
+
+
+def in_hbm(arrays):
+    return [pltpu.with_memory_space_constraint(a, pltpu.HBM) for a in arrays]
+
+
+def cut_cache(cache, head):
+    shape = (*cache.shape[:3], HD)
+
+    def body(head_ref, c_ref, o_ref, sem):
+        column = pl.multiple_of(head_ref[0] * HD, HD)
+        copy = pltpu.make_async_copy(c_ref.at[:, :, :, pl.ds(column, HD)], o_ref, sem)
+        copy.start()
+        copy.wait()
+
+    return pl.pallas_call(
+        body,
+        out_shape=pltpu.HBM(shape, BF16),
+        in_specs=[SMEM, FIXED],
+        out_specs=FIXED,
+        scratch_shapes=[pltpu.SemaphoreType.DMA],
+        compiler_params=params(2),
+        cost_estimate=estimate(0, 0),
+        name="cut_cache",
+    )(head, *in_hbm([cache]))
+
+
+def join_cache(parts):
+    def body(one_ref, two_ref, o_ref, sems):
+        copies = [
+            pltpu.make_async_copy(ref, o_ref.at[n], sems.at[n])
+            for n, ref in enumerate((one_ref, two_ref))
+        ]
+        for copy in copies:
+            copy.start()
+        for copy in copies:
+            copy.wait()
+
+    return pl.pallas_call(
+        body,
+        out_shape=pltpu.HBM((2, *parts[0].shape), BF16),
+        in_specs=[FIXED, FIXED],
+        out_specs=FIXED,
+        scratch_shapes=[pltpu.SemaphoreType.DMA((2,))],
+        compiler_params=params(2),
+        cost_estimate=estimate(0, 0),
+        name="join_cache",
+    )(*in_hbm(parts))
 
 
 def gather_blocks(pools, codes):
@@ -424,9 +527,9 @@
     ]
 
     s1 = both(tokens, tokens, "first")
-    kv = kv_partial(tokens, gains, w_keyvalue, order, (0, 1, 3, 2))
-    k_far = both(kv[:HALF, 3 * WIDE :], kv[HALF:, 3 * WIDE :], "first")
-    b1m, b1p, k_m, k_p, kv_near, cache = bar((*s1, *k_far, kv, cache))
+    kv_far, *kv = kv_partial(tokens, gains, w_keyvalue, order, (2, 0, 1, 3))
+    k_far = both(kv_far[:HALF], kv_far[HALF:], "first")
+    b1m, b1p, k_m, k_p, cache, kv_0, kv_1, kv_3 = bar((*s1, *k_far, cache, *kv))
     (near,) = assemble(
         [tokens, b1p, b1m],
         [((3 * WIDE, WIDE), [rows_piece(n * WIDE, WIDE, (n, 0)) for n in range(3)])],
@@ -434,22 +537,22 @@
     s2 = both(near, near, "second")
     s3 = both(
         *assemble(
-            [b1m, b1p, kv_near, k_m, k_p],
+            [b1m, b1p, kv_1, kv_3, k_m, k_p],
             [
                 (
                     (3 * HALF, WIDE),
                     [
                         rows_piece(0, HALF, (0, 0)),
-                        (HALF, 0, HALF, WIDE, [(2, 0, WIDE), (3, 0, 0)]),
-                        (2 * HALF, 0, HALF, WIDE, [(2, HALF, WIDE)]),
+                        rows_piece(HALF, HALF, (2, 0), (4, 0)),
+                        rows_piece(2 * HALF, HALF, (2, HALF)),
                     ],
                 ),
                 (
                     (3 * HALF, WIDE),
                     [
                         rows_piece(0, HALF, (1, HALF)),
-                        (HALF, 0, HALF, WIDE, [(2, 0, 2 * WIDE)]),
-                        (2 * HALF, 0, HALF, WIDE, [(2, HALF, 2 * WIDE), (4, 0, 0)]),
+                        rows_piece(HALF, HALF, (3, 0)),
+                        rows_piece(2 * HALF, HALF, (3, HALF), (5, 0)),
                     ],
                 ),
             ],
@@ -457,7 +560,7 @@
         "first",
     )
     kv_head = place * (w_query.shape[1] // HD) // (HEADS // KVH)
-    cache_head = lax.dynamic_slice_in_dim(cache, kv_head * HD, HD, 3)
+    cache_head = cut_cache(cache, kv_head.reshape(1))
     z_one = hop(cache_head, "z_one", 1)
     part = query_part(
         [((0, 0), [(0, 0, 0, WIDE)]), ((1, 0), [(1, 0, 0, WIDE)]), ((3, 0), [(2, 0, 0, WIDE)])],
@@ -467,10 +570,10 @@
         w_query,
         None,
     )
-    pool = jnp.stack([cache_head, z_one])
+    pool = join_cache([cache_head, z_one])
     b3m, b3p, b2m, b2p, pool, *part = bar((*s3, *s2, pool, *part))
     (to_next,) = assemble(
-        [b3m, b3p, kv_near, b2m],
+        [b3m, b3p, kv_0, b2m],
         [
             (
                 (5 * HALF + HALF // 4, WIDE),
@@ -481,7 +584,7 @@
         ],
     )
     (to_last,) = assemble(
-        [b3m, b3p, kv_near, b2p],
+        [b3m, b3p, kv_0, b2p],
         [
             (
                 (5 * HALF + HALF // 4, WIDE),
@@ -493,7 +596,7 @@
     )
     s5 = both(to_next, to_last, "second")
     (ksum,) = assemble(
-        [kv_near, b3m, b3p],
+        [kv_0, b3m, b3p],
         [((WIDE, WIDE), [(0, 0, WIDE, WIDE, [(0, 0, 0), (1, HALF, 0), (2, HALF, 0)])])],
     )
     z_two, near_twin = hop(pool, "z_two", 1), hop(pool, "core", 1)

time: 163 us -> 243 us (1.49)
  Pallas kernels: 46.2 us -> 142 us
  waiting for transfers between devices: 53.4 us -> 44.3 us
  local copies, waits for them, and re-layouts: 9.51 us -> 4.27 us
    pallas_call x8 -> x10, Pallas kernels: 12.6 us -> 109 us  [the longest x7 55.1 us: assemble(): pl.pallas_call(body, out_shape=[jax.ShapeDtypeStruct(shape, BF16) for sha...]
    ppermute x31, waiting for transfers between devices: 53.4 us -> 44.3 us  [hop(): return lax.ppermute(value, AXES, HOPS[axis, step])]
    unnamed x35 -> x25, local copies, waits for them, and re-layouts: 6.04 us -> 2.96 us
  transfers between devices with their start and end apart: 31 -> 31, of which waited for: 14 -> 11; matrix products, arithmetic and copies ran while one was open for 4% -> 1% of each run, Pallas kernels for 22% -> 45%
where the time goes in v5:
time: 243 us
  Pallas kernels  142 us (58%)
  starting transfers between devices  46.9 us (19%)
  waiting for transfers between devices  44.3 us (18%)
  other arithmetic  4.39 us (2%)
  local copies, waits for them, and re-layouts  4.27 us (2%)
    pallas_call x7, Pallas kernels, assemble(): pl.pallas_call(body, out_shape=[jax.ShapeDtypeStruct(shape, BF16) for sha...  55.1 us
    ppermute x31, starting transfers between devices, hop(): return lax.ppermute(value, AXES, HOPS[axis, step])  46.9 us
    ppermute x31, waiting for transfers between devices, hop(): return lax.ppermute(value, AXES, HOPS[axis, step])  44.3 us
    pallas_call x1, Pallas kernels, join_cache(): pl.pallas_call(body, out_shape=pltpu.HBM((2, *parts[0].shape), BF16), in_...  32.9 us
    pallas_call x1, Pallas kernels, cut_cache(): pl.pallas_call(body, out_shape=pltpu.HBM(shape, BF16), in_specs=[SMEM, FI...  17 us
    pallas_call x4, Pallas kernels, query_part(): pl.pallas_call(body, out_shape=(jax.ShapeDtypeStruct((WIDE, WIDE), F32),...  16.8 us
    pallas_call x2, Pallas kernels, output_part(): pl.pallas_call(body, out_shape=jax.ShapeDtypeStruct((count, WIDE, WIDE),...  8.55 us
    pallas_call x1, Pallas kernels, middle(): pl.pallas_call(body, out_shape=(jax.ShapeDtypeStruct((WIDE, WIDE), BF16),...  6.06 us
  transfers between devices with their start and end apart: 31, of which 11 were waited for; matrix products, arithmetic and copies ran while one was open for 1% of the time, Pallas kernels for 45%

profile of v5, /device:TPU:6, one launch (start us, length us, event | category | flops | bytes accessed | tf_op | source)
XLA Modules:
  0.0 242.6 jit_solution(5523107457669283437)
XLA Ops:
  0.0 1.6 collective-permute-start
  1.6 1.7 collective-permute-start.1
  4.0 1.0 copy-done.6
  5.0 3.6 %kv_partial.1 = (bf16[512,512]{1,0:T(8,128)(2,1)S(1)}, bf16[512,512]{1,0:T(8,128)(2,1)S(1)}, bf16[512,512]{1,0:T(8,128)(2,1)S(1)}, bf16[512,512]{1,0:T(8,128)(2,1)S(1)}) custom-call(s32[16]{0:T(128)S(1)} %fusion.29.order_ref, bf16[512,512]{1,0:T(8,128)(2,1)S(1)} %copy-done.6, f32[16,512]{1,0:T(8,128)S(1)} %reshape.81.g_ref.refs_3_.refs_4_.refs_2_, ...), custom_call_target="tpu_custom_call" | custom-call | tf_op jit(solution)/shard_map/kv_partial/pallas_call | solution.py:221
  9.1 2.9 %collective-permute-start.3 = (bf16[256,512]{1,0:T(8,128)(2,1)S(1)}, bf16[256,512]{1,0:T(8,128)(2,1)S(1)}, u32[]{:S(2)}, u32[]{:S(2)}) collective-permute-start(bf16[256,512]{1,0:T(8,128)(2,1)S(1)} %get-tuple-element.167), channel_id=1, source_target_pairs={{0,3},{1,0},{2,1},{3,2},{4,7},{5,4},{6,5},{7,6},{8,11},{9,8},{10,9... | collective-permute-start | bytes 786440 | tf_op jit(solution)/shard_map/ppermute | solution.py:49
  12.0 4.3 %collective-permute-done.2.refs_4_ = bf16[256,512]{1,0:T(8,128)(2,1)S(1)} collective-permute-done((bf16[256,512]{1,0:T(8,128)(2,1)S(1)}, bf16[256,512]{1,0:T(8,128)(2,1)S(1)}, u32[]{:S(2)}, u32[]{:S(2)}) %collective-permute-start.2) | collective-permute-done | bytes 262176 | tf_op jit(solution)/shard_map/ppermute | solution.py:49
  16.4 1.3 assemble.8
  18.1 1.6 collective-permute-start.7
  19.8 1.3 assemble.7
  21.1 0.8 collective-permute-start.4
  21.9 2.6 %collective-permute-start.5 = (bf16[768,512]{1,0:T(8,128)(2,1)}, bf16[768,512]{1,0:T(8,128)(2,1)S(1)}, u32[]{:S(2)}, u32[]{:S(2)}) collective-permute-start(bf16[768,512]{1,0:T(8,128)(2,1)} %get-tuple-element.80), channel_id=1, source_target_pairs={{0,3},{1,0},{2,1},{3,2},{4,7},{5,4},{6,5},{7,6},{8,11},{9,8},{10,9... | collective-permute-start | bytes 2359304 | tf_op jit(solution)/shard_map/ppermute | solution.py:49
  24.5 17.0 %cut_cache.1.one_ref = bf16[2,16,64,128]{3,2,1,0:T(8,128)(2,1)} custom-call(s32[1]{0:T(128)} %bitcast.head_ref, bf16[2,16,64,1024]{3,2,1,0:T(8,128)(2,1)} %c_ref), custom_call_target="tpu_custom_call" | custom-call | tf_op jit(solution)/shard_map/cut_cache/pallas_call | solution.py:324
  41.5 2.0 collective-permute-start.8
  43.5 3.0 %query_part.4 = (f32[512,512]{1,0:T(8,128)S(1)}, f32[512,128]{1,0:T(8,128)S(1)}) custom-call(s32[16]{0:T(128)S(1)} %fusion.29.order_ref, bf16[512,512]{1,0:T(8,128)(2,1)S(1)} %copy-done.8, bf16[512,512]{1,0:T(8,128)(2,1)S(1)} %copy-done.5, bf16[512,512]{1,0:T(8,128)(2,1)S(1)} %copy-done.3, f32[16,512]{1,0:T(8,128)S(1)} %reshape.81.g_ref.refs_3_.refs_4_.refs_2_, ...), custom_call_target="tpu_custom_call" | custom-call | tf_op jit(solution)/shard_map/query_part/pallas_call | solution.py:291
  46.5 4.5 %collective-permute-done.8.two_ref = bf16[2,16,64,128]{3,2,1,0:T(8,128)(2,1)S(1)} collective-permute-done((bf16[2,16,64,128]{3,2,1,0:T(8,128)(2,1)}, bf16[2,16,64,128]{3,2,1,0:T(8,128)(2,1)S(1)}, u32[]{:S(2)}, u32[]{:S(2)}) %collective-permute-start.8) | collective-permute-done | bytes 524320 | tf_op jit(solution)/shard_map/ppermute | solution.py:49
  51.8 32.9 %join_cache.1.refs_0_ = bf16[2,2,16,64,128]{4,3,2,1,0:T(8,128)(2,1)} custom-call(bf16[2,16,64,128]{3,2,1,0:T(8,128)(2,1)} %cut_cache.1.one_ref, bf16[2,16,64,128]{3,2,1,0:T(8,128)(2,1)} %copy-done.10), custom_call_target="tpu_custom_call" | custom-call | tf_op jit(solution)/shard_map/join_cache/pallas_call | solution.py:347
  84.7 25.1 %assemble.10 = bf16[1344,512]{1,0:T(8,128)(2,1)} custom-call(bf16[768,512]{1,0:T(8,128)(2,1)S(1)} %collective-permute-done.4.refs_0_.refs_1_, bf16[768,512]{1,0:T(8,128)(2,1)S(1)} %collective-permute-done.5.refs_1_.refs_2_, bf16[512,512]{1,0:T(8,128)(2,1)S(1)} %get-tuple-element.86.refs_2_.refs_0_, bf16[1536,512]{1,0:T(8,128)(2,1)} %collective-permute-done.7.refs_3_.refs_2_), custom_call_target="tpu_custom_call" | custom-call | tf_op jit(solution)/shard_map/assemble/pallas_call | solution.py:168
  109.8 0.9 collective-permute-start.10
  110.7 25.1 %assemble.9 = bf16[1344,512]{1,0:T(8,128)(2,1)} custom-call(bf16[768,512]{1,0:T(8,128)(2,1)S(1)} %collective-permute-done.4.refs_0_.refs_1_, bf16[768,512]{1,0:T(8,128)(2,1)S(1)} %collective-permute-done.5.refs_1_.refs_2_, bf16[512,512]{1,0:T(8,128)(2,1)S(1)} %get-tuple-element.86.refs_2_.refs_0_, bf16[1536,512]{1,0:T(8,128)(2,1)} %collective-permute-done.6.refs_3_), custom_call_target="tpu_custom_call" | custom-call | tf_op jit(solution)/shard_map/assemble/pallas_call | solution.py:168
  135.8 2.5 %collective-permute-start.9 = (bf16[1344,512]{1,0:T(8,128)(2,1)}, bf16[1344,512]{1,0:T(8,128)(2,1)}, u32[]{:S(2)}, u32[]{:S(2)}) collective-permute-start(bf16[1344,512]{1,0:T(8,128)(2,1)} %assemble.9), channel_id=1, source_target_pairs={{0,4},{1,5},{2,6},{3,7},{4,8},{5,9},{6,10},{7,11},{8,12},{9,13},{1... | collective-permute-start | bytes 4128776 | tf_op jit(solution)/shard_map/ppermute | solution.py:49
  138.3 4.0 %collective-permute-start.11 = (bf16[2,2,16,64,128]{4,3,2,1,0:T(8,128)(2,1)}, bf16[2,2,16,64,128]{4,3,2,1,0:T(8,128)(2,1)}, u32[]{:S(2)}, u32[]{:S(2)}) collective-permute-start(bf16[2,2,16,64,128]{4,3,2,1,0:T(8,128)(2,1)} %join_cache.1.refs_0_), channel_id=1, source_target_pairs={{0,96},{1,97},{2,98},{3,99},{4,100},{5,101},{6,102},{7,103},{8,104... | collective-permute-start | bytes 3145736 | tf_op jit(solution)/shard_map/ppermute | solution.py:49
  142.7 1.0 fusion.24
  144.3 6.5 %query_part.5 = (f32[512,512]{1,0:T(8,128)S(1)}, f32[512,128]{1,0:T(8,128)S(1)}) custom-call(s32[16]{0:T(128)S(1)} %fusion.29.order_ref, bf16[768,512]{1,0:T(8,128)(2,1)S(1)} %collective-permute-done.4.refs_0_.refs_1_, bf16[768,512]{1,0:T(8,128)(2,1)S(1)} %collective-permute-done.5.refs_1_.refs_2_, ...), custom_call_target="tpu_custom_call", output_to_operand_aliasing={{0}: (7, {}), {1}: (8, {})} | custom-call | tf_op jit(solution)/shard_map/query_part/pallas_call | solution.py:291
  150.8 4.6 %collective-permute-done.11.refs_1_ = bf16[2,2,16,64,128]{4,3,2,1,0:T(8,128)(2,1)} collective-permute-done((bf16[2,2,16,64,128]{4,3,2,1,0:T(8,128)(2,1)}, bf16[2,2,16,64,128]{4,3,2,1,0:T(8,128)(2,1)}, u32[]{:S(2)}, u32[]{:S(2)}) %collective-permute-start.11) | collective-permute-done | bytes 1048608 | tf_op jit(solution)/shard_map/ppermute | solution.py:49
  155.5 1.3 assemble.12
  156.8 2.7 %collective-permute-start.13 = (bf16[384,512]{1,0:T(8,128)(2,1)S(1)}, bf16[384,512]{1,0:T(8,128)(2,1)S(1)}, u32[]{:S(2)}, u32[]{:S(2)}) collective-permute-start(bf16[384,512]{1,0:T(8,128)(2,1)S(1)} %get-tuple-element.97), channel_id=1, source_target_pairs={{0,4},{1,5},{2,6},{3,7},{4,8},{5,9},{6,10},{7,11},{8,12},{9,13},{1... | collective-permute-start | bytes 1179656 | tf_op jit(solution)/shard_map/ppermute | solution.py:49
  159.5 5.3 %query_part.6 = (f32[512,512]{1,0:T(8,128)S(1)}, f32[512,128]{1,0:T(8,128)S(1)}) custom-call(s32[16]{0:T(128)S(1)} %fusion.29.order_ref, bf16[1344,512]{1,0:T(8,128)(2,1)} %collective-permute-done.10.refs_1_.refs_0_, bf16[1344,512]{1,0:T(8,128)(2,1)} %collective-permute-done.9.refs_0_.refs_1_, ...), custom_call_target="tpu_custom_call", output_to_operand_aliasing={{0}: (5, {}), {1}: (6, {})} | custom-call | tf_op jit(solution)/shard_map/query_part/pallas_call | solution.py:291
  164.9 1.0 copy-done.9
  165.9 2.2 gather_blocks.1.prefix_ref
  169.2 2.0 query_part.7
  171.3 3.6 %collective-permute-done.16.other_ref = bf16[512,128]{1,0:T(8,128)(2,1)S(1)} collective-permute-done((bf16[512,128]{1,0:T(8,128)(2,1)S(1)}, bf16[512,128]{1,0:T(8,128)(2,1)S(1)}, u32[]{:S(2)}, u32[]{:S(2)}) %collective-permute-start.16) | collective-permute-done | bytes 131104 | tf_op jit(solution)/shard_map/ppermute | solution.py:49
  174.9 6.1 %middle.1 = (bf16[512,512]{1,0:T(8,128)(2,1)S(1)}, bf16[4,512,512]{2,1,0:T(8,128)(2,1)S(1)}, bf16[8,2,320,128]{3,2,1,0:T(8,128)(2,1)S(1)}) custom-call(s32[16]{0:T(128)S(1)} %fusion.29.order_ref, s32[8]{0:T(128)S(1)} %get-tuple-element.134.len_ref, f32[512,512]{1,0:T(8,128)S(1)} %get-tuple-element.110.q_ref, ...), custom_call_target="tpu_custom_call", output_to_operand_aliasing={{2}: (8, {})} | custom-call | tf_op jit(solution)/shard_map/middle/pallas_call | solution.py:456
  181.3 3.3 %collective-permute-start.21 = (bf16[768,512]{1,0:T(8,128)(2,1)S(1)}, bf16[768,512]{1,0:T(8,128)(2,1)S(1)}, u32[]{:S(2)}, u32[]{:S(2)}) collective-permute-start(bf16[768,512]{1,0:T(8,128)(2,1)S(1)} %pad_maximum_fusion.2), channel_id=1, source_target_pairs={{0,4},{1,5},{2,6},{3,7},{4,8},{5,9},{6,10},{7,11},{8,12},{9,13},{1... | collective-permute-start | bytes 2359304 | tf_op jit(solution)/shard_map/ppermute | solution.py:49
  184.6 1.4 collective-permute-start.17
  186.6 4.3 %output_part.2 = bf16[6,512,512]{2,1,0:T(8,128)(2,1)S(1)} custom-call(s32[16]{0:T(128)S(1)} %fusion.29.order_ref, bf16[512,512]{1,0:T(8,128)(2,1)S(1)} %get-tuple-element.121.h_ref, bf16[512,8192]{1,0:T(8,128)(2,1)} %w_ref.5), custom_call_target="tpu_custom_call" | custom-call | tf_op jit(solution)/shard_map/output_part/pallas_call | solution.py:495
  190.9 6.0 %collective-permute-done.17 = bf16[256,512]{1,0:T(8,128)(2,1)S(1)} collective-permute-done((bf16[256,512]{1,0:T(8,128)(2,1)S(1)}, bf16[256,512]{1,0:T(8,128)(2,1)S(1)}, u32[]{:S(2)}, u32[]{:S(2)}) %collective-permute-start.17) | collective-permute-done | bytes 262176 | tf_op jit(solution)/shard_map/ppermute | solution.py:49
  198.0 1.0 collective-permute-start.20
  199.0 2.5 %collective-permute-start.19 = (bf16[512,512]{1,0:T(8,128)(2,1)S(1)}, bf16[512,512]{1,0:T(8,128)(2,1)S(1)}, u32[]{:S(2)}, u32[]{:S(2)}) collective-permute-start(bf16[512,512]{1,0:T(8,128)(2,1)S(1)} %pad_maximum_fusion.4), channel_id=1, source_target_pairs={{0,4},{1,5},{2,6},{3,7},{4,8},{5,9},{6,10},{7,11},{8,12},{9,13},{1... | collective-permute-start | bytes 1572872 | tf_op jit(solution)/shard_map/ppermute | solution.py:49
  201.8 3.5 %collective-permute-start.27 = (bf16[1024,512]{1,0:T(8,128)(2,1)S(1)}, bf16[1024,512]{1,0:T(8,128)(2,1)S(1)}, u32[]{:S(2)}, u32[]{:S(2)}) collective-permute-start(bf16[1024,512]{1,0:T(8,128)(2,1)S(1)} %pad_maximum_fusion), channel_id=1, source_target_pairs={{0,4},{1,5},{2,6},{3,7},{4,8},{5,9},{6,10},{7,11},{8,12},{9,13},{1... | collective-permute-start | bytes 3145736 | tf_op jit(solution)/shard_map/ppermute | solution.py:49
  205.3 4.3 %output_part.3 = bf16[6,512,512]{2,1,0:T(8,128)(2,1)S(1)} custom-call(s32[16]{0:T(128)S(1)} %fusion.29.order_ref, bf16[512,512]{1,0:T(8,128)(2,1)S(1)} %get-tuple-element.121.h_ref, bf16[512,8192]{1,0:T(8,128)(2,1)} %w_ref.5), custom_call_target="tpu_custom_call" | custom-call | tf_op jit(solution)/shard_map/output_part/pallas_call | solution.py:495
  210.2 3.0 %collective-permute-start.24 = (bf16[256,512]{1,0:T(8,128)(2,1)S(1)}, bf16[256,512]{1,0:T(8,128)(2,1)S(1)}, u32[]{:S(2)}, u32[]{:S(2)}) collective-permute-start(bf16[256,512]{1,0:T(8,128)(2,1)S(1)} %get-tuple-element.165), channel_id=1, source_target_pairs={{0,3},{1,0},{2,1},{3,2},{4,7},{5,4},{6,5},{7,6},{8,11},{9,8},{10,9... | collective-permute-start | bytes 786440 | tf_op jit(solution)/shard_map/ppermute | solution.py:49
  213.2 7.2 %collective-permute-done.23 = bf16[256,512]{1,0:T(8,128)(2,1)S(1)} collective-permute-done((bf16[256,512]{1,0:T(8,128)(2,1)S(1)}, bf16[256,512]{1,0:T(8,128)(2,1)S(1)}, u32[]{:S(2)}, u32[]{:S(2)}) %collective-permute-start.23) | collective-permute-done | bytes 262176 | tf_op jit(solution)/shard_map/ppermute | solution.py:49
  220.4 2.2 collective-permute-done.28
  223.4 3.4 %collective-permute-start.25 = (bf16[512,512]{1,0:T(8,128)(2,1)S(1)}, bf16[512,512]{1,0:T(8,128)(2,1)S(1)}, u32[]{:S(2)}, u32[]{:S(2)}) collective-permute-start(bf16[512,512]{1,0:T(8,128)(2,1)S(1)} %pad_maximum_fusion.6), channel_id=1, source_target_pairs={{0,4},{1,5},{2,6},{3,7},{4,8},{5,9},{6,10},{7,11},{8,12},{9,13},{1... | collective-permute-start | bytes 1572872 | tf_op jit(solution)/shard_map/ppermute | solution.py:49
  227.4 3.0 %collective-permute-start.30 = (bf16[512,512]{1,0:T(8,128)(2,1)S(1)}, bf16[512,512]{1,0:T(8,128)(2,1)S(1)}, u32[]{:S(2)}, u32[]{:S(2)}) collective-permute-start(bf16[512,512]{1,0:T(8,128)(2,1)S(1)} %pad_maximum_fusion.9), channel_id=1, source_target_pairs={{0,3},{1,0},{2,1},{3,2},{4,7},{5,4},{6,5},{7,6},{8,11},{9,8},{10,9... | collective-permute-start | bytes 1572872 | tf_op jit(solution)/shard_map/ppermute | solution.py:49
  230.4 7.7 %collective-permute-done.25 = bf16[512,512]{1,0:T(8,128)(2,1)S(1)} collective-permute-done((bf16[512,512]{1,0:T(8,128)(2,1)S(1)}, bf16[512,512]{1,0:T(8,128)(2,1)S(1)}, u32[]{:S(2)}, u32[]{:S(2)}) %collective-permute-start.25) | collective-permute-done | bytes 524320 | tf_op jit(solution)/shard_map/ppermute | solution.py:49
  238.1 3.4 %collective-permute-done.26 = bf16[512,512]{1,0:T(8,128)(2,1)S(1)} collective-permute-done((bf16[512,512]{1,0:T(8,128)(2,1)S(1)}, bf16[512,512]{1,0:T(8,128)(2,1)S(1)}, u32[]{:S(2)}, u32[]{:S(2)}) %collective-permute-start.26) | collective-permute-done | bytes 524320 | tf_op jit(solution)/shard_map/ppermute | solution.py:49
  241.5 1.1 fusion.5
  (86 shorter events, 8.9 us)
Async XLA Ops:
  0.0 142.3 %copy-start = (s32[64,4]{0,1:T(4,128)S(1)}, s32[64,4]{0,1:T(4,128)}, u32[]{:S(2)}) copy-start(s32[64,4]{0,1:T(4,128)} %param.14) | copy-start | bytes 3076
  0.0 16.4 %collective-permute-start = (bf16[512,512]{1,0:T(8,128)(2,1)}, bf16[512,512]{1,0:T(8,128)(2,1)S(1)}, u32[]{:S(2)}, u32[]{:S(2)}) collective-permute-start(bf16[512,512]{1,0:T(8,128)(2,1)} %refs_0_.3), channel_id=1, source_target_pairs={{0,1},{1,2},{2,3},{3,0},{4,5},{5,6},{6,7},{7,4},{8,9},{9,10},{10,1... | collective-permute-start | bytes 1572872 | tf_op jit(solution)/shard_map/ppermute | solution.py:49
  1.6 14.8 %collective-permute-start.1 = (bf16[512,512]{1,0:T(8,128)(2,1)}, bf16[512,512]{1,0:T(8,128)(2,1)S(1)}, u32[]{:S(2)}, u32[]{:S(2)}) collective-permute-start(bf16[512,512]{1,0:T(8,128)(2,1)} %refs_0_.3), channel_id=1, source_target_pairs={{0,3},{1,0},{2,1},{3,2},{4,7},{5,4},{6,5},{7,6},{8,11},{9,8},{10,9... | collective-permute-start | bytes 1572872 | tf_op jit(solution)/shard_map/ppermute | solution.py:49
  4.0 1.0 copy-start.6
  5.0 11.4 %copy-start.7 = (bf16[512,512]{1,0:T(8,128)(2,1)S(1)}, bf16[512,512]{1,0:T(8,128)(2,1)}, u32[]{:S(2)}) copy-start(bf16[512,512]{1,0:T(8,128)(2,1)} %refs_0_.3) | copy-start | bytes 1572868
  8.7 7.7 %collective-permute-start.2 = (bf16[256,512]{1,0:T(8,128)(2,1)S(1)}, bf16[256,512]{1,0:T(8,128)(2,1)S(1)}, u32[]{:S(2)}, u32[]{:S(2)}) collective-permute-start(bf16[256,512]{1,0:T(8,128)(2,1)S(1)} %get-tuple-element.168), channel_id=1, source_target_pairs={{0,1},{1,2},{2,3},{3,0},{4,5},{5,6},{6,7},{7,4},{8,9},{9,10},{10,1... | collective-permute-start | bytes 786440 | tf_op jit(solution)/shard_map/ppermute | solution.py:49
  9.1 7.2 %collective-permute-start.3 = (bf16[256,512]{1,0:T(8,128)(2,1)S(1)}, bf16[256,512]{1,0:T(8,128)(2,1)S(1)}, u32[]{:S(2)}, u32[]{:S(2)}) collective-permute-start(bf16[256,512]{1,0:T(8,128)(2,1)S(1)} %get-tuple-element.167), channel_id=1, source_target_pairs={{0,3},{1,0},{2,1},{3,2},{4,7},{5,4},{6,5},{7,6},{8,11},{9,8},{10,9... | collective-permute-start | bytes 786440 | tf_op jit(solution)/shard_map/ppermute | solution.py:49
  16.4 4.8 %copy-start.2 = (bf16[512,512]{1,0:T(8,128)(2,1)}, bf16[512,512]{1,0:T(8,128)(2,1)S(1)}, u32[]{:S(2)}) copy-start(bf16[512,512]{1,0:T(8,128)(2,1)S(1)} %collective-permute-done.refs_0_.refs_2_) | copy-start | bytes 1572868
  16.4 4.7 %copy-start.4 = (bf16[512,512]{1,0:T(8,128)(2,1)}, bf16[512,512]{1,0:T(8,128)(2,1)S(1)}, u32[]{:S(2)}) copy-start(bf16[512,512]{1,0:T(8,128)(2,1)S(1)} %collective-permute-done.1.refs_1_) | copy-start | bytes 1572868
  17.7 67.0 %collective-permute-start.6 = (bf16[1536,512]{1,0:T(8,128)(2,1)}, bf16[1536,512]{1,0:T(8,128)(2,1)}, u32[]{:S(2)}, u32[]{:S(2)}) collective-permute-start(bf16[1536,512]{1,0:T(8,128)(2,1)} %assemble.8), channel_id=1, source_target_pairs={{0,4},{1,5},{2,6},{3,7},{4,8},{5,9},{6,10},{7,11},{8,12},{9,13},{1... | collective-permute-start | bytes 4718600 | tf_op jit(solution)/shard_map/ppermute | solution.py:49
  18.1 66.6 %collective-permute-start.7 = (bf16[1536,512]{1,0:T(8,128)(2,1)}, bf16[1536,512]{1,0:T(8,128)(2,1)}, u32[]{:S(2)}, u32[]{:S(2)}) collective-permute-start(bf16[1536,512]{1,0:T(8,128)(2,1)} %assemble.8), channel_id=1, source_target_pairs={{0,12},{1,13},{2,14},{3,15},{4,0},{5,1},{6,2},{7,3},{8,4},{9,5},{1... | collective-permute-start | bytes 4718600 | tf_op jit(solution)/shard_map/ppermute | solution.py:49
  21.1 63.5 %collective-permute-start.4 = (bf16[768,512]{1,0:T(8,128)(2,1)}, bf16[768,512]{1,0:T(8,128)(2,1)S(1)}, u32[]{:S(2)}, u32[]{:S(2)}) collective-permute-start(bf16[768,512]{1,0:T(8,128)(2,1)} %get-tuple-element.79), channel_id=1, source_target_pairs={{0,1},{1,2},{2,3},{3,0},{4,5},{5,6},{6,7},{7,4},{8,9},{9,10},{10,1... | collective-permute-start | bytes 2359304 | tf_op jit(solution)/shard_map/ppermute | solution.py:49
  21.9 62.8 %collective-permute-start.5 = (bf16[768,512]{1,0:T(8,128)(2,1)}, bf16[768,512]{1,0:T(8,128)(2,1)S(1)}, u32[]{:S(2)}, u32[]{:S(2)}) collective-permute-start(bf16[768,512]{1,0:T(8,128)(2,1)} %get-tuple-element.80), channel_id=1, source_target_pairs={{0,3},{1,0},{2,1},{3,2},{4,7},{5,4},{6,5},{7,6},{8,11},{9,8},{10,9... | collective-permute-start | bytes 2359304 | tf_op jit(solution)/shard_map/ppermute | solution.py:49
  24.5 19.0 %copy-start.3 = (bf16[512,512]{1,0:T(8,128)(2,1)S(1)}, bf16[512,512]{1,0:T(8,128)(2,1)}, u32[]{:S(2)}) copy-start(bf16[512,512]{1,0:T(8,128)(2,1)} %copy-done.2) | copy-start | bytes 1572868
  24.5 19.0 %copy-start.5 = (bf16[512,512]{1,0:T(8,128)(2,1)S(1)}, bf16[512,512]{1,0:T(8,128)(2,1)}, u32[]{:S(2)}) copy-start(bf16[512,512]{1,0:T(8,128)(2,1)} %copy-done.4) | copy-start | bytes 1572868
  24.5 19.0 %copy-start.8 = (bf16[512,512]{1,0:T(8,128)(2,1)S(1)}, bf16[512,512]{1,0:T(8,128)(2,1)}, u32[]{:S(2)}) copy-start(bf16[512,512]{1,0:T(8,128)(2,1)} %refs_0_.3) | copy-start | bytes 1572868
  41.5 9.5 %collective-permute-start.8 = (bf16[2,16,64,128]{3,2,1,0:T(8,128)(2,1)}, bf16[2,16,64,128]{3,2,1,0:T(8,128)(2,1)S(1)}, u32[]{:S(2)}, u32[]{:S(2)}) collective-permute-start(bf16[2,16,64,128]{3,2,1,0:T(8,128)(2,1)} %cut_cache.1.one_ref), channel_id=1, source_target_pairs={{0,32},{1,33},{2,34},{3,35},{4,36},{5,37},{6,38},{7,39},{8,40},{9,... | collective-permute-start | bytes 1572872 | tf_op jit(solution)/shard_map/ppermute | solution.py:49
  51.0 0.8 copy-start.10
  109.8 32.7 %copy-start.11 = (s32[64]{0:T(128)S(1)}, s32[64]{0:T(128)}, u32[]{:S(2)}) copy-start(s32[64]{0:T(128)} %param.15) | copy-start | bytes 772
  109.8 45.6 %collective-permute-start.10 = (bf16[1344,512]{1,0:T(8,128)(2,1)}, bf16[1344,512]{1,0:T(8,128)(2,1)}, u32[]{:S(2)}, u32[]{:S(2)}) collective-permute-start(bf16[1344,512]{1,0:T(8,128)(2,1)} %assemble.10), channel_id=1, source_target_pairs={{0,12},{1,13},{2,14},{3,15},{4,0},{5,1},{6,2},{7,3},{8,4},{9,5},{1... | collective-permute-start | bytes 4128776 | tf_op jit(solution)/shard_map/ppermute | solution.py:49
  135.8 19.6 %collective-permute-start.9 = (bf16[1344,512]{1,0:T(8,128)(2,1)}, bf16[1344,512]{1,0:T(8,128)(2,1)}, u32[]{:S(2)}, u32[]{:S(2)}) collective-permute-start(bf16[1344,512]{1,0:T(8,128)(2,1)} %assemble.9), channel_id=1, source_target_pairs={{0,4},{1,5},{2,6},{3,7},{4,8},{5,9},{6,10},{7,11},{8,12},{9,13},{1... | collective-permute-start | bytes 4128776 | tf_op jit(solution)/shard_map/ppermute | solution.py:49
  138.3 17.1 %collective-permute-start.11 = (bf16[2,2,16,64,128]{4,3,2,1,0:T(8,128)(2,1)}, bf16[2,2,16,64,128]{4,3,2,1,0:T(8,128)(2,1)}, u32[]{:S(2)}, u32[]{:S(2)}) collective-permute-start(bf16[2,2,16,64,128]{4,3,2,1,0:T(8,128)(2,1)} %join_cache.1.refs_0_), channel_id=1, source_target_pairs={{0,96},{1,97},{2,98},{3,99},{4,100},{5,101},{6,102},{7,103},{8,104... | collective-permute-start | bytes 3145736 | tf_op jit(solution)/shard_map/ppermute | solution.py:49
  142.3 13.1 %collective-permute-start.12 = (bf16[2,2,16,64,128]{4,3,2,1,0:T(8,128)(2,1)}, bf16[2,2,16,64,128]{4,3,2,1,0:T(8,128)(2,1)}, u32[]{:S(2)}, u32[]{:S(2)}) collective-permute-start(bf16[2,2,16,64,128]{4,3,2,1,0:T(8,128)(2,1)} %join_cache.1.refs_0_), channel_id=1, source_target_pairs={{0,16},{1,17},{2,18},{3,19},{4,20},{5,21},{6,22},{7,23},{8,24},{9,... | collective-permute-start | bytes 3145736 | tf_op jit(solution)/shard_map/ppermute | solution.py:49
  155.4 9.5 %collective-permute-start.15 = (bf16[2,2,16,64,128]{4,3,2,1,0:T(8,128)(2,1)}, bf16[2,2,16,64,128]{4,3,2,1,0:T(8,128)(2,1)S(1)}, u32[]{:S(2)}, u32[]{:S(2)}) collective-permute-start(bf16[2,2,16,64,128]{4,3,2,1,0:T(8,128)(2,1)} %collective-permute-done.11.refs_1_), channel_id=1, source_target_pairs={{0,16},{1,17},{2,18},{3,19},{4,20},{5,21},{6,22},{7,23},{8,24},{9,... | collective-permute-start | bytes 3145736 | tf_op jit(solution)/shard_map/ppermute | solution.py:49
  156.8 11.2 %collective-permute-start.13 = (bf16[384,512]{1,0:T(8,128)(2,1)S(1)}, bf16[384,512]{1,0:T(8,128)(2,1)S(1)}, u32[]{:S(2)}, u32[]{:S(2)}) collective-permute-start(bf16[384,512]{1,0:T(8,128)(2,1)S(1)} %get-tuple-element.97), channel_id=1, source_target_pairs={{0,4},{1,5},{2,6},{3,7},{4,8},{5,9},{6,10},{7,11},{8,12},{9,13},{1... | collective-permute-start | bytes 1179656 | tf_op jit(solution)/shard_map/ppermute | solution.py:49
  159.5 9.0 %collective-permute-start.14 = (bf16[384,512]{1,0:T(8,128)(2,1)S(1)}, bf16[384,512]{1,0:T(8,128)(2,1)S(1)}, u32[]{:S(2)}, u32[]{:S(2)}) collective-permute-start(bf16[384,512]{1,0:T(8,128)(2,1)S(1)} %get-tuple-element.98), channel_id=1, source_target_pairs={{0,12},{1,13},{2,14},{3,15},{4,0},{5,1},{6,2},{7,3},{8,4},{9,5},{1... | collective-permute-start | bytes 1179656 | tf_op jit(solution)/shard_map/ppermute | solution.py:49
  164.9 1.0 copy-start.9
  169.1 5.8 %collective-permute-start.16 = (bf16[512,128]{1,0:T(8,128)(2,1)S(1)}, bf16[512,128]{1,0:T(8,128)(2,1)S(1)}, u32[]{:S(2)}, u32[]{:S(2)}) collective-permute-start(bf16[512,128]{1,0:T(8,128)(2,1)S(1)} %assemble.13.mine_ref), channel_id=1, source_target_pairs={{0,1},{1,0},{2,3},{3,2},{4,5},{5,4},{6,7},{7,6},{8,9},{9,8},{10,11... | collective-permute-start | bytes 393224 | tf_op jit(solution)/shard_map/ppermute | solution.py:49
  181.2 16.3 %collective-permute-start.22 = (bf16[768,512]{1,0:T(8,128)(2,1)S(1)}, bf16[768,512]{1,0:T(8,128)(2,1)S(1)}, u32[]{:S(2)}, u32[]{:S(2)}) collective-permute-start(bf16[768,512]{1,0:T(8,128)(2,1)S(1)} %pad_maximum_fusion.3), channel_id=1, source_target_pairs={{0,12},{1,13},{2,14},{3,15},{4,0},{5,1},{6,2},{7,3},{8,4},{9,5},{1... | collective-permute-start | bytes 2359304 | tf_op jit(solution)/shard_map/ppermute | solution.py:49
  181.3 16.1 %collective-permute-start.21 = (bf16[768,512]{1,0:T(8,128)(2,1)S(1)}, bf16[768,512]{1,0:T(8,128)(2,1)S(1)}, u32[]{:S(2)}, u32[]{:S(2)}) collective-permute-start(bf16[768,512]{1,0:T(8,128)(2,1)S(1)} %pad_maximum_fusion.2), channel_id=1, source_target_pairs={{0,4},{1,5},{2,6},{3,7},{4,8},{5,9},{6,10},{7,11},{8,12},{9,13},{1... | collective-permute-start | bytes 2359304 | tf_op jit(solution)/shard_map/ppermute | solution.py:49
  184.6 12.3 %collective-permute-start.17 = (bf16[256,512]{1,0:T(8,128)(2,1)S(1)}, bf16[256,512]{1,0:T(8,128)(2,1)S(1)}, u32[]{:S(2)}, u32[]{:S(2)}) collective-permute-start(bf16[256,512]{1,0:T(8,128)(2,1)S(1)} %get-tuple-element.164), channel_id=1, source_target_pairs={{0,4},{1,5},{2,6},{3,7},{4,8},{5,9},{6,10},{7,11},{8,12},{9,13},{1... | collective-permute-start | bytes 786440 | tf_op jit(solution)/shard_map/ppermute | solution.py:49
  186.0 11.3 %collective-permute-start.18 = (bf16[256,512]{1,0:T(8,128)(2,1)S(1)}, bf16[256,512]{1,0:T(8,128)(2,1)S(1)}, u32[]{:S(2)}, u32[]{:S(2)}) collective-permute-start(bf16[256,512]{1,0:T(8,128)(2,1)S(1)} %get-tuple-element.163), channel_id=1, source_target_pairs={{0,12},{1,13},{2,14},{3,15},{4,0},{5,1},{6,2},{7,3},{8,4},{9,5},{1... | collective-permute-start | bytes 786440 | tf_op jit(solution)/shard_map/ppermute | solution.py:49
  198.0 11.6 %collective-permute-start.20 = (bf16[512,512]{1,0:T(8,128)(2,1)S(1)}, bf16[512,512]{1,0:T(8,128)(2,1)S(1)}, u32[]{:S(2)}, u32[]{:S(2)}) collective-permute-start(bf16[512,512]{1,0:T(8,128)(2,1)S(1)} %pad_maximum_fusion.5), channel_id=1, source_target_pairs={{0,12},{1,13},{2,14},{3,15},{4,0},{5,1},{6,2},{7,3},{8,4},{9,5},{1... | collective-permute-start | bytes 1572872 | tf_op jit(solution)/shard_map/ppermute | solution.py:49
  199.0 10.6 %collective-permute-start.19 = (bf16[512,512]{1,0:T(8,128)(2,1)S(1)}, bf16[512,512]{1,0:T(8,128)(2,1)S(1)}, u32[]{:S(2)}, u32[]{:S(2)}) collective-permute-start(bf16[512,512]{1,0:T(8,128)(2,1)S(1)} %pad_maximum_fusion.4), channel_id=1, source_target_pairs={{0,4},{1,5},{2,6},{3,7},{4,8},{5,9},{6,10},{7,11},{8,12},{9,13},{1... | collective-permute-start | bytes 1572872 | tf_op jit(solution)/shard_map/ppermute | solution.py:49
  201.6 21.0 %collective-permute-start.28 = (bf16[1024,512]{1,0:T(8,128)(2,1)S(1)}, bf16[1024,512]{1,0:T(8,128)(2,1)S(1)}, u32[]{:S(2)}, u32[]{:S(2)}) collective-permute-start(bf16[1024,512]{1,0:T(8,128)(2,1)S(1)} %pad_maximum_fusion.1), channel_id=1, source_target_pairs={{0,12},{1,13},{2,14},{3,15},{4,0},{5,1},{6,2},{7,3},{8,4},{9,5},{1... | collective-permute-start | bytes 3145736 | tf_op jit(solution)/shard_map/ppermute | solution.py:49
  201.8 20.8 %collective-permute-start.27 = (bf16[1024,512]{1,0:T(8,128)(2,1)S(1)}, bf16[1024,512]{1,0:T(8,128)(2,1)S(1)}, u32[]{:S(2)}, u32[]{:S(2)}) collective-permute-start(bf16[1024,512]{1,0:T(8,128)(2,1)S(1)} %pad_maximum_fusion), channel_id=1, source_target_pairs={{0,4},{1,5},{2,6},{3,7},{4,8},{5,9},{6,10},{7,11},{8,12},{9,13},{1... | collective-permute-start | bytes 3145736 | tf_op jit(solution)/shard_map/ppermute | solution.py:49
  209.8 10.5 %collective-permute-start.23 = (bf16[256,512]{1,0:T(8,128)(2,1)S(1)}, bf16[256,512]{1,0:T(8,128)(2,1)S(1)}, u32[]{:S(2)}, u32[]{:S(2)}) collective-permute-start(bf16[256,512]{1,0:T(8,128)(2,1)S(1)} %get-tuple-element.166), channel_id=1, source_target_pairs={{0,1},{1,2},{2,3},{3,0},{4,5},{5,6},{6,7},{7,4},{8,9},{9,10},{10,1... | collective-permute-start | bytes 786440 | tf_op jit(solution)/shard_map/ppermute | solution.py:49
  210.2 10.2 %collective-permute-start.24 = (bf16[256,512]{1,0:T(8,128)(2,1)S(1)}, bf16[256,512]{1,0:T(8,128)(2,1)S(1)}, u32[]{:S(2)}, u32[]{:S(2)}) collective-permute-start(bf16[256,512]{1,0:T(8,128)(2,1)S(1)} %get-tuple-element.165), channel_id=1, source_target_pairs={{0,3},{1,0},{2,1},{3,2},{4,7},{5,4},{6,5},{7,6},{8,11},{9,8},{10,9... | collective-permute-start | bytes 786440 | tf_op jit(solution)/shard_map/ppermute | solution.py:49
  223.4 14.7 %collective-permute-start.25 = (bf16[512,512]{1,0:T(8,128)(2,1)S(1)}, bf16[512,512]{1,0:T(8,128)(2,1)S(1)}, u32[]{:S(2)}, u32[]{:S(2)}) collective-permute-start(bf16[512,512]{1,0:T(8,128)(2,1)S(1)} %pad_maximum_fusion.6), channel_id=1, source_target_pairs={{0,4},{1,5},{2,6},{3,7},{4,8},{5,9},{6,10},{7,11},{8,12},{9,13},{1... | collective-permute-start | bytes 1572872 | tf_op jit(solution)/shard_map/ppermute | solution.py:49
  226.8 14.6 %collective-permute-start.26 = (bf16[512,512]{1,0:T(8,128)(2,1)S(1)}, bf16[512,512]{1,0:T(8,128)(2,1)S(1)}, u32[]{:S(2)}, u32[]{:S(2)}) collective-permute-start(bf16[512,512]{1,0:T(8,128)(2,1)S(1)} %pad_maximum_fusion.7), channel_id=1, source_target_pairs={{0,12},{1,13},{2,14},{3,15},{4,0},{5,1},{6,2},{7,3},{8,4},{9,5},{1... | collective-permute-start | bytes 1572872 | tf_op jit(solution)/shard_map/ppermute | solution.py:49
  227.0 14.5 %collective-permute-start.29 = (bf16[512,512]{1,0:T(8,128)(2,1)S(1)}, bf16[512,512]{1,0:T(8,128)(2,1)S(1)}, u32[]{:S(2)}, u32[]{:S(2)}) collective-permute-start(bf16[512,512]{1,0:T(8,128)(2,1)S(1)} %pad_maximum_fusion.8), channel_id=1, source_target_pairs={{0,1},{1,2},{2,3},{3,0},{4,5},{5,6},{6,7},{7,4},{8,9},{9,10},{10,1... | collective-permute-start | bytes 1572872 | tf_op jit(solution)/shard_map/ppermute | solution.py:49
  227.3 15.3 %copy-start.1 = (s32[64,4]{0,1:T(4,128)S(1)}, s32[64,4]{0,1:T(4,128)}, u32[]{:S(2)}) copy-start(s32[64,4]{0,1:T(4,128)} %param.14) | copy-start | bytes 3076
  227.4 14.1 %collective-permute-start.30 = (bf16[512,512]{1,0:T(8,128)(2,1)S(1)}, bf16[512,512]{1,0:T(8,128)(2,1)S(1)}, u32[]{:S(2)}, u32[]{:S(2)}) collective-permute-start(bf16[512,512]{1,0:T(8,128)(2,1)S(1)} %pad_maximum_fusion.9), channel_id=1, source_target_pairs={{0,3},{1,0},{2,1},{3,2},{4,7},{5,4},{6,5},{7,6},{8,11},{9,8},{10,9... | collective-permute-start | bytes 1572872 | tf_op jit(solution)/shard_map/ppermute | solution.py:49

commit v6 on v5

--- a/solution.py
+++ b/solution.py
@@ -113,17 +113,13 @@
             for a, r, _ in terms:
                 low, high = needed.get(a, (r, r + rows))
                 needed[a] = (min(low, r), max(high, r + rows))
-        low = min([p[0] for p in summed], default=0)
-        high = max([p[0] + p[2] for p in summed], default=0)
-        plans.append((direct, summed, low, high))
+        plans.append((direct, summed))
     staged = sorted(needed)
-    built = [n for n, plan in enumerate(plans) if plan[1]]
-    n_copies = len(staged) + len(built) + sum(len(plan[0]) for plan in plans)
+    n_copies = len(staged) + sum(len(plan[0]) for plan in plans)
 
     def body(*refs):
         a_refs, o_refs = refs[:n_arrays], refs[n_arrays : n_arrays + n_outputs]
         stage = dict(zip(staged, refs[n_arrays + n_outputs :]))
-        build = dict(zip(built, refs[n_arrays + n_outputs + len(staged) :]))
         sems = refs[-1]
         inward, outward = [], []
         for n, a in enumerate(staged):
@@ -132,7 +128,7 @@
                 pltpu.make_async_copy(a_refs[a].at[pl.ds(low, high - low), :], stage[a], sems.at[n])
             )
         count = len(staged)
-        for o_ref, (direct, _, _, _) in zip(o_refs, plans):
+        for o_ref, (direct, _) in zip(o_refs, plans):
             for row, _, rows, _, terms in direct:
                 source, start, _ = terms[0]
                 outward.append(
@@ -145,8 +141,7 @@
             copy.start()
         for copy in inward:
             copy.wait()
-        for n in built:
-            _, summed, first, last = plans[n]
+        for o_ref, (_, summed) in zip(o_refs, plans):
             for row, column, rows, columns, terms in summed:
                 total = None
                 for a, r, c in terms:
@@ -155,21 +150,16 @@
                     if len(terms) > 1:
                         part = part.astype(F32)
                     total = part if total is None else total + part
-                build[n][row - first : row - first + rows, column : column + columns] = total.astype(BF16)
-            copy = pltpu.make_async_copy(build[n], o_refs[n].at[pl.ds(first, last - first), :], sems.at[count])
-            copy.start()
-            outward.append(copy)
-            count += 1
+                o_ref[row : row + rows, column : column + columns] = total.astype(BF16)
         for copy in outward:
             copy.wait()
 
     scratch = [pltpu.VMEM((needed[a][1] - needed[a][0], arrays[a].shape[1]), BF16) for a in staged]
-    scratch += [pltpu.VMEM((plans[n][3] - plans[n][2], outputs[n][0][1]), BF16) for n in built]
     return pl.pallas_call(
         body,
         out_shape=[jax.ShapeDtypeStruct(shape, BF16) for shape, _ in outputs],
         in_specs=[ANYWHERE] * n_arrays,
-        out_specs=[ANYWHERE] * n_outputs,
+        out_specs=[VMEM] * n_outputs,
         scratch_shapes=[*scratch, pltpu.SemaphoreType.DMA((n_copies,))],
         compiler_params=params(6),
         cost_estimate=estimate(0, 0),
@@ -306,54 +296,6 @@
         cost_estimate=estimate(0, 0),
         name="query_part",
     )(order, *in_vmem(arrays), gain, w_query, *in_vmem(carried))
-
-
-def in_hbm(arrays):
-    return [pltpu.with_memory_space_constraint(a, pltpu.HBM) for a in arrays]
-
-
-def cut_cache(cache, head):
-    shape = (*cache.shape[:3], HD)
-
-    def body(head_ref, c_ref, o_ref, sem):
-        column = pl.multiple_of(head_ref[0] * HD, HD)
-        copy = pltpu.make_async_copy(c_ref.at[:, :, :, pl.ds(column, HD)], o_ref, sem)
-        copy.start()
-        copy.wait()
-
-    return pl.pallas_call(
-        body,
-        out_shape=pltpu.HBM(shape, BF16),
-        in_specs=[SMEM, FIXED],
-        out_specs=FIXED,
-        scratch_shapes=[pltpu.SemaphoreType.DMA],
-        compiler_params=params(2),
-        cost_estimate=estimate(0, 0),
-        name="cut_cache",
-    )(head, *in_hbm([cache]))
-
-
-def join_cache(parts):
-    def body(one_ref, two_ref, o_ref, sems):
-        copies = [
-            pltpu.make_async_copy(ref, o_ref.at[n], sems.at[n])
-            for n, ref in enumerate((one_ref, two_ref))
-        ]
-        for copy in copies:
-            copy.start()
-        for copy in copies:
-            copy.wait()
-
-    return pl.pallas_call(
-        body,
-        out_shape=pltpu.HBM((2, *parts[0].shape), BF16),
-        in_specs=[FIXED, FIXED],
-        out_specs=FIXED,
-        scratch_shapes=[pltpu.SemaphoreType.DMA((2,))],
-        compiler_params=params(2),
-        cost_estimate=estimate(0, 0),
-        name="join_cache",
-    )(*in_hbm(parts))
 
 
 def gather_blocks(pools, codes):
@@ -560,7 +502,7 @@
         "first",
     )
     kv_head = place * (w_query.shape[1] // HD) // (HEADS // KVH)
-    cache_head = cut_cache(cache, kv_head.reshape(1))
+    cache_head = lax.dynamic_slice_in_dim(cache, kv_head * HD, HD, 3)
     z_one = hop(cache_head, "z_one", 1)
     part = query_part(
         [((0, 0), [(0, 0, 0, WIDE)]), ((1, 0), [(1, 0, 0, WIDE)]), ((3, 0), [(2, 0, 0, WIDE)])],
@@ -570,7 +512,7 @@
         w_query,
         None,
     )
-    pool = join_cache([cache_head, z_one])
+    pool = jnp.stack([cache_head, z_one])
     b3m, b3p, b2m, b2p, pool, *part = bar((*s3, *s2, pool, *part))
     (to_next,) = assemble(
         [b3m, b3p, kv_0, b2m],

time: 243 us -> 163 us (0.67)
  Pallas kernels: 142 us -> 45.7 us
  waiting for transfers between devices: 44.3 us -> 52.3 us
  local copies, waits for them, and re-layouts: 4.27 us -> 10.4 us
    pallas_call x2 -> x0, Pallas kernels: 49.9 us -> none  [the longest x1 32.9 us: join_cache(): pl.pallas_call(body, out_shape=pltpu.HBM((2, *parts[0].shape), BF16), in_...]
    pallas_call x7, Pallas kernels: 55.1 us -> 8.48 us  [assemble(): pl.pallas_call(body, out_shape=[jax.ShapeDtypeStruct(shape, BF16) for sha...]
    ppermute x31, waiting for transfers between devices: 44.3 us -> 52.3 us  [hop(): return lax.ppermute(value, AXES, HOPS[axis, step])]
    unnamed x25 -> x27, local copies, waits for them, and re-layouts: 2.96 us -> 6.94 us
  transfers between devices with their start and end apart: 31 -> 31, of which waited for: 11 -> 14; matrix products, arithmetic and copies ran while one was open for 1% -> 4% of each run, Pallas kernels for 45% -> 22%
where the time goes in v6:
time: 163 us; the launch traced here: 162 us
  waiting for transfers between devices  52.3 us (32%)
  starting transfers between devices  47.7 us (29%)
  Pallas kernels  45.7 us (28%)
  local copies, waits for them, and re-layouts  10.4 us (6%)
  other arithmetic  5.44 us (3%)
    ppermute x31, waiting for transfers between devices, hop(): return lax.ppermute(value, AXES, HOPS[axis, step])  52.3 us
    ppermute x31, starting transfers between devices, hop(): return lax.ppermute(value, AXES, HOPS[axis, step])  47.7 us
    pallas_call x4, Pallas kernels, query_part(): pl.pallas_call(body, out_shape=(jax.ShapeDtypeStruct((WIDE, WIDE), F32),...  16.8 us
    pallas_call x2, Pallas kernels, output_part(): pl.pallas_call(body, out_shape=jax.ShapeDtypeStruct((count, WIDE, WIDE),...  8.55 us
    pallas_call x7, Pallas kernels, assemble(): pl.pallas_call(body, out_shape=[jax.ShapeDtypeStruct(shape, BF16) for sha...  8.48 us
    unnamed x27, local copies, waits for them, and re-layouts  6.94 us
    pallas_call x1, Pallas kernels, middle(): pl.pallas_call(body, out_shape=(jax.ShapeDtypeStruct((WIDE, WIDE), BF16),...  6.06 us
    pallas_call x1, Pallas kernels, kv_partial(): pl.pallas_call(body, out_shape=[jax.ShapeDtypeStruct((WIDE, WIDE), BF16)]...  3.62 us
  transfers between devices with their start and end apart: 31, of which 14 were waited for; matrix products, arithmetic and copies ran while one was open for 4% of the time, Pallas kernels for 22%

profile of v6, /device:TPU:6, one launch (start us, length us, event | category | flops | bytes accessed | tf_op | source)
XLA Modules:
  0.0 162.1 jit_solution(10402952048908230465)
XLA Ops:
  0.0 1.6 collective-permute-start
  1.6 1.7 %collective-permute-start.1 = (bf16[512,512]{1,0:T(8,128)(2,1)}, bf16[512,512]{1,0:T(8,128)(2,1)S(1)}, u32[]{:S(2)}, u32[]{:S(2)}) collective-permute-start(bf16[512,512]{1,0:T(8,128)(2,1)} %refs_0_.3), channel_id=1, source_target_pairs={{0,3},{1,0},{2,1},{3,2},{4,7},{5,4},{6,5},{7,6},{8,11},{9,8},{10,9... | collective-permute-start | bytes 1572872 | tf_op jit(solution)/shard_map/ppermute | solution.py:49
  4.0 1.0 copy-done.6
  5.0 3.6 %kv_partial.1 = (bf16[512,512]{1,0:T(8,128)(2,1)S(1)}, bf16[512,512]{1,0:T(8,128)(2,1)S(1)}, bf16[512,512]{1,0:T(8,128)(2,1)S(1)}, bf16[512,512]{1,0:T(8,128)(2,1)S(1)}) custom-call(s32[16]{0:T(128)S(1)} %fusion.29.order_ref, bf16[512,512]{1,0:T(8,128)(2,1)S(1)} %copy-done.6, f32[16,512]{1,0:T(8,128)S(1)} %reshape.77.g_ref.refs_3_.refs_4_.refs_2_, ...), custom_call_target="tpu_custom_call" | custom-call | tf_op jit(solution)/shard_map/kv_partial/pallas_call | solution.py:211
  9.1 2.9 %collective-permute-start.3 = (bf16[256,512]{1,0:T(8,128)(2,1)S(1)}, bf16[256,512]{1,0:T(8,128)(2,1)S(1)}, u32[]{:S(2)}, u32[]{:S(2)}) collective-permute-start(bf16[256,512]{1,0:T(8,128)(2,1)S(1)} %get-tuple-element.167), channel_id=1, source_target_pairs={{0,3},{1,0},{2,1},{3,2},{4,7},{5,4},{6,5},{7,6},{8,11},{9,8},{10,9... | collective-permute-start | bytes 786440 | tf_op jit(solution)/shard_map/ppermute | solution.py:49
  12.0 4.3 %collective-permute-done.2.refs_4_ = bf16[256,512]{1,0:T(8,128)(2,1)S(1)} collective-permute-done((bf16[256,512]{1,0:T(8,128)(2,1)S(1)}, bf16[256,512]{1,0:T(8,128)(2,1)S(1)}, u32[]{:S(2)}, u32[]{:S(2)}) %collective-permute-start.2) | collective-permute-done | bytes 262176 | tf_op jit(solution)/shard_map/ppermute | solution.py:49
  17.1 1.4 assemble.8
  19.0 1.6 %collective-permute-start.7 = (bf16[1536,512]{1,0:T(8,128)(2,1)}, bf16[1536,512]{1,0:T(8,128)(2,1)}, u32[]{:S(2)}, u32[]{:S(2)}) collective-permute-start(bf16[1536,512]{1,0:T(8,128)(2,1)} %assemble.8), channel_id=1, source_target_pairs={{0,12},{1,13},{2,14},{3,15},{4,0},{5,1},{6,2},{7,3},{8,4},{9,5},{1... | collective-permute-start | bytes 4718600 | tf_op jit(solution)/shard_map/ppermute | solution.py:49
  22.7 2.6 %collective-permute-start.5 = (bf16[768,512]{1,0:T(8,128)(2,1)S(1)}, bf16[768,512]{1,0:T(8,128)(2,1)S(1)}, u32[]{:S(2)}, u32[]{:S(2)}) collective-permute-start(bf16[768,512]{1,0:T(8,128)(2,1)S(1)} %get-tuple-element.80), channel_id=1, source_target_pairs={{0,3},{1,0},{2,1},{3,2},{4,7},{5,4},{6,5},{7,6},{8,11},{9,8},{10,9... | collective-permute-start | bytes 2359304 | tf_op jit(solution)/shard_map/ppermute | solution.py:49
  25.3 1.1 constant_dynamic-slice_fusion.1
  26.4 2.0 %collective-permute-start.8 = (bf16[2,16,64,128]{3,2,1,0:T(8,128)(2,1)S(1)}, bf16[2,16,64,128]{3,2,1,0:T(8,128)(2,1)S(1)}, u32[]{:S(2)}, u32[]{:S(2)}) collective-permute-start(bf16[2,16,64,128]{3,2,1,0:T(8,128)(2,1)S(1)} %constant_dynamic-slice_fusion.1), channel_id=1, source_target_pairs={{0,32},{1,33},{2,34},{3,35},{4,36},{5,37},{6,38},{7,39},{8,40},{9,... | collective-permute-start | bytes 1572872 | tf_op jit(solution)/shard_map/ppermute | solution.py:49
  28.4 1.0 copy-done.3
  29.4 1.0 copy-done.5
  30.5 1.0 copy-done.8
  31.5 3.0 %query_part.4 = (f32[512,512]{1,0:T(8,128)S(1)}, f32[512,128]{1,0:T(8,128)S(1)}) custom-call(s32[16]{0:T(128)S(1)} %fusion.29.order_ref, bf16[512,512]{1,0:T(8,128)(2,1)S(1)} %copy-done.8, bf16[512,512]{1,0:T(8,128)(2,1)S(1)} %copy-done.5, bf16[512,512]{1,0:T(8,128)(2,1)S(1)} %copy-done.3, f32[16,512]{1,0:T(8,128)S(1)} %reshape.77.g_ref.refs_3_.refs_4_.refs_2_, ...), custom_call_target="tpu_custom_call" | custom-call | tf_op jit(solution)/shard_map/query_part/pallas_call | solution.py:281
  34.5 1.1 fusion.37
  35.7 1.1 pad_maximum_fusion.refs_0_
  36.7 7.0 %collective-permute-done.4.refs_0_.refs_1_ = bf16[768,512]{1,0:T(8,128)(2,1)S(1)} collective-permute-done((bf16[768,512]{1,0:T(8,128)(2,1)S(1)}, bf16[768,512]{1,0:T(8,128)(2,1)S(1)}, u32[]{:S(2)}, u32[]{:S(2)}) %collective-permute-start.4) | collective-permute-done | bytes 786464 | tf_op jit(solution)/shard_map/ppermute | solution.py:49
  43.7 4.0 %collective-permute-done.6.refs_3_ = bf16[1536,512]{1,0:T(8,128)(2,1)} collective-permute-done((bf16[1536,512]{1,0:T(8,128)(2,1)}, bf16[1536,512]{1,0:T(8,128)(2,1)}, u32[]{:S(2)}, u32[]{:S(2)}) %collective-permute-start.6) | collective-permute-done | bytes 1572896 | tf_op jit(solution)/shard_map/ppermute | solution.py:49
  47.7 1.6 collective-permute-done.7.refs_3_.refs_2_
  49.3 2.3 %assemble.10 = bf16[1344,512]{1,0:T(8,128)(2,1)} custom-call(bf16[768,512]{1,0:T(8,128)(2,1)S(1)} %collective-permute-done.4.refs_0_.refs_1_, bf16[768,512]{1,0:T(8,128)(2,1)S(1)} %collective-permute-done.5.refs_1_.refs_2_, bf16[512,512]{1,0:T(8,128)(2,1)S(1)} %get-tuple-element.86.refs_2_.refs_0_, bf16[1536,512]{1,0:T(8,128)(2,1)} %collective-permute-done.7.refs_3_.refs_2_), custom_call_target="tpu_custom_call" | custom-call | tf_op jit(solution)/shard_map/assemble/pallas_call | solution.py:158
  52.2 2.5 %assemble.9 = bf16[1344,512]{1,0:T(8,128)(2,1)} custom-call(bf16[768,512]{1,0:T(8,128)(2,1)S(1)} %collective-permute-done.4.refs_0_.refs_1_, bf16[768,512]{1,0:T(8,128)(2,1)S(1)} %collective-permute-done.5.refs_1_.refs_2_, bf16[512,512]{1,0:T(8,128)(2,1)S(1)} %get-tuple-element.86.refs_2_.refs_0_, bf16[1536,512]{1,0:T(8,128)(2,1)} %collective-permute-done.6.refs_3_), custom_call_target="tpu_custom_call" | custom-call | tf_op jit(solution)/shard_map/assemble/pallas_call | solution.py:158
  54.7 2.9 %collective-permute-start.9 = (bf16[1344,512]{1,0:T(8,128)(2,1)}, bf16[1344,512]{1,0:T(8,128)(2,1)}, u32[]{:S(2)}, u32[]{:S(2)}) collective-permute-start(bf16[1344,512]{1,0:T(8,128)(2,1)} %assemble.9), channel_id=1, source_target_pairs={{0,4},{1,5},{2,6},{3,7},{4,8},{5,9},{6,10},{7,11},{8,12},{9,13},{1... | collective-permute-start | bytes 4128776 | tf_op jit(solution)/shard_map/ppermute | solution.py:49
  57.5 4.1 %collective-permute-start.11 = (bf16[2,2,16,64,128]{4,3,2,1,0:T(8,128)(2,1)}, bf16[2,2,16,64,128]{4,3,2,1,0:T(8,128)(2,1)}, u32[]{:S(2)}, u32[]{:S(2)}) collective-permute-start(bf16[2,2,16,64,128]{4,3,2,1,0:T(8,128)(2,1)} %pad_maximum_fusion.refs_0_), channel_id=1, source_target_pairs={{0,96},{1,97},{2,98},{3,99},{4,100},{5,101},{6,102},{7,103},{8,104... | collective-permute-start | bytes 3145736 | tf_op jit(solution)/shard_map/ppermute | solution.py:49
  63.7 6.5 %query_part.5 = (f32[512,512]{1,0:T(8,128)S(1)}, f32[512,128]{1,0:T(8,128)S(1)}) custom-call(s32[16]{0:T(128)S(1)} %fusion.29.order_ref, bf16[768,512]{1,0:T(8,128)(2,1)S(1)} %collective-permute-done.4.refs_0_.refs_1_, bf16[768,512]{1,0:T(8,128)(2,1)S(1)} %collective-permute-done.5.refs_1_.refs_2_, ...), custom_call_target="tpu_custom_call", output_to_operand_aliasing={{0}: (7, {}), {1}: (8, {})} | custom-call | tf_op jit(solution)/shard_map/query_part/pallas_call | solution.py:281
  70.1 4.6 %collective-permute-done.11.refs_1_ = bf16[2,2,16,64,128]{4,3,2,1,0:T(8,128)(2,1)} collective-permute-done((bf16[2,2,16,64,128]{4,3,2,1,0:T(8,128)(2,1)}, bf16[2,2,16,64,128]{4,3,2,1,0:T(8,128)(2,1)}, u32[]{:S(2)}, u32[]{:S(2)}) %collective-permute-start.11) | collective-permute-done | bytes 1048608 | tf_op jit(solution)/shard_map/ppermute | solution.py:49
  74.9 1.2 assemble.12
  76.0 2.6 %collective-permute-start.13 = (bf16[384,512]{1,0:T(8,128)(2,1)S(1)}, bf16[384,512]{1,0:T(8,128)(2,1)S(1)}, u32[]{:S(2)}, u32[]{:S(2)}) collective-permute-start(bf16[384,512]{1,0:T(8,128)(2,1)S(1)} %get-tuple-element.97), channel_id=1, source_target_pairs={{0,4},{1,5},{2,6},{3,7},{4,8},{5,9},{6,10},{7,11},{8,12},{9,13},{1... | collective-permute-start | bytes 1179656 | tf_op jit(solution)/shard_map/ppermute | solution.py:49
  78.6 5.3 %query_part.6 = (f32[512,512]{1,0:T(8,128)S(1)}, f32[512,128]{1,0:T(8,128)S(1)}) custom-call(s32[16]{0:T(128)S(1)} %fusion.29.order_ref, bf16[1344,512]{1,0:T(8,128)(2,1)} %collective-permute-done.10.refs_1_.refs_0_, bf16[1344,512]{1,0:T(8,128)(2,1)} %collective-permute-done.9.refs_0_.refs_1_, ...), custom_call_target="tpu_custom_call", output_to_operand_aliasing={{0}: (5, {}), {1}: (6, {})} | custom-call | tf_op jit(solution)/shard_map/query_part/pallas_call | solution.py:281
  85.0 2.2 %gather_blocks.1.prefix_ref = bf16[8,2,320,128]{3,2,1,0:T(8,128)(2,1)S(1)} custom-call(s32[8,4]{1,0:T(8,128)S(1)} %fusion.25.code_ref, bf16[2,2,16,64,128]{4,3,2,1,0:T(8,128)(2,1)} %pad_maximum_fusion.refs_0_, bf16[2,2,16,64,128]{4,3,2,1,0:T(8,128)(2,1)} %collective-permute-done.11.refs_1_, bf16[2,2,16,64,128]{4,3,2,1,0:T(8,128)(2,1)} %collective-permute-done.12.refs_2_, ...), custom_call_target="tpu_custom_call" | custom-call | tf_op jit(solution)/shard_map/gather_blocks/pallas_call | solution.py:325
  89.0 2.0 %query_part.7 = (f32[512,512]{1,0:T(8,128)S(1)}, f32[512,128]{1,0:T(8,128)S(1)}) custom-call(s32[16]{0:T(128)S(1)} %fusion.29.order_ref, bf16[384,512]{1,0:T(8,128)(2,1)S(1)} %collective-permute-done.13.refs_0_.refs_1_, bf16[384,512]{1,0:T(8,128)(2,1)S(1)} %collective-permute-done.14.refs_1_.refs_2_, ...), custom_call_target="tpu_custom_call", output_to_operand_aliasing={{0}: (5, {}), {1}: (6, {})} | custom-call | tf_op jit(solution)/shard_map/query_part/pallas_call | solution.py:281
  91.0 3.0 %collective-permute-done.16.other_ref = bf16[512,128]{1,0:T(8,128)(2,1)S(1)} collective-permute-done((bf16[512,128]{1,0:T(8,128)(2,1)S(1)}, bf16[512,128]{1,0:T(8,128)(2,1)S(1)}, u32[]{:S(2)}, u32[]{:S(2)}) %collective-permute-start.16) | collective-permute-done | bytes 131104 | tf_op jit(solution)/shard_map/ppermute | solution.py:49
  94.0 6.1 %middle.1 = (bf16[512,512]{1,0:T(8,128)(2,1)S(1)}, bf16[4,512,512]{2,1,0:T(8,128)(2,1)S(1)}, bf16[8,2,320,128]{3,2,1,0:T(8,128)(2,1)S(1)}) custom-call(s32[16]{0:T(128)S(1)} %fusion.29.order_ref, s32[8]{0:T(128)S(1)} %get-tuple-element.134.len_ref, f32[512,512]{1,0:T(8,128)S(1)} %get-tuple-element.110.q_ref, ...), custom_call_target="tpu_custom_call", output_to_operand_aliasing={{2}: (8, {})} | custom-call | tf_op jit(solution)/shard_map/middle/pallas_call | solution.py:398
  100.4 3.3 %collective-permute-start.21 = (bf16[768,512]{1,0:T(8,128)(2,1)S(1)}, bf16[768,512]{1,0:T(8,128)(2,1)S(1)}, u32[]{:S(2)}, u32[]{:S(2)}) collective-permute-start(bf16[768,512]{1,0:T(8,128)(2,1)S(1)} %pad_maximum_fusion.3), channel_id=1, source_target_pairs={{0,4},{1,5},{2,6},{3,7},{4,8},{5,9},{6,10},{7,11},{8,12},{9,13},{1... | collective-permute-start | bytes 2359304 | tf_op jit(solution)/shard_map/ppermute | solution.py:49
  103.7 1.4 collective-permute-start.17
  105.8 4.3 %output_part.2 = bf16[6,512,512]{2,1,0:T(8,128)(2,1)S(1)} custom-call(s32[16]{0:T(128)S(1)} %fusion.29.order_ref, bf16[512,512]{1,0:T(8,128)(2,1)S(1)} %get-tuple-element.121.h_ref, bf16[512,8192]{1,0:T(8,128)(2,1)} %w_ref.5), custom_call_target="tpu_custom_call" | custom-call | tf_op jit(solution)/shard_map/output_part/pallas_call | solution.py:437
  110.0 6.0 %collective-permute-done.17 = bf16[256,512]{1,0:T(8,128)(2,1)S(1)} collective-permute-done((bf16[256,512]{1,0:T(8,128)(2,1)S(1)}, bf16[256,512]{1,0:T(8,128)(2,1)S(1)}, u32[]{:S(2)}, u32[]{:S(2)}) %collective-permute-start.17) | collective-permute-done | bytes 262176 | tf_op jit(solution)/shard_map/ppermute | solution.py:49
  118.1 2.5 %collective-permute-start.19 = (bf16[512,512]{1,0:T(8,128)(2,1)S(1)}, bf16[512,512]{1,0:T(8,128)(2,1)S(1)}, u32[]{:S(2)}, u32[]{:S(2)}) collective-permute-start(bf16[512,512]{1,0:T(8,128)(2,1)S(1)} %pad_maximum_fusion.5), channel_id=1, source_target_pairs={{0,4},{1,5},{2,6},{3,7},{4,8},{5,9},{6,10},{7,11},{8,12},{9,13},{1... | collective-permute-start | bytes 1572872 | tf_op jit(solution)/shard_map/ppermute | solution.py:49
  120.9 3.5 %collective-permute-start.27 = (bf16[1024,512]{1,0:T(8,128)(2,1)S(1)}, bf16[1024,512]{1,0:T(8,128)(2,1)S(1)}, u32[]{:S(2)}, u32[]{:S(2)}) collective-permute-start(bf16[1024,512]{1,0:T(8,128)(2,1)S(1)} %pad_maximum_fusion.1), channel_id=1, source_target_pairs={{0,4},{1,5},{2,6},{3,7},{4,8},{5,9},{6,10},{7,11},{8,12},{9,13},{1... | collective-permute-start | bytes 3145736 | tf_op jit(solution)/shard_map/ppermute | solution.py:49
  124.4 4.3 %output_part.3 = bf16[6,512,512]{2,1,0:T(8,128)(2,1)S(1)} custom-call(s32[16]{0:T(128)S(1)} %fusion.29.order_ref, bf16[512,512]{1,0:T(8,128)(2,1)S(1)} %get-tuple-element.121.h_ref, bf16[512,8192]{1,0:T(8,128)(2,1)} %w_ref.5), custom_call_target="tpu_custom_call" | custom-call | tf_op jit(solution)/shard_map/output_part/pallas_call | solution.py:437
  129.3 3.0 %collective-permute-start.24 = (bf16[256,512]{1,0:T(8,128)(2,1)S(1)}, bf16[256,512]{1,0:T(8,128)(2,1)S(1)}, u32[]{:S(2)}, u32[]{:S(2)}) collective-permute-start(bf16[256,512]{1,0:T(8,128)(2,1)S(1)} %get-tuple-element.165), channel_id=1, source_target_pairs={{0,3},{1,0},{2,1},{3,2},{4,7},{5,4},{6,5},{7,6},{8,11},{9,8},{10,9... | collective-permute-start | bytes 786440 | tf_op jit(solution)/shard_map/ppermute | solution.py:49
  132.3 7.2 %collective-permute-done.23 = bf16[256,512]{1,0:T(8,128)(2,1)S(1)} collective-permute-done((bf16[256,512]{1,0:T(8,128)(2,1)S(1)}, bf16[256,512]{1,0:T(8,128)(2,1)S(1)}, u32[]{:S(2)}, u32[]{:S(2)}) %collective-permute-start.23) | collective-permute-done | bytes 262176 | tf_op jit(solution)/shard_map/ppermute | solution.py:49
  139.5 2.3 %collective-permute-done.28 = bf16[1024,512]{1,0:T(8,128)(2,1)S(1)} collective-permute-done((bf16[1024,512]{1,0:T(8,128)(2,1)S(1)}, bf16[1024,512]{1,0:T(8,128)(2,1)S(1)}, u32[]{:S(2)}, u32[]{:S(2)}) %collective-permute-start.28) | collective-permute-done | bytes 1048608 | tf_op jit(solution)/shard_map/ppermute | solution.py:49
  142.5 3.4 %collective-permute-start.25 = (bf16[512,512]{1,0:T(8,128)(2,1)S(1)}, bf16[512,512]{1,0:T(8,128)(2,1)S(1)}, u32[]{:S(2)}, u32[]{:S(2)}) collective-permute-start(bf16[512,512]{1,0:T(8,128)(2,1)S(1)} %pad_maximum_fusion.7), channel_id=1, source_target_pairs={{0,4},{1,5},{2,6},{3,7},{4,8},{5,9},{6,10},{7,11},{8,12},{9,13},{1... | collective-permute-start | bytes 1572872 | tf_op jit(solution)/shard_map/ppermute | solution.py:49
  146.5 3.0 %collective-permute-start.30 = (bf16[512,512]{1,0:T(8,128)(2,1)S(1)}, bf16[512,512]{1,0:T(8,128)(2,1)S(1)}, u32[]{:S(2)}, u32[]{:S(2)}) collective-permute-start(bf16[512,512]{1,0:T(8,128)(2,1)S(1)} %pad_maximum_fusion.10), channel_id=1, source_target_pairs={{0,3},{1,0},{2,1},{3,2},{4,7},{5,4},{6,5},{7,6},{8,11},{9,8},{10,9... | collective-permute-start | bytes 1572872 | tf_op jit(solution)/shard_map/ppermute | solution.py:49
  149.5 7.9 %collective-permute-done.25 = bf16[512,512]{1,0:T(8,128)(2,1)S(1)} collective-permute-done((bf16[512,512]{1,0:T(8,128)(2,1)S(1)}, bf16[512,512]{1,0:T(8,128)(2,1)S(1)}, u32[]{:S(2)}, u32[]{:S(2)}) %collective-permute-start.25) | collective-permute-done | bytes 524320 | tf_op jit(solution)/shard_map/ppermute | solution.py:49
  157.4 3.5 %collective-permute-done.26 = bf16[512,512]{1,0:T(8,128)(2,1)S(1)} collective-permute-done((bf16[512,512]{1,0:T(8,128)(2,1)S(1)}, bf16[512,512]{1,0:T(8,128)(2,1)S(1)}, u32[]{:S(2)}, u32[]{:S(2)}) %collective-permute-start.26) | collective-permute-done | bytes 524320 | tf_op jit(solution)/shard_map/ppermute | solution.py:49
  161.0 1.1 fusion.5
  (89 shorter events, 15.0 us)
Async XLA Ops:
  0.0 61.7 %copy-start = (s32[64,4]{0,1:T(4,128)S(1)}, s32[64,4]{0,1:T(4,128)}, u32[]{:S(2)}) copy-start(s32[64,4]{0,1:T(4,128)} %param.14) | copy-start | bytes 3076
  0.0 17.1 %collective-permute-start = (bf16[512,512]{1,0:T(8,128)(2,1)}, bf16[512,512]{1,0:T(8,128)(2,1)S(1)}, u32[]{:S(2)}, u32[]{:S(2)}) collective-permute-start(bf16[512,512]{1,0:T(8,128)(2,1)} %refs_0_.3), channel_id=1, source_target_pairs={{0,1},{1,2},{2,3},{3,0},{4,5},{5,6},{6,7},{7,4},{8,9},{9,10},{10,1... | collective-permute-start | bytes 1572872 | tf_op jit(solution)/shard_map/ppermute | solution.py:49
  1.6 15.5 %collective-permute-start.1 = (bf16[512,512]{1,0:T(8,128)(2,1)}, bf16[512,512]{1,0:T(8,128)(2,1)S(1)}, u32[]{:S(2)}, u32[]{:S(2)}) collective-permute-start(bf16[512,512]{1,0:T(8,128)(2,1)} %refs_0_.3), channel_id=1, source_target_pairs={{0,3},{1,0},{2,1},{3,2},{4,7},{5,4},{6,5},{7,6},{8,11},{9,8},{10,9... | collective-permute-start | bytes 1572872 | tf_op jit(solution)/shard_map/ppermute | solution.py:49
  4.0 1.0 copy-start.6
  5.0 12.1 %copy-start.7 = (bf16[512,512]{1,0:T(8,128)(2,1)S(1)}, bf16[512,512]{1,0:T(8,128)(2,1)}, u32[]{:S(2)}) copy-start(bf16[512,512]{1,0:T(8,128)(2,1)} %refs_0_.3) | copy-start | bytes 1572868
  8.7 7.7 %collective-permute-start.2 = (bf16[256,512]{1,0:T(8,128)(2,1)S(1)}, bf16[256,512]{1,0:T(8,128)(2,1)S(1)}, u32[]{:S(2)}, u32[]{:S(2)}) collective-permute-start(bf16[256,512]{1,0:T(8,128)(2,1)S(1)} %get-tuple-element.168), channel_id=1, source_target_pairs={{0,1},{1,2},{2,3},{3,0},{4,5},{5,6},{6,7},{7,4},{8,9},{9,10},{10,1... | collective-permute-start | bytes 786440 | tf_op jit(solution)/shard_map/ppermute | solution.py:49
  9.1 7.2 %collective-permute-start.3 = (bf16[256,512]{1,0:T(8,128)(2,1)S(1)}, bf16[256,512]{1,0:T(8,128)(2,1)S(1)}, u32[]{:S(2)}, u32[]{:S(2)}) collective-permute-start(bf16[256,512]{1,0:T(8,128)(2,1)S(1)} %get-tuple-element.167), channel_id=1, source_target_pairs={{0,3},{1,0},{2,1},{3,2},{4,7},{5,4},{6,5},{7,6},{8,11},{9,8},{10,9... | collective-permute-start | bytes 786440 | tf_op jit(solution)/shard_map/ppermute | solution.py:49
  16.4 0.7 copy-start.9
  17.1 4.8 %copy-start.2 = (bf16[512,512]{1,0:T(8,128)(2,1)}, bf16[512,512]{1,0:T(8,128)(2,1)S(1)}, u32[]{:S(2)}) copy-start(bf16[512,512]{1,0:T(8,128)(2,1)S(1)} %collective-permute-done.refs_0_.refs_2_) | copy-start | bytes 1572868
  17.1 4.8 %copy-start.4 = (bf16[512,512]{1,0:T(8,128)(2,1)}, bf16[512,512]{1,0:T(8,128)(2,1)S(1)}, u32[]{:S(2)}) copy-start(bf16[512,512]{1,0:T(8,128)(2,1)S(1)} %collective-permute-done.1.refs_1_) | copy-start | bytes 1572868
  18.5 29.2 %collective-permute-start.6 = (bf16[1536,512]{1,0:T(8,128)(2,1)}, bf16[1536,512]{1,0:T(8,128)(2,1)}, u32[]{:S(2)}, u32[]{:S(2)}) collective-permute-start(bf16[1536,512]{1,0:T(8,128)(2,1)} %assemble.8), channel_id=1, source_target_pairs={{0,4},{1,5},{2,6},{3,7},{4,8},{5,9},{6,10},{7,11},{8,12},{9,13},{1... | collective-permute-start | bytes 4718600 | tf_op jit(solution)/shard_map/ppermute | solution.py:49
  19.0 30.4 %collective-permute-start.7 = (bf16[1536,512]{1,0:T(8,128)(2,1)}, bf16[1536,512]{1,0:T(8,128)(2,1)}, u32[]{:S(2)}, u32[]{:S(2)}) collective-permute-start(bf16[1536,512]{1,0:T(8,128)(2,1)} %assemble.8), channel_id=1, source_target_pairs={{0,12},{1,13},{2,14},{3,15},{4,0},{5,1},{6,2},{7,3},{8,4},{9,5},{1... | collective-permute-start | bytes 4718600 | tf_op jit(solution)/shard_map/ppermute | solution.py:49
  20.6 0.9 copy-start.10
  21.9 21.8 %collective-permute-start.4 = (bf16[768,512]{1,0:T(8,128)(2,1)S(1)}, bf16[768,512]{1,0:T(8,128)(2,1)S(1)}, u32[]{:S(2)}, u32[]{:S(2)}) collective-permute-start(bf16[768,512]{1,0:T(8,128)(2,1)S(1)} %get-tuple-element.79), channel_id=1, source_target_pairs={{0,1},{1,2},{2,3},{3,0},{4,5},{5,6},{6,7},{7,4},{8,9},{9,10},{10,1... | collective-permute-start | bytes 2359304 | tf_op jit(solution)/shard_map/ppermute | solution.py:49
  22.7 21.0 %collective-permute-start.5 = (bf16[768,512]{1,0:T(8,128)(2,1)S(1)}, bf16[768,512]{1,0:T(8,128)(2,1)S(1)}, u32[]{:S(2)}, u32[]{:S(2)}) collective-permute-start(bf16[768,512]{1,0:T(8,128)(2,1)S(1)} %get-tuple-element.80), channel_id=1, source_target_pairs={{0,3},{1,0},{2,1},{3,2},{4,7},{5,4},{6,5},{7,6},{8,11},{9,8},{10,9... | collective-permute-start | bytes 2359304 | tf_op jit(solution)/shard_map/ppermute | solution.py:49
  26.4 9.3 %collective-permute-start.8 = (bf16[2,16,64,128]{3,2,1,0:T(8,128)(2,1)S(1)}, bf16[2,16,64,128]{3,2,1,0:T(8,128)(2,1)S(1)}, u32[]{:S(2)}, u32[]{:S(2)}) collective-permute-start(bf16[2,16,64,128]{3,2,1,0:T(8,128)(2,1)S(1)} %constant_dynamic-slice_fusion.1), channel_id=1, source_target_pairs={{0,32},{1,33},{2,34},{3,35},{4,36},{5,37},{6,38},{7,39},{8,40},{9,... | collective-permute-start | bytes 1572872 | tf_op jit(solution)/shard_map/ppermute | solution.py:49
  28.4 1.0 copy-start.3
  29.4 1.0 copy-start.5
  30.5 1.0 copy-start.8
  51.7 10.1 %copy-start.12 = (s32[64]{0:T(128)S(1)}, s32[64]{0:T(128)}, u32[]{:S(2)}) copy-start(s32[64]{0:T(128)} %param.15) | copy-start | bytes 772
  51.7 23.1 %collective-permute-start.10 = (bf16[1344,512]{1,0:T(8,128)(2,1)}, bf16[1344,512]{1,0:T(8,128)(2,1)}, u32[]{:S(2)}, u32[]{:S(2)}) collective-permute-start(bf16[1344,512]{1,0:T(8,128)(2,1)} %assemble.10), channel_id=1, source_target_pairs={{0,12},{1,13},{2,14},{3,15},{4,0},{5,1},{6,2},{7,3},{8,4},{9,5},{1... | collective-permute-start | bytes 4128776 | tf_op jit(solution)/shard_map/ppermute | solution.py:49
  54.7 20.1 %collective-permute-start.9 = (bf16[1344,512]{1,0:T(8,128)(2,1)}, bf16[1344,512]{1,0:T(8,128)(2,1)}, u32[]{:S(2)}, u32[]{:S(2)}) collective-permute-start(bf16[1344,512]{1,0:T(8,128)(2,1)} %assemble.9), channel_id=1, source_target_pairs={{0,4},{1,5},{2,6},{3,7},{4,8},{5,9},{6,10},{7,11},{8,12},{9,13},{1... | collective-permute-start | bytes 4128776 | tf_op jit(solution)/shard_map/ppermute | solution.py:49
  57.5 17.2 %collective-permute-start.11 = (bf16[2,2,16,64,128]{4,3,2,1,0:T(8,128)(2,1)}, bf16[2,2,16,64,128]{4,3,2,1,0:T(8,128)(2,1)}, u32[]{:S(2)}, u32[]{:S(2)}) collective-permute-start(bf16[2,2,16,64,128]{4,3,2,1,0:T(8,128)(2,1)} %pad_maximum_fusion.refs_0_), channel_id=1, source_target_pairs={{0,96},{1,97},{2,98},{3,99},{4,100},{5,101},{6,102},{7,103},{8,104... | collective-permute-start | bytes 3145736 | tf_op jit(solution)/shard_map/ppermute | solution.py:49
  61.7 13.1 %collective-permute-start.12 = (bf16[2,2,16,64,128]{4,3,2,1,0:T(8,128)(2,1)}, bf16[2,2,16,64,128]{4,3,2,1,0:T(8,128)(2,1)}, u32[]{:S(2)}, u32[]{:S(2)}) collective-permute-start(bf16[2,2,16,64,128]{4,3,2,1,0:T(8,128)(2,1)} %pad_maximum_fusion.refs_0_), channel_id=1, source_target_pairs={{0,16},{1,17},{2,18},{3,19},{4,20},{5,21},{6,22},{7,23},{8,24},{9,... | collective-permute-start | bytes 3145736 | tf_op jit(solution)/shard_map/ppermute | solution.py:49
  74.8 9.2 %collective-permute-start.15 = (bf16[2,2,16,64,128]{4,3,2,1,0:T(8,128)(2,1)}, bf16[2,2,16,64,128]{4,3,2,1,0:T(8,128)(2,1)S(1)}, u32[]{:S(2)}, u32[]{:S(2)}) collective-permute-start(bf16[2,2,16,64,128]{4,3,2,1,0:T(8,128)(2,1)} %collective-permute-done.11.refs_1_), channel_id=1, source_target_pairs={{0,16},{1,17},{2,18},{3,19},{4,20},{5,21},{6,22},{7,23},{8,24},{9,... | collective-permute-start | bytes 3145736 | tf_op jit(solution)/shard_map/ppermute | solution.py:49
  76.0 11.2 %collective-permute-start.13 = (bf16[384,512]{1,0:T(8,128)(2,1)S(1)}, bf16[384,512]{1,0:T(8,128)(2,1)S(1)}, u32[]{:S(2)}, u32[]{:S(2)}) collective-permute-start(bf16[384,512]{1,0:T(8,128)(2,1)S(1)} %get-tuple-element.97), channel_id=1, source_target_pairs={{0,4},{1,5},{2,6},{3,7},{4,8},{5,9},{6,10},{7,11},{8,12},{9,13},{1... | collective-permute-start | bytes 1179656 | tf_op jit(solution)/shard_map/ppermute | solution.py:49
  78.6 9.0 %collective-permute-start.14 = (bf16[384,512]{1,0:T(8,128)(2,1)S(1)}, bf16[384,512]{1,0:T(8,128)(2,1)S(1)}, u32[]{:S(2)}, u32[]{:S(2)}) collective-permute-start(bf16[384,512]{1,0:T(8,128)(2,1)S(1)} %get-tuple-element.98), channel_id=1, source_target_pairs={{0,12},{1,13},{2,14},{3,15},{4,0},{5,1},{6,2},{7,3},{8,4},{9,5},{1... | collective-permute-start | bytes 1179656 | tf_op jit(solution)/shard_map/ppermute | solution.py:49
  84.0 1.0 copy-start.11
  88.1 5.9 %collective-permute-start.16 = (bf16[512,128]{1,0:T(8,128)(2,1)S(1)}, bf16[512,128]{1,0:T(8,128)(2,1)S(1)}, u32[]{:S(2)}, u32[]{:S(2)}) collective-permute-start(bf16[512,128]{1,0:T(8,128)(2,1)S(1)} %assemble.13.mine_ref), channel_id=1, source_target_pairs={{0,1},{1,0},{2,3},{3,2},{4,5},{5,4},{6,7},{7,6},{8,9},{9,8},{10,11... | collective-permute-start | bytes 393224 | tf_op jit(solution)/shard_map/ppermute | solution.py:49
  100.3 16.3 %collective-permute-start.22 = (bf16[768,512]{1,0:T(8,128)(2,1)S(1)}, bf16[768,512]{1,0:T(8,128)(2,1)S(1)}, u32[]{:S(2)}, u32[]{:S(2)}) collective-permute-start(bf16[768,512]{1,0:T(8,128)(2,1)S(1)} %pad_maximum_fusion.4), channel_id=1, source_target_pairs={{0,12},{1,13},{2,14},{3,15},{4,0},{5,1},{6,2},{7,3},{8,4},{9,5},{1... | collective-permute-start | bytes 2359304 | tf_op jit(solution)/shard_map/ppermute | solution.py:49
  100.4 16.1 %collective-permute-start.21 = (bf16[768,512]{1,0:T(8,128)(2,1)S(1)}, bf16[768,512]{1,0:T(8,128)(2,1)S(1)}, u32[]{:S(2)}, u32[]{:S(2)}) collective-permute-start(bf16[768,512]{1,0:T(8,128)(2,1)S(1)} %pad_maximum_fusion.3), channel_id=1, source_target_pairs={{0,4},{1,5},{2,6},{3,7},{4,8},{5,9},{6,10},{7,11},{8,12},{9,13},{1... | collective-permute-start | bytes 2359304 | tf_op jit(solution)/shard_map/ppermute | solution.py:49
  103.7 12.3 %collective-permute-start.17 = (bf16[256,512]{1,0:T(8,128)(2,1)S(1)}, bf16[256,512]{1,0:T(8,128)(2,1)S(1)}, u32[]{:S(2)}, u32[]{:S(2)}) collective-permute-start(bf16[256,512]{1,0:T(8,128)(2,1)S(1)} %get-tuple-element.164), channel_id=1, source_target_pairs={{0,4},{1,5},{2,6},{3,7},{4,8},{5,9},{6,10},{7,11},{8,12},{9,13},{1... | collective-permute-start | bytes 786440 | tf_op jit(solution)/shard_map/ppermute | solution.py:49
  105.1 11.3 %collective-permute-start.18 = (bf16[256,512]{1,0:T(8,128)(2,1)S(1)}, bf16[256,512]{1,0:T(8,128)(2,1)S(1)}, u32[]{:S(2)}, u32[]{:S(2)}) collective-permute-start(bf16[256,512]{1,0:T(8,128)(2,1)S(1)} %get-tuple-element.163), channel_id=1, source_target_pairs={{0,12},{1,13},{2,14},{3,15},{4,0},{5,1},{6,2},{7,3},{8,4},{9,5},{1... | collective-permute-start | bytes 786440 | tf_op jit(solution)/shard_map/ppermute | solution.py:49
  117.1 11.6 %collective-permute-start.20 = (bf16[512,512]{1,0:T(8,128)(2,1)S(1)}, bf16[512,512]{1,0:T(8,128)(2,1)S(1)}, u32[]{:S(2)}, u32[]{:S(2)}) collective-permute-start(bf16[512,512]{1,0:T(8,128)(2,1)S(1)} %pad_maximum_fusion.6), channel_id=1, source_target_pairs={{0,12},{1,13},{2,14},{3,15},{4,0},{5,1},{6,2},{7,3},{8,4},{9,5},{1... | collective-permute-start | bytes 1572872 | tf_op jit(solution)/shard_map/ppermute | solution.py:49
  118.1 10.6 %collective-permute-start.19 = (bf16[512,512]{1,0:T(8,128)(2,1)S(1)}, bf16[512,512]{1,0:T(8,128)(2,1)S(1)}, u32[]{:S(2)}, u32[]{:S(2)}) collective-permute-start(bf16[512,512]{1,0:T(8,128)(2,1)S(1)} %pad_maximum_fusion.5), channel_id=1, source_target_pairs={{0,4},{1,5},{2,6},{3,7},{4,8},{5,9},{6,10},{7,11},{8,12},{9,13},{1... | collective-permute-start | bytes 1572872 | tf_op jit(solution)/shard_map/ppermute | solution.py:49
  120.7 21.0 %collective-permute-start.28 = (bf16[1024,512]{1,0:T(8,128)(2,1)S(1)}, bf16[1024,512]{1,0:T(8,128)(2,1)S(1)}, u32[]{:S(2)}, u32[]{:S(2)}) collective-permute-start(bf16[1024,512]{1,0:T(8,128)(2,1)S(1)} %pad_maximum_fusion.2), channel_id=1, source_target_pairs={{0,12},{1,13},{2,14},{3,15},{4,0},{5,1},{6,2},{7,3},{8,4},{9,5},{1... | collective-permute-start | bytes 3145736 | tf_op jit(solution)/shard_map/ppermute | solution.py:49
  120.9 20.8 %collective-permute-start.27 = (bf16[1024,512]{1,0:T(8,128)(2,1)S(1)}, bf16[1024,512]{1,0:T(8,128)(2,1)S(1)}, u32[]{:S(2)}, u32[]{:S(2)}) collective-permute-start(bf16[1024,512]{1,0:T(8,128)(2,1)S(1)} %pad_maximum_fusion.1), channel_id=1, source_target_pairs={{0,4},{1,5},{2,6},{3,7},{4,8},{5,9},{6,10},{7,11},{8,12},{9,13},{1... | collective-permute-start | bytes 3145736 | tf_op jit(solution)/shard_map/ppermute | solution.py:49
  128.9 10.5 %collective-permute-start.23 = (bf16[256,512]{1,0:T(8,128)(2,1)S(1)}, bf16[256,512]{1,0:T(8,128)(2,1)S(1)}, u32[]{:S(2)}, u32[]{:S(2)}) collective-permute-start(bf16[256,512]{1,0:T(8,128)(2,1)S(1)} %get-tuple-element.166), channel_id=1, source_target_pairs={{0,1},{1,2},{2,3},{3,0},{4,5},{5,6},{6,7},{7,4},{8,9},{9,10},{10,1... | collective-permute-start | bytes 786440 | tf_op jit(solution)/shard_map/ppermute | solution.py:49
  129.3 10.2 %collective-permute-start.24 = (bf16[256,512]{1,0:T(8,128)(2,1)S(1)}, bf16[256,512]{1,0:T(8,128)(2,1)S(1)}, u32[]{:S(2)}, u32[]{:S(2)}) collective-permute-start(bf16[256,512]{1,0:T(8,128)(2,1)S(1)} %get-tuple-element.165), channel_id=1, source_target_pairs={{0,3},{1,0},{2,1},{3,2},{4,7},{5,4},{6,5},{7,6},{8,11},{9,8},{10,9... | collective-permute-start | bytes 786440 | tf_op jit(solution)/shard_map/ppermute | solution.py:49
  142.5 14.9 %collective-permute-start.25 = (bf16[512,512]{1,0:T(8,128)(2,1)S(1)}, bf16[512,512]{1,0:T(8,128)(2,1)S(1)}, u32[]{:S(2)}, u32[]{:S(2)}) collective-permute-start(bf16[512,512]{1,0:T(8,128)(2,1)S(1)} %pad_maximum_fusion.7), channel_id=1, source_target_pairs={{0,4},{1,5},{2,6},{3,7},{4,8},{5,9},{6,10},{7,11},{8,12},{9,13},{1... | collective-permute-start | bytes 1572872 | tf_op jit(solution)/shard_map/ppermute | solution.py:49
  146.0 15.0 %collective-permute-start.26 = (bf16[512,512]{1,0:T(8,128)(2,1)S(1)}, bf16[512,512]{1,0:T(8,128)(2,1)S(1)}, u32[]{:S(2)}, u32[]{:S(2)}) collective-permute-start(bf16[512,512]{1,0:T(8,128)(2,1)S(1)} %pad_maximum_fusion.8), channel_id=1, source_target_pairs={{0,12},{1,13},{2,14},{3,15},{4,0},{5,1},{6,2},{7,3},{8,4},{9,5},{1... | collective-permute-start | bytes 1572872 | tf_op jit(solution)/shard_map/ppermute | solution.py:49
  146.1 14.9 %collective-permute-start.29 = (bf16[512,512]{1,0:T(8,128)(2,1)S(1)}, bf16[512,512]{1,0:T(8,128)(2,1)S(1)}, u32[]{:S(2)}, u32[]{:S(2)}) collective-permute-start(bf16[512,512]{1,0:T(8,128)(2,1)S(1)} %pad_maximum_fusion.9), channel_id=1, source_target_pairs={{0,1},{1,2},{2,3},{3,0},{4,5},{5,6},{6,7},{7,4},{8,9},{9,10},{10,1... | collective-permute-start | bytes 1572872 | tf_op jit(solution)/shard_map/ppermute | solution.py:49
  146.4 15.7 %copy-start.1 = (s32[64,4]{0,1:T(4,128)S(1)}, s32[64,4]{0,1:T(4,128)}, u32[]{:S(2)}) copy-start(s32[64,4]{0,1:T(4,128)} %param.14) | copy-start | bytes 3076
  146.5 14.5 %collective-permute-start.30 = (bf16[512,512]{1,0:T(8,128)(2,1)S(1)}, bf16[512,512]{1,0:T(8,128)(2,1)S(1)}, u32[]{:S(2)}, u32[]{:S(2)}) collective-permute-start(bf16[512,512]{1,0:T(8,128)(2,1)S(1)} %pad_maximum_fusion.10), channel_id=1, source_target_pairs={{0,3},{1,0},{2,1},{3,2},{4,7},{5,4},{6,5},{7,6},{8,11},{9,8},{10,9... | collective-permute-start | bytes 1572872 | tf_op jit(solution)/shard_map/ppermute | solution.py:49

commit v7 on v2

--- a/solution.py
+++ b/solution.py
@@ -117,7 +117,7 @@
         out_shape=[pltpu.VMEM(shape, BF16) for shape, _ in outputs],
         in_specs=[VMEM] * n_arrays,
         out_specs=[VMEM] * len(outputs),
-        compiler_params=params(8),
+        compiler_params=params(4),
         cost_estimate=estimate(0, 0),
         name="assemble",
     )(*in_vmem(arrays))
@@ -127,11 +127,16 @@
     return (row, 0, rows, WIDE, [(a, r, 0) for a, r in terms])
 
 
-def packed(row, rows, *terms):
+def packed(row, lanes, rows, *terms):
     quarter = rows // 4
     pieces = []
     for k in range(4):
-        places = [(a, start + k * quarter, column) for a, start, column in terms]
+        places = []
+        for a, start, column in terms:
+            if column is None:
+                places.append((a, start, k * HD))
+            else:
+                places.append((a, start + k * quarter, column))
         pieces.append((row, k * HD, quarter, HD, places))
     return pieces
 
@@ -172,7 +177,7 @@
             pltpu.VMEM((WIDE, count * HD), BF16),
             pltpu.SemaphoreType.DMA((count,)),
         ],
-        compiler_params=params(7),
+        compiler_params=params(5),
         cost_estimate=estimate(0, 0),
         name="kv_partial",
     )(order, tokens, gain, w_keyvalue)
@@ -283,7 +288,7 @@
         in_specs=[SMEM] + [ANYWHERE] * 4,
         out_specs=VMEM,
         scratch_shapes=[pltpu.SemaphoreType.DMA((branches, PDEPTH))],
-        compiler_params=params(8),
+        compiler_params=params(4),
         cost_estimate=estimate(0, 0),
         name="gather_blocks",
     )(codes, *pools)
@@ -398,7 +403,7 @@
             pltpu.VMEM((count, WIDE, WIDE), BF16),
             pltpu.SemaphoreType.DMA((count,)),
         ],
-        compiler_params=params(7),
+        compiler_params=params(6),
         cost_estimate=estimate(0, 0),
         name="output_part",
     )(order, heads_out, w_output)
@@ -424,14 +429,19 @@
     ]
 
     s1 = both(tokens, tokens, "first")
-    kv = kv_partial(tokens, gains, w_keyvalue, order, (0, 1, 3, 2))
-    k_far = both(kv[:HALF, 3 * WIDE :], kv[HALF:, 3 * WIDE :], "first")
-    b1m, b1p, k_m, k_p, kv_near, cache = bar((*s1, *k_far, kv, cache))
+    kv_far = kv_partial(tokens, gains, w_keyvalue, order, (2,))
+    k_far = both(kv_far[:HALF], kv_far[HALF:], "first")
+    kv_near = kv_partial(tokens, gains, w_keyvalue, order, (0, 1, 3))
+    kv_head = place * (w_query.shape[1] // HD) // (HEADS // KVH)
+    cache_head = lax.dynamic_slice_in_dim(cache, kv_head * HD, HD, 3)
+    z_one = hop(cache_head, "z_one", 1)
+    b1m, b1p = bar(s1)
     (near,) = assemble(
         [tokens, b1p, b1m],
         [((3 * WIDE, WIDE), [rows_piece(n * WIDE, WIDE, (n, 0)) for n in range(3)])],
     )
     s2 = both(near, near, "second")
+    k_m, k_p, kv_near, z_one, b1m, b1p = bar((*k_far, kv_near, z_one, b1m, b1p))
     s3 = both(
         *assemble(
             [b1m, b1p, kv_near, k_m, k_p],
@@ -456,9 +466,6 @@
         ),
         "first",
     )
-    kv_head = place * (w_query.shape[1] // HD) // (HEADS // KVH)
-    cache_head = lax.dynamic_slice_in_dim(cache, kv_head * HD, HD, 3)
-    z_one = hop(cache_head, "z_one", 1)
     part = query_part(
         [((0, 0), [(0, 0, 0, WIDE)]), ((1, 0), [(1, 0, 0, WIDE)]), ((3, 0), [(2, 0, 0, WIDE)])],
         [tokens, b1p, b1m],
@@ -467,28 +474,26 @@
         w_query,
         None,
     )
-    b3m, b3p, b2m, b2p, z_one, *part = bar((*s3, *s2, z_one, *part))
+    pool = jnp.stack([cache_head, z_one])
+    z_two = hop(pool, "z_two", 1)
+    b3m, b3p, *part = bar((*s3, *part))
     ksum, to_next, to_last = assemble(
-        [b3m, b3p, kv_near, b2m, b2p],
+        [b3m, b3p, kv_near],
         [
             ((WIDE, WIDE), [(0, 0, WIDE, WIDE, [(2, 0, 0), (0, HALF, 0), (1, HALF, 0)])]),
             (
-                (5 * HALF + HALF // 4, WIDE),
+                (WIDE + HALF // 4, WIDE),
                 [rows_piece(0, HALF, (0, 0)), rows_piece(HALF, HALF, (1, 0))]
-                + [rows_piece(WIDE + n * HALF, HALF, (3, n * WIDE)) for n in range(3)]
-                + packed(5 * HALF, HALF, (2, 0, 2 * HD), (0, HALF, 2 * HD), (1, HALF, 2 * HD)),
+                + packed(WIDE, 0, HALF, (2, 0, 2 * HD), (0, HALF, 2 * HD), (1, HALF, 2 * HD)),
             ),
             (
-                (5 * HALF + HALF // 4, WIDE),
+                (WIDE + HALF // 4, WIDE),
                 [rows_piece(0, HALF, (0, 0)), rows_piece(HALF, HALF, (1, 0))]
-                + [rows_piece(WIDE + n * HALF, HALF, (4, n * WIDE + HALF)) for n in range(3)]
-                + packed(5 * HALF, HALF, (2, HALF, 2 * HD), (0, WIDE, 2 * HD), (1, WIDE, 2 * HD)),
+                + packed(WIDE, 0, HALF, (2, HALF, 2 * HD), (0, 2 * HALF, 2 * HD), (1, 2 * HALF, 2 * HD)),
             ),
         ],
     )
     s5 = both(to_next, to_last, "second")
-    pool = jnp.stack([cache_head, z_one])
-    z_two = hop(pool, "z_two", 1)
     near_twin = hop(pool, "core", 1)
     my_lengths = lax.dynamic_slice_in_dim(lengths, group * branch_count, branch_count, 0)
     my_parents = lax.dynamic_slice_in_dim(parents, group * branch_count, branch_count, 0)
@@ -511,24 +516,19 @@
     cosine = jnp.concatenate([cosine, cosine], axis=1)
     sine = jnp.concatenate([-sine, sine], axis=1)
 
-    part = query_part(
-        [
-            ((2, 0), [(0, 0, 0, HALF), (1, 0, HALF, HALF)]),
-            ((0, 1), [(2, 0, 0, WIDE)]),
-            ((1, 1), [(2, WIDE, 0, WIDE)]),
-            ((3, 1), [(2, 2 * WIDE, 0, WIDE)]),
-            ((0, 3), [(3, 0, 0, WIDE)]),
-            ((1, 3), [(3, WIDE, 0, WIDE)]),
-            ((3, 3), [(3, 2 * WIDE, 0, WIDE)]),
-        ],
-        [b3m, b3p, b2p, b2m],
-        order,
-        gains,
-        w_query,
-        part,
-    )
-    b5m, b5p, z_two, near_twin, cosine, sine, codes, *part = bar(
-        (*s5, z_two, near_twin, cosine, sine, codes, *part)
+    b2m, b2p = bar(s2)
+    s6 = both(
+        *assemble(
+            [b2m, b2p],
+            [
+                ((3 * HALF, WIDE), [rows_piece(n * HALF, HALF, (0, n * WIDE)) for n in range(3)]),
+                ((3 * HALF, WIDE), [rows_piece(n * HALF, HALF, (1, n * WIDE + HALF)) for n in range(3)]),
+            ],
+        ),
+        "second",
+    )
+    b5m, b5p, b2m, b2p, z_two, near_twin, cosine, sine, codes, *part = bar(
+        (*s5, b2m, b2p, z_two, near_twin, cosine, sine, codes, *part)
     )
     quarter = HALF // 4
     s7 = both(
@@ -558,7 +558,7 @@
                             k * HD,
                             quarter,
                             HD,
-                            [(2, (2 * k + t) * quarter, HD), (0, 5 * HALF, (2 * k + t) * HD)],
+                            [(2, (2 * k + t) * quarter, HD), (0, WIDE, (2 * k + t) * HD)],
                         )
                         for k in range(2)
                         for t in range(2)
@@ -577,7 +577,7 @@
                             k * HD,
                             quarter,
                             HD,
-                            [(2, (2 * k + t) * quarter, 3 * HD), (1, 5 * HALF, (2 * k + t - 4) * HD)],
+                            [(2, (2 * k + t) * quarter, 3 * HD), (1, WIDE, (2 * k + t - 4) * HD)],
                         )
                         for k in range(2, 4)
                         for t in range(2)
@@ -588,25 +588,25 @@
         "second",
     )
     far_twin = hop(z_two, "core", 1)
-    pools = [
-        pltpu.with_memory_space_constraint(a, pltpu.HBM) for a in (pool, z_two, near_twin, far_twin)
-    ]
-    prefix = gather_blocks(pools, codes)
     part = query_part(
         [
-            ((2, 1), [(0, 0, 0, WIDE)]),
-            ((2, 3), [(1, 0, 0, WIDE)]),
-            ((0, 2), [(1, WIDE, 0, HALF), (0, WIDE, HALF, HALF)]),
-            ((1, 2), [(1, WIDE + HALF, 0, HALF), (0, WIDE + HALF, HALF, HALF)]),
-            ((3, 2), [(1, 2 * WIDE, 0, HALF), (0, 2 * WIDE, HALF, HALF)]),
+            ((2, 0), [(0, 0, 0, HALF), (1, 0, HALF, HALF)]),
+            ((0, 1), [(2, 0, 0, WIDE)]),
+            ((1, 1), [(2, WIDE, 0, WIDE)]),
+            ((3, 1), [(2, 2 * WIDE, 0, WIDE)]),
+            ((0, 3), [(3, 0, 0, WIDE)]),
+            ((1, 3), [(3, WIDE, 0, WIDE)]),
+            ((3, 3), [(3, 2 * WIDE, 0, WIDE)]),
+            ((2, 1), [(4, 0, 0, WIDE)]),
+            ((2, 3), [(5, 0, 0, WIDE)]),
         ],
-        [b5p, b5m],
+        [b3m, b3p, b2p, b2m, b5p, b5m],
         order,
         gains,
         w_query,
         part,
     )
-    b7m, b7p, prefix, *part = bar((*s7, prefix, *part))
+    b7m, b7p, b6m, b6p, far_twin, *part = bar((*s7, *s6, far_twin, *part))
     (mine,) = assemble(
         [ksum, b7m, b7p],
         [
@@ -620,11 +620,18 @@
         ],
     )
     other = hop(mine, "twin", 1)
+    pools = [
+        pltpu.with_memory_space_constraint(a, pltpu.HBM) for a in (pool, z_two, near_twin, far_twin)
+    ]
+    prefix = gather_blocks(pools, codes)
     part = query_part(
         [
-            ((2, 2), [(0, 0, 0, HALF), (1, 0, HALF, HALF)]),
+            ((0, 2), [(0, 0, 0, HALF), (1, 0, HALF, HALF)]),
+            ((1, 2), [(0, HALF, 0, HALF), (1, HALF, HALF, HALF)]),
+            ((3, 2), [(0, 2 * HALF, 0, HALF), (1, 2 * HALF, HALF, HALF)]),
+            ((2, 2), [(2, 0, 0, HALF), (3, 0, HALF, HALF)]),
         ],
-        [b7m, b7p],
+        [b6m, b6p, b7m, b7p],
         order,
         gains,
         w_query,

time: 163 us -> 161 us (0.988)
  the two profiles are of different devices: /device:TPU:6 before, /device:TPU:25 now
where the time goes in v7:
time: 161 us; the launch traced here: 160 us
  waiting for transfers between devices  63.5 us (39%)
  Pallas kernels  42.8 us (27%)
  starting transfers between devices  40.2 us (25%)
  local copies, waits for them, and re-layouts  7.07 us (4%)
  other arithmetic  6.54 us (4%)
    ppermute x33, waiting for transfers between devices, hop(): return lax.ppermute(value, AXES, HOPS[axis, step])  63.5 us
    ppermute x33, starting transfers between devices, hop(): return lax.ppermute(value, AXES, HOPS[axis, step])  40.2 us
    pallas_call x3, Pallas kernels, query_part(): pl.pallas_call(body, out_shape=(jax.ShapeDtypeStruct((WIDE, WIDE), F32),...  14.5 us
    pallas_call x2, Pallas kernels, output_part(): pl.pallas_call(body, out_shape=jax.ShapeDtypeStruct((count, WIDE, WIDE),...  8.55 us
    pallas_call x6, Pallas kernels, assemble(): pl.pallas_call(body, out_shape=[pltpu.VMEM(shape, BF16) for shape, _ in o...  6.12 us
    pallas_call x1, Pallas kernels, middle(): pl.pallas_call(body, out_shape=(jax.ShapeDtypeStruct((WIDE, WIDE), BF16),...  6.08 us
    pallas_call x2, Pallas kernels, kv_partial(): pl.pallas_call(body, out_shape=jax.ShapeDtypeStruct((WIDE, count * HD), B...  5.25 us
  transfers between devices with their start and end apart: 33, of which 17 were waited for; matrix products, arithmetic and copies ran while one was open for 5% of the time, Pallas kernels for 23%

profile of v7, /device:TPU:25, one launch (start us, length us, event | category | flops | bytes accessed | tf_op | source)
XLA Modules:
  0.0 160.5 jit_solution(6678314362236296903)
XLA Ops:
  0.0 2.5 %collective-permute-start.4 = (bf16[512,512]{1,0:T(8,128)(2,1)}, bf16[512,512]{1,0:T(8,128)(2,1)S(1)}, u32[]{:S(2)}, u32[]{:S(2)}) collective-permute-start(bf16[512,512]{1,0:T(8,128)(2,1)} %refs_0_.3), channel_id=1, source_target_pairs={{0,3},{1,0},{2,1},{3,2},{4,7},{5,4},{6,5},{7,6},{8,11},{9,8},{10,9... | collective-permute-start | bytes 1572872 | tf_op jit(solution)/shard_map/ppermute | solution.py:49
  2.5 1.9 %constant_dynamic-slice_fusion.1 = bf16[2,16,64,128]{3,2,1,0:T(8,128)(2,1)} fusion(bf16[2,16,64,1024]{3,2,1,0:T(8,128)(2,1)} %param.13, s32[]{:T(128)S(6)} %select_n.119), kind=kLoop, calls=%fused_computation.108 | loop fusion | bytes 1048580 | tf_op jit(solution)/shard_map/dynamic_slice | solution.py:436
  4.4 3.8 %collective-permute-start.2 = (bf16[2,16,64,128]{3,2,1,0:T(8,128)(2,1)}, bf16[2,16,64,128]{3,2,1,0:T(8,128)(2,1)}, u32[]{:S(2)}, u32[]{:S(2)}) collective-permute-start(bf16[2,16,64,128]{3,2,1,0:T(8,128)(2,1)} %constant_dynamic-slice_fusion.1), channel_id=1, source_target_pairs={{0,32},{1,33},{2,34},{3,35},{4,36},{5,37},{6,38},{7,39},{8,40},{9,... | collective-permute-start | bytes 1572872 | tf_op jit(solution)/shard_map/ppermute | solution.py:49
  8.9 1.0 copy-done.2
  9.9 2.1 %kv_partial.2 = bf16[512,512]{1,0:T(8,128)(2,1)S(1)} custom-call(s32[16]{0:T(128)S(1)} %fusion.29.order_ref, bf16[512,512]{1,0:T(8,128)(2,1)S(1)} %copy-done.2, f32[16,512]{1,0:T(8,128)S(1)} %reshape.77.g_ref.refs_3_.refs_6_.refs_4_, bf16[2,512,1024]{2,1,0:T(8,128)(2,1)} %w_ref.5), custom_call_target="tpu_custom_call" | custom-call | tf_op jit(solution)/shard_map/kv_partial/pallas_call | solution.py:171
  12.1 2.7 %collective-permute-start.1 = (bf16[256,512]{1,0:T(8,128)(2,1)S(1)}, bf16[256,512]{1,0:T(8,128)(2,1)S(1)}, u32[]{:S(2)}, u32[]{:S(2)}) collective-permute-start(bf16[256,512]{1,0:T(8,128)(2,1)S(1)} %get-tuple-element.165), channel_id=1, source_target_pairs={{0,3},{1,0},{2,1},{3,2},{4,7},{5,4},{6,5},{7,6},{8,11},{9,8},{10,9... | collective-permute-start | bytes 786440 | tf_op jit(solution)/shard_map/ppermute | solution.py:49
  14.9 1.3 assemble.8
  16.6 3.1 %kv_partial.3.refs_2_ = bf16[512,1536]{1,0:T(8,128)(2,1)S(1)} custom-call(s32[16]{0:T(128)S(1)} %fusion.29.order_ref, bf16[512,512]{1,0:T(8,128)(2,1)S(1)} %copy-done.3, f32[16,512]{1,0:T(8,128)S(1)} %reshape.77.g_ref.refs_3_.refs_6_.refs_4_, bf16[2,512,1024]{2,1,0:T(8,128)(2,1)} %w_ref.5), custom_call_target="tpu_custom_call" | custom-call | tf_op jit(solution)/shard_map/kv_partial/pallas_call | solution.py:171
  19.7 1.5 collective-permute-done.refs_3_
  21.3 1.1 assemble.6
  23.9 2.7 %collective-permute-start.6 = (bf16[768,512]{1,0:T(8,128)(2,1)}, bf16[768,512]{1,0:T(8,128)(2,1)}, u32[]{:S(2)}, u32[]{:S(2)}) collective-permute-start(bf16[768,512]{1,0:T(8,128)(2,1)} %copy-done.4), channel_id=1, source_target_pairs={{0,3},{1,0},{2,1},{3,2},{4,7},{5,4},{6,5},{7,6},{8,11},{9,8},{10,9... | collective-permute-start | bytes 2359304 | tf_op jit(solution)/shard_map/ppermute | solution.py:49
  26.7 1.1 fusion.37
  27.7 2.1 %pad_maximum_fusion.refs_0_ = bf16[2,2,16,64,128]{4,3,2,1,0:T(8,128)(2,1)} fusion(bf16[1,2,16,64,128]{4,3,2,1,0:T(8,128)(2,1)} %bitcast.1, bf16[1,2,16,64,128]{4,3,2,1,0:T(8,128)(2,1)S(1)} %fusion.37), kind=kLoop, calls=%fused_computation | loop fusion | flops 524288 | bytes 2097152 | tf_op jit(solution)/shard_map/stack | solution.py:477
  29.9 12.6 %collective-permute-done.5.refs_0_ = bf16[768,512]{1,0:T(8,128)(2,1)} collective-permute-done((bf16[768,512]{1,0:T(8,128)(2,1)}, bf16[768,512]{1,0:T(8,128)(2,1)}, u32[]{:S(2)}, u32[]{:S(2)}) %collective-permute-start.5) | collective-permute-done | bytes 786464 | tf_op jit(solution)/shard_map/ppermute | solution.py:49
  42.9 3.0 %query_part.3 = (f32[512,512]{1,0:T(8,128)S(1)}, f32[512,128]{1,0:T(8,128)S(1)}) custom-call(s32[16]{0:T(128)S(1)} %fusion.29.order_ref, bf16[512,512]{1,0:T(8,128)(2,1)S(1)} %copy-done.3, bf16[512,512]{1,0:T(8,128)(2,1)S(1)} %collective-permute-done.4.refs_1_, bf16[512,512]{1,0:T(8,128)(2,1)S(1)} %collective-permute-done.3.refs_0_.refs_2_, ...), custom_call_target="tpu_custom_call" | custom-call | tf_op jit(solution)/shard_map/query_part/pallas_call | solution.py:241
  45.9 1.7 %assemble.7 = (bf16[512,512]{1,0:T(8,128)(2,1)S(1)}, bf16[576,512]{1,0:T(8,128)(2,1)S(1)}, bf16[576,512]{1,0:T(8,128)(2,1)S(1)}) custom-call(bf16[768,512]{1,0:T(8,128)(2,1)} %collective-permute-done.5.refs_0_, bf16[768,512]{1,0:T(8,128)(2,1)} %collective-permute-done.6.refs_1_, bf16[512,1536]{1,0:T(8,128)(2,1)S(1)} %kv_partial.3.refs_2_), custom_call_target="tpu_custom_call" | custom-call | tf_op jit(solution)/shard_map/assemble/pallas_call | solution.py:115
  47.6 1.9 %collective-permute-start.7 = (bf16[576,512]{1,0:T(8,128)(2,1)S(1)}, bf16[576,512]{1,0:T(8,128)(2,1)S(1)}, u32[]{:S(2)}, u32[]{:S(2)}) collective-permute-start(bf16[576,512]{1,0:T(8,128)(2,1)S(1)} %get-tuple-element.81), channel_id=1, source_target_pairs={{0,4},{1,5},{2,6},{3,7},{4,8},{5,9},{6,10},{7,11},{8,12},{9,13},{1... | collective-permute-start | bytes 1769480 | tf_op jit(solution)/shard_map/ppermute | solution.py:49
  51.5 5.2 %collective-permute-done.11.refs_1_ = bf16[2,2,16,64,128]{4,3,2,1,0:T(8,128)(2,1)} collective-permute-done((bf16[2,2,16,64,128]{4,3,2,1,0:T(8,128)(2,1)}, bf16[2,2,16,64,128]{4,3,2,1,0:T(8,128)(2,1)}, u32[]{:S(2)}, u32[]{:S(2)}) %collective-permute-start.11) | collective-permute-done | bytes 1048608 | tf_op jit(solution)/shard_map/ppermute | solution.py:49
  56.8 1.1 collective-permute-done.7.refs_0_.refs_5_
  57.9 1.9 %collective-permute-done.8.refs_1_.refs_4_ = bf16[576,512]{1,0:T(8,128)(2,1)S(1)} collective-permute-done((bf16[576,512]{1,0:T(8,128)(2,1)S(1)}, bf16[576,512]{1,0:T(8,128)(2,1)S(1)}, u32[]{:S(2)}, u32[]{:S(2)}) %collective-permute-start.8) | collective-permute-done | bytes 589856 | tf_op jit(solution)/shard_map/ppermute | solution.py:49
  59.8 3.9 %collective-permute-start.17 = (bf16[2,2,16,64,128]{4,3,2,1,0:T(8,128)(2,1)}, bf16[2,2,16,64,128]{4,3,2,1,0:T(8,128)(2,1)S(1)}, u32[]{:S(2)}, u32[]{:S(2)}) collective-permute-start(bf16[2,2,16,64,128]{4,3,2,1,0:T(8,128)(2,1)} %collective-permute-done.11.refs_1_), channel_id=1, source_target_pairs={{0,16},{1,17},{2,18},{3,19},{4,20},{5,21},{6,22},{7,23},{8,24},{9,... | collective-permute-start | bytes 3145736 | tf_op jit(solution)/shard_map/ppermute | solution.py:49
  63.7 2.0 %assemble.10 = (bf16[768,512]{1,0:T(8,128)(2,1)S(1)}, bf16[768,512]{1,0:T(8,128)(2,1)S(1)}) custom-call(bf16[1536,512]{1,0:T(8,128)(2,1)} %collective-permute-done.9.refs_0_.refs_3_, bf16[1536,512]{1,0:T(8,128)(2,1)} %collective-permute-done.10.refs_1_.refs_2_), custom_call_target="tpu_custom_call" | custom-call | tf_op jit(solution)/shard_map/assemble/pallas_call | solution.py:115
  65.7 2.0 %collective-permute-start.15 = (bf16[768,512]{1,0:T(8,128)(2,1)S(1)}, bf16[768,512]{1,0:T(8,128)(2,1)S(1)}, u32[]{:S(2)}, u32[]{:S(2)}) collective-permute-start(bf16[768,512]{1,0:T(8,128)(2,1)S(1)} %get-tuple-element.93), channel_id=1, source_target_pairs={{0,4},{1,5},{2,6},{3,7},{4,8},{5,9},{6,10},{7,11},{8,12},{9,13},{1... | collective-permute-start | bytes 2359304 | tf_op jit(solution)/shard_map/ppermute | solution.py:49
  67.8 2.7 %collective-permute-start.13 = (bf16[384,512]{1,0:T(8,128)(2,1)S(1)}, bf16[384,512]{1,0:T(8,128)(2,1)S(1)}, u32[]{:S(2)}, u32[]{:S(2)}) collective-permute-start(bf16[384,512]{1,0:T(8,128)(2,1)S(1)} %get-tuple-element.91), channel_id=1, source_target_pairs={{0,4},{1,5},{2,6},{3,7},{4,8},{5,9},{6,10},{7,11},{8,12},{9,13},{1... | collective-permute-start | bytes 1179656 | tf_op jit(solution)/shard_map/ppermute | solution.py:49
  70.6 8.0 %query_part.4 = (f32[512,512]{1,0:T(8,128)S(1)}, f32[512,128]{1,0:T(8,128)S(1)}) custom-call(s32[16]{0:T(128)S(1)} %fusion.29.order_ref, bf16[768,512]{1,0:T(8,128)(2,1)} %collective-permute-done.5.refs_0_, bf16[768,512]{1,0:T(8,128)(2,1)} %collective-permute-done.6.refs_1_, ...), custom_call_target="tpu_custom_call", output_to_operand_aliasing={{0}: (9, {}), {1}: (10, {})} | custom-call | tf_op jit(solution)/shard_map/query_part/pallas_call | solution.py:241
  78.6 2.6 %collective-permute-done.13.refs_2_.refs_1_ = bf16[384,512]{1,0:T(8,128)(2,1)S(1)} collective-permute-done((bf16[384,512]{1,0:T(8,128)(2,1)S(1)}, bf16[384,512]{1,0:T(8,128)(2,1)S(1)}, u32[]{:S(2)}, u32[]{:S(2)}) %collective-permute-start.13) | collective-permute-done | bytes 393248 | tf_op jit(solution)/shard_map/ppermute | solution.py:49
  81.1 2.9 %collective-permute-done.14.refs_3_.refs_2_ = bf16[384,512]{1,0:T(8,128)(2,1)S(1)} collective-permute-done((bf16[384,512]{1,0:T(8,128)(2,1)S(1)}, bf16[384,512]{1,0:T(8,128)(2,1)S(1)}, u32[]{:S(2)}, u32[]{:S(2)}) %collective-permute-start.14) | collective-permute-done | bytes 393248 | tf_op jit(solution)/shard_map/ppermute | solution.py:49
  85.0 2.3 %gather_blocks.1.prefix_ref = bf16[8,2,320,128]{3,2,1,0:T(8,128)(2,1)S(1)} custom-call(s32[8,4]{1,0:T(8,128)S(1)} %fusion.25.code_ref, bf16[2,2,16,64,128]{4,3,2,1,0:T(8,128)(2,1)} %pad_maximum_fusion.refs_0_, bf16[2,2,16,64,128]{4,3,2,1,0:T(8,128)(2,1)} %collective-permute-done.11.refs_1_, bf16[2,2,16,64,128]{4,3,2,1,0:T(8,128)(2,1)} %collective-permute-done.12.refs_2_, ...), custom_call_target="tpu_custom_call" | custom-call | tf_op jit(solution)/shard_map/gather_blocks/pallas_call | solution.py:285
  87.3 3.6 %query_part.5 = (f32[512,512]{1,0:T(8,128)S(1)}, f32[512,128]{1,0:T(8,128)S(1)}) custom-call(s32[16]{0:T(128)S(1)} %fusion.29.order_ref, bf16[768,512]{1,0:T(8,128)(2,1)S(1)} %collective-permute-done.15.refs_0_, bf16[768,512]{1,0:T(8,128)(2,1)S(1)} %collective-permute-done.16.refs_1_, ...), custom_call_target="tpu_custom_call", output_to_operand_aliasing={{0}: (7, {}), {1}: (8, {})} | custom-call | tf_op jit(solution)/shard_map/query_part/pallas_call | solution.py:241
  90.9 6.1 %middle.1 = (bf16[512,512]{1,0:T(8,128)(2,1)S(1)}, bf16[4,512,512]{2,1,0:T(8,128)(2,1)S(1)}, bf16[8,2,320,128]{3,2,1,0:T(8,128)(2,1)S(1)}) custom-call(s32[16]{0:T(128)S(1)} %fusion.29.order_ref, s32[8]{0:T(128)S(1)} %get-tuple-element.132.len_ref, f32[512,512]{1,0:T(8,128)S(1)} %get-tuple-element.108.q_ref, ...), custom_call_target="tpu_custom_call", output_to_operand_aliasing={{2}: (8, {})} | custom-call | tf_op jit(solution)/shard_map/middle/pallas_call | solution.py:358
  97.6 1.2 collective-permute-start.24
  99.5 2.1 %collective-permute-start.19 = (bf16[256,512]{1,0:T(8,128)(2,1)S(1)}, bf16[256,512]{1,0:T(8,128)(2,1)S(1)}, u32[]{:S(2)}, u32[]{:S(2)}) collective-permute-start(bf16[256,512]{1,0:T(8,128)(2,1)S(1)} %get-tuple-element.162), channel_id=1, source_target_pairs={{0,4},{1,5},{2,6},{3,7},{4,8},{5,9},{6,10},{7,11},{8,12},{9,13},{1... | collective-permute-start | bytes 786440 | tf_op jit(solution)/shard_map/ppermute | solution.py:49
  101.5 4.3 %output_part.2 = bf16[6,512,512]{2,1,0:T(8,128)(2,1)S(1)} custom-call(s32[16]{0:T(128)S(1)} %fusion.29.order_ref, bf16[512,512]{1,0:T(8,128)(2,1)S(1)} %get-tuple-element.121.h_ref, bf16[512,8192]{1,0:T(8,128)(2,1)} %w_ref.7), custom_call_target="tpu_custom_call" | custom-call | tf_op jit(solution)/shard_map/output_part/pallas_call | solution.py:397
  105.8 6.7 %collective-permute-done.20 = bf16[256,512]{1,0:T(8,128)(2,1)S(1)} collective-permute-done((bf16[256,512]{1,0:T(8,128)(2,1)S(1)}, bf16[256,512]{1,0:T(8,128)(2,1)S(1)}, u32[]{:S(2)}, u32[]{:S(2)}) %collective-permute-start.20) | collective-permute-done | bytes 262176 | tf_op jit(solution)/shard_map/ppermute | solution.py:49
  113.5 1.6 collective-permute-start.22
  115.2 1.4 collective-permute-start.27
  116.8 4.3 %output_part.3 = bf16[6,512,512]{2,1,0:T(8,128)(2,1)S(1)} custom-call(s32[16]{0:T(128)S(1)} %fusion.29.order_ref, bf16[512,512]{1,0:T(8,128)(2,1)S(1)} %get-tuple-element.121.h_ref, bf16[512,8192]{1,0:T(8,128)(2,1)} %w_ref.7), custom_call_target="tpu_custom_call" | custom-call | tf_op jit(solution)/shard_map/output_part/pallas_call | solution.py:397
  121.6 1.7 %collective-permute-done.22 = bf16[512,512]{1,0:T(8,128)(2,1)S(1)} collective-permute-done((bf16[512,512]{1,0:T(8,128)(2,1)S(1)}, bf16[512,512]{1,0:T(8,128)(2,1)S(1)}, u32[]{:S(2)}, u32[]{:S(2)}) %collective-permute-start.22) | collective-permute-done | bytes 524320 | tf_op jit(solution)/shard_map/ppermute | solution.py:49
  123.6 3.0 %collective-permute-start.30 = (bf16[256,512]{1,0:T(8,128)(2,1)S(1)}, bf16[256,512]{1,0:T(8,128)(2,1)S(1)}, u32[]{:S(2)}, u32[]{:S(2)}) collective-permute-start(bf16[256,512]{1,0:T(8,128)(2,1)S(1)} %get-tuple-element.163), channel_id=1, source_target_pairs={{0,3},{1,0},{2,1},{3,2},{4,7},{5,4},{6,5},{7,6},{8,11},{9,8},{10,9... | collective-permute-start | bytes 786440 | tf_op jit(solution)/shard_map/ppermute | solution.py:49
  126.7 6.1 %collective-permute-done.30 = bf16[256,512]{1,0:T(8,128)(2,1)S(1)} collective-permute-done((bf16[256,512]{1,0:T(8,128)(2,1)S(1)}, bf16[256,512]{1,0:T(8,128)(2,1)S(1)}, u32[]{:S(2)}, u32[]{:S(2)}) %collective-permute-start.30) | collective-permute-done | bytes 262176 | tf_op jit(solution)/shard_map/ppermute | solution.py:49
  132.8 3.4 %collective-permute-done.29 = bf16[256,512]{1,0:T(8,128)(2,1)S(1)} collective-permute-done((bf16[256,512]{1,0:T(8,128)(2,1)S(1)}, bf16[256,512]{1,0:T(8,128)(2,1)S(1)}, u32[]{:S(2)}, u32[]{:S(2)}) %collective-permute-start.29) | collective-permute-done | bytes 262176 | tf_op jit(solution)/shard_map/ppermute | solution.py:49
  136.2 1.2 collective-permute-done.28
  138.1 3.0 %collective-permute-start.32 = (bf16[512,512]{1,0:T(8,128)(2,1)S(1)}, bf16[512,512]{1,0:T(8,128)(2,1)S(1)}, u32[]{:S(2)}, u32[]{:S(2)}) collective-permute-start(bf16[512,512]{1,0:T(8,128)(2,1)S(1)} %pad_maximum_fusion.10), channel_id=1, source_target_pairs={{0,3},{1,0},{2,1},{3,2},{4,7},{5,4},{6,5},{7,6},{8,11},{9,8},{10,9... | collective-permute-start | bytes 1572872 | tf_op jit(solution)/shard_map/ppermute | solution.py:49
  141.4 2.7 %collective-permute-start.25 = (bf16[512,512]{1,0:T(8,128)(2,1)S(1)}, bf16[512,512]{1,0:T(8,128)(2,1)S(1)}, u32[]{:S(2)}, u32[]{:S(2)}) collective-permute-start(bf16[512,512]{1,0:T(8,128)(2,1)S(1)} %pad_maximum_fusion.7), channel_id=1, source_target_pairs={{0,4},{1,5},{2,6},{3,7},{4,8},{5,9},{6,10},{7,11},{8,12},{9,13},{1... | collective-permute-start | bytes 1572872 | tf_op jit(solution)/shard_map/ppermute | solution.py:49
  144.2 6.0 %collective-permute-done.32 = bf16[512,512]{1,0:T(8,128)(2,1)S(1)} collective-permute-done((bf16[512,512]{1,0:T(8,128)(2,1)S(1)}, bf16[512,512]{1,0:T(8,128)(2,1)S(1)}, u32[]{:S(2)}, u32[]{:S(2)}) %collective-permute-start.32) | collective-permute-done | bytes 524320 | tf_op jit(solution)/shard_map/ppermute | solution.py:49
  150.2 5.3 %collective-permute-done.26 = bf16[512,512]{1,0:T(8,128)(2,1)S(1)} collective-permute-done((bf16[512,512]{1,0:T(8,128)(2,1)S(1)}, bf16[512,512]{1,0:T(8,128)(2,1)S(1)}, u32[]{:S(2)}, u32[]{:S(2)}) %collective-permute-start.26) | collective-permute-done | bytes 524320 | tf_op jit(solution)/shard_map/ppermute | solution.py:49
  155.5 3.8 %collective-permute-done.31 = bf16[512,512]{1,0:T(8,128)(2,1)S(1)} collective-permute-done((bf16[512,512]{1,0:T(8,128)(2,1)S(1)}, bf16[512,512]{1,0:T(8,128)(2,1)S(1)}, u32[]{:S(2)}, u32[]{:S(2)}) %collective-permute-start.31) | collective-permute-done | bytes 524320 | tf_op jit(solution)/shard_map/ppermute | solution.py:49
  159.3 1.1 fusion.5
  (80 shorter events, 10.8 us)
Async XLA Ops:
  0.0 42.5 %copy-start = (s32[64,4]{0,1:T(4,128)S(1)}, s32[64,4]{0,1:T(4,128)}, u32[]{:S(2)}) copy-start(s32[64,4]{0,1:T(4,128)} %param.14) | copy-start | bytes 3076
  0.0 14.8 %collective-permute-start.4 = (bf16[512,512]{1,0:T(8,128)(2,1)}, bf16[512,512]{1,0:T(8,128)(2,1)S(1)}, u32[]{:S(2)}, u32[]{:S(2)}) collective-permute-start(bf16[512,512]{1,0:T(8,128)(2,1)} %refs_0_.3), channel_id=1, source_target_pairs={{0,3},{1,0},{2,1},{3,2},{4,7},{5,4},{6,5},{7,6},{8,11},{9,8},{10,9... | collective-permute-start | bytes 1572872 | tf_op jit(solution)/shard_map/ppermute | solution.py:49
  2.5 12.4 %collective-permute-start.3 = (bf16[512,512]{1,0:T(8,128)(2,1)}, bf16[512,512]{1,0:T(8,128)(2,1)S(1)}, u32[]{:S(2)}, u32[]{:S(2)}) collective-permute-start(bf16[512,512]{1,0:T(8,128)(2,1)} %refs_0_.3), channel_id=1, source_target_pairs={{0,1},{1,2},{2,3},{3,0},{4,5},{5,6},{6,7},{7,4},{8,9},{9,10},{10,1... | collective-permute-start | bytes 1572872 | tf_op jit(solution)/shard_map/ppermute | solution.py:49
  4.4 16.9 %collective-permute-start.2 = (bf16[2,16,64,128]{3,2,1,0:T(8,128)(2,1)}, bf16[2,16,64,128]{3,2,1,0:T(8,128)(2,1)}, u32[]{:S(2)}, u32[]{:S(2)}) collective-permute-start(bf16[2,16,64,128]{3,2,1,0:T(8,128)(2,1)} %constant_dynamic-slice_fusion.1), channel_id=1, source_target_pairs={{0,32},{1,33},{2,34},{3,35},{4,36},{5,37},{6,38},{7,39},{8,40},{9,... | collective-permute-start | bytes 1572872 | tf_op jit(solution)/shard_map/ppermute | solution.py:49
  8.9 1.0 copy-start.2
  9.9 4.9 %copy-start.3 = (bf16[512,512]{1,0:T(8,128)(2,1)S(1)}, bf16[512,512]{1,0:T(8,128)(2,1)}, u32[]{:S(2)}) copy-start(bf16[512,512]{1,0:T(8,128)(2,1)} %refs_0_.3) | copy-start | bytes 1572868
  12.1 7.6 %collective-permute-start.1 = (bf16[256,512]{1,0:T(8,128)(2,1)S(1)}, bf16[256,512]{1,0:T(8,128)(2,1)S(1)}, u32[]{:S(2)}, u32[]{:S(2)}) collective-permute-start(bf16[256,512]{1,0:T(8,128)(2,1)S(1)} %get-tuple-element.165), channel_id=1, source_target_pairs={{0,3},{1,0},{2,1},{3,2},{4,7},{5,4},{6,5},{7,6},{8,11},{9,8},{10,9... | collective-permute-start | bytes 786440 | tf_op jit(solution)/shard_map/ppermute | solution.py:49
  14.8 6.4 %collective-permute-start = (bf16[256,512]{1,0:T(8,128)(2,1)S(1)}, bf16[256,512]{1,0:T(8,128)(2,1)S(1)}, u32[]{:S(2)}, u32[]{:S(2)}) collective-permute-start(bf16[256,512]{1,0:T(8,128)(2,1)S(1)} %get-tuple-element.166), channel_id=1, source_target_pairs={{0,1},{1,2},{2,3},{3,0},{4,5},{5,6},{6,7},{7,4},{8,9},{9,10},{10,1... | collective-permute-start | bytes 786440 | tf_op jit(solution)/shard_map/ppermute | solution.py:49
  16.1 33.3 %collective-permute-start.10 = (bf16[1536,512]{1,0:T(8,128)(2,1)}, bf16[1536,512]{1,0:T(8,128)(2,1)}, u32[]{:S(2)}, u32[]{:S(2)}) collective-permute-start(bf16[1536,512]{1,0:T(8,128)(2,1)} %assemble.8), channel_id=1, source_target_pairs={{0,12},{1,13},{2,14},{3,15},{4,0},{5,1},{6,2},{7,3},{8,4},{9,5},{1... | collective-permute-start | bytes 4718600 | tf_op jit(solution)/shard_map/ppermute | solution.py:49
  22.3 0.9 copy-start.4
  23.2 19.4 %copy-start.6 = (s32[64]{0:T(128)S(1)}, s32[64]{0:T(128)}, u32[]{:S(2)}) copy-start(s32[64]{0:T(128)} %param.15) | copy-start | bytes 772
  23.2 19.3 %collective-permute-start.5 = (bf16[768,512]{1,0:T(8,128)(2,1)}, bf16[768,512]{1,0:T(8,128)(2,1)}, u32[]{:S(2)}, u32[]{:S(2)}) collective-permute-start(bf16[768,512]{1,0:T(8,128)(2,1)} %get-tuple-element.75), channel_id=1, source_target_pairs={{0,1},{1,2},{2,3},{3,0},{4,5},{5,6},{6,7},{7,4},{8,9},{9,10},{10,1... | collective-permute-start | bytes 2359304 | tf_op jit(solution)/shard_map/ppermute | solution.py:49
  23.2 28.3 %collective-permute-start.9 = (bf16[1536,512]{1,0:T(8,128)(2,1)}, bf16[1536,512]{1,0:T(8,128)(2,1)}, u32[]{:S(2)}, u32[]{:S(2)}) collective-permute-start(bf16[1536,512]{1,0:T(8,128)(2,1)} %assemble.8), channel_id=1, source_target_pairs={{0,4},{1,5},{2,6},{3,7},{4,8},{5,9},{6,10},{7,11},{8,12},{9,13},{1... | collective-permute-start | bytes 4718600 | tf_op jit(solution)/shard_map/ppermute | solution.py:49
  23.9 21.9 %collective-permute-start.6 = (bf16[768,512]{1,0:T(8,128)(2,1)}, bf16[768,512]{1,0:T(8,128)(2,1)}, u32[]{:S(2)}, u32[]{:S(2)}) collective-permute-start(bf16[768,512]{1,0:T(8,128)(2,1)} %copy-done.4), channel_id=1, source_target_pairs={{0,3},{1,0},{2,1},{3,2},{4,7},{5,4},{6,5},{7,6},{8,11},{9,8},{10,9... | collective-permute-start | bytes 2359304 | tf_op jit(solution)/shard_map/ppermute | solution.py:49
  29.9 21.7 %collective-permute-start.12 = (bf16[2,2,16,64,128]{4,3,2,1,0:T(8,128)(2,1)}, bf16[2,2,16,64,128]{4,3,2,1,0:T(8,128)(2,1)}, u32[]{:S(2)}, u32[]{:S(2)}) collective-permute-start(bf16[2,2,16,64,128]{4,3,2,1,0:T(8,128)(2,1)} %pad_maximum_fusion.refs_0_), channel_id=1, source_target_pairs={{0,16},{1,17},{2,18},{3,19},{4,20},{5,21},{6,22},{7,23},{8,24},{9,... | collective-permute-start | bytes 3145736 | tf_op jit(solution)/shard_map/ppermute | solution.py:49
  42.5 14.3 %collective-permute-start.11 = (bf16[2,2,16,64,128]{4,3,2,1,0:T(8,128)(2,1)}, bf16[2,2,16,64,128]{4,3,2,1,0:T(8,128)(2,1)}, u32[]{:S(2)}, u32[]{:S(2)}) collective-permute-start(bf16[2,2,16,64,128]{4,3,2,1,0:T(8,128)(2,1)} %pad_maximum_fusion.refs_0_), channel_id=1, source_target_pairs={{0,96},{1,97},{2,98},{3,99},{4,100},{5,101},{6,102},{7,103},{8,104... | collective-permute-start | bytes 3145736 | tf_op jit(solution)/shard_map/ppermute | solution.py:49
  47.6 10.3 %collective-permute-start.7 = (bf16[576,512]{1,0:T(8,128)(2,1)S(1)}, bf16[576,512]{1,0:T(8,128)(2,1)S(1)}, u32[]{:S(2)}, u32[]{:S(2)}) collective-permute-start(bf16[576,512]{1,0:T(8,128)(2,1)S(1)} %get-tuple-element.81), channel_id=1, source_target_pairs={{0,4},{1,5},{2,6},{3,7},{4,8},{5,9},{6,10},{7,11},{8,12},{9,13},{1... | collective-permute-start | bytes 1769480 | tf_op jit(solution)/shard_map/ppermute | solution.py:49
  49.4 10.3 %collective-permute-start.8 = (bf16[576,512]{1,0:T(8,128)(2,1)S(1)}, bf16[576,512]{1,0:T(8,128)(2,1)S(1)}, u32[]{:S(2)}, u32[]{:S(2)}) collective-permute-start(bf16[576,512]{1,0:T(8,128)(2,1)S(1)} %get-tuple-element.82), channel_id=1, source_target_pairs={{0,12},{1,13},{2,14},{3,15},{4,0},{5,1},{6,2},{7,3},{8,4},{9,5},{1... | collective-permute-start | bytes 1769480 | tf_op jit(solution)/shard_map/ppermute | solution.py:49
  59.8 24.2 %collective-permute-start.17 = (bf16[2,2,16,64,128]{4,3,2,1,0:T(8,128)(2,1)}, bf16[2,2,16,64,128]{4,3,2,1,0:T(8,128)(2,1)S(1)}, u32[]{:S(2)}, u32[]{:S(2)}) collective-permute-start(bf16[2,2,16,64,128]{4,3,2,1,0:T(8,128)(2,1)} %collective-permute-done.11.refs_1_), channel_id=1, source_target_pairs={{0,16},{1,17},{2,18},{3,19},{4,20},{5,21},{6,22},{7,23},{8,24},{9,... | collective-permute-start | bytes 3145736 | tf_op jit(solution)/shard_map/ppermute | solution.py:49
  65.7 18.3 %collective-permute-start.15 = (bf16[768,512]{1,0:T(8,128)(2,1)S(1)}, bf16[768,512]{1,0:T(8,128)(2,1)S(1)}, u32[]{:S(2)}, u32[]{:S(2)}) collective-permute-start(bf16[768,512]{1,0:T(8,128)(2,1)S(1)} %get-tuple-element.93), channel_id=1, source_target_pairs={{0,4},{1,5},{2,6},{3,7},{4,8},{5,9},{6,10},{7,11},{8,12},{9,13},{1... | collective-permute-start | bytes 2359304 | tf_op jit(solution)/shard_map/ppermute | solution.py:49
  67.7 16.3 %collective-permute-start.16 = (bf16[768,512]{1,0:T(8,128)(2,1)S(1)}, bf16[768,512]{1,0:T(8,128)(2,1)S(1)}, u32[]{:S(2)}, u32[]{:S(2)}) collective-permute-start(bf16[768,512]{1,0:T(8,128)(2,1)S(1)} %get-tuple-element.94), channel_id=1, source_target_pairs={{0,12},{1,13},{2,14},{3,15},{4,0},{5,1},{6,2},{7,3},{8,4},{9,5},{1... | collective-permute-start | bytes 2359304 | tf_op jit(solution)/shard_map/ppermute | solution.py:49
  67.8 13.3 %collective-permute-start.13 = (bf16[384,512]{1,0:T(8,128)(2,1)S(1)}, bf16[384,512]{1,0:T(8,128)(2,1)S(1)}, u32[]{:S(2)}, u32[]{:S(2)}) collective-permute-start(bf16[384,512]{1,0:T(8,128)(2,1)S(1)} %get-tuple-element.91), channel_id=1, source_target_pairs={{0,4},{1,5},{2,6},{3,7},{4,8},{5,9},{6,10},{7,11},{8,12},{9,13},{1... | collective-permute-start | bytes 1179656 | tf_op jit(solution)/shard_map/ppermute | solution.py:49
  70.6 13.4 %collective-permute-start.14 = (bf16[384,512]{1,0:T(8,128)(2,1)S(1)}, bf16[384,512]{1,0:T(8,128)(2,1)S(1)}, u32[]{:S(2)}, u32[]{:S(2)}) collective-permute-start(bf16[384,512]{1,0:T(8,128)(2,1)S(1)} %get-tuple-element.92), channel_id=1, source_target_pairs={{0,12},{1,13},{2,14},{3,15},{4,0},{5,1},{6,2},{7,3},{8,4},{9,5},{1... | collective-permute-start | bytes 1179656 | tf_op jit(solution)/shard_map/ppermute | solution.py:49
  84.0 1.0 copy-start.5
  84.1 6.8 %collective-permute-start.18 = (bf16[512,128]{1,0:T(8,128)(2,1)S(1)}, bf16[512,128]{1,0:T(8,128)(2,1)S(1)}, u32[]{:S(2)}, u32[]{:S(2)}) collective-permute-start(bf16[512,128]{1,0:T(8,128)(2,1)S(1)} %assemble.11.mine_ref), channel_id=1, source_target_pairs={{0,1},{1,0},{2,3},{3,2},{4,5},{5,4},{6,7},{7,6},{8,9},{9,8},{10,11... | collective-permute-start | bytes 393224 | tf_op jit(solution)/shard_map/ppermute | solution.py:49
  97.2 15.5 %collective-permute-start.23 = (bf16[768,512]{1,0:T(8,128)(2,1)S(1)}, bf16[768,512]{1,0:T(8,128)(2,1)S(1)}, u32[]{:S(2)}, u32[]{:S(2)}) collective-permute-start(bf16[768,512]{1,0:T(8,128)(2,1)S(1)} %pad_maximum_fusion.3), channel_id=1, source_target_pairs={{0,4},{1,5},{2,6},{3,7},{4,8},{5,9},{6,10},{7,11},{8,12},{9,13},{1... | collective-permute-start | bytes 2359304 | tf_op jit(solution)/shard_map/ppermute | solution.py:49
  97.6 15.1 %collective-permute-start.24 = (bf16[768,512]{1,0:T(8,128)(2,1)S(1)}, bf16[768,512]{1,0:T(8,128)(2,1)S(1)}, u32[]{:S(2)}, u32[]{:S(2)}) collective-permute-start(bf16[768,512]{1,0:T(8,128)(2,1)S(1)} %pad_maximum_fusion.4), channel_id=1, source_target_pairs={{0,12},{1,13},{2,14},{3,15},{4,0},{5,1},{6,2},{7,3},{8,4},{9,5},{1... | collective-permute-start | bytes 2359304 | tf_op jit(solution)/shard_map/ppermute | solution.py:49
  98.9 13.7 %collective-permute-start.20 = (bf16[256,512]{1,0:T(8,128)(2,1)S(1)}, bf16[256,512]{1,0:T(8,128)(2,1)S(1)}, u32[]{:S(2)}, u32[]{:S(2)}) collective-permute-start(bf16[256,512]{1,0:T(8,128)(2,1)S(1)} %get-tuple-element.161), channel_id=1, source_target_pairs={{0,12},{1,13},{2,14},{3,15},{4,0},{5,1},{6,2},{7,3},{8,4},{9,5},{1... | collective-permute-start | bytes 786440 | tf_op jit(solution)/shard_map/ppermute | solution.py:49
  99.5 13.1 %collective-permute-start.19 = (bf16[256,512]{1,0:T(8,128)(2,1)S(1)}, bf16[256,512]{1,0:T(8,128)(2,1)S(1)}, u32[]{:S(2)}, u32[]{:S(2)}) collective-permute-start(bf16[256,512]{1,0:T(8,128)(2,1)S(1)} %get-tuple-element.162), channel_id=1, source_target_pairs={{0,4},{1,5},{2,6},{3,7},{4,8},{5,9},{6,10},{7,11},{8,12},{9,13},{1... | collective-permute-start | bytes 786440 | tf_op jit(solution)/shard_map/ppermute | solution.py:49
  113.2 8.4 %collective-permute-start.21 = (bf16[512,512]{1,0:T(8,128)(2,1)S(1)}, bf16[512,512]{1,0:T(8,128)(2,1)S(1)}, u32[]{:S(2)}, u32[]{:S(2)}) collective-permute-start(bf16[512,512]{1,0:T(8,128)(2,1)S(1)} %pad_maximum_fusion.5), channel_id=1, source_target_pairs={{0,4},{1,5},{2,6},{3,7},{4,8},{5,9},{6,10},{7,11},{8,12},{9,13},{1... | collective-permute-start | bytes 1572872 | tf_op jit(solution)/shard_map/ppermute | solution.py:49
  113.5 9.8 %collective-permute-start.22 = (bf16[512,512]{1,0:T(8,128)(2,1)S(1)}, bf16[512,512]{1,0:T(8,128)(2,1)S(1)}, u32[]{:S(2)}, u32[]{:S(2)}) collective-permute-start(bf16[512,512]{1,0:T(8,128)(2,1)S(1)} %pad_maximum_fusion.6), channel_id=1, source_target_pairs={{0,12},{1,13},{2,14},{3,15},{4,0},{5,1},{6,2},{7,3},{8,4},{9,5},{1... | collective-permute-start | bytes 1572872 | tf_op jit(solution)/shard_map/ppermute | solution.py:49
  115.2 21.1 %collective-permute-start.27 = (bf16[1024,512]{1,0:T(8,128)(2,1)S(1)}, bf16[1024,512]{1,0:T(8,128)(2,1)S(1)}, u32[]{:S(2)}, u32[]{:S(2)}) collective-permute-start(bf16[1024,512]{1,0:T(8,128)(2,1)S(1)} %pad_maximum_fusion.1), channel_id=1, source_target_pairs={{0,4},{1,5},{2,6},{3,7},{4,8},{5,9},{6,10},{7,11},{8,12},{9,13},{1... | collective-permute-start | bytes 3145736 | tf_op jit(solution)/shard_map/ppermute | solution.py:49
  116.7 20.7 %collective-permute-start.28 = (bf16[1024,512]{1,0:T(8,128)(2,1)S(1)}, bf16[1024,512]{1,0:T(8,128)(2,1)S(1)}, u32[]{:S(2)}, u32[]{:S(2)}) collective-permute-start(bf16[1024,512]{1,0:T(8,128)(2,1)S(1)} %pad_maximum_fusion.2), channel_id=1, source_target_pairs={{0,12},{1,13},{2,14},{3,15},{4,0},{5,1},{6,2},{7,3},{8,4},{9,5},{1... | collective-permute-start | bytes 3145736 | tf_op jit(solution)/shard_map/ppermute | solution.py:49
  123.6 9.2 %collective-permute-start.30 = (bf16[256,512]{1,0:T(8,128)(2,1)S(1)}, bf16[256,512]{1,0:T(8,128)(2,1)S(1)}, u32[]{:S(2)}, u32[]{:S(2)}) collective-permute-start(bf16[256,512]{1,0:T(8,128)(2,1)S(1)} %get-tuple-element.163), channel_id=1, source_target_pairs={{0,3},{1,0},{2,1},{3,2},{4,7},{5,4},{6,5},{7,6},{8,11},{9,8},{10,9... | collective-permute-start | bytes 786440 | tf_op jit(solution)/shard_map/ppermute | solution.py:49
  126.6 9.6 %collective-permute-start.29 = (bf16[256,512]{1,0:T(8,128)(2,1)S(1)}, bf16[256,512]{1,0:T(8,128)(2,1)S(1)}, u32[]{:S(2)}, u32[]{:S(2)}) collective-permute-start(bf16[256,512]{1,0:T(8,128)(2,1)S(1)} %get-tuple-element.164), channel_id=1, source_target_pairs={{0,1},{1,2},{2,3},{3,0},{4,5},{5,6},{6,7},{7,4},{8,9},{9,10},{10,1... | collective-permute-start | bytes 786440 | tf_op jit(solution)/shard_map/ppermute | solution.py:49
  138.1 12.1 %collective-permute-start.32 = (bf16[512,512]{1,0:T(8,128)(2,1)S(1)}, bf16[512,512]{1,0:T(8,128)(2,1)S(1)}, u32[]{:S(2)}, u32[]{:S(2)}) collective-permute-start(bf16[512,512]{1,0:T(8,128)(2,1)S(1)} %pad_maximum_fusion.10), channel_id=1, source_target_pairs={{0,3},{1,0},{2,1},{3,2},{4,7},{5,4},{6,5},{7,6},{8,11},{9,8},{10,9... | collective-permute-start | bytes 1572872 | tf_op jit(solution)/shard_map/ppermute | solution.py:49
  141.2 14.3 %collective-permute-start.26 = (bf16[512,512]{1,0:T(8,128)(2,1)S(1)}, bf16[512,512]{1,0:T(8,128)(2,1)S(1)}, u32[]{:S(2)}, u32[]{:S(2)}) collective-permute-start(bf16[512,512]{1,0:T(8,128)(2,1)S(1)} %pad_maximum_fusion.8), channel_id=1, source_target_pairs={{0,12},{1,13},{2,14},{3,15},{4,0},{5,1},{6,2},{7,3},{8,4},{9,5},{1... | collective-permute-start | bytes 1572872 | tf_op jit(solution)/shard_map/ppermute | solution.py:49
  141.4 14.1 %collective-permute-start.25 = (bf16[512,512]{1,0:T(8,128)(2,1)S(1)}, bf16[512,512]{1,0:T(8,128)(2,1)S(1)}, u32[]{:S(2)}, u32[]{:S(2)}) collective-permute-start(bf16[512,512]{1,0:T(8,128)(2,1)S(1)} %pad_maximum_fusion.7), channel_id=1, source_target_pairs={{0,4},{1,5},{2,6},{3,7},{4,8},{5,9},{6,10},{7,11},{8,12},{9,13},{1... | collective-permute-start | bytes 1572872 | tf_op jit(solution)/shard_map/ppermute | solution.py:49
  144.1 16.4 %copy-start.1 = (s32[64,4]{0,1:T(4,128)S(1)}, s32[64,4]{0,1:T(4,128)}, u32[]{:S(2)}) copy-start(s32[64,4]{0,1:T(4,128)} %param.14) | copy-start | bytes 3076
  144.1 15.2 %collective-permute-start.31 = (bf16[512,512]{1,0:T(8,128)(2,1)S(1)}, bf16[512,512]{1,0:T(8,128)(2,1)S(1)}, u32[]{:S(2)}, u32[]{:S(2)}) collective-permute-start(bf16[512,512]{1,0:T(8,128)(2,1)S(1)} %pad_maximum_fusion.9), channel_id=1, source_target_pairs={{0,1},{1,2},{2,3},{3,0},{4,5},{5,6},{6,7},{7,4},{8,9},{9,10},{10,1... | collective-permute-start | bytes 1572872 | tf_op jit(solution)/shard_map/ppermute | solution.py:49
